TPU v7x, 32 devices: a whole 2x2x4 slice. The times are simulated.
32 devices in a mesh: dp: 16 (over z, x, core), tensor: 2 (over y).
Axes of the slice: x: 2, y: 2, z: 4, core: 2. Of those that a mesh axis runs over, the one named last changes fastest.
Arguments:
- hidden_in: bfloat16 [24576, 1024], P(('dp', 'tensor')), may hold values from -6 to 6
- norm_gain: bfloat16 [1024], P('dp'), may hold values from 0.5 to 1.5
- projection_gate_inner: bfloat16 [1024, 2, 2048], P('dp', None, 'tensor'), may hold values from -0.1875 to 0.1875
- proj_state: bfloat16 [1024, 256], P('dp'), may hold values from -0.1875 to 0.1875
- proj_step: bfloat16 [1024, 32], P('dp', 'tensor'), may hold values from -0.09375 to 0.09375
- conv_inner: bfloat16 [4, 2, 1024], P(None, 'tensor', 'dp'), may hold values from -3 to 3
- conv_inner_bias: bfloat16 [2, 1024], P('tensor', 'dp'), may hold values from -3 to 3
- conv_state: bfloat16 [4, 256], P(None, 'dp'), may hold values from -3 to 3
- conv_state_bias: bfloat16 [256], P('dp'), may hold values from -3 to 3
- decay_log: bfloat16 [32], P('tensor'), may hold values from 0 to 2.75
- skip_gain: bfloat16 [32], P('tensor'), may hold values from 0.5 to 1.5
- step_bias: bfloat16 [32], P('tensor'), may hold values from -4.5 to -1.5
- gate_gain: bfloat16 [2, 1024], P('tensor', 'dp'), may hold values from 0.5 to 1.5
- proj_out: bfloat16 [2048, 1024], P('tensor', 'dp'), may hold values from -0.125 to 0.125
- lengths: int32 [16, 4], P('dp'), may hold values from 0 to 1536, as said below
- cotangent: bfloat16 [24576, 1024], P(('dp', 'tensor')), may hold values from -6 to 6
Outputs:
- block_out: bfloat16 [24576, 1024], P(('dp', 'tensor'))
- grad_hidden: float32 [24576, 1024], P(('dp', 'tensor'))
- grad_norm_gain: float32 [1024], P('dp')
- grad_proj_gate_inner: float32 [1024, 2, 2048], P('dp', None, 'tensor')
- grad_proj_state: float32 [1024, 256], P('dp')
- grad_proj_step: float32 [1024, 32], P('dp', 'tensor')
- grad_conv_inner: float32 [4, 2, 1024], P(None, 'tensor', 'dp')
- grad_conv_inner_bias: float32 [2, 1024], P('tensor', 'dp')
- grad_conv_state: float32 [4, 256], P(None, 'dp')
- grad_conv_state_bias: float32 [256], P('dp')
- grad_decay_log: float32 [32], P('tensor')
- grad_skip_gain: float32 [32], P('tensor')
- grad_step_bias: float32 [32], P('tensor')
- grad_gate_gain: float32 [2, 1024], P('tensor', 'dp')
- grad_proj_out: float32 [2048, 1024], P('tensor', 'dp')
Inputs may be any that keep to these rules, and one draw needn't show every extreme that they name: Row d lists the lengths of the sequences packed from the start of block d; each row sums to at most 1536; in every draw some row is one sequence of 1536 tokens.
All inputs are finite; a program needn't handle non-finite values.
Results may differ from a plain program's by a relative error of at most 0.012.
Values may be sent and summed in bfloat16 or wider, within the bound.
No kernel may reach another device: no remote copies, remote signals or barrier semaphores. Data moves between devices by JAX's collectives and lax.ppermute only.
A program may use at most 192 MiB of HBM per device.

v0:
```python
import jax
import jax.numpy as jnp
from jax import lax
from jax.sharding import PartitionSpec as P

GROUP = 256


norm_eps = 1e-05
highest_precision_mode = lax.Precision.HIGHEST


def sequence_layout(lengths_row, block_len):
    places = jnp.arange(block_len, dtype=jnp.int32)
    seq_ends = jnp.cumsum(lengths_row)
    starts = seq_ends - lengths_row
    seq_ids = jnp.sum((places[:, None] >= seq_ends[None, :]).astype(jnp.int32), axis=1)
    slot_count = lengths_row.shape[0]
    bounds = jnp.concatenate([starts, seq_ends[-1:]])
    labels = jnp.arange(slot_count + 1, dtype=jnp.int32)
    own_start = jnp.sum(jnp.where(seq_ids[:, None] == labels[None, :], bounds[None, :], 0), axis=1)
    return (seq_ids, places - own_start, seq_ids < slot_count)


def group_masks(seq_ids, group_count, group_len):
    seq_groups = seq_ids.reshape(group_count, group_len)
    tail_ids = seq_groups[:, -1]
    inner_index = jnp.arange(group_len, dtype=jnp.int32)
    intra_mask = (seq_groups[:, :, None] == seq_groups[:, None, :]) & (
        inner_index[:, None] >= inner_index[None, :]
    )[None]
    tail_mask = seq_groups == tail_ids[:, None]
    prev_tail = jnp.concatenate([jnp.full((1,), -1, jnp.int32), tail_ids[:-1]])
    enter_mask = seq_groups == prev_tail[:, None]
    carry_mask = tail_ids == prev_tail
    return (intra_mask, tail_mask, enter_mask, carry_mask)


def causal_conv(values, kernel, offset_row, position):
    steps_all = kernel.shape[0]
    channels = values.shape[1]
    summed = offset_row[None, :] + kernel[steps_all - 1][None, :] * values
    for offset in range(1, steps_all):
        earlier = jnp.concatenate(
            [jnp.zeros((offset, channels), values.dtype), values[:-offset]], axis=0
        )
        summed = summed + jnp.where(
            position[:, None] >= offset, kernel[steps_all - 1 - offset][None, :] * earlier, 0.0
        )
    return summed


def conv_backward(upstream, values, kernel, position):
    steps_all = kernel.shape[0]
    channels = values.shape[1]
    grad_values = kernel[steps_all - 1][None, :] * upstream
    kernel_rows = [jnp.sum(upstream * values, axis=0)]
    for offset in range(1, steps_all):
        masked = jnp.where(position[:, None] >= offset, upstream, 0.0)
        kernel_rows.append(jnp.sum(masked[offset:] * values[:-offset], axis=0))
        grad_values = grad_values + jnp.concatenate(
            [
                kernel[steps_all - 1 - offset][None, :] * masked[offset:],
                jnp.zeros((offset, channels), upstream.dtype),
            ],
            axis=0,
        )
    return (grad_values, jnp.stack(kernel_rows[::-1]), jnp.sum(upstream, axis=0))


def silu_slope(values):
    logistic = jax.nn.sigmoid(values)
    return logistic * (1.0 + values * (1.0 - logistic))


def group_terms(cum_head, step_head, scores_c, masks):
    intra_mask, tail_mask, enter_mask, carry_mask = masks
    group_count, group_len = tail_mask.shape
    cum_c = cum_head.reshape(group_count, group_len)
    step_c = step_head.reshape(group_count, group_len)
    last_cum = cum_c[:, -1]
    prev_cum = jnp.concatenate([jnp.zeros((1,), jnp.float32), last_cum[:-1]])
    log_gap = cum_c[:, :, None] - cum_c[:, None, :]
    factor = jnp.exp(jnp.where(intra_mask, log_gap, 0.0))
    weights = jnp.where(intra_mask, factor * scores_c * step_c[:, None, :], 0.0)
    key_factor = jnp.where(tail_mask, jnp.exp(last_cum[:, None] - cum_c), 0.0)
    query_factor = jnp.where(enter_mask, jnp.exp(cum_c - prev_cum[:, None]), 0.0)
    state_decay = jnp.where(carry_mask, jnp.exp(last_cum - prev_cum), 0.0)
    return (step_c, factor, weights, key_factor, query_factor, state_decay)


def group_states(decayed, values_c, state_decay):
    group_state = jnp.einsum("csn,csp->cnp", decayed, values_c, preferred_element_type=jnp.float32)

    def advance(state_now, pieces):
        return (pieces[0] * state_now + pieces[1], state_now)

    initial = jnp.zeros(group_state.shape[1:], jnp.float32)
    final_state, prev_states = lax.scan(advance, initial, (state_decay, group_state))
    return prev_states


def on_device(
    hidden_in,
    norm_gain,
    projection_gate_inner,
    proj_state,
    proj_step,
    conv_inner,
    conv_inner_bias,
    conv_state,
    conv_state_bias,
    decay_log,
    skip_gain,
    step_bias,
    gate_gain,
    proj_out,
    lengths,
    cotangent,
):
    tensor_count = lax.axis_size("tensor")
    tensor_rank = lax.axis_index("tensor")
    shard_rank = lax.axis_index("dp")
    shard_count = lax.axis_size("dp")
    half_rows = hidden_in.shape[0]
    model_width = hidden_in.shape[1]
    block_len = half_rows * tensor_count
    inner_local = proj_out.shape[0]
    heads_local = decay_log.shape[0]
    head_size = inner_local // heads_local
    state_size = proj_state.shape[1] // 2
    inner_all = inner_local * tensor_count
    kernel_len = conv_inner.shape[0]
    group_len = GROUP
    group_count = block_len // group_len
    gathered = (
        lax.all_gather(norm_gain, "dp", axis=0, tiled=True),
        lax.all_gather(projection_gate_inner, "dp", axis=0, tiled=True),
        lax.all_gather(proj_state, "dp", axis=0, tiled=True),
        lax.all_gather(proj_step, "dp", axis=0, tiled=True),
        lax.all_gather(conv_inner, "dp", axis=2, tiled=True),
        lax.all_gather(conv_inner_bias, "dp", axis=1, tiled=True),
        lax.all_gather(conv_state, "dp", axis=1, tiled=True),
        lax.all_gather(conv_state_bias, "dp", axis=0, tiled=True),
        lax.all_gather(gate_gain, "dp", axis=1, tiled=True),
        lax.all_gather(proj_out, "dp", axis=1, tiled=True),
    )
    norm_gain_all = gathered[0]
    gate_inner_all = gathered[1]
    state_proj_all = gathered[2]
    step_proj_all = gathered[3]
    inner_kernel_all = gathered[4]
    inner_bias_all = gathered[5]
    state_kernel_all = gathered[6]
    state_bias_all = gathered[7]
    gate_gain_all = gathered[8]
    out_proj_all = gathered[9]
    seq_ids, position, valid_rows = sequence_layout(lengths[0], block_len)
    valid_half = lax.dynamic_slice_in_dim(valid_rows, tensor_rank * half_rows, half_rows)
    masks = group_masks(seq_ids, group_count, group_len)
    intra_mask = masks[0]
    last_slot = jnp.arange(group_len, dtype=jnp.int32) == group_len - 1
    hidden_wide = hidden_in.astype(jnp.float32)
    inv_rms = lax.rsqrt(jnp.mean(hidden_wide * hidden_wide, axis=1, keepdims=True) + norm_eps)
    normed_half = (hidden_wide * inv_rms * norm_gain_all.astype(jnp.float32)[None, :]).astype(
        jnp.bfloat16
    )
    normalized_rows = lax.all_gather(normed_half, "tensor", axis=0, tiled=True)
    gate_inner_preactivation = jnp.dot(
        normalized_rows,
        gate_inner_all.reshape(model_width, 2 * inner_local),
        preferred_element_type=jnp.float32,
    ).reshape(block_len, 2, inner_local)
    gate_pre = gate_inner_preactivation[:, 0]
    inner_pre = gate_inner_preactivation[:, 1]
    state_pre = jnp.dot(normalized_rows, state_proj_all, preferred_element_type=jnp.float32)
    step_pre = jnp.dot(normalized_rows, step_proj_all, preferred_element_type=jnp.float32)
    inner_conv = causal_conv(
        inner_pre,
        inner_kernel_all.reshape(kernel_len, inner_local).astype(jnp.float32),
        inner_bias_all.reshape(inner_local).astype(jnp.float32),
        position,
    )
    state_conv = causal_conv(
        state_pre,
        state_kernel_all.astype(jnp.float32),
        state_bias_all.astype(jnp.float32),
        position,
    )
    inner_act = jax.nn.silu(inner_conv).astype(jnp.bfloat16)
    state_act = jax.nn.silu(state_conv).astype(jnp.bfloat16)
    keys_c = state_act[:, :state_size].reshape(group_count, group_len, state_size)
    queries_c = state_act[:, state_size:].reshape(group_count, group_len, state_size)
    keys_wide = keys_c.astype(jnp.float32)
    queries_wide = queries_c.astype(jnp.float32)
    step_in = step_pre + step_bias.astype(jnp.float32)[None, :]
    step_size = jax.nn.softplus(step_in)
    decay_rate = -jnp.exp(decay_log.astype(jnp.float32))
    cum_decay = jnp.cumsum(step_size * decay_rate[None, :], axis=0)
    scores_c = jnp.einsum("ctn,csn->cts", queries_c, keys_c, preferred_element_type=jnp.float32)
    inner_heads = inner_act.reshape(block_len, heads_local, head_size).transpose(1, 0, 2)

    def forward_head(carried):
        cum_head, step_head, values_head = carried
        step_c, factor, weights, key_factor, query_factor, state_decay = group_terms(
            cum_head, step_head, scores_c, masks
        )
        values_c = values_head.reshape(group_count, group_len, head_size)
        intra_part = jnp.einsum(
            "cts,csp->ctp",
            weights.astype(jnp.bfloat16),
            values_c,
            preferred_element_type=jnp.float32,
        )
        decayed = ((key_factor * step_c)[:, :, None] * keys_wide).astype(jnp.bfloat16)
        prev_states = group_states(decayed, values_c, state_decay)
        inter_part = query_factor[:, :, None] * jnp.einsum(
            "ctn,cnp->ctp", queries_wide, prev_states, precision=highest_precision_mode
        )
        return (intra_part + inter_part).reshape(block_len, head_size)

    mixed_heads = lax.map(forward_head, (cum_decay.T, step_size.T, inner_heads))
    inner_values = inner_act.reshape(block_len, heads_local, head_size).astype(jnp.float32)
    skip_wide = skip_gain.astype(jnp.float32)
    mixed = (mixed_heads.transpose(1, 0, 2) + skip_wide[None, :, None] * inner_values).reshape(
        block_len, inner_local
    )
    silu_gate = jax.nn.silu(gate_pre)
    gated = mixed * silu_gate
    square_sum = lax.psum(jnp.sum(gated * gated, axis=1), "tensor")
    inv_gate = lax.rsqrt(square_sum / inner_all + norm_eps)
    out_low = (
        gated * inv_gate[:, None] * gate_gain_all.reshape(inner_local).astype(jnp.float32)[None, :]
    ).astype(jnp.bfloat16)
    mix_part = jnp.dot(out_low, out_proj_all, preferred_element_type=jnp.float32)
    mix_half = lax.psum_scatter(
        mix_part.astype(jnp.bfloat16), "tensor", scatter_dimension=0, tiled=True
    ).astype(jnp.float32)
    block_out = (hidden_wide + jnp.where(valid_half[:, None], mix_half, 0.0)).astype(jnp.bfloat16)
    cotangent_all = lax.all_gather(cotangent, "tensor", axis=0, tiled=True)
    cotangent_live = jnp.where(valid_rows[:, None], cotangent_all, jnp.zeros_like(cotangent_all))
    grad_proj_out = lax.dot_general(
        out_low, cotangent_live, (((0,), (0,)), ((), ())), preferred_element_type=jnp.float32
    )
    grad_out_low = lax.dot_general(
        cotangent_live, out_proj_all, (((1,), (1,)), ((), ())), preferred_element_type=jnp.float32
    )
    grad_gate_gain = jnp.sum(grad_out_low * gated * inv_gate[:, None], axis=0)
    scaled = grad_out_low * gate_gain_all.reshape(inner_local).astype(jnp.float32)[None, :]
    inner_dot = lax.psum(jnp.sum(scaled * gated, axis=1), "tensor")
    grad_gated = inv_gate[:, None] * scaled - gated * (inv_gate**3 * inner_dot / inner_all)[:, None]
    grad_mixed = grad_gated * silu_gate
    grad_gate_pre = grad_gated * mixed * silu_slope(gate_pre)
    grad_mixed_heads = grad_mixed.reshape(block_len, heads_local, head_size)
    grad_skip = jnp.sum(grad_mixed_heads * inner_values, axis=(0, 2))
    grad_rounded = grad_mixed_heads.transpose(1, 0, 2).astype(jnp.bfloat16)

    def backward_head(totals, carried):
        grad_scores, grad_query_acc, grad_key_acc = totals
        cum_head, step_head, values_head, upstream = carried
        step_c, factor, weights, key_factor, query_factor, state_decay = group_terms(
            cum_head, step_head, scores_c, masks
        )
        values_c = values_head.reshape(group_count, group_len, head_size)
        upstream_group_rows = upstream.reshape(group_count, group_len, head_size)
        key_step = key_factor * step_c
        decayed = (key_step[:, :, None] * keys_wide).astype(jnp.bfloat16)
        prev_states = group_states(decayed, values_c, state_decay)
        grad_weights = jnp.where(
            intra_mask,
            jnp.einsum(
                "ctp,csp->cts", upstream_group_rows, values_c, preferred_element_type=jnp.float32
            ),
            0.0,
        )
        grad_values = jnp.einsum(
            "cts,ctp->csp",
            weights.astype(jnp.bfloat16),
            upstream_group_rows,
            preferred_element_type=jnp.float32,
        )
        product = grad_weights * factor
        grad_scores = grad_scores + product * step_c[:, None, :]
        grad_step = jnp.sum(product * scores_c, axis=1)
        grad_gap = product * scores_c * step_c[:, None, :]
        grad_cum = jnp.sum(grad_gap, axis=2) - jnp.sum(grad_gap, axis=1)
        upstream_wide = upstream_group_rows.astype(jnp.float32)
        state_read = jnp.einsum(
            "ctn,cnp->ctp", queries_wide, prev_states, precision=highest_precision_mode
        )
        entry_term = jnp.sum(upstream_wide * state_read, axis=2) * query_factor
        grad_query_acc = grad_query_acc + query_factor[:, :, None] * jnp.einsum(
            "ctp,cnp->ctn", upstream_wide, prev_states, precision=highest_precision_mode
        )
        grad_read = jnp.einsum(
            "ctn,ctp->cnp",
            queries_wide * query_factor[:, :, None],
            upstream_wide,
            precision=highest_precision_mode,
        )
        shifted_read = jnp.concatenate([grad_read[1:], jnp.zeros_like(grad_read[:1])])
        decay_shifted_down = jnp.concatenate([state_decay[1:], jnp.zeros((1,), jnp.float32)])

        def retreat(grad_next, pieces):
            grad_now = pieces[1] + pieces[0] * grad_next
            return (grad_now, grad_now)

        final_grad, grad_states = lax.scan(
            retreat, jnp.zeros_like(grad_read[0]), (decay_shifted_down, shifted_read), reverse=True
        )
        decay_term = jnp.sum(grad_states * prev_states, axis=(1, 2)) * state_decay
        grad_decayed = jnp.einsum(
            "csp,cnp->csn",
            values_c.astype(jnp.float32),
            grad_states,
            precision=highest_precision_mode,
        )
        grad_values = grad_values + jnp.einsum(
            "csn,cnp->csp",
            decayed.astype(jnp.float32),
            grad_states,
            precision=highest_precision_mode,
        )
        grad_key_acc = grad_key_acc + key_step[:, :, None] * grad_decayed
        key_dot = jnp.sum(grad_decayed * keys_wide, axis=2)
        grad_step = grad_step + key_dot * key_factor
        key_term = key_dot * key_step
        grad_cum = grad_cum + entry_term - key_term
        from_prev = jnp.sum(entry_term, axis=1) + decay_term
        to_last = (
            jnp.sum(key_term, axis=1)
            + decay_term
            - jnp.concatenate([from_prev[1:], jnp.zeros((1,), jnp.float32)])
        )
        grad_cum = grad_cum + jnp.where(last_slot[None, :], to_last[:, None], 0.0)
        return (
            (grad_scores, grad_query_acc, grad_key_acc),
            (
                grad_values.reshape(block_len, head_size),
                grad_step.reshape(block_len),
                grad_cum.reshape(block_len),
            ),
        )

    score_zero = jnp.zeros((group_count, group_len, group_len), jnp.float32)
    state_zero = jnp.zeros((group_count, group_len, state_size), jnp.float32)
    totals, outputs_heads = lax.scan(
        backward_head,
        (score_zero, state_zero, state_zero),
        (cum_decay.T, step_size.T, inner_heads, grad_rounded),
    )
    grad_scores, grad_query_acc, grad_key_acc = totals
    grad_values_heads, grad_step_direct, grad_cum = outputs_heads
    gradient_logarithm_decay = lax.cumsum(grad_cum, axis=1, reverse=True)
    grad_step_total = grad_step_direct + gradient_logarithm_decay * decay_rate[:, None]
    grad_decay_local = jnp.sum(gradient_logarithm_decay * step_size.T, axis=1) * decay_rate
    grad_step_in = grad_step_total * jax.nn.sigmoid(step_in.T)
    grad_step_bias_local = jnp.sum(grad_step_in, axis=1)
    grad_step_low = grad_step_in.T.astype(jnp.bfloat16)
    grad_queries = (
        grad_query_acc
        + jnp.einsum("cts,csn->ctn", grad_scores, keys_wide, precision=highest_precision_mode)
    ).reshape(block_len, state_size)
    grad_keys = (
        grad_key_acc
        + jnp.einsum("cts,ctn->csn", grad_scores, queries_wide, precision=highest_precision_mode)
    ).reshape(block_len, state_size)
    grad_state_act = lax.psum(
        jnp.concatenate([grad_keys, grad_queries], axis=1).astype(jnp.bfloat16), "tensor"
    ).astype(jnp.float32)
    grad_inner_act = (
        grad_values_heads.transpose(1, 0, 2) + skip_wide[None, :, None] * grad_mixed_heads
    ).reshape(block_len, inner_local)
    grad_inner_pre, grad_kernel_inner, grad_bias_inner = conv_backward(
        grad_inner_act * silu_slope(inner_conv),
        inner_pre,
        inner_kernel_all.reshape(kernel_len, inner_local).astype(jnp.float32),
        position,
    )
    grad_state_pre, grad_kernel_state, grad_bias_state = conv_backward(
        grad_state_act * silu_slope(state_conv),
        state_pre,
        state_kernel_all.astype(jnp.float32),
        position,
    )
    grad_zx_low = (
        jnp.stack([grad_gate_pre, grad_inner_pre], axis=1)
        .astype(jnp.bfloat16)
        .reshape(block_len, 2 * inner_local)
    )
    grad_state_low = grad_state_pre.astype(jnp.bfloat16)
    grad_proj_gate_inner = lax.dot_general(
        normalized_rows, grad_zx_low, (((0,), (0,)), ((), ())), preferred_element_type=jnp.float32
    ).reshape(model_width, 2, inner_local)
    grad_proj_state = lax.dot_general(
        normalized_rows,
        grad_state_low,
        (((0,), (0,)), ((), ())),
        preferred_element_type=jnp.float32,
    )
    grad_proj_step = lax.dot_general(
        normalized_rows, grad_step_low, (((0,), (0,)), ((), ())), preferred_element_type=jnp.float32
    )
    state_term = lax.dot_general(
        grad_state_low, state_proj_all, (((1,), (1,)), ((), ())), preferred_element_type=jnp.float32
    )
    grad_normed = lax.dot_general(
        grad_zx_low,
        gate_inner_all.reshape(model_width, 2 * inner_local),
        (((1,), (1,)), ((), ())),
        preferred_element_type=jnp.float32,
    )
    grad_normed = grad_normed + lax.dot_general(
        grad_step_low, step_proj_all, (((1,), (1,)), ((), ())), preferred_element_type=jnp.float32
    )
    grad_normed = grad_normed + jnp.where(tensor_rank == 0, state_term, 0.0)
    grad_normed_half = lax.psum_scatter(
        grad_normed.astype(jnp.bfloat16), "tensor", scatter_dimension=0, tiled=True
    ).astype(jnp.float32)
    grad_gain_local = jnp.sum(grad_normed_half * hidden_wide * inv_rms, axis=0)
    scaled_in = grad_normed_half * norm_gain_all.astype(jnp.float32)[None, :]
    grad_hidden = (
        inv_rms * scaled_in
        - hidden_wide * inv_rms**3 * jnp.mean(scaled_in * hidden_wide, axis=1, keepdims=True)
        + cotangent.astype(jnp.float32)
    )
    heads_all = heads_local * tensor_count
    head_terms = jnp.stack([grad_decay_local, grad_skip, grad_step_bias_local])
    head_vector = lax.dynamic_update_slice_in_dim(
        jnp.zeros((3, heads_all), jnp.float32), head_terms, tensor_rank * heads_local, 1
    )
    head_sum, gain_sum = lax.psum((head_vector, grad_gain_local), ("dp", "tensor"))
    own_heads = lax.dynamic_slice_in_dim(head_sum, tensor_rank * heads_local, heads_local, 1)
    gain_shard = model_width // shard_count
    grad_norm_gain = lax.dynamic_slice_in_dim(gain_sum, shard_rank * gain_shard, gain_shard)
    summed = (
        lax.psum_scatter(grad_proj_gate_inner, "dp", scatter_dimension=0, tiled=True),
        lax.psum_scatter(grad_proj_state, "dp", scatter_dimension=0, tiled=True),
        lax.psum_scatter(grad_proj_step, "dp", scatter_dimension=0, tiled=True),
        lax.psum_scatter(
            grad_kernel_inner.reshape(kernel_len, 1, inner_local),
            "dp",
            scatter_dimension=2,
            tiled=True,
        ),
        lax.psum_scatter(
            grad_bias_inner.reshape(1, inner_local), "dp", scatter_dimension=1, tiled=True
        ),
        lax.psum_scatter(grad_kernel_state, "dp", scatter_dimension=1, tiled=True),
        lax.psum_scatter(grad_bias_state, "dp", scatter_dimension=0, tiled=True),
        lax.psum_scatter(
            grad_gate_gain.reshape(1, inner_local), "dp", scatter_dimension=1, tiled=True
        ),
        lax.psum_scatter(grad_proj_out, "dp", scatter_dimension=1, tiled=True),
    )
    out_grad_final = summed[8]
    return (
        block_out,
        grad_hidden,
        grad_norm_gain,
        summed[0],
        summed[1],
        summed[2],
        summed[3],
        summed[4],
        summed[5],
        summed[6],
        own_heads[0],
        own_heads[1],
        own_heads[2],
        summed[7],
        out_grad_final,
    )


def solution(mesh):
    placed = (
        P(("dp", "tensor"), None),
        P("dp"),
        P("dp", None, "tensor"),
        P("dp", None),
        P("dp", "tensor"),
        P(None, "tensor", "dp"),
        P("tensor", "dp"),
        P(None, "dp"),
        P("dp"),
        P("tensor"),
        P("tensor"),
        P("tensor"),
        P("tensor", "dp"),
        P("tensor", "dp"),
        P("dp", None),
        P(("dp", "tensor"), None),
    )
    return jax.shard_map(
        on_device,
        mesh=mesh,
        in_specs=placed,
        out_specs=(
            P(("dp", "tensor"), None),
            P(("dp", "tensor"), None),
            P("dp"),
            P("dp", None, "tensor"),
            P("dp", None),
            P("dp", "tensor"),
            P(None, "tensor", "dp"),
            P("tensor", "dp"),
            P(None, "dp"),
            P("dp"),
            P("tensor"),
            P("tensor"),
            P("tensor"),
            P("tensor", "dp"),
            P("tensor", "dp"),
        ),
        check_vma=False,
    )
```

profile of v0, /device:TPU:0, one launch (start us, length us, event | category | flops | bytes accessed | tf_op | source)
XLA Modules:
  0.0 1938.5 jit_solution(11757749403528694896)
XLA Ops:
  13.2 35.4 %all-reduce.19 = (bf16[1024]{0:T(1024)(128)(2,1)S(1)}, bf16[256]{0:T(256)(128)(2,1)S(1)}, bf16[1024]{0:T(1024)(128)(2,1)S(1)}, bf16[1024]{0:T(1024)(128)(2,1)S(1)}) all-reduce(bf16[1024]{0:T(1024)(128)(2,1)S(1)} %dynamic-update-slice, bf16[256]{0:T(256)(128)(2,1)S(1)} %dynamic-update-slice.1, ...), channel_id=1, replica_groups=mesh['dp'=16,'tensor'=2] {'dp'}, use_global_device_ids=true, to_apply=%add.13 | all-reduce | flops 3328 | bytes 13312
  65.7 17.1 all-gather.1
  83.1 19.2 all-gather
  102.5 19.8 %all_gather.43 = bf16[4,1,1024]{0,1,2:T(2,128)(2,1)S(1)} all-gather(bf16[4,1,64]{0,1,2:T(2,128)(2,1)S(1)} %copy.406), channel_id=1, replica_groups=mesh['dp'=16,'tensor'=2] {'dp'}, dimensions={2}, use_global_device_ids=true | all-gather | bytes 8704 | tf_op jit(solution)/shard_map/all_gather | solution.py:141
  122.9 21.8 %slice_reduce_fusion.7 = (f32[1024]{0:T(1024)S(1)}, f32[1024]{0:T(1024)S(1)}, f32[1024]{0:T(1024)S(1)}, f32[1024]{0:T(1024)S(1)}) fusion(f32[4,1,1024]{0,1,2:T(1,128)S(1)} %convert_element_type.146), kind=kLoop, calls=%fused_computation.201 | loop fusion | bytes 32768 | tf_op jit(solution)/shard_map/slice | solution.py:42
  144.8 21.4 %all_gather.41 = bf16[1024,256]{1,0:T(8,128)(2,1)S(1)} all-gather(bf16[64,256]{1,0:T(8,128)(2,1)S(1)} %copy-done.52), channel_id=1, replica_groups=mesh['dp'=16,'tensor'=2] {'dp'}, dimensions={0}, use_global_device_ids=true | all-gather | bytes 557056 | tf_op jit(solution)/shard_map/all_gather | solution.py:139
  188.8 11.2 fusion.60
  209.2 11.3 multiply_convert_fusion.6
  228.6 273.6 %while.121 = (s32[]{:T(128)}, f32[16,1536,64]{1,2,0:T(8,128)}, f32[16,1536]{1,0:T(8,128)}, f32[6,256,256]{2,1,0:T(8,128)}, f32[16,1536]{1,0:T(8,128)S(1)}, /*ind...) while((s32[]{:T(128)}, f32[16,1536,64]{1,2,0:T(8,128)}, ...), condition=%wide.region_9.10_spmd.clone.clone, body=%wide.region_6.9_spmd.clone.sunk.clone | while | flops 230268432 | bytes 8660559 | solution.py:222
  235.3 7.7 while.120
  252.4 7.7 while.120
  269.4 7.7 while.120
  286.5 7.7 while.120
  303.6 7.7 while.120
  320.6 7.7 while.120
  337.7 7.7 while.120
  354.8 7.7 while.120
  371.9 7.7 while.120
  388.9 7.7 while.120
  406.0 7.7 while.120
  423.0 7.7 while.120
  440.1 7.7 while.120
  457.2 7.7 while.120
  474.2 7.7 while.120
  515.4 8.6 multiply_reduce_fusion.14
  535.8 13.5 multiply_reduce_fusion.7
  554.3 11.9 fusion.56
  590.5 631.5 %while.124 = (s32[]{:T(128)}, f32[6,256,256]{2,1,0:T(8,128)}, f32[6,256,128]{2,1,0:T(8,128)}, f32[6,256,128]{1,2,0:T(8,128)}, f32[16,1536,64]{1,2,0:T(8,128)}, /...) while((s32[]{:T(128)}, f32[6,256,256]{2,1,0:T(8,128)}, ...), condition=%wide.region_28.29_spmd.clone.clone, body=%wide.region_15.28_spmd.clone.sunk.clone | while | flops 867421504 | bytes 30606508 | solution.py:347
  604.2 8.3 while.123
  641.1 8.3 while.123
  680.7 8.3 while.123
  720.4 8.3 while.123
  760.0 8.3 while.123
  799.6 8.3 while.123
  839.2 8.3 while.123
  878.8 8.3 while.123
  918.5 8.3 while.123
  958.1 8.3 while.123
  997.7 8.3 while.123
  1037.4 8.3 while.123
  1077.0 8.3 while.123
  1116.6 8.3 while.123
  1156.3 8.3 while.123
  1195.9 8.3 while.123
  1222.0 9.0 bitcast_add_fusion.4
  1239.5 21.1 %reduce-window.21 = f32[16,12,128]{2,1,0:T(8,128)} reduce-window(f32[16,12,128]{2,1,0:T(8,128)} %reshape.586, f32[]{:T(128)} %constant.193.clone.1), window={size=1x1x128 pad=0_0x0_0x0_127}, to_apply=%region_29.30 | reduce-window | flops 3121152 | bytes 196612 | tf_op jit(solution)/shard_map/reduce-window.3
  1268.6 8.3 fusion.100
  1276.9 7.8 multiply_reduce_fusion.10
  1309.8 10.3 add_bitcast_fusion
  1321.7 8.7 fusion.110
  1351.1 7.8 convolution_convert_fusion
  1365.9 8.8 copy.424
  1374.8 10.9 fusion.46
  1389.0 9.4 fusion.80
  1401.2 17.0 reduce-scatter.35.cloned.1.call-done
  1419.6 57.4 %reduce-scatter.33.cloned.1.call-done = f32[64,4]{1,0:T(8,128)} async-done(((f32[1024,4]{1,0:T(8,128)}), f32[64,4]{1,0:T(8,128)}) %reduce-scatter.33.cloned.1.call-update) | async-done | bytes 1040
  1478.5 56.8 %reduce-scatter.31.cloned.1.call-done = f32[64,16]{1,0:T(8,128)} async-done(((f32[1024,16]{1,0:T(8,128)}), f32[64,16]{1,0:T(8,128)}) %reduce-scatter.31.cloned.1.call-update) | async-done | bytes 4112
  1536.7 29.8 %all-reduce.17 = f32[256]{0:T(256)S(1)} all-reduce(f32[256]{0:T(256)S(1)} %get-tuple-element.1203), channel_id=10, replica_groups=mesh['dp'=16,'tensor'=2] {'dp'}, use_global_device_ids=true, to_apply=%region_52.53.clone | all-reduce | flops 256 | bytes 2048
  1567.1 26.0 %reduce-scatter.37.cloned.1.call-done = f32[16,4]{1,0:T(8,128)} async-done(((f32[256,4]{1,0:T(8,128)}), f32[16,4]{1,0:T(8,128)}) %reduce-scatter.37.cloned.1.call-update) | async-done | bytes 272
  1594.5 44.0 %reduce-scatter.23.cloned.1.call-done = bf16[768,1024]{1,0:T(8,128)(2,1)} async-done(((bf16[1536,1024]{1,0:T(8,128)(2,1)}), bf16[768,1024]{1,0:T(8,128)(2,1)}) %reduce-scatter.23.cloned.1.call-update) | async-done | bytes 1572880 | tf_op jit(solution)/shard_map/reduce_scatter | solution.py:417
  1641.2 39.9 %all-reduce.18 = (f32[1024]{0:T(1024)S(1)}, f32[3,32]{1,0:T(4,128)S(1)}) all-reduce(f32[1024]{0:T(1024)S(1)} %get-tuple-element.1201, f32[3,32]{1,0:T(4,128)S(1)} %dynamic_update_slice.50), channel_id=1, replica_groups=mesh['dp'=16,'tensor'=2] {'dp','tensor'}, use_global_device_ids=true, to_apply=%region_35.36 | all-reduce | flops 1120 | bytes 8960 | tf_op jit(solution)/shard_map/psum | solution.py:432
  1689.6 104.7 %reduce-scatter.25.cloned.1.call-done = f32[64,2,1024]{2,0,1:T(8,128)} async-done(((f32[1024,2,1024]{2,0,1:T(8,128)}), f32[64,2,1024]{2,0,1:T(8,128)}) %reduce-scatter.25.cloned.1.call-update) | async-done | bytes 524304 | tf_op jit(solution)/shard_map/reduce_scatter | solution.py:437
  1796.6 59.5 %reduce-scatter.27.cloned.1.call-done = f32[64,256]{1,0:T(8,128)} async-done(((f32[1024,256]{1,0:T(8,128)}), f32[64,256]{1,0:T(8,128)}) %reduce-scatter.27.cloned.1.call-update) | async-done | bytes 65552 | tf_op jit(solution)/shard_map/reduce_scatter | solution.py:438
  1856.0 75.7 %reduce-scatter.29.cloned.1.call-done = f32[1024,64]{0,1:T(8,128)} async-done(((f32[1024,1024]{0,1:T(8,128)}), f32[1024,64]{0,1:T(8,128)}) %reduce-scatter.29.cloned.1.call-update) | async-done | bytes 262160 | tf_op jit(solution)/shard_map/reduce_scatter | solution.py:454
  (2590 shorter events, 1226.8 us)
Async XLA Ops:
  7.2 159.0 %all-gather.7.cloned.1.call-start = ((), (), s32[]{:S(2)}) async-start(), calls=%async_computation.10 | async-start | bytes 4718592 | tf_op jit(solution)/shard_map/all_gather | solution.py:168
  51.7 14.0 copy-start.75
  51.7 31.3 %copy-start.76 = (bf16[4,1,64]{2,0,1:T(4,128)(2,1)S(1)}, bf16[4,1,64]{2,0,1:T(4,128)(2,1)}, u32[]{:S(2)}) copy-start(bf16[4,1,64]{2,0,1:T(4,128)(2,1)} %param.31) | copy-start | bytes 1540
  51.7 31.4 %copy-start.73 = (bf16[64,16]{0,1:T(8,128)(2,1)S(1)}, bf16[64,16]{0,1:T(8,128)(2,1)}, u32[]{:S(2)}) copy-start(bf16[64,16]{0,1:T(8,128)(2,1)} %param.30) | copy-start | bytes 6148
  54.8 127.8 %all-gather.9.cloned.1.call-start = ((), (), s32[]{:S(2)}) async-start(), calls=%async_computation.11 | async-start | bytes 4456448 | tf_op jit(solution)/shard_map/all_gather | solution.py:138
  55.6 89.1 %copy-start.52 = (bf16[64,256]{1,0:T(8,128)(2,1)S(1)}, bf16[64,256]{1,0:T(8,128)(2,1)}, u32[]{:S(2)}) copy-start(bf16[64,256]{1,0:T(8,128)(2,1)} %param.29) | copy-start | bytes 98308
  55.6 480.1 %all-gather.13.cloned.1.call-start = ((), (), s32[]{:S(2)}) async-start(), calls=%async_computation.14 | async-start | bytes 4718592 | tf_op jit(solution)/shard_map/all_gather | solution.py:240
  56.4 479.4 %all-gather.11.cloned.1.call-start = ((), (), s32[]{:S(2)}) async-start(), calls=%async_computation.12 | async-start | bytes 2228224 | tf_op jit(solution)/shard_map/all_gather | solution.py:146
  57.0 1273.5 %all-reduce.22.cloned.1.call-start = ((), (), s32[]{:S(2)}) async-start(), calls=%async_computation.15 | async-start | bytes 1572864 | tf_op jit(solution)/shard_map/psum | solution.py:368
  62.0 112.4 %copy-start.70 = (f32[16]{0:T(128)}, f32[16]{0:T(128)S(1)}, u32[]{:S(2)}) copy-start(f32[16]{0:T(128)S(1)} %exponential_negate_fusion) | copy-start | bytes 196
  62.0 504.2 %copy-start.48 = (f32[1024]{0:T(1024)}, f32[1024]{0:T(1024)S(1)}, u32[]{:S(2)}) copy-start(f32[1024]{0:T(1024)S(1)} %mul.835) | copy-start | bytes 12292
  83.0 86.3 %copy-start.60 = (f32[1,256]{1,0:T(1,128)}, f32[1,256]{1,0:T(1,128)S(1)}, u32[]{:S(2)}) copy-start(f32[1,256]{1,0:T(1,128)S(1)} %get-tuple-element.1377) | copy-start | bytes 3076
  83.0 86.3 %copy-start.62 = (f32[1,256]{1,0:T(1,128)}, f32[1,256]{1,0:T(1,128)S(1)}, u32[]{:S(2)}) copy-start(f32[1,256]{1,0:T(1,128)S(1)} %get-tuple-element.1376) | copy-start | bytes 3076
  83.0 86.3 %copy-start.64 = (f32[1,256]{1,0:T(1,128)}, f32[1,256]{1,0:T(1,128)S(1)}, u32[]{:S(2)}) copy-start(f32[1,256]{1,0:T(1,128)S(1)} %get-tuple-element.1375) | copy-start | bytes 3076
  83.0 86.3 %copy-start.66 = (f32[1,256]{1,0:T(1,128)}, f32[1,256]{1,0:T(1,128)S(1)}, u32[]{:S(2)}) copy-start(f32[1,256]{1,0:T(1,128)S(1)} %get-tuple-element.1374) | copy-start | bytes 3076
  102.5 71.9 %copy-start.32 = (bf16[1024,16]{0,1:T(8,128)(2,1)}, bf16[1024,16]{0,1:T(8,128)(2,1)S(1)}, u32[]{:S(2)}) copy-start(bf16[1024,16]{0,1:T(8,128)(2,1)S(1)} %reshape.608) | copy-start | bytes 98308
  144.7 64.4 %copy-start.42 = (f32[1024]{0:T(1024)}, f32[1024]{0:T(1024)S(1)}, u32[]{:S(2)}) copy-start(f32[1024]{0:T(1024)S(1)} %get-tuple-element.1207) | copy-start | bytes 12292
  144.7 64.4 %copy-start.44 = (f32[1024]{0:T(1024)}, f32[1024]{0:T(1024)S(1)}, u32[]{:S(2)}) copy-start(f32[1024]{0:T(1024)S(1)} %get-tuple-element.1206) | copy-start | bytes 12292
  144.7 64.4 %copy-start.46 = (f32[1024]{0:T(1024)}, f32[1024]{0:T(1024)S(1)}, u32[]{:S(2)}) copy-start(f32[1024]{0:T(1024)S(1)} %get-tuple-element.1208) | copy-start | bytes 12292
  144.8 64.4 %copy-start.50 = (f32[1024]{0:T(1024)}, f32[1024]{0:T(1024)S(1)}, u32[]{:S(2)}) copy-start(f32[1024]{0:T(1024)S(1)} %get-tuple-element.1205) | copy-start | bytes 12292
  524.1 11.7 copy-start.68
  535.7 30.5 %copy-start.36 = (f32[1536]{0:T(1024)}, f32[1536]{0:T(1024)S(1)}, u32[]{:S(2)}) copy-start(f32[1536]{0:T(1024)S(1)} %add_rsqrt_fusion) | copy-start | bytes 18436
  554.3 11.9 copy-start.4
  554.3 11.9 copy-start.7
  554.3 13.9 copy-start.8
  590.5 13.0 copy-start.29
  627.4 12.9 copy-start.29
  667.0 13.0 copy-start.29
  706.7 12.9 copy-start.29
  746.3 12.9 copy-start.29
  785.9 13.0 copy-start.29
  825.5 13.0 copy-start.29
  865.1 13.0 copy-start.29
  904.8 12.9 copy-start.29
  944.4 13.0 copy-start.29
  984.0 12.9 copy-start.29
  1023.7 13.0 copy-start.29
  1063.3 12.9 copy-start.29
  1102.9 13.0 copy-start.29
  1142.6 13.0 copy-start.29
  1182.2 13.0 copy-start.29
  1231.0 32.6 %copy-start.6 = (f32[6,256,128]{1,2,0:T(8,128)S(1)}, f32[6,256,128]{1,2,0:T(8,128)}, u32[]{:S(2)}) copy-start(f32[6,256,128]{1,2,0:T(8,128)} %get-tuple-element.626) | copy-start | bytes 2359300
  1231.0 33.7 %copy-start.5 = (f32[6,256,128]{2,1,0:T(8,128)S(1)}, f32[6,256,128]{2,1,0:T(8,128)}, u32[]{:S(2)}) copy-start(f32[6,256,128]{2,1,0:T(8,128)} %get-tuple-element.628) | copy-start | bytes 2359300
  1231.0 33.7 %copy-start.17 = (bf16[1536,128]{1,0:T(8,128)(2,1)S(1)}, bf16[1536,128]{1,0:T(8,128)(2,1)}, u32[]{:S(2)}) copy-start(bf16[1536,128]{1,0:T(8,128)(2,1)} %copy-done.16) | copy-start | bytes 1179652
  1237.8 26.9 %copy-start.18 = (f32[6,256,256]{2,1,0:T(8,128)S(1)}, f32[6,256,256]{2,1,0:T(8,128)}, u32[]{:S(2)}) copy-start(f32[6,256,256]{2,1,0:T(8,128)} %get-tuple-element.627) | copy-start | bytes 4718596
  1268.5 131.4 %reduce-scatter.39.cloned.1.call-start = ((), (), s32[]{:S(2)}) async-start(), calls=%async_computation.24 | async-start | bytes 557056
  1268.5 16.2 slice-start
  1268.5 16.2 slice-start.1
  1300.5 117.7 %reduce-scatter.35.cloned.1.call-start = ((), (), s32[]{:S(2)}) async-start(), calls=%async_computation.22 | async-start | bytes 557056
  1303.4 173.5 %reduce-scatter.33.cloned.1.call-start = ((), (), s32[]{:S(2)}) async-start(), calls=%async_computation.21 | async-start | bytes 557056
  1307.5 227.8 %reduce-scatter.31.cloned.1.call-start = ((), (), s32[]{:S(2)}) async-start(), calls=%async_computation.20 | async-start | bytes 557056
  1309.7 283.4 %reduce-scatter.37.cloned.1.call-start = ((), (), s32[]{:S(2)}) async-start(), calls=%async_computation.23 | async-start | bytes 139264
  1309.8 12.0 copy-start.13
  1309.8 12.0 copy-start.22
  1338.3 300.2 %reduce-scatter.23.cloned.1.call-start = ((), (), s32[]{:S(2)}) async-start(), calls=%async_computation.16 | async-start | bytes 4718592 | tf_op jit(solution)/shard_map/reduce_scatter | solution.py:417
  1349.5 335.7 %reduce-scatter.21.cloned.1.call-start = ((), (), s32[]{:S(2)}) async-start(), calls=%async_computation.13 | async-start | bytes 4718592 | tf_op jit(solution)/shard_map/reduce_scatter | solution.py:236
  1358.9 435.4 %reduce-scatter.25.cloned.1.call-start = ((), (), s32[]{:S(2)}) async-start(), calls=%async_computation.17 | async-start | bytes 8912896 | tf_op jit(solution)/shard_map/reduce_scatter | solution.py:437
  1385.7 470.3 %reduce-scatter.27.cloned.1.call-start = ((), (), s32[]{:S(2)}) async-start(), calls=%async_computation.18 | async-start | bytes 1114112 | tf_op jit(solution)/shard_map/reduce_scatter | solution.py:438
  1388.9 542.8 %reduce-scatter.29.cloned.1.call-start = ((), (), s32[]{:S(2)}) async-start(), calls=%async_computation.19 | async-start | bytes 4456448 | tf_op jit(solution)/shard_map/reduce_scatter | solution.py:454
  1398.4 240.1 %copy-start.9 = (bf16[768,1024]{1,0:T(8,128)(2,1)S(1)}, bf16[768,1024]{1,0:T(8,128)(2,1)}, u32[]{:S(2)}) copy-start(bf16[768,1024]{1,0:T(8,128)(2,1)} %param.26) | copy-start | bytes 4718596
  1398.4 240.1 %copy-start.39 = (f32[768]{0:T(1024)S(1)}, f32[768]{0:T(1024)}, u32[]{:S(2)}) copy-start(f32[768]{0:T(1024)} %copy-done.38) | copy-start | bytes 9220
  1398.4 240.1 %copy-start.41 = (f32[1024]{0:T(1024)S(1)}, f32[1024]{0:T(1024)}, u32[]{:S(2)}) copy-start(f32[1024]{0:T(1024)} %copy-done.40) | copy-start | bytes 12292
  1398.5 286.8 %copy-start.21 = (bf16[768,1024]{1,0:T(8,128)(2,1)S(1)}, bf16[768,1024]{1,0:T(8,128)(2,1)}, u32[]{:S(2)}) copy-start(bf16[768,1024]{1,0:T(8,128)(2,1)} %param.41) | copy-start | bytes 4718596
  1398.5 286.7 %copy-start.57 = (f32[768]{0:T(1024)S(1)}, f32[768]{0:T(1024)}, u32[]{:S(2)}) copy-start(f32[768]{0:T(1024)} %get-tuple-element.1372) | copy-start | bytes 9220
  (112 other events, 440.8 us)
Sparse Core Ops, SparseCore 0:
  54.9 42.2 all-gather.6
  100.0 53.4 all-gather.8
  155.0 43.3 all-gather.12
  200.5 41.4 all-gather.10
  1268.6 31.5 all-reduce.21
  1304.0 55.7 reduce-scatter.38
  1363.3 54.8 reduce-scatter.34
  1422.2 54.7 reduce-scatter.32
  1480.5 54.7 reduce-scatter.30
  1539.0 54.0 reduce-scatter.36
  1596.1 42.4 reduce-scatter.22
  1640.6 44.5 reduce-scatter.20
  1689.8 104.4 reduce-scatter.24
  1798.8 57.1 reduce-scatter.26
  1860.3 71.3 reduce-scatter.28
where the time goes:
time: 1960 us; the launch traced here: 1940 us
  local copies, waits for them, and re-layouts  500 us (26%)
  waiting for transfers between devices  446 us (23%)
  matrix products  387 us (20%)
  other arithmetic  380 us (19%)
  blocking collectives  193 us (10%)
    dynamic_slice x480, local copies, waits for them, and re-layouts, group_states(): lax.scan(advance, initial, (state_decay, group_state))  179 us
    unnamed x20, waiting for transfers between devices  159 us
    add x192, other arithmetic, advance(): return (pieces[0] * state_now + pieces[1], state_now)  119 us
    reduce_scatter x1, waiting for transfers between devices, on_device(): lax.psum_scatter(grad_proj_gate_inner, 'dp', scatter_dimension=0, tiled=T...  105 us
    reduce_scatter x1, waiting for transfers between devices, on_device(): lax.psum_scatter(grad_proj_out, 'dp', scatter_dimension=1, tiled=True)  75.7 us
    dynamic_update_slice x288, other arithmetic, group_states(): lax.scan(advance, initial, (state_decay, group_state))  66.2 us
    unnamed x2, blocking collectives  65.2 us
    dot_general x16, matrix products, backward_head(): jnp.einsum('ctp,csp->cts', upstream_group_rows, values_c, preferred_eleme...  64.3 us
  transfers between devices with their start and end apart: 15, of which 9 were waited for; matrix products, arithmetic and copies ran while one was open for 27% of the time, Pallas kernels for 0%

commit v1 on v0

v1 whole, which is shorter than its diff:
```python
import functools

import jax
import jax.numpy as jnp
from jax import lax
from jax.experimental import pallas as pl
from jax.experimental.pallas import tpu as pltpu
from jax.sharding import PartitionSpec as P

GROUP = 256
HALF = GROUP // 2
LANES = 128
PAIR_HEADS = 2
NORM_EPS = 1e-05
LOG2E = 1.4426950408889634
MASKED = -1e30
VMEM_BYTES = 56 * 1024 * 1024

F32 = jnp.float32
BF16 = jnp.bfloat16

ROW_NORM, ROW_TAP, ROW_BIAS, ROW_GATE, ROW_SKIP = 0, 1, 5, 6, 7


def nn(left, right):
    return lax.dot_general(left, right, (((1,), (0,)), ((), ())), preferred_element_type=F32)


def nt(left, right):
    return lax.dot_general(left, right, (((1,), (1,)), ((), ())), preferred_element_type=F32)


def tn(left, right):
    return lax.dot_general(left, right, (((0,), (0,)), ((), ())), preferred_element_type=F32)


def split3(value):
    high = value.astype(BF16)
    rest = value - high.astype(F32)
    mid = rest.astype(BF16)
    low = (rest - mid.astype(F32)).astype(BF16)
    return high, mid, low


def exact_left(ones, value):
    high, mid, low = split3(value)
    return nn(ones, high) + nn(ones, mid) + nn(ones, low)


def three_in_lanes(value, heads):
    high, mid, low = split3(value)
    lane = lax.broadcasted_iota(jnp.int32, value.shape, 1)
    parts = jnp.where(
        lane < heads,
        high.astype(F32),
        jnp.where(lane < 2 * heads, mid.astype(F32), low.astype(F32)),
    )
    return parts.astype(BF16)


def spread_matrix(heads, head_size):
    shape = (LANES, heads * head_size)
    lane = lax.broadcasted_iota(jnp.int32, shape, 0)
    channel = lax.broadcasted_iota(jnp.int32, shape, 1)
    owner = channel // head_size
    hit = (lane == owner) | (lane == owner + heads) | (lane == owner + 2 * heads)
    return hit.astype(F32).astype(BF16)


def collect_matrix(heads, head_size):
    shape = (heads * head_size, LANES)
    lane = lax.broadcasted_iota(jnp.int32, shape, 1)
    owner = lax.broadcasted_iota(jnp.int32, shape, 0) // head_size
    hit = (lane == owner) | (lane == owner + heads) | (lane == owner + 2 * heads)
    return hit.astype(F32).astype(BF16)


def lower_matrix(upper=False):
    row = lax.broadcasted_iota(jnp.int32, (GROUP, GROUP), 0)
    col = lax.broadcasted_iota(jnp.int32, (GROUP, GROUP), 1)
    hit = (col >= row) if upper else (col <= row)
    return hit.astype(F32).astype(BF16)


def sequence_ends(len_ref):
    ends, total = [], jnp.int32(0)
    for slot in range(len_ref.shape[1]):
        total = total + len_ref[0, slot]
        ends.append(total)
    return ends


def sequence_of(ends, token):
    found = (token >= ends[0]).astype(jnp.int32)
    for end in ends[1:]:
        found = found + (token >= end).astype(jnp.int32)
    return found


def scalar_sequence_of(ends, token):
    found = jnp.where(token >= ends[0], 1, 0)
    for end in ends[1:]:
        found = found + jnp.where(token >= end, 1, 0)
    return found


def position_of(ends, token):
    start = jnp.zeros_like(token)
    for end in ends:
        start = jnp.where(token >= end, end, start)
    return token - start


def tokens_column(first, rows=GROUP):
    return first + lax.broadcasted_iota(jnp.int32, (rows, 1), 0)


def additive_mask(ends, first, transposed):
    rows = first + lax.broadcasted_iota(jnp.int32, (GROUP, GROUP), 0)
    cols = first + lax.broadcasted_iota(jnp.int32, (GROUP, GROUP), 1)
    ordered = (cols >= rows) if transposed else (rows >= cols)
    kept = (sequence_of(ends, rows) == sequence_of(ends, cols)) & ordered
    return jnp.where(kept, 0.0, MASKED)


def softplus(value):
    return jnp.maximum(value, 0.0) + jnp.log1p(jnp.exp(-jnp.abs(value)))


def sigmoid(value):
    return 1.0 / (1.0 + jnp.exp(-value))


def decay_terms(ends, first, step_in, rate, lower):
    group = first // GROUP
    step = softplus(step_in)
    cum = exact_left(lower, step * (rate * LOG2E))
    last = cum[GROUP - 1 : GROUP, :]
    sequence = sequence_of(ends, tokens_column(first))
    tail = scalar_sequence_of(ends, first + GROUP - 1)
    before = jnp.where(group > 0, scalar_sequence_of(ends, first - 1), -1)
    in_tail = (sequence == tail).astype(F32)
    entered = (sequence == before).astype(F32)
    carried = jnp.where(tail == before, 1.0, 0.0)
    key_factor = jnp.exp2(last - cum) * in_tail
    entry = jnp.exp2(cum) * entered
    decay = jnp.exp2(last) * carried
    return step, cum, key_factor, entry, decay


def head_masks():
    lane = lax.broadcasted_iota(jnp.int32, (1, LANES), 1)
    first = (lane < LANES // 2).astype(F32)
    return first, 1.0 - first


def forward_kernel(
    rank_ref, len_ref, own_ref, other_ref, w_ref, rows_ref, taps_ref, head_ref,
    normed_ref, ipre_ref, spre_ref, sact_ref, stepin_ref, mixed_ref, sprev_ref,
    ext, state, spread, lower, fac, read, mask, scores, weighted,
):
    inner = rows_ref.shape[1]
    channels = ext.shape[1]
    heads = inner // (LANES // PAIR_HEADS)
    size = sprev_ref.shape[0]
    group = pl.program_id(0)
    first = group * GROUP
    ends = sequence_ends(len_ref)

    @pl.when(group == 0)
    def _():
        ext[0:8, :] = jnp.zeros((8, channels), F32)
        state[...] = jnp.zeros_like(state)
        spread[...] = spread_matrix(heads, LANES // PAIR_HEADS)
        lower[...] = lower_matrix()

    mine = rank_ref[0, 0] == group // (pl.num_programs(0) // 2)
    gain = rows_ref[ROW_NORM : ROW_NORM + 1, :]
    for part in range(4):
        sl = slice(part * 64, part * 64 + 64)
        hidden = jnp.where(mine, own_ref[sl, :].astype(F32), other_ref[sl, :].astype(F32))
        inv = lax.rsqrt(jnp.mean(hidden * hidden, axis=1, keepdims=True) + NORM_EPS)
        normed_ref[sl, :] = (hidden * inv * gain).astype(BF16)

    pre = nn(normed_ref[...], w_ref[...])
    ext[8 : 8 + GROUP, :] = pre[:, :channels]
    ipre_ref[...] = pre[:, :inner]
    spre_ref[...] = pre[:, inner:channels]
    lane = lax.broadcasted_iota(jnp.int32, (1, LANES), 1)
    step_in = jnp.where(lane < 3 * heads, pre[:, channels:], 0.0) + head_ref[0:1, :]
    stepin_ref[...] = step_in

    token = tokens_column(first)
    position = position_of(ends, token)
    keep = [(position >= offset).astype(F32) for offset in (1, 2, 3)]

    def conv(sl, taps, bias):
        total = bias + taps[3:4, :] * ext[8 : 8 + GROUP, sl]
        for offset in (1, 2, 3):
            total = total + keep[offset - 1] * (
                taps[3 - offset : 4 - offset, :] * ext[8 - offset : 8 - offset + GROUP, sl]
            )
        return total

    for part in range(2):
        sl = slice(inner + part * size, inner + (part + 1) * size)
        own = slice(part * size, (part + 1) * size)
        total = conv(sl, taps_ref[0:4, own], taps_ref[4:5, own])
        sact_ref[:, own] = (total * sigmoid(total)).astype(BF16)
    keys = sact_ref[:, :size]
    queries = sact_ref[:, size:]
    scores[...] = nt(queries, keys)
    mask[...] = additive_mask(ends, first, False)

    step, cum, key_factor, entry, decay = decay_terms(
        ends, first, step_in, head_ref[1:2, :], lower[...]
    )
    cum_rows = cum.T
    stacked = jnp.concatenate(
        [step, key_factor * step, entry, jnp.broadcast_to(decay, (16, LANES))], axis=0
    )
    fac[...] = nn(three_in_lanes(stacked, heads), spread[...])
    held = state[...].astype(BF16)
    sprev_ref[...] = held
    read[...] = nn(queries, held)

    masks = head_masks()
    for pair in range(inner // LANES):
        sl = slice(pair * LANES, (pair + 1) * LANES)
        total = conv(sl, rows_ref[ROW_TAP : ROW_TAP + 4, sl], rows_ref[ROW_BIAS : ROW_BIAS + 1, sl])
        values = (total * sigmoid(total)).astype(BF16).astype(F32)
        stepped = values * fac[0:GROUP, sl]
        weighted[:, sl] = (values * fac[GROUP : 2 * GROUP, sl]).astype(BF16)
        top, bottom, low_values, high_values = [], [], [], []
        for which in range(PAIR_HEADS):
            head = pair * PAIR_HEADS + which
            column = cum[:, head : head + 1]
            row = cum_rows[head : head + 1, :]

            def factor(rs, cs):
                gap = column[rs] - row[:, cs] + mask[rs, cs]
                return (jnp.exp2(gap) * scores[rs, cs]).astype(BF16)

            lo, hi = slice(0, HALF), slice(HALF, GROUP)
            top.append(factor(lo, lo))
            bottom.append(factor(hi, lo))
            bottom.append(factor(hi, hi))
            masked = (stepped * masks[which]).astype(BF16)
            low_values.append(masked[:HALF])
            high_values.append(masked)
        upper_part = nn(jnp.concatenate(top, axis=1), jnp.concatenate(low_values, axis=0))
        lower_part = nn(jnp.concatenate(bottom, axis=1), jnp.concatenate(high_values, axis=0))
        rest = fac[2 * GROUP : 3 * GROUP, sl] * read[:, sl] + (
            rows_ref[ROW_SKIP : ROW_SKIP + 1, sl] * values
        )
        mixed_ref[0:HALF, sl] = upper_part + rest[:HALF]
        mixed_ref[HALF:GROUP, sl] = lower_part + rest[HALF:]

    state[...] = fac[3 * GROUP : 3 * GROUP + 1, :] * state[...] + tn(keys, weighted[...])
    ext[0:8, :] = ext[GROUP : GROUP + 8, :]


def gate_kernel(
    rank_ref, len_ref, own_ref, other_ref, normed_ref, mixed_ref, w_ref, proj_ref, rows_ref,
    gate_ref, gol_ref, live_ref, sums_ref,
):
    group = pl.program_id(0)
    first = group * GROUP
    ends = sequence_ends(len_ref)
    mine = rank_ref[0, 0] == group // (pl.num_programs(0) // 2)
    valid = tokens_column(first) < ends[-1]
    cotangent = jnp.where(mine, own_ref[...].astype(F32), other_ref[...].astype(F32))
    live_ref[...] = jnp.where(valid, cotangent, 0.0).astype(BF16)
    gate_ref[...] = nn(normed_ref[...], w_ref[...])
    gol_ref[...] = nn(live_ref[...], proj_ref[...])
    gain = rows_ref[ROW_GATE : ROW_GATE + 1, :]
    lane = lax.broadcasted_iota(jnp.int32, (64, LANES), 1)
    pieces = []
    for part in range(4):
        sl = slice(part * 64, part * 64 + 64)
        gate = gate_ref[sl, :]
        gated = mixed_ref[sl, :] * (gate * sigmoid(gate))
        square = jnp.sum(gated * gated, axis=1, keepdims=True)
        inner = jnp.sum(gol_ref[sl, :] * gain * gated, axis=1, keepdims=True)
        pieces.append(jnp.where(lane < 4, square, inner))
    sums_ref[...] = jnp.concatenate(pieces, axis=0).T[0:8, :]


def gate_grad_kernel(
    own_sums_ref, other_sums_ref, gate_ref, gol_ref, mixed_ref, rows_ref,
    low_ref, first_ref, ggp_ref, gain_ref, *, inner_all,
):
    @pl.when(pl.program_id(0) == 0)
    def _():
        gain_ref[...] = jnp.zeros_like(gain_ref)

    totals = own_sums_ref[...] + other_sums_ref[...]
    columns = jnp.concatenate([totals, jnp.zeros((LANES - 8, GROUP), F32)], axis=0).T
    inv_all = lax.rsqrt(columns[:, 0:1] / inner_all + NORM_EPS)
    slope_all = inv_all * inv_all * inv_all * columns[:, 4:5] / inner_all
    gain = rows_ref[ROW_GATE : ROW_GATE + 1, :]
    total = jnp.zeros((1, gate_ref.shape[1]), F32)
    for part in range(8):
        sl = slice(part * 32, part * 32 + 32)
        inv, slope = inv_all[sl], slope_all[sl]
        gate, gol, mixed = gate_ref[sl, :], gol_ref[sl, :], mixed_ref[sl, :]
        logistic = sigmoid(gate)
        silu = gate * logistic
        gated = mixed * silu
        scaled = gated * inv
        low_ref[sl, :] = (scaled * gain).astype(BF16)
        total = total + jnp.sum(gol * scaled, axis=0, keepdims=True)
        grad = inv * (gol * gain) - gated * slope
        first_ref[sl, :] = (grad * silu).astype(BF16)
        ggp_ref[sl, :] = (grad * mixed * (logistic * (1.0 + gate * (1.0 - logistic)))).astype(BF16)
    gain_ref[0:1, :] += total


def backward_kernel(
    len_ref, ipre_ref, halo_ref, sact_ref, stepin_ref, mixed_ref, first_ref, sprev_ref,
    rows_ref, head_ref,
    gip_ref, gkq_ref, gstep_ref, conv_ref, heads_ref,
    ext, cext, gstate, spread, collect, lower, upper, fac, reads, mask, scores, gscores,
    stepped_all, weighted, entered, sums_high, sums_low,
):
    inner = rows_ref.shape[1]
    heads = inner // (LANES // PAIR_HEADS)
    size = sprev_ref.shape[0]
    turn = pl.program_id(0)
    group = pl.num_programs(0) - 1 - turn
    first = group * GROUP
    ends = sequence_ends(len_ref)

    @pl.when(turn == 0)
    def _():
        cext[GROUP : GROUP + 8, :] = jnp.zeros((8, inner), F32)
        gstate[...] = jnp.zeros_like(gstate)
        spread[...] = spread_matrix(heads, LANES // PAIR_HEADS)
        collect[...] = collect_matrix(heads, LANES // PAIR_HEADS)
        lower[...] = lower_matrix()
        upper[...] = lower_matrix(upper=True)
        conv_ref[...] = jnp.zeros_like(conv_ref)
        heads_ref[...] = jnp.zeros_like(heads_ref)

    ext[0:8, :] = jnp.where(group > 0, halo_ref[...], 0.0)
    ext[8 : 8 + GROUP, :] = ipre_ref[...]
    token = tokens_column(first)
    position = position_of(ends, token)
    keep = [(position >= offset).astype(F32) for offset in (1, 2, 3)]
    ahead = [(position_of(ends, token + offset) >= offset).astype(F32) for offset in (1, 2, 3)]

    step_in = stepin_ref[...]
    rate = head_ref[1:2, :]
    step, cum, key_factor, entry, decay = decay_terms(ends, first, step_in, rate, lower[...])
    cum_rows = cum.T
    key_step = key_factor * step
    stacked = jnp.concatenate(
        [step, key_step, entry, jnp.broadcast_to(decay, (16, LANES))], axis=0
    )
    fac[...] = nn(three_in_lanes(stacked, heads), spread[...])

    keys = sact_ref[:, :size]
    queries = sact_ref[:, size:]
    scores[...] = nt(keys, queries)
    mask[...] = additive_mask(ends, first, True)
    gscores[...] = jnp.zeros_like(gscores)
    held = gstate[...].astype(BF16)
    reads[...] = nn(keys, held)

    masks = head_masks()
    lo, hi = slice(0, HALF), slice(HALF, GROUP)
    for pair in range(inner // LANES):
        sl = slice(pair * LANES, (pair + 1) * LANES)
        taps = rows_ref[ROW_TAP : ROW_TAP + 4, sl]
        shifted = [ext[8 - offset : 8 - offset + GROUP, sl] for offset in range(4)]
        total = rows_ref[ROW_BIAS : ROW_BIAS + 1, sl] + taps[3:4, :] * shifted[0]
        for offset in (1, 2, 3):
            total = total + keep[offset - 1] * (taps[3 - offset : 4 - offset, :] * shifted[offset])
        logistic = sigmoid(total)
        values = (total * logistic).astype(BF16).astype(F32)
        slope = logistic * (1.0 + total * (1.0 - logistic))
        step_wide = fac[0:GROUP, sl]
        key_wide = fac[GROUP : 2 * GROUP, sl]
        stepped = (values * step_wide).astype(BF16)
        stepped_wide = stepped.astype(F32)
        weighted[:, sl] = (values * key_wide).astype(BF16)
        upstream = first_ref[:, sl]
        upstream_wide = upstream.astype(F32)
        entered[:, sl] = (upstream_wide * fac[2 * GROUP : 3 * GROUP, sl]).astype(BF16)

        top, bottom, top_grads, low_grads = [], [], [], []
        g00 = g01 = g11 = None
        for which in range(PAIR_HEADS):
            head = pair * PAIR_HEADS + which
            column = cum[:, head : head + 1]
            row = cum_rows[head : head + 1, :]
            masked = (upstream_wide * masks[which]).astype(BF16)
            grads = nt(stepped, masked)

            def factors(rs, cs):
                gap = row[:, cs] - column[rs] + mask[rs, cs]
                factor = jnp.exp2(gap)
                return (factor * scores[rs, cs]).astype(BF16), factor * grads[rs, cs]

            a00, d00 = factors(lo, lo)
            a01, d01 = factors(lo, hi)
            a11, d11 = factors(hi, hi)
            g00 = d00 if g00 is None else g00 + d00
            g01 = d01 if g01 is None else g01 + d01
            g11 = d11 if g11 is None else g11 + d11
            top.extend([a00, a01])
            bottom.append(a11)
            top_grads.append(masked)
            low_grads.append(masked[HALF:])
        gscores[lo, lo] += g00
        gscores[lo, hi] += g01
        gscores[hi, hi] += g11
        raw = jnp.concatenate(
            [
                nn(jnp.concatenate(top, axis=1), jnp.concatenate(top_grads, axis=0)),
                nn(jnp.concatenate(bottom, axis=1), jnp.concatenate(low_grads, axis=0)),
            ],
            axis=0,
        )
        skip = rows_ref[ROW_SKIP : ROW_SKIP + 1, sl]
        across = reads[:, sl]

        def keep_sum(index, value):
            high = value.astype(BF16)
            sums_high[index * GROUP : (index + 1) * GROUP, sl] = high
            sums_low[index * GROUP : (index + 1) * GROUP, sl] = (
                value - high.astype(F32)
            ).astype(BF16)

        keep_sum(0, upstream_wide * (mixed_ref[:, sl] - skip * values) - stepped_wide * raw)
        keep_sum(1, values * raw)
        keep_sum(2, values * across)
        conv_ref[5:6, sl] += jnp.sum(upstream_wide * values, axis=0, keepdims=True)
        inner_grad = step_wide * raw + key_wide * across + skip * upstream_wide
        grad = inner_grad * slope
        cext[0:GROUP, sl] = grad
        conv_ref[3:4, sl] += jnp.sum(grad * shifted[0], axis=0, keepdims=True)
        conv_ref[4:5, sl] += jnp.sum(grad, axis=0, keepdims=True)
        result = taps[3:4, :] * grad
        for offset in (1, 2, 3):
            conv_ref[3 - offset : 4 - offset, sl] += jnp.sum(
                keep[offset - 1] * grad * shifted[offset], axis=0, keepdims=True
            )
            result = result + ahead[offset - 1] * (
                taps[3 - offset : 4 - offset, :] * cext[offset : offset + GROUP, sl]
            )
        gip_ref[:, sl] = result.astype(BF16)

    cext[GROUP : GROUP + 8, :] = cext[0:8, :]
    state = sprev_ref[...]
    grad_scores = gscores[...].astype(BF16)
    gkq_ref[:, :size] = (nn(grad_scores, queries) + nt(weighted[...], held)).astype(BF16)
    gkq_ref[:, size:] = (tn(grad_scores, keys) + nt(entered[...], state)).astype(BF16)

    collected = nn(sums_high[...], collect[...]) + nn(sums_low[...], collect[...])
    balance = collected[:GROUP]
    direct = collected[GROUP : 2 * GROUP]
    key_dot = collected[2 * GROUP :]
    product = jnp.sum(gstate[...] * state.astype(F32), axis=0, keepdims=True)
    product_high = product.astype(BF16)
    product_low = (product - product_high.astype(F32)).astype(BF16)
    rows16 = jnp.concatenate(
        [jnp.broadcast_to(product_high, (8, inner)), jnp.broadcast_to(product_low, (8, inner))],
        axis=0,
    ).astype(BF16)
    carried = nn(rows16, collect[...])
    carry_term = decay * (carried[0:1, :] + carried[8:9, :])
    moved = key_step * key_dot
    grad_log = (
        exact_left(upper[...], balance) + carry_term + exact_left(lower[...], moved) - moved
    )
    grad_step = direct + key_factor * key_dot + grad_log * rate
    lane = lax.broadcasted_iota(jnp.int32, (1, LANES), 1)
    grad_step_in = jnp.where(lane < heads, grad_step * sigmoid(step_in), 0.0)
    gstep_ref[...] = grad_step_in.astype(BF16)
    heads_ref[0:1, :] += jnp.sum(grad_log * step * rate, axis=0, keepdims=True)
    heads_ref[1:2, :] += jnp.sum(grad_step_in, axis=0, keepdims=True)
    gstate[...] = fac[3 * GROUP : 3 * GROUP + 1, :] * gstate[...] + tn(queries, entered[...])


def state_grad_kernel(
    len_ref, own_ref, other_ref, spre_ref, taps_ref, gsp_ref, conv_ref, ext, cext
):
    rows, channels = spre_ref.shape
    ends = sequence_ends(len_ref)
    ext[0:8, :] = jnp.zeros((8, channels), F32)
    ext[8 : 8 + rows, :] = spre_ref[...]
    cext[rows : rows + 8, :] = jnp.zeros((8, channels), F32)
    conv_ref[...] = jnp.zeros_like(conv_ref)
    for group in range(rows // GROUP):
        base = group * GROUP
        token = tokens_column(base)
        position = position_of(ends, token)
        for part in range(channels // LANES):
            sl = slice(part * LANES, (part + 1) * LANES)
            shifted = [
                ext[base + 8 - offset : base + 8 - offset + GROUP, sl] for offset in range(4)
            ]
            total = taps_ref[4:5, sl] + taps_ref[3:4, sl] * shifted[0]
            for offset in (1, 2, 3):
                keep = (position >= offset).astype(F32)
                total = total + keep * (taps_ref[3 - offset : 4 - offset, sl] * shifted[offset])
            logistic = sigmoid(total)
            slope = logistic * (1.0 + total * (1.0 - logistic))
            upstream = own_ref[base : base + GROUP, sl].astype(F32) + other_ref[
                base : base + GROUP, sl
            ].astype(F32)
            grad = upstream * slope
            cext[base : base + GROUP, sl] = grad
            conv_ref[4:5, sl] += jnp.sum(grad, axis=0, keepdims=True)
            conv_ref[3:4, sl] += jnp.sum(grad * shifted[0], axis=0, keepdims=True)
            for offset in (1, 2, 3):
                keep = (position >= offset).astype(F32)
                conv_ref[3 - offset : 4 - offset, sl] += jnp.sum(
                    keep * grad * shifted[offset], axis=0, keepdims=True
                )
    for group in range(rows // GROUP):
        base = group * GROUP
        token = tokens_column(base)
        for part in range(channels // LANES):
            sl = slice(part * LANES, (part + 1) * LANES)
            result = taps_ref[3:4, sl] * cext[base : base + GROUP, sl]
            for offset in (1, 2, 3):
                ahead = (position_of(ends, token + offset) >= offset).astype(F32)
                result = result + ahead * (
                    taps_ref[3 - offset : 4 - offset, sl]
                    * cext[base + offset : base + offset + GROUP, sl]
                )
            gsp_ref[base : base + GROUP, sl] = result.astype(BF16)


def shape_of(dims, dtype):
    return jax.ShapeDtypeStruct(dims, dtype)


def params(**kwargs):
    return pltpu.CompilerParams(vmem_limit_bytes=VMEM_BYTES, **kwargs)


SMEM_SPEC = pl.BlockSpec(memory_space=pltpu.SMEM)


def whole(*dims):
    return pl.BlockSpec(dims, lambda i: (0,) * len(dims))


def on_device(
    hidden_in,
    norm_gain,
    projection_gate_inner,
    proj_state,
    proj_step,
    conv_inner,
    conv_inner_bias,
    conv_state,
    conv_state_bias,
    decay_log,
    skip_gain,
    step_bias,
    gate_gain,
    proj_out,
    lengths,
    cotangent,
):
    tensor_count = lax.axis_size("tensor")
    tensor_rank = lax.axis_index("tensor")
    shard_rank = lax.axis_index("dp")
    shard_count = lax.axis_size("dp")
    half_rows, width = hidden_in.shape
    tokens = half_rows * tensor_count
    groups = tokens // GROUP
    half_groups = groups // 2
    inner = proj_out.shape[0]
    inner_all = inner * tensor_count
    heads = decay_log.shape[0]
    head_size = inner // heads
    size = proj_state.shape[1] // 2
    taps = conv_inner.shape[0]
    shard = width // shard_count
    channels = inner + 2 * size
    swap = [(0, 1), (1, 0)]

    def exchange(value):
        return lax.ppermute(value, "tensor", swap)

    hidden_other = exchange(hidden_in)
    cotangent_other = exchange(cotangent)

    state_shard = conv_state.shape[1]
    bias_column = jnp.pad(conv_state_bias, (0, shard - state_shard))
    columns = jnp.concatenate(
        [
            proj_step, proj_step, proj_step,
            norm_gain[:, None],
            conv_inner.reshape(taps, shard).T,
            conv_inner_bias.reshape(shard, 1),
            gate_gain.reshape(shard, 1),
            conv_state.reshape(shard, 1),
            bias_column[:, None],
        ],
        axis=1,
    )
    columns = jnp.pad(columns, ((0, 0), (0, LANES - columns.shape[1])))
    first_shard = jnp.concatenate([projection_gate_inner[:, 1], proj_state, columns], axis=1)
    second_shard = jnp.concatenate([projection_gate_inner[:, 0], proj_out.T], axis=1)
    w_first = lax.all_gather(first_shard, "dp", axis=0, tiled=True)
    w_second = lax.all_gather(second_shard, "dp", axis=0, tiled=True)
    w_inner = w_first[:, :inner]
    w_state = w_first[:, inner:channels]
    w_step = w_first[:, channels:]
    w_gate = w_second[:, :inner]
    w_out = w_second[:, inner:]

    base = 3 * heads
    small = w_step[:, base : base + 9].astype(F32).T
    skip_row = jnp.repeat(skip_gain.astype(F32), head_size)[None, :]
    rows = jnp.concatenate([small[0:7], skip_row], axis=0)
    state_taps = small[7].reshape(shard_count, taps, state_shard).transpose(1, 0, 2)
    state_taps = state_taps.reshape(taps, 2 * size)
    state_bias = small[8].reshape(shard_count, shard)[:, :state_shard].reshape(1, 2 * size)
    state_rows = jnp.concatenate(
        [state_taps, state_bias, jnp.zeros((3, 2 * size), F32)], axis=0
    )
    rate = -jnp.exp(decay_log.astype(F32))
    head_rows = jnp.stack([jnp.tile(step_bias.astype(F32), 3), jnp.tile(rate, 3)])
    head_rows = jnp.pad(head_rows, ((0, 6), (0, LANES - base)))
    rank = tensor_rank.astype(jnp.int32).reshape(1, 1)

    def by_group(lanes):
        return pl.BlockSpec((GROUP, lanes), lambda i: (i, 0))

    half_block = pl.BlockSpec((GROUP, width), lambda i: (i % half_groups, 0))
    normed, inner_pre, state_pre, state_act, step_in, mixed, prev_states = pl.pallas_call(
        forward_kernel,
        grid=(groups,),
        in_specs=[
            SMEM_SPEC, SMEM_SPEC, half_block, half_block,
            whole(width, channels + LANES), whole(8, inner), whole(8, 2 * size), whole(8, LANES),
        ],
        out_specs=[
            by_group(width), by_group(inner), by_group(2 * size), by_group(2 * size),
            by_group(LANES), by_group(inner), pl.BlockSpec((size, inner), lambda i: (i, 0)),
        ],
        out_shape=[
            shape_of((tokens, width), BF16),
            shape_of((tokens, inner), F32),
            shape_of((tokens, 2 * size), F32),
            shape_of((tokens, 2 * size), BF16),
            shape_of((tokens, LANES), F32),
            shape_of((tokens, inner), F32),
            shape_of((groups * size, inner), BF16),
        ],
        scratch_shapes=[
            pltpu.VMEM((GROUP + 8, channels), F32),
            pltpu.VMEM((size, inner), F32),
            pltpu.VMEM((LANES, inner), BF16),
            pltpu.VMEM((GROUP, GROUP), BF16),
            pltpu.VMEM((3 * GROUP + 16, inner), F32),
            pltpu.VMEM((GROUP, inner), F32),
            pltpu.VMEM((GROUP, GROUP), F32),
            pltpu.VMEM((GROUP, GROUP), F32),
            pltpu.VMEM((GROUP, inner), BF16),
        ],
        compiler_params=params(),
        name="mixer_forward",
    )(rank, lengths, hidden_in, hidden_other, w_first, rows, state_rows, head_rows)

    gate_pre, grad_out_low, live, sums = pl.pallas_call(
        gate_kernel,
        grid=(groups,),
        in_specs=[
            SMEM_SPEC, SMEM_SPEC, half_block, half_block, by_group(width), by_group(inner),
            pl.BlockSpec((width, inner), lambda i: (0, 0)),
            pl.BlockSpec((width, inner), lambda i: (0, 1)),
            whole(8, inner),
        ],
        out_specs=[
            by_group(inner), by_group(inner), by_group(width),
            pl.BlockSpec((8, GROUP), lambda i: (0, i)),
        ],
        out_shape=[
            shape_of((tokens, inner), F32),
            shape_of((tokens, inner), F32),
            shape_of((tokens, width), BF16),
            shape_of((8, tokens), F32),
        ],
        compiler_params=params(),
        name="gate_forward",
    )(rank, lengths, cotangent, cotangent_other, normed, mixed, w_second, w_second, rows)

    sums_other = exchange(sums)
    sum_block = pl.BlockSpec((8, GROUP), lambda i: (0, i))
    out_low, grad_first, grad_gate_low, gain_rows = pl.pallas_call(
        functools.partial(gate_grad_kernel, inner_all=inner_all),
        grid=(groups,),
        in_specs=[
            sum_block, sum_block, by_group(inner), by_group(inner), by_group(inner),
            whole(8, inner),
        ],
        out_specs=[by_group(inner), by_group(inner), by_group(inner), whole(8, inner)],
        out_shape=[
            shape_of((tokens, inner), BF16),
            shape_of((tokens, inner), BF16),
            shape_of((tokens, inner), BF16),
            shape_of((8, inner), F32),
        ],
        compiler_params=params(),
        name="gate_backward",
    )(sums, sums_other, gate_pre, grad_out_low, mixed, rows)

    first_grads = jnp.concatenate(
        [tn(live, out_low).astype(BF16), tn(normed, grad_gate_low).astype(BF16)], axis=1
    )
    first_sum = lax.psum_scatter(first_grads, "dp", scatter_dimension=0, tiled=True)

    def rows_of(value, which):
        return lax.dynamic_slice_in_dim(value, which * half_rows, half_rows)

    mix_away = nt(rows_of(out_low, 1 - tensor_rank), w_out).astype(BF16)
    mix_here = nt(rows_of(out_low, tensor_rank), w_out)
    mix = mix_here + exchange(mix_away).astype(F32)
    slot = tensor_rank * half_rows + jnp.arange(half_rows, dtype=jnp.int32)
    valid_half = slot < jnp.sum(lengths[0])
    hidden_wide = hidden_in.astype(F32)
    block_out = (hidden_wide + jnp.where(valid_half[:, None], mix, 0.0)).astype(BF16)

    last = groups - 1
    grad_inner_low, grad_kq, grad_step_low, conv_rows, head_sums = pl.pallas_call(
        backward_kernel,
        grid=(groups,),
        in_specs=[
            SMEM_SPEC,
            pl.BlockSpec((GROUP, inner), lambda i: (last - i, 0)),
            pl.BlockSpec(
                (8, inner), lambda i: (jnp.maximum((last - i) * (GROUP // 8) - 1, 0), 0)
            ),
            pl.BlockSpec((GROUP, 2 * size), lambda i: (last - i, 0)),
            pl.BlockSpec((GROUP, LANES), lambda i: (last - i, 0)),
            pl.BlockSpec((GROUP, inner), lambda i: (last - i, 0)),
            pl.BlockSpec((GROUP, inner), lambda i: (last - i, 0)),
            pl.BlockSpec((size, inner), lambda i: (last - i, 0)),
            whole(8, inner), whole(8, LANES),
        ],
        out_specs=[
            pl.BlockSpec((GROUP, inner), lambda i: (last - i, 0)),
            pl.BlockSpec((GROUP, 2 * size), lambda i: (last - i, 0)),
            pl.BlockSpec((GROUP, LANES), lambda i: (last - i, 0)),
            whole(8, inner), whole(8, LANES),
        ],
        out_shape=[
            shape_of((tokens, inner), BF16),
            shape_of((tokens, 2 * size), BF16),
            shape_of((tokens, LANES), BF16),
            shape_of((8, inner), F32),
            shape_of((8, LANES), F32),
        ],
        scratch_shapes=[
            pltpu.VMEM((GROUP + 8, inner), F32),
            pltpu.VMEM((GROUP + 8, inner), F32),
            pltpu.VMEM((size, inner), F32),
            pltpu.VMEM((LANES, inner), BF16),
            pltpu.VMEM((inner, LANES), BF16),
            pltpu.VMEM((GROUP, GROUP), BF16),
            pltpu.VMEM((GROUP, GROUP), BF16),
            pltpu.VMEM((3 * GROUP + 16, inner), F32),
            pltpu.VMEM((GROUP, inner), F32),
            pltpu.VMEM((GROUP, GROUP), F32),
            pltpu.VMEM((GROUP, GROUP), F32),
            pltpu.VMEM((GROUP, GROUP), F32),
            pltpu.VMEM((GROUP, inner), BF16),
            pltpu.VMEM((GROUP, inner), BF16),
            pltpu.VMEM((GROUP, inner), BF16),
            pltpu.VMEM((3 * GROUP, inner), BF16),
            pltpu.VMEM((3 * GROUP, inner), BF16),
        ],
        compiler_params=params(),
        name="mixer_backward",
    )(
        lengths, inner_pre, inner_pre, state_act, step_in, mixed, grad_first, prev_states,
        rows, head_rows,
    )

    grad_kq_other = exchange(grad_kq)

    def partial_normed(which):
        return (
            nt(rows_of(grad_gate_low, which), w_gate)
            + nt(rows_of(grad_inner_low, which), w_inner)
            + nt(rows_of(grad_step_low, which), w_step)
        )

    normed_away = exchange(partial_normed(1 - tensor_rank).astype(BF16))
    normed_here = partial_normed(tensor_rank)
    grad_inner_weight = tn(normed, grad_inner_low).astype(BF16)
    grad_step_weight = tn(normed, grad_step_low).astype(BF16)

    grad_state_low, state_conv_rows = pl.pallas_call(
        state_grad_kernel,
        in_specs=[SMEM_SPEC] + [pl.BlockSpec(memory_space=pltpu.VMEM)] * 4,
        out_specs=[pl.BlockSpec(memory_space=pltpu.VMEM)] * 2,
        out_shape=[shape_of((tokens, 2 * size), BF16), shape_of((8, 2 * size), F32)],
        scratch_shapes=[
            pltpu.VMEM((tokens + 8, 2 * size), F32),
            pltpu.VMEM((tokens + 8, 2 * size), F32),
        ],
        compiler_params=params(),
        name="state_backward",
    )(lengths, grad_kq, grad_kq_other, state_pre, state_rows)

    grad_state_weight = tn(normed, grad_state_low).astype(BF16)
    second_grads = jnp.concatenate(
        [grad_inner_weight, grad_state_weight, grad_step_weight], axis=1
    )
    second_sum = lax.psum_scatter(second_grads, "dp", scatter_dimension=0, tiled=True)

    grad_normed = normed_here + normed_away.astype(F32)
    grad_normed = grad_normed + nt(rows_of(grad_state_low, tensor_rank), w_state)
    gain = rows[ROW_NORM][None, :]
    inv_rms = lax.rsqrt(jnp.mean(hidden_wide * hidden_wide, axis=1, keepdims=True) + NORM_EPS)
    grad_gain_local = jnp.sum(grad_normed * hidden_wide * inv_rms, axis=0)
    scaled_in = grad_normed * gain
    grad_hidden = (
        inv_rms * scaled_in
        - hidden_wide * inv_rms**3 * jnp.mean(scaled_in * hidden_wide, axis=1, keepdims=True)
        + cotangent.astype(F32)
    )

    skip_sums = conv_rows[5].reshape(heads, head_size).sum(axis=1)
    pieces = jnp.concatenate(
        [
            conv_rows[0:5].reshape(-1),
            gain_rows[0],
            state_conv_rows[0:5].reshape(-1),
            head_sums[0:2].reshape(-1),
            jnp.pad(skip_sums, (0, LANES - heads)),
            grad_gain_local,
        ]
    )
    placed = jnp.where(
        jnp.arange(tensor_count, dtype=jnp.int32)[:, None] == tensor_rank, pieces[None, :], 0.0
    )
    small_sum = lax.psum(placed, ("dp", "tensor"))
    mine = lax.dynamic_index_in_dim(small_sum, tensor_rank, 0, keepdims=False)

    def take(value, start, length):
        return value[start : start + length]

    at = 0
    conv_all = take(mine, at, 5 * inner).reshape(5, inner)
    at += 5 * inner
    gate_gain_all = take(mine, at, inner)
    at += inner
    state_conv_all = take(mine, at, 10 * size).reshape(5, 2 * size)
    at += 10 * size
    head_all = take(mine, at, 3 * LANES).reshape(3, LANES)
    at += 3 * LANES
    gain_all = jnp.sum(small_sum[:, at : at + width], axis=0)

    def own_shard(value, length):
        return lax.dynamic_slice_in_dim(value, shard_rank * length, length, value.ndim - 1)

    conv_own = own_shard(conv_all, shard)
    state_own = own_shard(state_conv_all, state_shard)
    gate_grad_own = first_sum[:, width:].astype(F32)
    inner_grad_own = second_sum[:, :inner].astype(F32)
    return (
        block_out,
        grad_hidden,
        own_shard(gain_all, shard),
        jnp.stack([gate_grad_own, inner_grad_own], axis=1),
        second_sum[:, inner:channels].astype(F32),
        second_sum[:, channels : channels + heads].astype(F32),
        conv_own[0:4][:, None, :],
        conv_own[4:5],
        state_own[0:4],
        state_own[4],
        head_all[0, :heads],
        head_all[2, :heads],
        head_all[1, :heads],
        own_shard(gate_gain_all, shard)[None, :],
        first_sum[:, :inner].astype(F32).T,
    )


def solution(mesh):
    placed = (
        P(("dp", "tensor"), None),
        P("dp"),
        P("dp", None, "tensor"),
        P("dp", None),
        P("dp", "tensor"),
        P(None, "tensor", "dp"),
        P("tensor", "dp"),
        P(None, "dp"),
        P("dp"),
        P("tensor"),
        P("tensor"),
        P("tensor"),
        P("tensor", "dp"),
        P("tensor", "dp"),
        P("dp", None),
        P(("dp", "tensor"), None),
    )
    return jax.shard_map(
        on_device,
        mesh=mesh,
        in_specs=placed,
        out_specs=(
            P(("dp", "tensor"), None),
            P(("dp", "tensor"), None),
            P("dp"),
            P("dp", None, "tensor"),
            P("dp", None),
            P("dp", "tensor"),
            P(None, "tensor", "dp"),
            P("tensor", "dp"),
            P(None, "dp"),
            P("dp"),
            P("tensor"),
            P("tensor"),
            P("tensor"),
            P("tensor", "dp"),
            P("tensor", "dp"),
        ),
        check_vma=False,
    )
```

time: 1960 us -> 553 us (0.28)
  local copies, waits for them, and re-layouts: 500 us -> 47.5 us
  other arithmetic: 380 us -> 21.2 us
  matrix products: 387 us -> 52.2 us
  blocking collectives: 193 us -> 0 us
  waiting for transfers between devices: 446 us -> 281 us
  Pallas kernels: 0 us -> 121 us
    dot_general x174 -> x14, matrix products: 378 us -> 52.2 us  [the longest x9 31.1 us: nt(): lax.dot_general(left, right, (((1,), (1,)), ((), ())), preferred_element_...]
    reduce_scatter x5 -> x0, waiting for transfers between devices: 287 us -> none  [the longest x1 105 us: on_device(): lax.psum_scatter(grad_proj_gate_inner, 'dp', scatter_dimension=0, tiled=T...]
    dynamic_slice x547 -> x4, local copies, waits for them, and re-layouts: 238 us -> 1.97 us  [own_shard(): lax.dynamic_slice_in_dim(value, shard_rank * length, length, value.ndim - 1)]
    add x226 -> x0, other arithmetic: 142 us -> none  [the longest x192 119 us: advance(): return (pieces[0] * state_now + pieces[1], state_now)]
    pallas_call x0 -> x5, Pallas kernels: none -> 121 us  [the longest x1 53.3 us: on_device(): pl.pallas_call(backward_kernel, grid=(groups,), in_specs=[SMEM_SPEC, pl.B...]
    all_gather x4 -> x0, blocking collectives: 77.6 us -> none  [the longest x1 21.4 us: on_device(): lax.all_gather(proj_state, 'dp', axis=0, tiled=True)]
    dynamic_update_slice x65 -> x0, local copies, waits for them, and re-layouts: 71.5 us -> none  [the longest x32 46.1 us: on_device(): lax.scan(backward_head, (score_zero, state_zero, state_zero), (cum_decay....]
    dynamic_update_slice x288 -> x0, other arithmetic: 66.2 us -> none  [group_states(): lax.scan(advance, initial, (state_decay, group_state))]
  transfers between devices with their start and end apart: 15 -> 11, of which waited for: 9 -> 8; matrix products, arithmetic and copies ran while one was open for 27% -> 17% of each run, Pallas kernels for 0% -> 7%
where the time goes in v1:
time: 553 us; the launch traced here: 545 us
  waiting for transfers between devices  281 us (51%)
  Pallas kernels  121 us (22%)
  matrix products  52.2 us (9%)
  local copies, waits for them, and re-layouts  47.5 us (9%)
  other arithmetic  21.2 us (4%)
  between operations  14.7 us (3%)
  starting transfers between devices  8.59 us (2%)
    unnamed x7, waiting for transfers between devices  135 us
    pallas_call x1, Pallas kernels, on_device(): pl.pallas_call(backward_kernel, grid=(groups,), in_specs=[SMEM_SPEC, pl.B...  53.3 us
    psum x1, waiting for transfers between devices, on_device(): small_sum = lax.psum(placed, ('dp', 'tensor'))  44.7 us
    ppermute x6, waiting for transfers between devices, exchange(): return lax.ppermute(value, 'tensor', swap)  40.9 us
    all_gather x1, waiting for transfers between devices, on_device(): w_first = lax.all_gather(first_shard, 'dp', axis=0, tiled=True)  38.9 us
    dot_general x9, matrix products, nt(): lax.dot_general(left, right, (((1,), (1,)), ((), ())), preferred_element_...  31.1 us
    pallas_call x1, Pallas kernels, on_device(): pl.pallas_call(forward_kernel, grid=(groups,), in_specs=[SMEM_SPEC, SMEM_...  27.8 us
    dot_general x5, matrix products, tn(): lax.dot_general(left, right, (((0,), (0,)), ((), ())), preferred_element_...  21.1 us
  transfers between devices with their start and end apart: 11, of which 8 were waited for; matrix products, arithmetic and copies ran while one was open for 17% of the time, Pallas kernels for 7%

profile of v1, /device:TPU:0, one launch (start us, length us, event | category | flops | bytes accessed | tf_op | source)
XLA Modules:
  0.0 545.4 jit_solution(18233743590454033906)
XLA Ops:
  7.2 1.6 fusion.60
  10.3 1.4 copy.40
  11.7 0.8 copy.41
  12.5 1.4 copy.44
  13.8 1.4 copy.45
  15.2 1.4 copy.46
  16.5 1.4 reshape.122
  17.9 1.5 concatenate.24
  19.4 1.5 fusion.49
  21.0 1.6 pad_maximum_fusion.2
  22.7 3.0 collective-permute-start.1
  25.8 0.7 broadcast_in_dim.56
  29.2 38.9 %all-gather.3.cloned.1.call-done.w_ref = bf16[1024,1408]{1,0:T(8,128)(2,1)} async-done(((bf16[64,1408]{1,0:T(8,128)(2,1)}), bf16[1024,1408]{1,0:T(8,128)(2,1)}) %all-gather.3.cloned.1.call-update) | async-done | bytes 2883600 | tf_op jit(solution)/shard_map/all_gather | solution.py:611
  68.1 1.1 slice.146
  71.1 27.8 %mixer_forward.1 = (bf16[1536,1024]{1,0:T(8,128)(2,1)}, f32[1536,1024]{1,0:T(8,128)}, f32[1536,256]{1,0:T(8,128)}, bf16[1536,256]{1,0:T(8,128)(2,1)}, f32[1536,1...) custom-call(s32[1,1]{1,0:T(1,128)} %bitcast.rank_ref, s32[1,4]{1,0:T(1,128)} %len_ref.7, ...), custom_call_target="tpu_custom_call" | custom-call | tf_op jit(solution)/shard_map/mixer_forward/pallas_call | solution.py:638
  98.8 20.9 %all-gather.5.cloned.1.call-done.w_ref.proj_ref = bf16[1024,2048]{1,0:T(8,128)(2,1)} async-done(((bf16[64,2048]{1,0:T(8,128)(2,1)}), bf16[1024,2048]{1,0:T(8,128)(2,1)}) %all-gather.5.cloned.1.call-update) | async-done | bytes 4194320 | tf_op jit(solution)/shard_map/all_gather | solution.py:612
  119.8 16.7 %gate_forward.1 = (f32[1536,1024]{1,0:T(8,128)}, f32[1536,1024]{1,0:T(8,128)}, bf16[1536,1024]{1,0:T(8,128)(2,1)}, f32[8,1536]{1,0:T(8,128)}) custom-call(s32[1,1]{1,0:T(1,128)} %bitcast.rank_ref, s32[1,4]{1,0:T(1,128)} %len_ref.7, bf16[768,1024]{1,0:T(8,128)(2,1)} %own_ref.3, bf16[768,1024]{1,0:T(8,128)(2,1)} %collective-permute-done.other_ref, ...), custom_call_target="tpu_custom_call" | custom-call | tf_op jit(solution)/shard_map/gate_forward/pallas_call | solution.py:673
  136.5 1.5 collective-permute-start.2
  138.5 2.3 collective-permute-done.2.other_sums_ref
  141.4 13.4 %gate_backward.1 = (bf16[1536,1024]{1,0:T(8,128)(2,1)}, bf16[1536,1024]{1,0:T(8,128)(2,1)}, bf16[1536,1024]{1,0:T(8,128)(2,1)}, f32[8,1024]{1,0:T(8,128)}) custom-call(f32[8,1536]{1,0:T(8,128)} %get-tuple-element.39.own_sums_ref, f32[8,1536]{1,0:T(8,128)} %copy-done.12, f32[1536,1024]{1,0:T(8,128)} %get-tuple-element.40.gate_ref, ...), custom_call_target="tpu_custom_call" | custom-call | tf_op jit(solution)/shard_map/gate_backward/pallas_call | solution.py:698
  154.8 53.3 %mixer_backward.1 = (bf16[1536,1024]{1,0:T(8,128)(2,1)}, bf16[1536,256]{1,0:T(8,128)(2,1)}, bf16[1536,128]{1,0:T(8,128)(2,1)}, f32[8,1024]{1,0:T(8,128)}, f32[8,128]{1,0:T(8,128)}) custom-call(s32[1,4]{1,0:T(1,128)} %len_ref.7, f32[1536,1024]{1,0:T(8,128)} %get-tuple-element.44.ipre_ref.halo_ref, f32[1536,1024]{1,0:T(8,128)} %get-tuple-element.44.ipre_ref.halo_ref, ...), custom_call_target="tpu_custom_call" | custom-call | tf_op jit(solution)/shard_map/mixer_backward/pallas_call | solution.py:733
  208.2 0.9 slice_reduce_fusion.3
  209.1 0.8 reshape.116
  210.5 0.8 slice.125
  211.3 1.5 collective-permute-start.5
  213.4 2.7 convolution_convert_fusion.4
  216.8 1.8 fusion.8
  218.9 1.0 copy-done.19
  219.9 3.0 add_convert_fusion
  224.1 3.5 fusion.10
  227.6 2.3 fusion.45
  229.8 3.6 fusion.14
  233.4 5.0 convolution_convert_fusion
  238.4 9.5 %state_backward.1 = (bf16[1536,256]{1,0:T(8,128)(2,1)}, f32[8,256]{1,0:T(8,128)}) custom-call(s32[1,4]{1,0:T(1,128)} %len_ref.7, bf16[1536,256]{1,0:T(8,128)(2,1)} %get-tuple-element.51.own_ref, bf16[1536,256]{1,0:T(8,128)(2,1)} %collective-permute-done.5.other_ref, f32[1536,256]{1,0:T(8,128)} %get-tuple-element.52.spre_ref, ...), custom_call_target="tpu_custom_call" | custom-call | tf_op jit(solution)/shard_map/state_backward/pallas_call | solution.py:802
  247.9 0.8 reshape.117
  248.8 0.8 constant_dynamic-update-slice_fusion.3
  249.6 3.2 convolution_convert_fusion.3
  252.8 11.0 %collective-permute-done.4 = bf16[768,1024]{1,0:T(8,128)(2,1)} collective-permute-done((bf16[768,1024]{1,0:T(8,128)(2,1)}, bf16[768,1024]{1,0:T(8,128)(2,1)}, u32[]{:S(2)}, u32[]{:S(2)}) %collective-permute-start.4) | collective-permute-done | bytes 1572896 | tf_op jit(solution)/shard_map/ppermute | solution.py:589
  263.8 6.7 %fusion.7 = (f32[1024]{0:T(1024)S(1)}, f32[768]{0:T(1024)S(1)}, f32[768,1024]{1,0:T(8,128)}) fusion(bf16[768,1024]{1,0:T(8,128)(2,1)S(1)} %copy-done.1, f32[768]{0:T(1024)S(1)} %get-tuple-element.99, f32[1024]{0:T(1024)S(1)} %bitcast.62, bf16[1024,1408]{1,0:T(8,128)(2,1)} %all-gather.3.cloned.1.call-done.w_ref, bf16[1536,256]{1,0:T(8,128)(2,1)S(1)} %copy-done.10, ...), kind=kOutput, calls=%fused_computation.13 | convolution fusion | flops 412088576 | bytes 16661508 | tf_op jit(solution)/shard_map/dot_general | solution.py:30
  270.6 0.7 broadcast_select_fusion
  271.4 3.4 pad_maximum_fusion.1
  274.8 4.6 copy.57
  279.7 6.5 %convolution_convert_fusion.1 = bf16[1024,1024]{0,1:T(8,128)(2,1)S(1)} fusion(bf16[1536,1024]{1,0:T(8,128)(2,1)} %get-tuple-element.37.normed_ref, bf16[1536,1024]{1,0:T(8,128)(2,1)} %get-tuple-element.43), kind=kOutput, calls=%fused_computation.18 | convolution fusion | flops 3222274048 | bytes 8388608 | tf_op jit(solution)/shard_map/dot_general | solution.py:34
  286.2 3.8 convolution_convert_fusion.2
  290.0 2.4 pad_maximum_fusion
  292.4 6.5 %copy.55 = bf16[1024,2048]{1,0:T(8,128)(2,1)} copy(bf16[1024,2048]{0,1:T(8,128)(2,1)} %pad_maximum_fusion) | data formatting | bytes 8388608
  299.0 5.2 fusion.20
  304.2 1.5 collective-permute-start.3
  307.0 4.6 fusion.4
  311.6 27.6 %collective-permute-done.3 = bf16[768,1024]{1,0:T(8,128)(2,1)} collective-permute-done((bf16[768,1024]{1,0:T(8,128)(2,1)}, bf16[768,1024]{1,0:T(8,128)(2,1)}, u32[]{:S(2)}, u32[]{:S(2)}) %collective-permute-start.3) | collective-permute-done | bytes 1572896 | tf_op jit(solution)/shard_map/ppermute | solution.py:589
  339.1 4.6 fusion
  343.7 44.7 %all-reduce.6.cloned.1.call-done = f32[2,8832]{1,0:T(2,128)} async-done(((f32[2,8832]{1,0:T(2,128)}), f32[2,8832]{1,0:T(2,128)}) %all-reduce.6.cloned.1.call-update) | async-done | bytes 70672 | tf_op jit(solution)/shard_map/psum | solution.py:847
  388.4 0.8 dynamic-slice_reduce_fusion
  390.4 0.8 dynamic-slice_reduce_fusion.1
  393.2 1.2 dynamic-slice.5
  394.4 0.8 dynamic-slice_reduce_fusion.2
  395.7 63.4 %reduce-scatter.9.cloned.1.call-done = bf16[64,1408]{1,0:T(8,128)(2,1)} async-done(((bf16[1024,1408]{1,0:T(8,128)(2,1)}), bf16[64,1408]{1,0:T(8,128)(2,1)}) %reduce-scatter.9.cloned.1.call-update) | async-done | bytes 180240
  459.1 0.9 slice.159
  460.2 0.8 slice.160
  461.0 0.7 copy.53
  463.2 71.7 %reduce-scatter.7.cloned.1.call-done = bf16[64,2048]{1,0:T(8,128)(2,1)} async-done(((bf16[1024,2048]{1,0:T(8,128)(2,1)}), bf16[64,2048]{1,0:T(8,128)(2,1)}) %reduce-scatter.7.cloned.1.call-update) | async-done | bytes 262160
  534.9 1.0 fusion.59
  536.2 1.1 copy.52
  537.6 0.9 copy.54
  (113 shorter events, 18.3 us)
Async XLA Ops:
  7.2 15.5 %copy-start = (bf16[768,1024]{1,0:T(8,128)(2,1)S(1)}, bf16[768,1024]{1,0:T(8,128)(2,1)}, u32[]{:S(2)}) copy-start(bf16[768,1024]{1,0:T(8,128)(2,1)} %own_ref.2) | copy-start | bytes 4718596
  7.2 18.6 %copy-start.5 = (bf16[768,1024]{1,0:T(8,128)(2,1)S(1)}, bf16[768,1024]{1,0:T(8,128)(2,1)}, u32[]{:S(2)}) copy-start(bf16[768,1024]{1,0:T(8,128)(2,1)} %own_ref.3) | copy-start | bytes 4718596
  7.2 60.9 %all-gather.3.cloned.1.call-start = ((), (), s32[]{:S(2)}) async-start(), calls=%async_computation.2 | async-start | bytes 3063808 | tf_op jit(solution)/shard_map/all_gather | solution.py:611
  20.9 98.9 %all-gather.5.cloned.1.call-start = ((), (), s32[]{:S(2)}) async-start(), calls=%async_computation.3 | async-start | bytes 4456448 | tf_op jit(solution)/shard_map/all_gather | solution.py:612
  22.7 365.7 %all-reduce.6.cloned.1.call-start = ((), (), s32[]{:S(2)}) async-start(), calls=%async_computation.4 | async-start | bytes 141312 | tf_op jit(solution)/shard_map/psum | solution.py:847
  22.7 48.3 %collective-permute-start.1 = (bf16[768,1024]{1,0:T(8,128)(2,1)S(1)}, bf16[768,1024]{1,0:T(8,128)(2,1)}, u32[]{:S(2)}, u32[]{:S(2)}) collective-permute-start(bf16[768,1024]{1,0:T(8,128)(2,1)S(1)} %copy-done), channel_id=1, source_target_pairs={{0,1},{1,0},{2,3},{3,2},{4,5},{5,4},{6,7},{7,6},{8,9},{9,8},{10,11... | collective-permute-start | bytes 4718600 | tf_op jit(solution)/shard_map/ppermute | solution.py:589
  25.8 73.1 %collective-permute-start = (bf16[768,1024]{1,0:T(8,128)(2,1)S(1)}, bf16[768,1024]{1,0:T(8,128)(2,1)}, u32[]{:S(2)}, u32[]{:S(2)}) collective-permute-start(bf16[768,1024]{1,0:T(8,128)(2,1)S(1)} %copy-done.5), channel_id=1, source_target_pairs={{0,1},{1,0},{2,3},{3,2},{4,5},{5,4},{6,7},{7,6},{8,9},{9,8},{10,11... | collective-permute-start | bytes 4718600 | tf_op jit(solution)/shard_map/ppermute | solution.py:589
  136.5 4.4 collective-permute-start.2
  140.8 0.6 copy-start.12
  208.1 8.0 %copy-start.7 = (bf16[1024,1408]{1,0:T(8,128)(2,1)S(1)}, bf16[1024,1408]{1,0:T(8,128)(2,1)}, u32[]{:S(2)}) copy-start(bf16[1024,1408]{1,0:T(8,128)(2,1)} %all-gather.3.cloned.1.call-done.w_ref) | copy-start | bytes 8650756
  208.1 8.0 %copy-start.9 = (bf16[1536,128]{1,0:T(8,128)(2,1)S(1)}, bf16[1536,128]{1,0:T(8,128)(2,1)}, u32[]{:S(2)}) copy-start(bf16[1536,128]{1,0:T(8,128)(2,1)} %get-tuple-element.50) | copy-start | bytes 1179652
  211.3 27.1 %collective-permute-start.5 = (bf16[1536,256]{1,0:T(8,128)(2,1)}, bf16[1536,256]{1,0:T(8,128)(2,1)}, u32[]{:S(2)}, u32[]{:S(2)}) collective-permute-start(bf16[1536,256]{1,0:T(8,128)(2,1)} %get-tuple-element.51.own_ref), channel_id=1, source_target_pairs={{0,1},{1,0},{2,3},{3,2},{4,5},{5,4},{6,7},{7,6},{8,9},{9,8},{10,11... | collective-permute-start | bytes 2359304 | tf_op jit(solution)/shard_map/ppermute | solution.py:589
  213.4 3.3 copy-start.20
  216.8 2.2 copy-start.2
  216.8 3.2 copy-start.19
  222.9 40.9 %collective-permute-start.4 = (bf16[768,1024]{1,0:T(8,128)(2,1)}, bf16[768,1024]{1,0:T(8,128)(2,1)}, u32[]{:S(2)}, u32[]{:S(2)}) collective-permute-start(bf16[768,1024]{1,0:T(8,128)(2,1)} %add_convert_fusion), channel_id=1, source_target_pairs={{0,1},{1,0},{2,3},{3,2},{4,5},{5,4},{6,7},{7,6},{8,9},{9,8},{10,11... | collective-permute-start | bytes 4718600 | tf_op jit(solution)/shard_map/ppermute | solution.py:589
  229.8 3.6 copy-start.8
  238.3 10.4 %copy-start.11 = (f32[8832]{0:T(1024)S(1)}, f32[8832]{0:T(1024)}, u32[]{:S(2)}) copy-start(f32[8832]{0:T(1024)} %constant_dynamic-update-slice_fusion.5) | copy-start | bytes 105988
  238.4 11.2 %copy-start.15 = (f32[16]{0:T(128)S(1)}, f32[16]{0:T(128)}, u32[]{:S(2)}) copy-start(f32[16]{0:T(128)} %reduce_sum.57) | copy-start | bytes 196
  247.9 15.9 %copy-start.1 = (bf16[768,1024]{1,0:T(8,128)(2,1)S(1)}, bf16[768,1024]{1,0:T(8,128)(2,1)}, u32[]{:S(2)}) copy-start(bf16[768,1024]{1,0:T(8,128)(2,1)} %own_ref.2) | copy-start | bytes 4718596
  247.9 15.9 %copy-start.10 = (bf16[1536,256]{1,0:T(8,128)(2,1)S(1)}, bf16[1536,256]{1,0:T(8,128)(2,1)}, u32[]{:S(2)}) copy-start(bf16[1536,256]{1,0:T(8,128)(2,1)} %get-tuple-element.53) | copy-start | bytes 2359300
  248.7 15.1 %copy-start.4 = (f32[768,1024]{1,0:T(8,128)S(1)}, f32[768,1024]{1,0:T(8,128)}, u32[]{:S(2)}) copy-start(f32[768,1024]{1,0:T(8,128)} %fusion.45) | copy-start | bytes 9437188
  263.8 6.7 %copy-start.14 = (pred[2]{0:T(512)(128)(4,1)S(1)}, pred[2]{0:T(512)(128)(4,1)}, u32[]{:S(2)}) copy-start(pred[2]{0:T(512)(128)(4,1)} %iota_compare_fusion.3) | copy-start | bytes 10
  271.3 187.8 %reduce-scatter.9.cloned.1.call-start = ((), (), s32[]{:S(2)}) async-start(), calls=%async_computation.6 | async-start | bytes 3063808
  279.4 255.5 %reduce-scatter.7.cloned.1.call-start = ((), (), s32[]{:S(2)}) async-start(), calls=%async_computation.5 | async-start | bytes 4456448
  279.7 6.5 %copy-start.16 = (bf16[1536,1024]{1,0:T(8,128)(2,1)S(1)}, bf16[1536,1024]{1,0:T(8,128)(2,1)}, u32[]{:S(2)}) copy-start(bf16[1536,1024]{1,0:T(8,128)(2,1)} %get-tuple-element.42) | copy-start | bytes 9437188
  279.7 6.5 %copy-start.18 = (bf16[1536,1024]{1,0:T(8,128)(2,1)S(1)}, bf16[1536,1024]{1,0:T(8,128)(2,1)}, u32[]{:S(2)}) copy-start(bf16[1536,1024]{1,0:T(8,128)(2,1)} %get-tuple-element.58) | copy-start | bytes 9437188
  299.0 6.7 %copy-start.13 = (s32[1,4]{1,0:T(1,128)S(1)}, s32[1,4]{1,0:T(1,128)}, u32[]{:S(2)}) copy-start(s32[1,4]{1,0:T(1,128)} %len_ref.7) | copy-start | bytes 52
  299.0 8.0 %copy-start.6 = (bf16[768,1024]{1,0:T(8,128)(2,1)S(1)}, bf16[768,1024]{1,0:T(8,128)(2,1)}, u32[]{:S(2)}) copy-start(bf16[768,1024]{1,0:T(8,128)(2,1)} %own_ref.3) | copy-start | bytes 4718596
  304.2 35.0 %collective-permute-start.3 = (bf16[768,1024]{1,0:T(8,128)(2,1)}, bf16[768,1024]{1,0:T(8,128)(2,1)}, u32[]{:S(2)}, u32[]{:S(2)}) collective-permute-start(bf16[768,1024]{1,0:T(8,128)(2,1)} %fusion.20), channel_id=1, source_target_pairs={{0,1},{1,0},{2,3},{3,2},{4,5},{5,4},{6,7},{7,6},{8,9},{9,8},{10,11... | collective-permute-start | bytes 4718600 | tf_op jit(solution)/shard_map/ppermute | solution.py:589
  306.9 32.2 %copy-start.3 = (bf16[1024,2048]{1,0:T(8,128)(2,1)S(1)}, bf16[1024,2048]{1,0:T(8,128)(2,1)}, u32[]{:S(2)}) copy-start(bf16[1024,2048]{1,0:T(8,128)(2,1)} %all-gather.5.cloned.1.call-done.w_ref.proj_ref) | copy-start | bytes 12582916
  307.0 32.2 %copy-start.17 = (bf16[1536,1024]{1,0:T(8,128)(2,1)S(1)}, bf16[1536,1024]{1,0:T(8,128)(2,1)}, u32[]{:S(2)}) copy-start(bf16[1536,1024]{1,0:T(8,128)(2,1)} %get-tuple-element.42) | copy-start | bytes 9437188
Sparse Core Ops, SparseCore 0:
  21.0 47.0 all-gather.2
  70.9 48.8 all-gather.4
  271.4 116.9 all-reduce.5
  392.0 66.9 reduce-scatter.8
  463.3 71.5 reduce-scatter.6

commit v2 on v1

--- a/solution.py
+++ b/solution.py
@@ -16,6 +16,8 @@
 MASKED = -1e30
 VMEM_BYTES = 56 * 1024 * 1024
 
+LANE_CONV, LANE_GATE, LANE_STATE, LANE_HEADS = 16, 21, 24, 32
+
 F32 = jnp.float32
 BF16 = jnp.bfloat16
 
@@ -75,6 +77,38 @@
     return hit.astype(F32).astype(BF16)
 
 
+def spaced_matrix(narrow, wide, narrow_shard, wide_shard, compress):
+    shape = (wide, narrow) if compress else (narrow, wide)
+    at_wide = lax.broadcasted_iota(jnp.int32, shape, 0 if compress else 1)
+    at_narrow = lax.broadcasted_iota(jnp.int32, shape, 1 if compress else 0)
+    owner, place = at_wide // wide_shard, at_wide % wide_shard
+    hit = (place < narrow_shard) & (at_narrow == owner * narrow_shard + place)
+    return hit.astype(F32).astype(BF16)
+
+
+def pack_kernel(
+    state_ref, step_ref, norm_ref, conv_ref, bias_ref, gate_ref, taps_ref, taps_bias_ref,
+    out_ref, turned, lanes,
+):
+    shard, heads = step_ref.shape
+    states = state_ref.shape[1]
+    state_shard = taps_ref.shape[1]
+    base = 3 * heads
+    turned[...] = jnp.zeros_like(turned)
+    turned[base : base + 1, 0:shard] = norm_ref[...].astype(F32)
+    turned[base + 1 : base + 5, 0:shard] = conv_ref[...].astype(F32)
+    turned[base + 5 : base + 6, 0:shard] = bias_ref[...].astype(F32)
+    turned[base + 6 : base + 7, 0:shard] = gate_ref[...].astype(F32)
+    turned[base + 8 : base + 12, 0:state_shard] = taps_ref[...].astype(F32)
+    turned[base + 12 : base + 13, 0:state_shard] = taps_bias_ref[...].astype(F32)
+    lanes[...] = jnp.zeros_like(lanes)
+    step = step_ref[...].astype(F32)
+    for copy in range(3):
+        lanes[:, copy * heads : (copy + 1) * heads] = step
+    out_ref[:, :states] = state_ref[...]
+    out_ref[:, states:] = (turned[...].T[0:shard, :] + lanes[...]).astype(BF16)
+
+
 def lower_matrix(upper=False):
     row = lax.broadcasted_iota(jnp.int32, (GROUP, GROUP), 0)
     col = lax.broadcasted_iota(jnp.int32, (GROUP, GROUP), 1)
@@ -128,7 +162,7 @@
 
 
 def sigmoid(value):
-    return 1.0 / (1.0 + jnp.exp(-value))
+    return 0.5 * jnp.tanh(0.5 * value) + 0.5
 
 
 def decay_terms(ends, first, step_in, rate, lower):
@@ -155,9 +189,10 @@
 
 
 def forward_kernel(
-    rank_ref, len_ref, own_ref, other_ref, w_ref, rows_ref, taps_ref, head_ref,
-    normed_ref, ipre_ref, spre_ref, sact_ref, stepin_ref, mixed_ref, sprev_ref,
-    ext, state, spread, lower, fac, read, mask, scores, weighted,
+    rank_ref, len_ref, own_ref, other_ref, w_ref, rest_ref, head_ref,
+    normed_ref, normed_t_ref, ipre_ref, spre_ref, sact_ref, stepin_ref, mixed_ref, sprev_ref,
+    rows_ref, taps_ref,
+    ext, state, spread, lower, fac, read, mask, scores, weighted, *, shard, state_shard,
 ):
     inner = rows_ref.shape[1]
     channels = ext.shape[1]
@@ -173,6 +208,16 @@
         state[...] = jnp.zeros_like(state)
         spread[...] = spread_matrix(heads, LANES // PAIR_HEADS)
         lower[...] = lower_matrix()
+        packed = rest_ref[:, 2 * size :].astype(F32).T
+        base = 3 * heads
+        rows_ref[0:7, :] = packed[base : base + 7, :]
+        once = lax.broadcasted_iota(jnp.int32, (16, LANES), 1) < heads
+        skip_row = jnp.where(once, head_ref[2:3, :], 0.0).astype(BF16)
+        rows_ref[7:8, :] = nn(skip_row, spread[...])[0:1, :]
+        taps_ref[...] = nn(
+            packed[base + 8 : base + 16, :].astype(BF16),
+            spaced_matrix(2 * size, rest_ref.shape[0], state_shard, shard, True),
+        )
 
     mine = rank_ref[0, 0] == group // (pl.num_programs(0) // 2)
     gain = rows_ref[ROW_NORM : ROW_NORM + 1, :]
@@ -182,12 +227,15 @@
         inv = lax.rsqrt(jnp.mean(hidden * hidden, axis=1, keepdims=True) + NORM_EPS)
         normed_ref[sl, :] = (hidden * inv * gain).astype(BF16)
 
+    normed_t_ref[...] = normed_ref[...].T
     pre = nn(normed_ref[...], w_ref[...])
-    ext[8 : 8 + GROUP, :] = pre[:, :channels]
-    ipre_ref[...] = pre[:, :inner]
-    spre_ref[...] = pre[:, inner:channels]
+    ext[8 : 8 + GROUP, 0:inner] = pre
+    ipre_ref[...] = pre
+    rest = nn(normed_ref[...], rest_ref[...])
+    ext[8 : 8 + GROUP, inner:channels] = rest[:, : 2 * size]
+    spre_ref[...] = rest[:, : 2 * size]
     lane = lax.broadcasted_iota(jnp.int32, (1, LANES), 1)
-    step_in = jnp.where(lane < 3 * heads, pre[:, channels:], 0.0) + head_ref[0:1, :]
+    step_in = jnp.where(lane < 3 * heads, rest[:, 2 * size :], 0.0) + head_ref[0:1, :]
     stepin_ref[...] = step_in
 
     token = tokens_column(first)
@@ -262,7 +310,7 @@
 
 def gate_kernel(
     rank_ref, len_ref, own_ref, other_ref, normed_ref, mixed_ref, w_ref, proj_ref, rows_ref,
-    gate_ref, gol_ref, live_ref, sums_ref,
+    gate_ref, gol_ref, live_t_ref, sums_ref,
 ):
     group = pl.program_id(0)
     first = group * GROUP
@@ -270,9 +318,10 @@
     mine = rank_ref[0, 0] == group // (pl.num_programs(0) // 2)
     valid = tokens_column(first) < ends[-1]
     cotangent = jnp.where(mine, own_ref[...].astype(F32), other_ref[...].astype(F32))
-    live_ref[...] = jnp.where(valid, cotangent, 0.0).astype(BF16)
+    live = jnp.where(valid, cotangent, 0.0).astype(BF16)
+    live_t_ref[...] = live.T
     gate_ref[...] = nn(normed_ref[...], w_ref[...])
-    gol_ref[...] = nn(live_ref[...], proj_ref[...])
+    gol_ref[...] = nn(live, proj_ref[...])
     gain = rows_ref[ROW_GATE : ROW_GATE + 1, :]
     lane = lax.broadcasted_iota(jnp.int32, (64, LANES), 1)
     pieces = []
@@ -314,6 +363,18 @@
         first_ref[sl, :] = (grad * silu).astype(BF16)
         ggp_ref[sl, :] = (grad * mixed * (logistic * (1.0 + gate * (1.0 - logistic)))).astype(BF16)
     gain_ref[0:1, :] += total
+
+
+def early_grad_kernel(live_t_ref, low_ref, normed_t_ref, ggp_ref, out_ref):
+    half = pl.num_programs(0) // 2
+
+    @pl.when(pl.program_id(0) < half)
+    def _():
+        out_ref[...] = nn(live_t_ref[...], low_ref[...]).astype(BF16)
+
+    @pl.when(pl.program_id(0) >= half)
+    def _():
+        out_ref[...] = nn(normed_t_ref[...], ggp_ref[...]).astype(BF16)
 
 
 def backward_kernel(
@@ -461,15 +522,19 @@
     balance = collected[:GROUP]
     direct = collected[GROUP : 2 * GROUP]
     key_dot = collected[2 * GROUP :]
-    product = jnp.sum(gstate[...] * state.astype(F32), axis=0, keepdims=True)
-    product_high = product.astype(BF16)
-    product_low = (product - product_high.astype(F32)).astype(BF16)
-    rows16 = jnp.concatenate(
-        [jnp.broadcast_to(product_high, (8, inner)), jnp.broadcast_to(product_low, (8, inner))],
-        axis=0,
-    ).astype(BF16)
-    carried = nn(rows16, collect[...])
-    carry_term = decay * (carried[0:1, :] + carried[8:9, :])
+
+    def row_collect(value):
+        high = value.astype(BF16)
+        low = (value - high.astype(F32)).astype(BF16)
+        rows16 = jnp.concatenate(
+            [jnp.broadcast_to(high, (8, inner)), jnp.broadcast_to(low, (8, inner))], axis=0
+        )
+        found = nn(rows16, collect[...])
+        return found[0:1, :] + found[8:9, :]
+
+    carry_term = decay * row_collect(
+        jnp.sum(gstate[...] * state.astype(F32), axis=0, keepdims=True)
+    )
     moved = key_step * key_dot
     grad_log = (
         exact_left(upper[...], balance) + carry_term + exact_left(lower[...], moved) - moved
@@ -482,11 +547,18 @@
     heads_ref[1:2, :] += jnp.sum(grad_step_in, axis=0, keepdims=True)
     gstate[...] = fac[3 * GROUP : 3 * GROUP + 1, :] * gstate[...] + tn(queries, entered[...])
 
+    @pl.when(turn == pl.num_programs(0) - 1)
+    def _():
+        heads_ref[2:3, :] = row_collect(conv_ref[5:6, :])
+
 
 def state_grad_kernel(
-    len_ref, own_ref, other_ref, spre_ref, taps_ref, gsp_ref, conv_ref, ext, cext
+    len_ref, own_ref, other_ref, spre_ref, taps_ref, normed_t_ref, gstep_ref, inner_rows_ref,
+    gain_ref, heads_ref,
+    gsp_ref, rest_ref, conv_ref, ext, cext, turned, *, shard, state_shard, heads,
 ):
     rows, channels = spre_ref.shape
+    width = rest_ref.shape[0]
     ends = sequence_ends(len_ref)
     ext[0:8, :] = jnp.zeros((8, channels), F32)
     ext[8 : 8 + rows, :] = spre_ref[...]
@@ -532,6 +604,21 @@
                     * cext[base + offset : base + offset + GROUP, sl]
                 )
             gsp_ref[base : base + GROUP, sl] = result.astype(BF16)
+    rest_ref[:, :channels] = nn(normed_t_ref[...], gsp_ref[...]).astype(BF16)
+    step_part = nn(normed_t_ref[...], gstep_ref[...])
+    turned[...] = jnp.zeros_like(turned)
+    turned[LANE_CONV : LANE_CONV + 5, :] = inner_rows_ref[0:5, :]
+    turned[LANE_GATE : LANE_GATE + 1, :] = gain_ref[0:1, :]
+    turned[LANE_STATE : LANE_STATE + 8, :] = nn(
+        conv_ref[...].astype(BF16), spaced_matrix(channels, width, state_shard, shard, False)
+    )
+    columns = jnp.concatenate([heads_ref[...], jnp.zeros((LANES - 8, LANES), F32)], axis=0).T
+    for which in range(3):
+        start = LANE_HEADS + which * heads
+        turned[start : start + heads, :] = jnp.broadcast_to(
+            columns[0:heads, which : which + 1], (heads, width)
+        )
+    rest_ref[:, channels:] = (step_part + turned[...].T).astype(BF16)
 
 
 def shape_of(dims, dtype):
@@ -547,6 +634,44 @@
 
 def whole(*dims):
     return pl.BlockSpec(dims, lambda i: (0,) * len(dims))
+
+
+def bit_order(count, spread_first):
+    bits = list(range(count.bit_length() - 1))
+    return [0] + bits[2:] + [1] if spread_first and len(bits) > 1 else bits
+
+
+def flip(value, bit, count):
+    return lax.ppermute(value, "dp", [(i, i ^ (1 << bit)) for i in range(count)])
+
+
+def gather_by_bits(value, rank, count, spread_first):
+    held = []
+    rows, lanes = value.shape
+    for bit in reversed(bit_order(count, spread_first)):
+        other = flip(value, bit, count)
+        held = sorted(held + [bit], reverse=True)
+        low = (rank >> bit) & 1 == 0
+        value = jnp.stack(
+            [jnp.where(low, value, other), jnp.where(low, other, value)], axis=held.index(bit)
+        )
+    return value.reshape(count * rows, lanes)
+
+
+def scatter_by_bits(value, rank, count, spread_first):
+    left = list(reversed(range(count.bit_length() - 1)))
+    rows, lanes = value.shape[0] // count, value.shape[1]
+    value = value.reshape([2] * len(left) + [rows, lanes])
+    for bit in bit_order(count, spread_first):
+        axis = left.index(bit)
+        mine = (rank >> bit) & 1
+        away = lax.dynamic_index_in_dim(value, 1 - mine, axis, keepdims=False)
+        here = lax.dynamic_index_in_dim(value, mine, axis, keepdims=False)
+        left.remove(bit)
+        value = here.astype(F32) + flip(away, bit, count).astype(F32)
+        if left:
+            value = value.astype(BF16)
+    return value
 
 
 def on_device(
@@ -589,71 +714,68 @@
         return lax.ppermute(value, "tensor", swap)
 
     hidden_other = exchange(hidden_in)
-    cotangent_other = exchange(cotangent)
+    cotangent_other = exchange(lax.optimization_barrier((cotangent, hidden_other))[0])
 
     state_shard = conv_state.shape[1]
-    bias_column = jnp.pad(conv_state_bias, (0, shard - state_shard))
-    columns = jnp.concatenate(
-        [
-            proj_step, proj_step, proj_step,
-            norm_gain[:, None],
-            conv_inner.reshape(taps, shard).T,
-            conv_inner_bias.reshape(shard, 1),
-            gate_gain.reshape(shard, 1),
-            conv_state.reshape(shard, 1),
-            bias_column[:, None],
-        ],
-        axis=1,
-    )
-    columns = jnp.pad(columns, ((0, 0), (0, LANES - columns.shape[1])))
-    first_shard = jnp.concatenate([projection_gate_inner[:, 1], proj_state, columns], axis=1)
+    rest_shard = pl.pallas_call(
+        pack_kernel,
+        in_specs=[pl.BlockSpec(memory_space=pltpu.VMEM)] * 8,
+        out_specs=pl.BlockSpec(memory_space=pltpu.VMEM),
+        out_shape=shape_of((shard, 2 * size + LANES), BF16),
+        scratch_shapes=[
+            pltpu.VMEM((LANES, max(LANES, shard)), F32),
+            pltpu.VMEM((shard, LANES), F32),
+        ],
+        compiler_params=params(),
+        name="pack_small",
+    )(
+        proj_state, proj_step, norm_gain[None, :], conv_inner.reshape(taps, shard),
+        conv_inner_bias, gate_gain, conv_state, conv_state_bias[None, :],
+    )
     second_shard = jnp.concatenate([projection_gate_inner[:, 0], proj_out.T], axis=1)
-    w_first = lax.all_gather(first_shard, "dp", axis=0, tiled=True)
     w_second = lax.all_gather(second_shard, "dp", axis=0, tiled=True)
-    w_inner = w_first[:, :inner]
-    w_state = w_first[:, inner:channels]
-    w_step = w_first[:, channels:]
+    w_inner = gather_by_bits(projection_gate_inner[:, 1], shard_rank, shard_count, False)
+    w_rest = gather_by_bits(rest_shard, shard_rank, shard_count, True)
+    w_state = w_rest[:, : 2 * size]
+    w_step = w_rest[:, 2 * size :]
     w_gate = w_second[:, :inner]
     w_out = w_second[:, inner:]
 
-    base = 3 * heads
-    small = w_step[:, base : base + 9].astype(F32).T
-    skip_row = jnp.repeat(skip_gain.astype(F32), head_size)[None, :]
-    rows = jnp.concatenate([small[0:7], skip_row], axis=0)
-    state_taps = small[7].reshape(shard_count, taps, state_shard).transpose(1, 0, 2)
-    state_taps = state_taps.reshape(taps, 2 * size)
-    state_bias = small[8].reshape(shard_count, shard)[:, :state_shard].reshape(1, 2 * size)
-    state_rows = jnp.concatenate(
-        [state_taps, state_bias, jnp.zeros((3, 2 * size), F32)], axis=0
-    )
     rate = -jnp.exp(decay_log.astype(F32))
-    head_rows = jnp.stack([jnp.tile(step_bias.astype(F32), 3), jnp.tile(rate, 3)])
-    head_rows = jnp.pad(head_rows, ((0, 6), (0, LANES - base)))
+    head_rows = jnp.stack([step_bias.astype(F32), rate, skip_gain.astype(F32)])
+    head_rows = jnp.pad(jnp.tile(head_rows, (1, 3)), ((0, 5), (0, LANES - 3 * heads)))
     rank = tensor_rank.astype(jnp.int32).reshape(1, 1)
 
     def by_group(lanes):
         return pl.BlockSpec((GROUP, lanes), lambda i: (i, 0))
 
     half_block = pl.BlockSpec((GROUP, width), lambda i: (i % half_groups, 0))
-    normed, inner_pre, state_pre, state_act, step_in, mixed, prev_states = pl.pallas_call(
-        forward_kernel,
+    (
+        normed, normed_t, inner_pre, state_pre, state_act, step_in, mixed, prev_states, rows,
+        state_rows,
+    ) = pl.pallas_call(
+        functools.partial(forward_kernel, shard=shard, state_shard=state_shard),
         grid=(groups,),
         in_specs=[
             SMEM_SPEC, SMEM_SPEC, half_block, half_block,
-            whole(width, channels + LANES), whole(8, inner), whole(8, 2 * size), whole(8, LANES),
+            whole(width, inner), whole(width, 2 * size + LANES), whole(8, LANES),
         ],
         out_specs=[
-            by_group(width), by_group(inner), by_group(2 * size), by_group(2 * size),
+            by_group(width), pl.BlockSpec((width, GROUP), lambda i: (0, i)), by_group(inner), by_group(2 * size), by_group(2 * size),
             by_group(LANES), by_group(inner), pl.BlockSpec((size, inner), lambda i: (i, 0)),
+            whole(8, inner), whole(8, 2 * size),
         ],
         out_shape=[
             shape_of((tokens, width), BF16),
+            shape_of((width, tokens), BF16),
             shape_of((tokens, inner), F32),
             shape_of((tokens, 2 * size), F32),
             shape_of((tokens, 2 * size), BF16),
             shape_of((tokens, LANES), F32),
             shape_of((tokens, inner), F32),
             shape_of((groups * size, inner), BF16),
+            shape_of((8, inner), F32),
+            shape_of((8, 2 * size), F32),
         ],
         scratch_shapes=[
             pltpu.VMEM((GROUP + 8, channels), F32),
@@ -668,9 +790,9 @@
         ],
         compiler_params=params(),
         name="mixer_forward",
-    )(rank, lengths, hidden_in, hidden_other, w_first, rows, state_rows, head_rows)
-
-    gate_pre, grad_out_low, live, sums = pl.pallas_call(
+    )(rank, lengths, hidden_in, hidden_other, w_inner, w_rest, head_rows)
+
+    gate_pre, grad_out_low, live_t, sums = pl.pallas_call(
         gate_kernel,
         grid=(groups,),
         in_specs=[
@@ -680,13 +802,13 @@
             whole(8, inner),
         ],
         out_specs=[
-            by_group(inner), by_group(inner), by_group(width),
+            by_group(inner), by_group(inner), pl.BlockSpec((width, GROUP), lambda i: (0, i)),
             pl.BlockSpec((8, GROUP), lambda i: (0, i)),
         ],
         out_shape=[
             shape_of((tokens, inner), F32),
             shape_of((tokens, inner), F32),
-            shape_of((tokens, width), BF16),
+            shape_of((width, tokens), BF16),
             shape_of((8, tokens), F32),
         ],
         compiler_params=params(),
@@ -713,15 +835,31 @@
         name="gate_backward",
     )(sums, sums_other, gate_pre, grad_out_low, mixed, rows)
 
-    first_grads = jnp.concatenate(
-        [tn(live, out_low).astype(BF16), tn(normed, grad_gate_low).astype(BF16)], axis=1
-    )
-    first_sum = lax.psum_scatter(first_grads, "dp", scatter_dimension=0, tiled=True)
+    tiles = 2 * inner // GROUP
+    half_tiles = tiles // 2
+    first_grads = pl.pallas_call(
+        early_grad_kernel,
+        grid=(tiles,),
+        in_specs=[
+            whole(width, tokens),
+            pl.BlockSpec((tokens, GROUP), lambda i: (0, jnp.minimum(i, half_tiles - 1))),
+            whole(width, tokens),
+            pl.BlockSpec((tokens, GROUP), lambda i: (0, jnp.maximum(i - half_tiles, 0))),
+        ],
+        out_specs=pl.BlockSpec((width, GROUP), lambda i: (0, i)),
+        out_shape=shape_of((width, 2 * inner), BF16),
+        compiler_params=params(),
+        name="early_weight_grads",
+    )(live_t, out_low, normed_t, grad_gate_low)
 
     def rows_of(value, which):
         return lax.dynamic_slice_in_dim(value, which * half_rows, half_rows)
 
     mix_away = nt(rows_of(out_low, 1 - tensor_rank), w_out).astype(BF16)
+    grad_first, first_grads, mix_away = lax.optimization_barrier(
+        (grad_first, first_grads, mix_away)
+    )
+    first_sum = lax.psum_scatter(first_grads, "dp", scatter_dimension=0, tiled=True)
     mix_here = nt(rows_of(out_low, tensor_rank), w_out)
     mix = mix_here + exchange(mix_away).astype(F32)
     slot = tensor_rank * half_rows + jnp.arange(half_rows, dtype=jnp.int32)
@@ -796,33 +934,36 @@
 
     normed_away = exchange(partial_normed(1 - tensor_rank).astype(BF16))
     normed_here = partial_normed(tensor_rank)
-    grad_inner_weight = tn(normed, grad_inner_low).astype(BF16)
-    grad_step_weight = tn(normed, grad_step_low).astype(BF16)
-
-    grad_state_low, state_conv_rows = pl.pallas_call(
-        state_grad_kernel,
-        in_specs=[SMEM_SPEC] + [pl.BlockSpec(memory_space=pltpu.VMEM)] * 4,
-        out_specs=[pl.BlockSpec(memory_space=pltpu.VMEM)] * 2,
-        out_shape=[shape_of((tokens, 2 * size), BF16), shape_of((8, 2 * size), F32)],
+    inner_sum = scatter_by_bits(
+        nn(normed_t, grad_inner_low).astype(BF16), shard_rank, shard_count, False
+    )
+
+    vmem = pl.BlockSpec(memory_space=pltpu.VMEM)
+    grad_state_low, rest_grads = pl.pallas_call(
+        functools.partial(
+            state_grad_kernel, shard=shard, state_shard=state_shard, heads=heads
+        ),
+        in_specs=[SMEM_SPEC] + [vmem] * 9,
+        out_specs=[vmem] * 2,
+        out_shape=[shape_of((tokens, 2 * size), BF16), shape_of((width, 2 * size + LANES), BF16)],
         scratch_shapes=[
+            pltpu.VMEM((8, 2 * size), F32),
             pltpu.VMEM((tokens + 8, 2 * size), F32),
             pltpu.VMEM((tokens + 8, 2 * size), F32),
+            pltpu.VMEM((LANES, width), F32),
         ],
         compiler_params=params(),
         name="state_backward",
-    )(lengths, grad_kq, grad_kq_other, state_pre, state_rows)
-
-    grad_state_weight = tn(normed, grad_state_low).astype(BF16)
-    second_grads = jnp.concatenate(
-        [grad_inner_weight, grad_state_weight, grad_step_weight], axis=1
-    )
-    second_sum = lax.psum_scatter(second_grads, "dp", scatter_dimension=0, tiled=True)
+    )(
+        lengths, grad_kq, grad_kq_other, state_pre, state_rows, normed_t, grad_step_low,
+        conv_rows, gain_rows, head_sums,
+    )
+    rest_sum = scatter_by_bits(rest_grads, shard_rank, shard_count, True)
 
     grad_normed = normed_here + normed_away.astype(F32)
     grad_normed = grad_normed + nt(rows_of(grad_state_low, tensor_rank), w_state)
     gain = rows[ROW_NORM][None, :]
     inv_rms = lax.rsqrt(jnp.mean(hidden_wide * hidden_wide, axis=1, keepdims=True) + NORM_EPS)
-    grad_gain_local = jnp.sum(grad_normed * hidden_wide * inv_rms, axis=0)
     scaled_in = grad_normed * gain
     grad_hidden = (
         inv_rms * scaled_in
@@ -830,59 +971,40 @@
         + cotangent.astype(F32)
     )
 
-    skip_sums = conv_rows[5].reshape(heads, head_size).sum(axis=1)
-    pieces = jnp.concatenate(
-        [
-            conv_rows[0:5].reshape(-1),
-            gain_rows[0],
-            state_conv_rows[0:5].reshape(-1),
-            head_sums[0:2].reshape(-1),
-            jnp.pad(skip_sums, (0, LANES - heads)),
-            grad_gain_local,
-        ]
-    )
-    placed = jnp.where(
-        jnp.arange(tensor_count, dtype=jnp.int32)[:, None] == tensor_rank, pieces[None, :], 0.0
-    )
-    small_sum = lax.psum(placed, ("dp", "tensor"))
-    mine = lax.dynamic_index_in_dim(small_sum, tensor_rank, 0, keepdims=False)
-
-    def take(value, start, length):
-        return value[start : start + length]
-
-    at = 0
-    conv_all = take(mine, at, 5 * inner).reshape(5, inner)
-    at += 5 * inner
-    gate_gain_all = take(mine, at, inner)
-    at += inner
-    state_conv_all = take(mine, at, 10 * size).reshape(5, 2 * size)
-    at += 10 * size
-    head_all = take(mine, at, 3 * LANES).reshape(3, LANES)
-    at += 3 * LANES
-    gain_all = jnp.sum(small_sum[:, at : at + width], axis=0)
-
-    def own_shard(value, length):
-        return lax.dynamic_slice_in_dim(value, shard_rank * length, length, value.ndim - 1)
-
-    conv_own = own_shard(conv_all, shard)
-    state_own = own_shard(state_conv_all, state_shard)
-    gate_grad_own = first_sum[:, width:].astype(F32)
-    inner_grad_own = second_sum[:, :inner].astype(F32)
+    gate_grad_own = first_sum[:, inner:].astype(F32)
+    state_grad_own = rest_sum[:, : 2 * size]
+    small = rest_sum[:, 2 * size :]
+    step_grad_own = small[:, :heads]
+
+    def by_row(grad, weight):
+        return jnp.sum(grad * weight.astype(F32), axis=1)
+
+    gain_part = (
+        by_row(gate_grad_own, projection_gate_inner[:, 0])
+        + by_row(inner_sum, projection_gate_inner[:, 1])
+        + by_row(step_grad_own, proj_step)
+        + jnp.where(tensor_rank == 0, by_row(state_grad_own, proj_state), 0.0)
+    )
+    gain_own = (gain_part + exchange(gain_part)) / norm_gain.astype(F32)
+
+    conv_own = small[:, LANE_CONV : LANE_CONV + 5].T
+    state_own = small[:state_shard, LANE_STATE : LANE_STATE + 5].T
+    head_all = small[0, LANE_HEADS : LANE_HEADS + 3 * heads].reshape(3, heads)
     return (
         block_out,
         grad_hidden,
-        own_shard(gain_all, shard),
-        jnp.stack([gate_grad_own, inner_grad_own], axis=1),
-        second_sum[:, inner:channels].astype(F32),
-        second_sum[:, channels : channels + heads].astype(F32),
+        gain_own,
+        jnp.stack([gate_grad_own, inner_sum], axis=1),
+        state_grad_own,
+        step_grad_own,
         conv_own[0:4][:, None, :],
         conv_own[4:5],
         state_own[0:4],
         state_own[4],
-        head_all[0, :heads],
-        head_all[2, :heads],
-        head_all[1, :heads],
-        own_shard(gate_gain_all, shard)[None, :],
+        head_all[0],
+        head_all[2],
+        head_all[1],
+        small[:, LANE_GATE][None, :],
         first_sum[:, :inner].astype(F32).T,
     )
 

time: 553 us -> 357 us (0.65)
  waiting for transfers between devices: 281 us -> 88.5 us
  local copies, waits for them, and re-layouts: 47.5 us -> 25.4 us
  starting transfers between devices: 8.59 us -> 27.3 us
  Pallas kernels: 121 us -> 136 us
  matrix products: 52.2 us -> 40.4 us
    unnamed x7 -> x2, waiting for transfers between devices: 135 us -> 0.03 us
    ppermute x0 -> x16, waiting for transfers between devices: none -> 79.2 us  [flip(): return lax.ppermute(value, 'dp', [(i, i ^ 1 << bit) for i in range(count)])]
    psum x1 -> x0, waiting for transfers between devices: 44.7 us -> none  [on_device(): small_sum = lax.psum(placed, ('dp', 'tensor'))]
    all_gather x1 -> x0, waiting for transfers between devices: 38.9 us -> none  [on_device(): w_first = lax.all_gather(first_shard, 'dp', axis=0, tiled=True)]
    ppermute x6 -> x7, waiting for transfers between devices: 40.9 us -> 9.22 us  [exchange(): return lax.ppermute(value, 'tensor', swap)]
    all_gather x1, waiting for transfers between devices: 20.9 us -> 0.02 us  [on_device(): w_second = lax.all_gather(second_shard, 'dp', axis=0, tiled=True)]
    ppermute x0 -> x16, starting transfers between devices: none -> 19.4 us  [flip(): return lax.ppermute(value, 'dp', [(i, i ^ 1 << bit) for i in range(count)])]
    pallas_call x2 -> x4, Pallas kernels: 37.3 us -> 53.3 us  [the longest x1 28.1 us: on_device(): pl.pallas_call(functools.partial(forward_kernel, shard=shard, state_shard...]
  transfers between devices with their start and end apart: 11 -> 25, of which waited for: 8 -> 13; matrix products, arithmetic and copies ran while one was open for 17% -> 17% of each run, Pallas kernels for 7% -> 11%
where the time goes in v2:
time: 357 us; the launch traced here: 353 us
  Pallas kernels  136 us (38%)
  waiting for transfers between devices  88.5 us (25%)
  matrix products  40.4 us (11%)
  starting transfers between devices  27.3 us (8%)
  local copies, waits for them, and re-layouts  25.4 us (7%)
  other arithmetic  20.2 us (6%)
  between operations  15 us (4%)
    ppermute x16, waiting for transfers between devices, flip(): return lax.ppermute(value, 'dp', [(i, i ^ 1 << bit) for i in range(count)])  79.2 us
    pallas_call x1, Pallas kernels, on_device(): pl.pallas_call(backward_kernel, grid=(groups,), in_specs=[SMEM_SPEC, pl.B...  53.3 us
    dot_general x9, matrix products, nt(): lax.dot_general(left, right, (((1,), (1,)), ((), ())), preferred_element_...  34.5 us
    pallas_call x1, Pallas kernels, on_device(): pl.pallas_call(functools.partial(forward_kernel, shard=shard, state_shard...  28.1 us
    ppermute x16, starting transfers between devices, flip(): return lax.ppermute(value, 'dp', [(i, i ^ 1 << bit) for i in range(count)])  19.4 us
    pallas_call x1, Pallas kernels, on_device(): pl.pallas_call(gate_kernel, grid=(groups,), in_specs=[SMEM_SPEC, SMEM_SPE...  16.4 us
    pallas_call x1, Pallas kernels, on_device(): pl.pallas_call(early_grad_kernel, grid=(tiles,), in_specs=[whole(width, t...  13.4 us
    pallas_call x1, Pallas kernels, on_device(): pl.pallas_call(functools.partial(gate_grad_kernel, inner_all=inner_all),...  13.2 us
  transfers between devices with their start and end apart: 25, of which 13 were waited for; matrix products, arithmetic and copies ran while one was open for 17% of the time, Pallas kernels for 11%

profile of v2, /device:TPU:0, one launch (start us, length us, event | category | flops | bytes accessed | tf_op | source)
XLA Modules:
  0.0 352.9 jit_solution(15752051876864186106)
XLA Ops:
  7.2 1.5 fusion.62
  9.5 1.6 pad_maximum_fusion.7
  11.2 1.4 copy.82.step_ref
  12.6 1.5 pack_small.1
  14.1 2.9 collective-permute-start.6
  17.1 2.7 collective-permute-start.2
  19.8 1.5 collective-permute-start
  22.1 1.2 collective-permute-start.7
  23.4 8.9 %collective-permute-done.2 = bf16[64,1024]{1,0:T(8,128)(2,1)S(1)} collective-permute-done((bf16[64,1024]{1,0:T(8,128)(2,1)S(1)}, bf16[64,1024]{1,0:T(8,128)(2,1)S(1)}, u32[]{:S(2)}, u32[]{:S(2)}) %collective-permute-start.2) | collective-permute-done | bytes 131104 | tf_op jit(solution)/shard_map/ppermute | solution.py:645
  32.4 1.4 collective-permute-start.3
  33.8 3.1 collective-permute-done.7
  36.9 6.9 %collective-permute-done.3 = bf16[2,64,1024]{2,1,0:T(8,128)(2,1)S(1)} collective-permute-done((bf16[2,64,1024]{2,1,0:T(8,128)(2,1)S(1)}, bf16[2,64,1024]{2,1,0:T(8,128)(2,1)S(1)}, u32[]{:S(2)}, u32[]{:S(2)}) %collective-permute-start.3) | collective-permute-done | bytes 262176 | tf_op jit(solution)/shard_map/ppermute | solution.py:645
  45.2 14.3 %collective-permute-done.8 = bf16[2,2,64,384]{3,2,1,0:T(8,128)(2,1)S(1)} collective-permute-done((bf16[2,2,64,384]{3,2,1,0:T(8,128)(2,1)S(1)}, bf16[2,2,64,384]{3,2,1,0:T(8,128)(2,1)S(1)}, u32[]{:S(2)}, u32[]{:S(2)}) %collective-permute-start.8) | collective-permute-done | bytes 196640 | tf_op jit(solution)/shard_map/ppermute | solution.py:645
  59.6 9.1 %collective-permute-done.4 = bf16[2,2,64,1024]{3,2,0,1:T(8,128)(2,1)S(1)} collective-permute-done((bf16[2,2,64,1024]{3,2,0,1:T(8,128)(2,1)S(1)}, bf16[2,2,64,1024]{3,2,0,1:T(8,128)(2,1)S(1)}, u32[]{:S(2)}, u32[]{:S(2)}) %collective-permute-start.4) | collective-permute-done | bytes 524320 | tf_op jit(solution)/shard_map/ppermute | solution.py:645
  68.8 1.6 collective-permute-start.1
  70.4 1.1 pad_maximum_fusion.1
  73.5 1.6 collective-permute-done.9
  75.1 1.1 select_bitcast_fusion.5
  76.3 1.0 copy.83
  77.3 1.4 select_bitcast_fusion.1
  78.9 1.5 copy.81
  80.4 28.1 %mixer_forward.1 = (bf16[1536,1024]{1,0:T(8,128)(2,1)}, bf16[1024,1536]{1,0:T(8,128)(2,1)}, f32[1536,1024]{1,0:T(8,128)}, f32[1536,256]{1,0:T(8,128)}, bf16[1536...) custom-call(s32[1,1]{1,0:T(1,128)} %bitcast.rank_ref, ...), custom_call_target="tpu_custom_call" | custom-call | tf_op jit(solution)/shard_map/mixer_forward/pallas_call | solution.py:756
  108.6 16.4 %gate_forward.1 = (f32[1536,1024]{1,0:T(8,128)}, f32[1536,1024]{1,0:T(8,128)}, bf16[1024,1536]{1,0:T(8,128)(2,1)}, f32[8,1536]{1,0:T(8,128)}) custom-call(s32[1,1]{1,0:T(1,128)} %bitcast.rank_ref, s32[1,4]{1,0:T(1,128)} %len_ref.7, bf16[768,1024]{1,0:T(8,128)(2,1)} %own_ref.3, bf16[768,1024]{1,0:T(8,128)(2,1)} %collective-permute-done.1.other_ref, ...), custom_call_target="tpu_custom_call" | custom-call | tf_op jit(solution)/shard_map/gate_forward/pallas_call | solution.py:795
  127.5 1.9 collective-permute-done.10.other_sums_ref
  130.0 13.2 %gate_backward.1 = (bf16[1536,1024]{1,0:T(8,128)(2,1)}, bf16[1536,1024]{1,0:T(8,128)(2,1)}, bf16[1536,1024]{1,0:T(8,128)(2,1)}, f32[8,1024]{1,0:T(8,128)}) custom-call(f32[8,1536]{1,0:T(8,128)} %get-tuple-element.48.own_sums_ref, f32[8,1536]{1,0:T(8,128)} %copy-done.24, f32[1536,1024]{1,0:T(8,128)} %get-tuple-element.49.gate_ref, ...), custom_call_target="tpu_custom_call" | custom-call | tf_op jit(solution)/shard_map/gate_backward/pallas_call | solution.py:820
  143.3 13.4 %early_weight_grads.1 = bf16[1024,2048]{1,0:T(8,128)(2,1)} custom-call(bf16[1024,1536]{1,0:T(8,128)(2,1)} %get-tuple-element.53.live_t_ref, bf16[1536,1024]{1,0:T(8,128)(2,1)} %get-tuple-element.51.low_ref, bf16[1024,1536]{1,0:T(8,128)(2,1)} %get-tuple-element.54.normed_t_ref, bf16[1536,1024]{1,0:T(8,128)(2,1)} %get-tuple-element.55.ggp_ref), custom_call_target="tpu_custom_call" | custom-call | tf_op jit(solution)/shard_map/early_weight_grads/pallas_call | solution.py:840
  156.6 4.6 %fusion.15 = bf16[768,1024]{1,0:T(8,128)(2,1)} fusion(bf16[1024,2048]{1,0:T(8,128)(2,1)} %all-gather.2.cloned.1.call-done.w_ref.proj_ref, bf16[1536,1024]{1,0:T(8,128)(2,1)S(1)} %copy-done.11, s32[]{:T(128)S(6)} %select_n.186), kind=kOutput, calls=%fused_computation.24 | convolution fusion | flops 1611399168 | bytes 5242884 | tf_op jit(solution)/shard_map/dot_general | solution.py:32
  161.3 53.3 %mixer_backward.1 = (bf16[1536,1024]{1,0:T(8,128)(2,1)}, bf16[1536,256]{1,0:T(8,128)(2,1)}, bf16[1536,128]{1,0:T(8,128)(2,1)}, f32[8,1024]{1,0:T(8,128)}, f32[8,128]{1,0:T(8,128)}) custom-call(s32[1,4]{1,0:T(1,128)} %len_ref.7, f32[1536,1024]{1,0:T(8,128)} %get-tuple-element.57.ipre_ref.halo_ref, f32[1536,1024]{1,0:T(8,128)} %get-tuple-element.57.ipre_ref.halo_ref, ...), custom_call_target="tpu_custom_call" | custom-call | tf_op jit(solution)/shard_map/mixer_backward/pallas_call | solution.py:871
  214.6 5.9 %convolution_convert_fusion = bf16[1024,1024]{1,0:T(8,128)(2,1)S(1)} fusion(bf16[1024,1536]{1,0:T(8,128)(2,1)S(1)} %copy-done.2, bf16[1536,1024]{1,0:T(8,128)(2,1)} %get-tuple-element.62), kind=kOutput, calls=%fused_computation.15 | convolution fusion | flops 3222274048 | bytes 8388608 | tf_op jit(solution)/shard_map/dot_general | solution.py:28
  220.5 3.5 fusion.19
  224.2 1.1 copy.109
  227.4 5.8 %add_convert_fusion = bf16[768,1024]{1,0:T(8,128)(2,1)} fusion(f32[768,1024]{1,0:T(8,128)S(1)} %fusion.46, f32[768,1024]{1,0:T(8,128)} %fusion.19, bf16[1024,2048]{1,0:T(8,128)(2,1)} %all-gather.2.cloned.1.call-done.w_ref.proj_ref, bf16[1536,1024]{1,0:T(8,128)(2,1)S(1)} %copy-done.14, s32[]{:T(128)S(6)} %select_n.186), kind=kOutput, calls=%fused_computation.11 | convolution fusion | flops 1612972032 | bytes 11534340 | tf_op jit(solution)/shard_map/dot_general | solution.py:32
  234.1 1.2 collective-permute-start.11
  235.2 3.5 fusion.22
  238.7 7.3 %collective-permute-done.13.other_ref = bf16[1536,256]{1,0:T(8,128)(2,1)S(1)} collective-permute-done((bf16[1536,256]{1,0:T(8,128)(2,1)S(1)}, bf16[1536,256]{1,0:T(8,128)(2,1)S(1)}, u32[]{:S(2)}, u32[]{:S(2)}) %collective-permute-start.13) | collective-permute-done | bytes 786464 | tf_op jit(solution)/shard_map/ppermute | solution.py:714
  246.0 0.9 copy-done.20
  246.9 10.2 %state_backward.1 = (bf16[1536,256]{1,0:T(8,128)(2,1)}, bf16[1024,384]{1,0:T(8,128)(2,1)}) custom-call(s32[1,4]{1,0:T(1,128)} %len_ref.7, bf16[1536,256]{1,0:T(8,128)(2,1)} %get-tuple-element.64.own_ref, bf16[1536,256]{1,0:T(8,128)(2,1)} %copy-done.20, f32[1536,256]{1,0:T(8,128)} %get-tuple-element.65.spre_ref, f32[8,256]{1,0:T(8,128)} %get-tuple-element.66.taps_ref, ...), custom_call_target="tpu_custom_call" | custom-call | tf_op jit(solution)/shard_map/state_backward/pallas_call | solution.py:942
  257.1 1.5 constant_dynamic-slice_fusion
  258.7 4.9 %fusion.9 = f32[768,1024]{1,0:T(8,128)} fusion(bf16[1024,2048]{1,0:T(8,128)(2,1)S(1)} %copy-done, bf16[1536,1024]{1,0:T(8,128)(2,1)} %get-tuple-element.55.ggp_ref, s32[]{:T(128)S(6)} %select_n.185), kind=kOutput, calls=%fused_computation.18 | convolution fusion | flops 1610612736 | bytes 6815748 | tf_op jit(solution)/shard_map/dot_general | solution.py:32
  263.9 1.4 copy.88
  266.3 2.2 fusion.48
  268.6 16.7 %collective-permute-done.19 = bf16[2,2,64,384]{2,3,1,0:T(8,128)(2,1)S(1)} collective-permute-done((bf16[2,2,64,384]{2,3,1,0:T(8,128)(2,1)S(1)}, bf16[2,2,64,384]{2,3,1,0:T(8,128)(2,1)S(1)}, u32[]{:S(2)}, u32[]{:S(2)}) %collective-permute-start.19) | collective-permute-done | bytes 196640 | tf_op jit(solution)/shard_map/ppermute | solution.py:645
  285.4 2.4 collective-permute-start.20
  287.8 1.6 fusion.6
  289.5 13.1 %collective-permute-done.20 = bf16[2,64,384]{1,2,0:T(8,128)(2,1)S(1)} collective-permute-done((bf16[2,64,384]{1,2,0:T(8,128)(2,1)S(1)}, bf16[2,64,384]{1,2,0:T(8,128)(2,1)S(1)}, u32[]{:S(2)}, u32[]{:S(2)}) %collective-permute-start.20) | collective-permute-done | bytes 98336 | tf_op jit(solution)/shard_map/ppermute | solution.py:645
  302.7 1.1 collective-permute-start.21
  304.6 1.0 collective-permute-start.15
  305.6 2.2 collective-permute-done.21
  309.9 1.0 fusion.63
  313.8 1.4 slice_reduce_fusion
  315.2 1.2 slice_bitcast_fusion.2
  316.4 1.3 multiply_reduce_fusion.2
  317.7 1.1 collective-permute-done.15
  318.7 1.2 fusion.35
  320.0 1.4 collective-permute-start.16
  321.5 6.3 %fusion = bf16[768,1024]{1,0:T(8,128)(2,1)} fusion(bf16[768,1024]{1,0:T(8,128)(2,1)S(1)} %copy-done.1, bf16[768,1024]{1,0:T(8,128)(2,1)} %collective-permute-done.11, pred[768]{0:T(1024)(128)(4,1)S(1)} %add_compare_fusion, bf16[1024,2048]{1,0:T(8,128)(2,1)} %all-gather.2.cloned.1.call-done.w_ref.proj_ref, bf16[1536,1024]{1,0:T(8,128)(2,1)} %get-tuple-element.51.low_ref, ...), kind=kOutput, calls=%fused_computation.4 | convolution fusion | flops 1615331328 | bytes 8389380 | tf_op jit(solution)/shard_map/dot_general | solution.py:32
  327.8 3.2 fusion.1
  331.2 3.2 collective-permute-start.17
  334.3 2.5 fusion.4
  336.8 2.2 collective-permute-done.17
  339.2 1.1 fusion.44
  340.3 2.0 collective-permute-start.22
  342.3 1.7 convert_bitcast_fusion.1
  344.1 1.2 copy.90
  (143 shorter events, 20.4 us)
Async XLA Ops:
  7.2 101.4 %all-gather.2.cloned.1.call-start = ((), (), s32[]{:S(2)}) async-start(), calls=%async_computation.1 | async-start | bytes 4456448 | tf_op jit(solution)/shard_map/all_gather | solution.py:736
  8.7 0.7 copy-start.15
  8.7 23.6 %copy-start.9 = (bf16[64,1,1024]{2,1,0:T(2,128)(2,1)}, bf16[64,1,1024]{2,1,0:T(2,128)(2,1)S(1)}, u32[]{:S(2)}) copy-start(bf16[64,1,1024]{2,1,0:T(2,128)(2,1)S(1)} %get-tuple-element.174) | copy-start | bytes 393220
  11.1 328.0 %reduce-scatter.2.cloned.1.call-start = ((), (), s32[]{:S(2)}) async-start(), calls=%async_computation.2 | async-start | bytes 4456448 | tf_op jit(solution)/shard_map/reduce_scatter | solution.py:862
  14.1 7.2 %collective-permute-start.6 = (bf16[64,384]{1,0:T(8,128)(2,1)}, bf16[64,384]{1,0:T(8,128)(2,1)S(1)}, u32[]{:S(2)}, u32[]{:S(2)}) collective-permute-start(bf16[64,384]{1,0:T(8,128)(2,1)} %pack_small.1), channel_id=1, source_target_pairs={{0,4},{2,6},{4,0},{6,2},{8,12},{10,14},{12,8},{14,10},{16,20},{18,... | collective-permute-start | bytes 147464 | tf_op jit(solution)/shard_map/ppermute | solution.py:645
  17.1 15.2 %collective-permute-start.2 = (bf16[64,1024]{1,0:T(8,128)(2,1)S(1)}, bf16[64,1024]{1,0:T(8,128)(2,1)S(1)}, u32[]{:S(2)}, u32[]{:S(2)}) collective-permute-start(bf16[64,1024]{1,0:T(8,128)(2,1)S(1)} %bitcast.137), channel_id=1, source_target_pairs={{0,16},{2,18},{4,20},{6,22},{8,24},{10,26},{12,28},{14,30},{16,0},... | collective-permute-start | bytes 393224 | tf_op jit(solution)/shard_map/ppermute | solution.py:645
  19.8 49.0 %collective-permute-start = (bf16[768,1024]{1,0:T(8,128)(2,1)}, bf16[768,1024]{1,0:T(8,128)(2,1)}, u32[]{:S(2)}, u32[]{:S(2)}) collective-permute-start(bf16[768,1024]{1,0:T(8,128)(2,1)} %own_ref.2), channel_id=1, source_target_pairs={{0,1},{1,0},{2,3},{3,2},{4,5},{5,4},{6,7},{7,6},{8,9},{9,8},{10,11... | collective-permute-start | bytes 4718600 | tf_op jit(solution)/shard_map/ppermute | solution.py:714
  22.1 14.7 %collective-permute-start.7 = (bf16[2,64,384]{2,1,0:T(8,128)(2,1)S(1)}, bf16[2,64,384]{2,1,0:T(8,128)(2,1)S(1)}, u32[]{:S(2)}, u32[]{:S(2)}) collective-permute-start(bf16[2,64,384]{2,1,0:T(8,128)(2,1)S(1)} %pad_maximum_fusion.9), channel_id=1, source_target_pairs={{0,16},{2,18},{4,20},{6,22},{8,24},{10,26},{12,28},{14,30},{16,0},... | collective-permute-start | bytes 294920 | tf_op jit(solution)/shard_map/ppermute | solution.py:645
  32.4 36.4 %copy-start.7 = (bf16[768,1024]{1,0:T(8,128)(2,1)S(1)}, bf16[768,1024]{1,0:T(8,128)(2,1)}, u32[]{:S(2)}) copy-start(bf16[768,1024]{1,0:T(8,128)(2,1)} %own_ref.3) | copy-start | bytes 4718596
  32.4 11.3 %collective-permute-start.3 = (bf16[2,64,1024]{2,1,0:T(8,128)(2,1)S(1)}, bf16[2,64,1024]{2,1,0:T(8,128)(2,1)S(1)}, u32[]{:S(2)}, u32[]{:S(2)}) collective-permute-start(bf16[2,64,1024]{2,1,0:T(8,128)(2,1)S(1)} %pad_maximum_fusion.6), channel_id=1, source_target_pairs={{0,8},{2,10},{4,12},{6,14},{8,0},{10,2},{12,4},{14,6},{16,24},{18,... | collective-permute-start | bytes 786440 | tf_op jit(solution)/shard_map/ppermute | solution.py:645
  43.8 28.3 %copy-start.32 = (bf16[16]{0:T(256)(128)(2,1)S(1)}, bf16[16]{0:T(256)(128)(2,1)}, u32[]{:S(2)}) copy-start(bf16[16]{0:T(256)(128)(2,1)} %param.25) | copy-start | bytes 100
  43.9 28.3 %copy-start.28 = (bf16[16]{0:T(256)(128)(2,1)S(1)}, bf16[16]{0:T(256)(128)(2,1)}, u32[]{:S(2)}) copy-start(bf16[16]{0:T(256)(128)(2,1)} %param.26) | copy-start | bytes 100
  43.9 28.3 %copy-start.29 = (bf16[16]{0:T(256)(128)(2,1)S(1)}, bf16[16]{0:T(256)(128)(2,1)}, u32[]{:S(2)}) copy-start(bf16[16]{0:T(256)(128)(2,1)} %param.27) | copy-start | bytes 100
  43.9 28.4 %copy-start.26 = (s32[1,4]{1,0:T(1,128)S(1)}, s32[1,4]{1,0:T(1,128)}, u32[]{:S(2)}) copy-start(s32[1,4]{1,0:T(1,128)} %len_ref.7) | copy-start | bytes 52
  43.9 24.8 %collective-permute-start.4 = (bf16[2,2,64,1024]{3,2,0,1:T(8,128)(2,1)S(1)}, bf16[2,2,64,1024]{3,2,0,1:T(8,128)(2,1)S(1)}, u32[]{:S(2)}, u32[]{:S(2)}) collective-permute-start(bf16[2,2,64,1024]{3,2,0,1:T(8,128)(2,1)S(1)} %pad_maximum_fusion.3), channel_id=1, source_target_pairs={{0,4},{2,6},{4,0},{6,2},{8,12},{10,14},{12,8},{14,10},{16,20},{18,... | collective-permute-start | bytes 1572872 | tf_op jit(solution)/shard_map/ppermute | solution.py:645
  44.5 15.1 %collective-permute-start.8 = (bf16[2,2,64,384]{3,2,1,0:T(8,128)(2,1)S(1)}, bf16[2,2,64,384]{3,2,1,0:T(8,128)(2,1)S(1)}, u32[]{:S(2)}, u32[]{:S(2)}) collective-permute-start(bf16[2,2,64,384]{3,2,1,0:T(8,128)(2,1)S(1)} %pad_maximum_fusion.8), channel_id=1, source_target_pairs={{0,8},{2,10},{4,12},{6,14},{8,0},{10,2},{12,4},{14,6},{16,24},{18,... | collective-permute-start | bytes 589832 | tf_op jit(solution)/shard_map/ppermute | solution.py:645
  68.8 39.8 %collective-permute-start.1 = (bf16[768,1024]{1,0:T(8,128)(2,1)S(1)}, bf16[768,1024]{1,0:T(8,128)(2,1)}, u32[]{:S(2)}, u32[]{:S(2)}) collective-permute-start(bf16[768,1024]{1,0:T(8,128)(2,1)S(1)} %copy-done.7), channel_id=1, source_target_pairs={{0,1},{1,0},{2,3},{3,2},{4,5},{5,4},{6,7},{7,6},{8,9},{9,8},{10,11... | collective-permute-start | bytes 4718600 | tf_op jit(solution)/shard_map/ppermute | solution.py:714
  71.5 5.8 %collective-permute-start.5 = (bf16[2,2,2,64,1024]{4,3,0,1,2:T(8,128)(2,1)}, bf16[2,2,2,64,1024]{4,3,0,1,2:T(8,128)(2,1)}, u32[]{:S(2)}, u32[]{:S(2)}) collective-permute-start(bf16[2,2,2,64,1024]{4,3,0,1,2:T(8,128)(2,1)} %pad_maximum_fusion.1), channel_id=1, source_target_pairs={{0,2},{2,0},{4,6},{6,4},{8,10},{10,8},{12,14},{14,12},{16,18},{18,... | collective-permute-start | bytes 3145736 | tf_op jit(solution)/shard_map/ppermute | solution.py:645
  71.5 3.6 %collective-permute-start.9 = (bf16[2,2,2,64,384]{4,3,2,0,1:T(8,128)(2,1)S(1)}, bf16[2,2,2,64,384]{4,3,2,0,1:T(8,128)(2,1)}, u32[]{:S(2)}, u32[]{:S(2)}) collective-permute-start(bf16[2,2,2,64,384]{4,3,2,0,1:T(8,128)(2,1)S(1)} %pad_maximum_fusion.5), channel_id=1, source_target_pairs={{0,2},{2,0},{4,6},{6,4},{8,10},{10,8},{12,14},{14,12},{16,18},{18,... | collective-permute-start | bytes 1179656 | tf_op jit(solution)/shard_map/ppermute | solution.py:645
  108.6 17.4 %copy-start.23 = (bf16[64,256]{1,0:T(8,128)(2,1)S(1)}, bf16[64,256]{1,0:T(8,128)(2,1)}, u32[]{:S(2)}) copy-start(bf16[64,256]{1,0:T(8,128)(2,1)} %state_ref.1) | copy-start | bytes 98308
  125.0 4.4 %collective-permute-start.10 = (f32[8,1536]{1,0:T(8,128)}, f32[8,1536]{1,0:T(8,128)S(1)}, u32[]{:S(2)}, u32[]{:S(2)}) collective-permute-start(f32[8,1536]{1,0:T(8,128)} %get-tuple-element.48.own_sums_ref), channel_id=1, source_target_pairs={{0,1},{1,0},{2,3},{3,2},{4,5},{5,4},{6,7},{7,6},{8,9},{9,8},{10,11... | collective-permute-start | bytes 147464 | tf_op jit(solution)/shard_map/ppermute | solution.py:714
  129.4 0.6 copy-start.24
  143.3 13.4 %copy-start.11 = (bf16[1536,1024]{1,0:T(8,128)(2,1)S(1)}, bf16[1536,1024]{1,0:T(8,128)(2,1)}, u32[]{:S(2)}) copy-start(bf16[1536,1024]{1,0:T(8,128)(2,1)} %get-tuple-element.51.low_ref) | copy-start | bytes 9437188
  161.3 53.3 %copy-start.2 = (bf16[1024,1536]{1,0:T(8,128)(2,1)S(1)}, bf16[1024,1536]{1,0:T(8,128)(2,1)}, u32[]{:S(2)}) copy-start(bf16[1024,1536]{1,0:T(8,128)(2,1)} %get-tuple-element.54.normed_t_ref) | copy-start | bytes 9437188
  214.6 5.9 %copy-start.5 = (bf16[2,2,2,2,64,1024]{5,4,3,2,1,0:T(8,128)(2,1)S(1)}, bf16[2,2,2,2,64,1024]{5,4,3,2,1,0:T(8,128)(2,1)}, u32[]{:S(2)}) copy-start(bf16[2,2,2,2,64,1024]{5,4,3,2,1,0:T(8,128)(2,1)} %copy.81) | copy-start | bytes 6291460
  214.6 5.9 %copy-start.30 = (bf16[1536,1024]{1,0:T(8,128)(2,1)S(1)}, bf16[1536,1024]{1,0:T(8,128)(2,1)}, u32[]{:S(2)}) copy-start(bf16[1536,1024]{1,0:T(8,128)(2,1)} %get-tuple-element.62) | copy-start | bytes 9437188
  224.2 1.4 copy-start.19
  224.2 1.7 copy-start.4
  224.2 1.8 copy-start.17
  225.4 62.5 %collective-permute-start.14 = (bf16[2,2,2,64,1024]{4,3,0,1,2:T(8,128)(2,1)}, bf16[2,2,2,64,1024]{4,3,0,1,2:T(8,128)(2,1)}, u32[]{:S(2)}, u32[]{:S(2)}) collective-permute-start(bf16[2,2,2,64,1024]{4,3,0,1,2:T(8,128)(2,1)} %bitcast.124), channel_id=1, source_target_pairs={{0,2},{2,0},{4,6},{6,4},{8,10},{10,8},{12,14},{14,12},{16,18},{18,... | collective-permute-start | bytes 3145736 | tf_op jit(solution)/shard_map/ppermute | solution.py:645
  225.4 2.0 copy-start.14
  225.7 20.4 %collective-permute-start.13 = (bf16[1536,256]{1,0:T(8,128)(2,1)S(1)}, bf16[1536,256]{1,0:T(8,128)(2,1)S(1)}, u32[]{:S(2)}, u32[]{:S(2)}) collective-permute-start(bf16[1536,256]{1,0:T(8,128)(2,1)S(1)} %copy-done.19), channel_id=1, source_target_pairs={{0,1},{1,0},{2,3},{3,2},{4,5},{5,4},{6,7},{7,6},{8,9},{9,8},{10,11... | collective-permute-start | bytes 2359304 | tf_op jit(solution)/shard_map/ppermute | solution.py:714
  227.4 7.8 %copy-start.6 = (bf16[2,2,2,2,64,1024]{5,4,3,2,1,0:T(8,128)(2,1)S(1)}, bf16[2,2,2,2,64,1024]{5,4,3,2,1,0:T(8,128)(2,1)}, u32[]{:S(2)}) copy-start(bf16[2,2,2,2,64,1024]{5,4,3,2,1,0:T(8,128)(2,1)} %copy.81) | copy-start | bytes 6291460
  227.4 7.8 %copy-start.31 = (bf16[1536,1024]{1,0:T(8,128)(2,1)S(1)}, bf16[1536,1024]{1,0:T(8,128)(2,1)}, u32[]{:S(2)}) copy-start(bf16[1536,1024]{1,0:T(8,128)(2,1)} %get-tuple-element.62) | copy-start | bytes 9437188
  233.2 94.6 %collective-permute-start.12 = (bf16[768,1024]{1,0:T(8,128)(2,1)}, bf16[768,1024]{1,0:T(8,128)(2,1)}, u32[]{:S(2)}, u32[]{:S(2)}) collective-permute-start(bf16[768,1024]{1,0:T(8,128)(2,1)} %add_convert_fusion), channel_id=1, source_target_pairs={{0,1},{1,0},{2,3},{3,2},{4,5},{5,4},{6,7},{7,6},{8,9},{9,8},{10,11... | collective-permute-start | bytes 4718600 | tf_op jit(solution)/shard_map/ppermute | solution.py:714
  234.1 87.4 %collective-permute-start.11 = (bf16[768,1024]{1,0:T(8,128)(2,1)}, bf16[768,1024]{1,0:T(8,128)(2,1)}, u32[]{:S(2)}, u32[]{:S(2)}) collective-permute-start(bf16[768,1024]{1,0:T(8,128)(2,1)} %fusion.15), channel_id=1, source_target_pairs={{0,1},{1,0},{2,3},{3,2},{4,5},{5,4},{6,7},{7,6},{8,9},{9,8},{10,11... | collective-permute-start | bytes 4718600 | tf_op jit(solution)/shard_map/ppermute | solution.py:714
  246.0 0.9 copy-start.20
  246.9 11.8 %copy-start = (bf16[1024,2048]{1,0:T(8,128)(2,1)S(1)}, bf16[1024,2048]{1,0:T(8,128)(2,1)}, u32[]{:S(2)}) copy-start(bf16[1024,2048]{1,0:T(8,128)(2,1)} %all-gather.2.cloned.1.call-done.w_ref.proj_ref) | copy-start | bytes 12582916
  258.6 5.3 %collective-permute-start.18 = (bf16[2,2,2,64,384]{4,3,2,1,0:T(8,128)(2,1)S(1)}, bf16[2,2,2,64,384]{4,3,2,1,0:T(8,128)(2,1)}, u32[]{:S(2)}, u32[]{:S(2)}) collective-permute-start(bf16[2,2,2,64,384]{4,3,2,1,0:T(8,128)(2,1)S(1)} %get-tuple-element.162), channel_id=1, source_target_pairs={{0,2},{2,0},{4,6},{6,4},{8,10},{10,8},{12,14},{14,12},{16,18},{18,... | collective-permute-start | bytes 1179656 | tf_op jit(solution)/shard_map/ppermute | solution.py:645
  265.3 1.0 copy-start.18
  265.6 19.6 %collective-permute-start.19 = (bf16[2,2,64,384]{2,3,1,0:T(8,128)(2,1)S(1)}, bf16[2,2,64,384]{2,3,1,0:T(8,128)(2,1)S(1)}, u32[]{:S(2)}, u32[]{:S(2)}) collective-permute-start(bf16[2,2,64,384]{2,3,1,0:T(8,128)(2,1)S(1)} %dynamic-slice_bitcast_fusion.1), channel_id=1, source_target_pairs={{0,8},{2,10},{4,12},{6,14},{8,0},{10,2},{12,4},{14,6},{16,24},{18,... | collective-permute-start | bytes 589832 | tf_op jit(solution)/shard_map/ppermute | solution.py:645
  285.3 24.6 %copy-start.21 = (bf16[64,256]{0,1:T(8,128)(2,1)S(1)}, bf16[64,256]{0,1:T(8,128)(2,1)}, u32[]{:S(2)}) copy-start(bf16[64,256]{0,1:T(8,128)(2,1)} %copy.89) | copy-start | bytes 98308
  285.4 31.0 %copy-start.25 = (bf16[64,16]{0,1:T(8,128)(2,1)S(1)}, bf16[64,16]{0,1:T(8,128)(2,1)}, u32[]{:S(2)}) copy-start(bf16[64,16]{0,1:T(8,128)(2,1)} %param.20) | copy-start | bytes 6148
  285.4 17.2 %collective-permute-start.20 = (bf16[2,64,384]{1,2,0:T(8,128)(2,1)S(1)}, bf16[2,64,384]{1,2,0:T(8,128)(2,1)S(1)}, u32[]{:S(2)}, u32[]{:S(2)}) collective-permute-start(bf16[2,64,384]{1,2,0:T(8,128)(2,1)S(1)} %dynamic-slice_bitcast_fusion.4), channel_id=1, source_target_pairs={{0,16},{2,18},{4,20},{6,22},{8,24},{10,26},{12,28},{14,30},{16,0},... | collective-permute-start | bytes 294920 | tf_op jit(solution)/shard_map/ppermute | solution.py:645
  289.5 32.0 %copy-start.1 = (bf16[768,1024]{1,0:T(8,128)(2,1)S(1)}, bf16[768,1024]{1,0:T(8,128)(2,1)}, u32[]{:S(2)}) copy-start(bf16[768,1024]{1,0:T(8,128)(2,1)} %own_ref.2) | copy-start | bytes 4718596
  302.7 5.1 %collective-permute-start.21 = (bf16[64,384]{0,1:T(8,128)(2,1)S(1)}, bf16[64,384]{0,1:T(8,128)(2,1)S(1)}, u32[]{:S(2)}, u32[]{:S(2)}) collective-permute-start(bf16[64,384]{0,1:T(8,128)(2,1)S(1)} %dynamic-slice_bitcast_fusion.6), channel_id=1, source_target_pairs={{0,4},{2,6},{4,0},{6,2},{8,12},{10,14},{12,8},{14,10},{16,20},{18,... | collective-permute-start | bytes 147464 | tf_op jit(solution)/shard_map/ppermute | solution.py:645
  304.6 14.1 %collective-permute-start.15 = (bf16[2,2,64,1024]{3,2,0,1:T(8,128)(2,1)}, bf16[2,2,64,1024]{3,2,0,1:T(8,128)(2,1)}, u32[]{:S(2)}, u32[]{:S(2)}) collective-permute-start(bf16[2,2,64,1024]{3,2,0,1:T(8,128)(2,1)} %dynamic-slice_bitcast_fusion), channel_id=1, source_target_pairs={{0,4},{2,6},{4,0},{6,2},{8,12},{10,14},{12,8},{14,10},{16,20},{18,... | collective-permute-start | bytes 1572872 | tf_op jit(solution)/shard_map/ppermute | solution.py:645
  320.0 7.8 %copy-start.3 = (f32[768,1024]{1,0:T(8,128)S(1)}, f32[768,1024]{1,0:T(8,128)}, u32[]{:S(2)}) copy-start(f32[768,1024]{1,0:T(8,128)} %fusion.48) | copy-start | bytes 9437188
  320.0 7.8 %copy-start.12 = (f32[768,1024]{1,0:T(8,128)S(1)}, f32[768,1024]{1,0:T(8,128)}, u32[]{:S(2)}) copy-start(f32[768,1024]{1,0:T(8,128)} %fusion.22) | copy-start | bytes 9437188
  320.0 7.8 %copy-start.13 = (f32[768,1024]{1,0:T(8,128)S(1)}, f32[768,1024]{1,0:T(8,128)}, u32[]{:S(2)}) copy-start(f32[768,1024]{1,0:T(8,128)} %fusion.9) | copy-start | bytes 9437188
  320.0 7.8 %copy-start.22 = (bf16[1536,256]{1,0:T(8,128)(2,1)S(1)}, bf16[1536,256]{1,0:T(8,128)(2,1)}, u32[]{:S(2)}) copy-start(bf16[1536,256]{1,0:T(8,128)(2,1)} %get-tuple-element.70) | copy-start | bytes 2359300
  320.0 11.0 %collective-permute-start.16 = (bf16[2,64,1024]{2,1,0:T(8,128)(2,1)S(1)}, bf16[2,64,1024]{2,1,0:T(8,128)(2,1)S(1)}, u32[]{:S(2)}, u32[]{:S(2)}) collective-permute-start(bf16[2,64,1024]{2,1,0:T(8,128)(2,1)S(1)} %dynamic-slice_bitcast_fusion.3), channel_id=1, source_target_pairs={{0,8},{2,10},{4,12},{6,14},{8,0},{10,2},{12,4},{14,6},{16,24},{18,... | collective-permute-start | bytes 786440 | tf_op jit(solution)/shard_map/ppermute | solution.py:645
  327.8 6.5 %copy-start.8 = (bf16[768,1024]{1,0:T(8,128)(2,1)S(1)}, bf16[768,1024]{1,0:T(8,128)(2,1)}, u32[]{:S(2)}) copy-start(bf16[768,1024]{1,0:T(8,128)(2,1)} %own_ref.3) | copy-start | bytes 4718596
  331.2 7.8 %collective-permute-start.17 = (bf16[64,1024]{1,0:T(8,128)(2,1)S(1)}, bf16[64,1024]{1,0:T(8,128)(2,1)S(1)}, u32[]{:S(2)}, u32[]{:S(2)}) collective-permute-start(bf16[64,1024]{1,0:T(8,128)(2,1)S(1)} %dynamic-slice_bitcast_fusion.5), channel_id=1, source_target_pairs={{0,16},{2,18},{4,20},{6,22},{8,24},{10,26},{12,28},{14,30},{16,0},... | collective-permute-start | bytes 393224 | tf_op jit(solution)/shard_map/ppermute | solution.py:645
  334.3 4.7 %copy-start.10 = (bf16[64,1,1024]{2,1,0:T(2,128)(2,1)S(1)}, bf16[64,1,1024]{2,1,0:T(2,128)(2,1)}, u32[]{:S(2)}) copy-start(bf16[64,1,1024]{2,1,0:T(2,128)(2,1)} %copy-done.9) | copy-start | bytes 393220
  334.3 4.8 %copy-start.16 = (bf16[64,1,1024]{2,1,0:T(2,128)(2,1)S(1)}, bf16[64,1,1024]{2,1,0:T(2,128)(2,1)}, u32[]{:S(2)}) copy-start(bf16[64,1,1024]{2,1,0:T(2,128)(2,1)} %copy-done.15) | copy-start | bytes 393220
  336.8 8.5 %copy-start.27 = (bf16[64]{0:T(256)(128)(2,1)S(1)}, bf16[64]{0:T(256)(128)(2,1)}, u32[]{:S(2)}) copy-start(bf16[64]{0:T(256)(128)(2,1)} %param.17) | copy-start | bytes 388
  340.3 5.0 %collective-permute-start.22 = (f32[64]{0:T(128)S(1)}, f32[64]{0:T(128)S(1)}, u32[]{:S(2)}, u32[]{:S(2)}) collective-permute-start(f32[64]{0:T(128)S(1)} %fusion.61), channel_id=1, source_target_pairs={{0,1},{1,0},{2,3},{3,2},{4,5},{5,4},{6,7},{7,6},{8,9},{9,8},{10,11... | collective-permute-start | bytes 776 | tf_op jit(solution)/shard_map/ppermute | solution.py:714
Sparse Core Ops, SparseCore 0:
  11.3 67.2 all-gather.1
  225.5 82.3 reduce-scatter.1

commit v3 on v2

--- a/solution.py
+++ b/solution.py
@@ -16,7 +16,8 @@
 MASKED = -1e30
 VMEM_BYTES = 56 * 1024 * 1024
 
-LANE_CONV, LANE_GATE, LANE_STATE, LANE_HEADS = 16, 21, 24, 32
+LANE_CONV, LANE_GATE, LANE_STATE, LANE_HEADS, LANE_GAIN = 16, 21, 24, 32, 127
+HALO = 16
 
 F32 = jnp.float32
 BF16 = jnp.bfloat16
@@ -45,8 +46,9 @@
 
 
 def exact_left(ones, value):
-    high, mid, low = split3(value)
-    return nn(ones, high) + nn(ones, mid) + nn(ones, low)
+    lanes = value.shape[1]
+    found = nn(ones, jnp.concatenate(split3(value), axis=1))
+    return found[:, :lanes] + found[:, lanes : 2 * lanes] + found[:, 2 * lanes :]
 
 
 def three_in_lanes(value, heads):
@@ -320,19 +322,26 @@
     cotangent = jnp.where(mine, own_ref[...].astype(F32), other_ref[...].astype(F32))
     live = jnp.where(valid, cotangent, 0.0).astype(BF16)
     live_t_ref[...] = live.T
-    gate_ref[...] = nn(normed_ref[...], w_ref[...])
-    gol_ref[...] = nn(live, proj_ref[...])
-    gain = rows_ref[ROW_GATE : ROW_GATE + 1, :]
-    lane = lax.broadcasted_iota(jnp.int32, (64, LANES), 1)
-    pieces = []
-    for part in range(4):
-        sl = slice(part * 64, part * 64 + 64)
-        gate = gate_ref[sl, :]
-        gated = mixed_ref[sl, :] * (gate * sigmoid(gate))
-        square = jnp.sum(gated * gated, axis=1, keepdims=True)
-        inner = jnp.sum(gol_ref[sl, :] * gain * gated, axis=1, keepdims=True)
-        pieces.append(jnp.where(lane < 4, square, inner))
-    sums_ref[...] = jnp.concatenate(pieces, axis=0).T[0:8, :]
+    square = jnp.zeros((GROUP, LANES), F32)
+    inner = jnp.zeros((GROUP, LANES), F32)
+    for part in range(gate_ref.shape[1] // GROUP):
+        sl = slice(part * GROUP, (part + 1) * GROUP)
+        gate = nn(normed_ref[...], w_ref[:, sl])
+        gol = nn(live, proj_ref[:, sl])
+        gate_ref[:, sl] = gate
+        gol_ref[:, sl] = gol
+        gated = mixed_ref[:, sl] * (gate * sigmoid(gate))
+        squares = gated * gated
+        inners = gol * rows_ref[ROW_GATE : ROW_GATE + 1, sl] * gated
+        square = square + squares[:, :LANES] + squares[:, LANES:]
+        inner = inner + inners[:, :LANES] + inners[:, LANES:]
+    lane = lax.broadcasted_iota(jnp.int32, (GROUP, LANES), 1)
+    columns = jnp.where(
+        lane < 4,
+        jnp.sum(square, axis=1, keepdims=True),
+        jnp.sum(inner, axis=1, keepdims=True),
+    )
+    sums_ref[...] = columns.T[0:8, :]
 
 
 def gate_grad_kernel(
@@ -382,7 +391,7 @@
     rows_ref, head_ref,
     gip_ref, gkq_ref, gstep_ref, conv_ref, heads_ref,
     ext, cext, gstate, spread, collect, lower, upper, fac, reads, mask, scores, gscores,
-    stepped_all, weighted, entered, sums_high, sums_low,
+    weighted, entered, sums,
 ):
     inner = rows_ref.shape[1]
     heads = inner // (LANES // PAIR_HEADS)
@@ -451,21 +460,23 @@
 
         top, bottom, top_grads, low_grads = [], [], [], []
         g00 = g01 = g11 = None
+        split_up = [(upstream_wide * one).astype(BF16) for one in masks]
+        grads_low = nt(stepped[HALF:], jnp.concatenate([one[HALF:] for one in split_up], axis=0))
         for which in range(PAIR_HEADS):
             head = pair * PAIR_HEADS + which
             column = cum[:, head : head + 1]
             row = cum_rows[head : head + 1, :]
-            masked = (upstream_wide * masks[which]).astype(BF16)
-            grads = nt(stepped, masked)
-
-            def factors(rs, cs):
+            masked = split_up[which]
+            grads_top = nt(stepped[:HALF], masked)
+
+            def factors(rs, cs, grads):
                 gap = row[:, cs] - column[rs] + mask[rs, cs]
                 factor = jnp.exp2(gap)
-                return (factor * scores[rs, cs]).astype(BF16), factor * grads[rs, cs]
-
-            a00, d00 = factors(lo, lo)
-            a01, d01 = factors(lo, hi)
-            a11, d11 = factors(hi, hi)
+                return (factor * scores[rs, cs]).astype(BF16), factor * grads
+
+            a00, d00 = factors(lo, lo, grads_top[:, lo])
+            a01, d01 = factors(lo, hi, grads_top[:, hi])
+            a11, d11 = factors(hi, hi, grads_low[:, which * HALF : (which + 1) * HALF])
             g00 = d00 if g00 is None else g00 + d00
             g01 = d01 if g01 is None else g01 + d01
             g11 = d11 if g11 is None else g11 + d11
@@ -486,16 +497,12 @@
         skip = rows_ref[ROW_SKIP : ROW_SKIP + 1, sl]
         across = reads[:, sl]
 
-        def keep_sum(index, value):
-            high = value.astype(BF16)
-            sums_high[index * GROUP : (index + 1) * GROUP, sl] = high
-            sums_low[index * GROUP : (index + 1) * GROUP, sl] = (
-                value - high.astype(F32)
-            ).astype(BF16)
-
-        keep_sum(0, upstream_wide * (mixed_ref[:, sl] - skip * values) - stepped_wide * raw)
-        keep_sum(1, values * raw)
-        keep_sum(2, values * across)
+        balance = upstream_wide * (mixed_ref[:, sl] - skip * values) - stepped_wide * raw
+        high = balance.astype(BF16)
+        sums[0:GROUP, sl] = high
+        sums[GROUP : 2 * GROUP, sl] = (balance - high.astype(F32)).astype(BF16)
+        sums[2 * GROUP : 3 * GROUP, sl] = (values * raw).astype(BF16)
+        sums[3 * GROUP : 4 * GROUP, sl] = (values * across).astype(BF16)
         conv_ref[5:6, sl] += jnp.sum(upstream_wide * values, axis=0, keepdims=True)
         inner_grad = step_wide * raw + key_wide * across + skip * upstream_wide
         grad = inner_grad * slope
@@ -518,10 +525,10 @@
     gkq_ref[:, :size] = (nn(grad_scores, queries) + nt(weighted[...], held)).astype(BF16)
     gkq_ref[:, size:] = (tn(grad_scores, keys) + nt(entered[...], state)).astype(BF16)
 
-    collected = nn(sums_high[...], collect[...]) + nn(sums_low[...], collect[...])
-    balance = collected[:GROUP]
-    direct = collected[GROUP : 2 * GROUP]
-    key_dot = collected[2 * GROUP :]
+    collected = nn(sums[...], collect[...])
+    balance = collected[:GROUP] + collected[GROUP : 2 * GROUP]
+    direct = collected[2 * GROUP : 3 * GROUP]
+    key_dot = collected[3 * GROUP :]
 
     def row_collect(value):
         high = value.astype(BF16)
@@ -553,57 +560,66 @@
 
 
 def state_grad_kernel(
-    len_ref, own_ref, other_ref, spre_ref, taps_ref, normed_t_ref, gstep_ref, inner_rows_ref,
-    gain_ref, heads_ref,
+    rank_ref, len_ref, own_ref, other_ref, spre_ref, taps_ref, normed_t_ref, gstep_ref,
+    inner_rows_ref, gain_ref, heads_ref,
     gsp_ref, rest_ref, conv_ref, ext, cext, turned, *, shard, state_shard, heads,
 ):
-    rows, channels = spre_ref.shape
+    rows, channels = own_ref.shape
     width = rest_ref.shape[0]
+    half = rows - HALO
+    rank = rank_ref[0, 0]
+    base = pl.multiple_of(rank * (half - HALO), HALO)
+    chunk = window_chunk(rows)
     ends = sequence_ends(len_ref)
-    ext[0:8, :] = jnp.zeros((8, channels), F32)
-    ext[8 : 8 + rows, :] = spre_ref[...]
+    before = spre_ref[pl.ds(pl.multiple_of(jnp.maximum(base - 8, 0), 8), 8), :]
+    ext[0:8, :] = jnp.where(rank > 0, before, 0.0)
+    ext[8 : 8 + rows, :] = spre_ref[pl.ds(base, rows), :]
     cext[rows : rows + 8, :] = jnp.zeros((8, channels), F32)
     conv_ref[...] = jnp.zeros_like(conv_ref)
-    for group in range(rows // GROUP):
-        base = group * GROUP
-        token = tokens_column(base)
+    gsp_ref[...] = jnp.zeros_like(gsp_ref)
+    for at in range(0, rows, chunk):
+        token = tokens_column(base + at, chunk)
         position = position_of(ends, token)
+        owned = ((token >= rank * half) & (token < (rank + 1) * half)).astype(F32)
+        keep = [(position >= offset).astype(F32) for offset in (1, 2, 3)]
         for part in range(channels // LANES):
             sl = slice(part * LANES, (part + 1) * LANES)
-            shifted = [
-                ext[base + 8 - offset : base + 8 - offset + GROUP, sl] for offset in range(4)
-            ]
+            shifted = [ext[at + 8 - offset : at + 8 - offset + chunk, sl] for offset in range(4)]
             total = taps_ref[4:5, sl] + taps_ref[3:4, sl] * shifted[0]
             for offset in (1, 2, 3):
-                keep = (position >= offset).astype(F32)
-                total = total + keep * (taps_ref[3 - offset : 4 - offset, sl] * shifted[offset])
+                total = total + keep[offset - 1] * (
+                    taps_ref[3 - offset : 4 - offset, sl] * shifted[offset]
+                )
             logistic = sigmoid(total)
             slope = logistic * (1.0 + total * (1.0 - logistic))
-            upstream = own_ref[base : base + GROUP, sl].astype(F32) + other_ref[
-                base : base + GROUP, sl
+            upstream = own_ref[at : at + chunk, sl].astype(F32) + other_ref[
+                at : at + chunk, sl
             ].astype(F32)
             grad = upstream * slope
-            cext[base : base + GROUP, sl] = grad
+            cext[at : at + chunk, sl] = grad
+            grad = grad * owned
             conv_ref[4:5, sl] += jnp.sum(grad, axis=0, keepdims=True)
             conv_ref[3:4, sl] += jnp.sum(grad * shifted[0], axis=0, keepdims=True)
             for offset in (1, 2, 3):
-                keep = (position >= offset).astype(F32)
                 conv_ref[3 - offset : 4 - offset, sl] += jnp.sum(
-                    keep * grad * shifted[offset], axis=0, keepdims=True
+                    keep[offset - 1] * grad * shifted[offset], axis=0, keepdims=True
                 )
-    for group in range(rows // GROUP):
-        base = group * GROUP
-        token = tokens_column(base)
+    for at in range(0, rows, chunk):
+        token = tokens_column(base + at, chunk)
+        owned = ((token >= rank * half) & (token < (rank + 1) * half)).astype(F32)
+        ahead = [
+            (position_of(ends, token + offset) >= offset).astype(F32) for offset in (1, 2, 3)
+        ]
         for part in range(channels // LANES):
             sl = slice(part * LANES, (part + 1) * LANES)
-            result = taps_ref[3:4, sl] * cext[base : base + GROUP, sl]
+            result = taps_ref[3:4, sl] * cext[at : at + chunk, sl]
             for offset in (1, 2, 3):
-                ahead = (position_of(ends, token + offset) >= offset).astype(F32)
-                result = result + ahead * (
+                result = result + ahead[offset - 1] * (
                     taps_ref[3 - offset : 4 - offset, sl]
-                    * cext[base + offset : base + offset + GROUP, sl]
+                    * cext[at + offset : at + offset + chunk, sl]
                 )
-            gsp_ref[base : base + GROUP, sl] = result.astype(BF16)
+            place = pl.ds(pl.multiple_of(base + at, HALO), chunk)
+            gsp_ref[place, sl] = (result * owned).astype(BF16)
     rest_ref[:, :channels] = nn(normed_t_ref[...], gsp_ref[...]).astype(BF16)
     step_part = nn(normed_t_ref[...], gstep_ref[...])
     turned[...] = jnp.zeros_like(turned)
@@ -621,12 +637,73 @@
     rest_ref[:, channels:] = (step_part + turned[...].T).astype(BF16)
 
 
+def window_chunk(rows):
+    return max(n for n in range(HALO, GROUP + 1, HALO) if rows % n == 0)
+
+
+def finish_kernel(
+    first_ref, inner_ref, rest_ref, weight_ref, state_ref, step_ref, pgi_ref, packed_ref
+):
+    width = first_ref.shape[1]
+    states = state_ref.shape[1]
+    heads = step_ref.shape[1]
+    shard = step_ref.shape[0]
+    gate = first_ref[...].astype(F32)
+    inner = inner_ref[...]
+    rest = rest_ref[...]
+    pgi_ref[:, 0:1, :] = gate[:, None, :]
+    pgi_ref[:, 1:2, :] = inner[:, None, :]
+    weight = weight_ref[...].astype(F32)
+    product = jnp.sum(gate * weight[:, :width] + inner * weight[:, width:], axis=1, keepdims=True)
+    product += jnp.sum(rest[:, :states] * state_ref[...].astype(F32), axis=1, keepdims=True)
+    small = rest[:, states:]
+    product += jnp.sum(small[:, :heads] * step_ref[...].astype(F32), axis=1, keepdims=True)
+    lane = lax.broadcasted_iota(jnp.int32, (shard, LANES), 1)
+    packed_ref[:, :states] = rest[:, :states]
+    packed_ref[:, states:] = jnp.where(lane == LANE_GAIN, product, small)
+
+
+def unpack_kernel(
+    own_ref, other_ref, norm_ref,
+    state_ref, step_ref, gain_ref, conv_ref, bias_ref, taps_ref, taps_bias_ref,
+    decay_ref, skip_ref, step_bias_ref, gate_ref,
+):
+    shard, states = state_ref.shape
+    heads = step_ref.shape[1]
+    state_shard = taps_ref.shape[1]
+    state_ref[...] = own_ref[:, :states] + other_ref[:, :states]
+    small = own_ref[:, states:]
+    both = small + other_ref[:, states:]
+    step_ref[...] = small[:, :heads]
+
+    def turn(value):
+        if shard < LANES:
+            value = jnp.concatenate([value, jnp.zeros((LANES - shard, LANES), F32)], axis=0)
+        return value.T
+
+    small_rows, both_rows = turn(small), turn(both)
+    gain_ref[...] = both_rows[LANE_GAIN : LANE_GAIN + 1, :shard] / norm_ref[...].astype(F32)
+    conv_ref[...] = small_rows[LANE_CONV : LANE_CONV + 4, :shard]
+    bias_ref[...] = small_rows[LANE_CONV + 4 : LANE_CONV + 5, :shard]
+    gate_ref[...] = small_rows[LANE_GATE : LANE_GATE + 1, :shard]
+    taps_ref[...] = both_rows[LANE_STATE : LANE_STATE + 4, :state_shard]
+    taps_bias_ref[...] = both_rows[LANE_STATE + 4 : LANE_STATE + 5, :state_shard]
+    first = small[0:8, :]
+    for which, out_ref in enumerate((decay_ref, step_bias_ref, skip_ref)):
+        start = LANE_HEADS + which * heads
+        out_ref[...] = pltpu.roll(first, LANES - start, 1)[0:1, :heads]
+
+
 def shape_of(dims, dtype):
     return jax.ShapeDtypeStruct(dims, dtype)
 
 
 def params(**kwargs):
     return pltpu.CompilerParams(vmem_limit_bytes=VMEM_BYTES, **kwargs)
+
+
+def cost(micros):
+    return pl.CostEstimate(flops=int(micros * 1.1e9), bytes_accessed=0, transcendentals=0)
 
 
 SMEM_SPEC = pl.BlockSpec(memory_space=pltpu.SMEM)
@@ -645,17 +722,20 @@
     return lax.ppermute(value, "dp", [(i, i ^ (1 << bit)) for i in range(count)])
 
 
-def gather_by_bits(value, rank, count, spread_first):
-    held = []
+def gather_by_bits(value, rank, count, spread_first, before_second=None):
+    held, begun = [], []
     rows, lanes = value.shape
     for bit in reversed(bit_order(count, spread_first)):
+        if len(begun) == 1 and before_second is not None:
+            value = lax.optimization_barrier((value, before_second))[0]
+        begun.append(value)
         other = flip(value, bit, count)
         held = sorted(held + [bit], reverse=True)
         low = (rank >> bit) & 1 == 0
         value = jnp.stack(
             [jnp.where(low, value, other), jnp.where(low, other, value)], axis=held.index(bit)
         )
-    return value.reshape(count * rows, lanes)
+    return value.reshape(count * rows, lanes), begun
 
 
 def scatter_by_bits(value, rank, count, spread_first):
@@ -713,7 +793,13 @@
     def exchange(value):
         return lax.ppermute(value, "tensor", swap)
 
-    hidden_other = exchange(hidden_in)
+    pieces = []
+    for part in range(half_groups):
+        piece = hidden_in[part * GROUP : (part + 1) * GROUP]
+        if pieces:
+            piece = lax.optimization_barrier((piece, pieces[-1]))[0]
+        pieces.append(exchange(piece))
+    hidden_other = jnp.concatenate(pieces, axis=0)
     cotangent_other = exchange(lax.optimization_barrier((cotangent, hidden_other))[0])
 
     state_shard = conv_state.shape[1]
@@ -727,15 +813,19 @@
             pltpu.VMEM((shard, LANES), F32),
         ],
         compiler_params=params(),
+        cost_estimate=cost(2),
         name="pack_small",
     )(
         proj_state, proj_step, norm_gain[None, :], conv_inner.reshape(taps, shard),
         conv_inner_bias, gate_gain, conv_state, conv_state_bias[None, :],
     )
+    w_inner, begun = gather_by_bits(
+        projection_gate_inner[:, 1], shard_rank, shard_count, False, pieces[0]
+    )
+    w_rest, _ = gather_by_bits(rest_shard, shard_rank, shard_count, True)
     second_shard = jnp.concatenate([projection_gate_inner[:, 0], proj_out.T], axis=1)
+    second_shard = lax.optimization_barrier((second_shard, begun[min(2, len(begun) - 1)]))[0]
     w_second = lax.all_gather(second_shard, "dp", axis=0, tiled=True)
-    w_inner = gather_by_bits(projection_gate_inner[:, 1], shard_rank, shard_count, False)
-    w_rest = gather_by_bits(rest_shard, shard_rank, shard_count, True)
     w_state = w_rest[:, : 2 * size]
     w_step = w_rest[:, 2 * size :]
     w_gate = w_second[:, :inner]
@@ -789,6 +879,7 @@
             pltpu.VMEM((GROUP, inner), BF16),
         ],
         compiler_params=params(),
+        cost_estimate=cost(2),
         name="mixer_forward",
     )(rank, lengths, hidden_in, hidden_other, w_inner, w_rest, head_rows)
 
@@ -812,6 +903,7 @@
             shape_of((8, tokens), F32),
         ],
         compiler_params=params(),
+        cost_estimate=cost(16),
         name="gate_forward",
     )(rank, lengths, cotangent, cotangent_other, normed, mixed, w_second, w_second, rows)
 
@@ -832,6 +924,7 @@
             shape_of((8, inner), F32),
         ],
         compiler_params=params(),
+        cost_estimate=cost(13),
         name="gate_backward",
     )(sums, sums_other, gate_pre, grad_out_low, mixed, rows)
 
@@ -849,6 +942,7 @@
         out_specs=pl.BlockSpec((width, GROUP), lambda i: (0, i)),
         out_shape=shape_of((width, 2 * inner), BF16),
         compiler_params=params(),
+        cost_estimate=cost(13),
         name="early_weight_grads",
     )(live_t, out_low, normed_t, grad_gate_low)
 
@@ -860,13 +954,8 @@
         (grad_first, first_grads, mix_away)
     )
     first_sum = lax.psum_scatter(first_grads, "dp", scatter_dimension=0, tiled=True)
+    mix_other = exchange(mix_away)
     mix_here = nt(rows_of(out_low, tensor_rank), w_out)
-    mix = mix_here + exchange(mix_away).astype(F32)
-    slot = tensor_rank * half_rows + jnp.arange(half_rows, dtype=jnp.int32)
-    valid_half = slot < jnp.sum(lengths[0])
-    hidden_wide = hidden_in.astype(F32)
-    block_out = (hidden_wide + jnp.where(valid_half[:, None], mix, 0.0)).astype(BF16)
-
     last = groups - 1
     grad_inner_low, grad_kq, grad_step_low, conv_rows, head_sums = pl.pallas_call(
         backward_kernel,
@@ -912,18 +1001,29 @@
             pltpu.VMEM((GROUP, GROUP), F32),
             pltpu.VMEM((GROUP, inner), BF16),
             pltpu.VMEM((GROUP, inner), BF16),
-            pltpu.VMEM((GROUP, inner), BF16),
-            pltpu.VMEM((3 * GROUP, inner), BF16),
-            pltpu.VMEM((3 * GROUP, inner), BF16),
+            pltpu.VMEM((4 * GROUP, inner), BF16),
         ],
         compiler_params=params(),
+        cost_estimate=cost(2),
         name="mixer_backward",
     )(
         lengths, inner_pre, inner_pre, state_act, step_in, mixed, grad_first, prev_states,
         rows, head_rows,
     )
 
-    grad_kq_other = exchange(grad_kq)
+    window = half_rows + HALO
+    kq_own = lax.dynamic_slice_in_dim(grad_kq, tensor_rank * (half_rows - HALO), window)
+    kq_away = lax.dynamic_slice_in_dim(grad_kq, (1 - tensor_rank) * (half_rows - HALO), window)
+    kq_other = exchange(kq_away)
+    grad_inner_low, kq_other, mix_other, first_sum = lax.optimization_barrier(
+        (grad_inner_low, kq_other, mix_other, first_sum)
+    )
+    mix = mix_here + mix_other.astype(F32)
+    slot = tensor_rank * half_rows + jnp.arange(half_rows, dtype=jnp.int32)
+    valid_half = slot < jnp.sum(lengths[0])
+    hidden_wide = hidden_in.astype(F32)
+    block_out = (hidden_wide + jnp.where(valid_half[:, None], mix, 0.0)).astype(BF16)
+
 
     def partial_normed(which):
         return (
@@ -943,19 +1043,20 @@
         functools.partial(
             state_grad_kernel, shard=shard, state_shard=state_shard, heads=heads
         ),
-        in_specs=[SMEM_SPEC] + [vmem] * 9,
+        in_specs=[SMEM_SPEC, SMEM_SPEC] + [vmem] * 9,
         out_specs=[vmem] * 2,
         out_shape=[shape_of((tokens, 2 * size), BF16), shape_of((width, 2 * size + LANES), BF16)],
         scratch_shapes=[
             pltpu.VMEM((8, 2 * size), F32),
-            pltpu.VMEM((tokens + 8, 2 * size), F32),
-            pltpu.VMEM((tokens + 8, 2 * size), F32),
+            pltpu.VMEM((window + 8, 2 * size), F32),
+            pltpu.VMEM((window + 8, 2 * size), F32),
             pltpu.VMEM((LANES, width), F32),
         ],
         compiler_params=params(),
+        cost_estimate=cost(8),
         name="state_backward",
     )(
-        lengths, grad_kq, grad_kq_other, state_pre, state_rows, normed_t, grad_step_low,
+        rank, lengths, kq_own, kq_other, state_pre, state_rows, normed_t, grad_step_low,
         conv_rows, gain_rows, head_sums,
     )
     rest_sum = scatter_by_bits(rest_grads, shard_rank, shard_count, True)
@@ -971,40 +1072,52 @@
         + cotangent.astype(F32)
     )
 
-    gate_grad_own = first_sum[:, inner:].astype(F32)
-    state_grad_own = rest_sum[:, : 2 * size]
-    small = rest_sum[:, 2 * size :]
-    step_grad_own = small[:, :heads]
-
-    def by_row(grad, weight):
-        return jnp.sum(grad * weight.astype(F32), axis=1)
-
-    gain_part = (
-        by_row(gate_grad_own, projection_gate_inner[:, 0])
-        + by_row(inner_sum, projection_gate_inner[:, 1])
-        + by_row(step_grad_own, proj_step)
-        + jnp.where(tensor_rank == 0, by_row(state_grad_own, proj_state), 0.0)
-    )
-    gain_own = (gain_part + exchange(gain_part)) / norm_gain.astype(F32)
-
-    conv_own = small[:, LANE_CONV : LANE_CONV + 5].T
-    state_own = small[:state_shard, LANE_STATE : LANE_STATE + 5].T
-    head_all = small[0, LANE_HEADS : LANE_HEADS + 3 * heads].reshape(3, heads)
+    grad_pgi, packed = pl.pallas_call(
+        finish_kernel,
+        in_specs=[vmem] * 6,
+        out_specs=[vmem] * 2,
+        out_shape=[shape_of((shard, 2, inner), F32), shape_of((shard, 2 * size + LANES), F32)],
+        compiler_params=params(),
+        cost_estimate=cost(1),
+        name="finish",
+    )(
+        first_sum[:, inner:], inner_sum, rest_sum,
+        projection_gate_inner.reshape(shard, 2 * inner), proj_state, proj_step,
+    )
+    (
+        grad_state, grad_step, grad_gain, grad_conv, grad_bias, grad_taps, grad_taps_bias,
+        grad_decay, grad_skip, grad_step_bias, grad_gate_gain,
+    ) = pl.pallas_call(
+        unpack_kernel,
+        in_specs=[vmem] * 3,
+        out_specs=[vmem] * 11,
+        out_shape=[
+            shape_of(dims, F32)
+            for dims in (
+                (shard, 2 * size), (shard, heads), (1, shard), (taps, shard), (1, shard),
+                (taps, state_shard), (1, state_shard), (1, heads), (1, heads), (1, heads),
+                (1, shard),
+            )
+        ],
+        compiler_params=params(),
+        cost_estimate=cost(1),
+        name="unpack_small",
+    )(packed, exchange(packed), norm_gain[None, :])
     return (
         block_out,
         grad_hidden,
-        gain_own,
-        jnp.stack([gate_grad_own, inner_sum], axis=1),
-        state_grad_own,
-        step_grad_own,
-        conv_own[0:4][:, None, :],
-        conv_own[4:5],
-        state_own[0:4],
-        state_own[4],
-        head_all[0],
-        head_all[2],
-        head_all[1],
-        small[:, LANE_GATE][None, :],
+        grad_gain[0],
+        grad_pgi,
+        grad_state,
+        grad_step,
+        grad_conv[:, None, :],
+        grad_bias,
+        grad_taps,
+        grad_taps_bias[0],
+        grad_decay[0],
+        grad_skip[0],
+        grad_step_bias[0],
+        grad_gate_gain,
         first_sum[:, :inner].astype(F32).T,
     )
 

time: 357 us -> 335 us (0.938)
  other arithmetic: 20.2 us -> 13.5 us
  local copies, waits for them, and re-layouts: 25.4 us -> 19.5 us
  waiting for transfers between devices: 88.5 us -> 82.9 us
  starting transfers between devices: 27.3 us -> 31.6 us
  Pallas kernels: 136 us -> 132 us
    ppermute x16, waiting for transfers between devices: 79.2 us -> 45.9 us  [flip(): return lax.ppermute(value, 'dp', [(i, i ^ 1 << bit) for i in range(count)])]
    ppermute x7 -> x9, waiting for transfers between devices: 9.22 us -> 26.7 us  [exchange(): return lax.ppermute(value, 'tensor', swap)]
    reduce_scatter x1, waiting for transfers between devices: 0.01 us -> 10.3 us  [on_device(): lax.psum_scatter(first_grads, 'dp', scatter_dimension=0, tiled=True)]
    pallas_call x1, Pallas kernels: 53.3 us -> 46.5 us  [on_device(): pl.pallas_call(backward_kernel, grid=(groups,), in_specs=[SMEM_SPEC, pl.B...]
    ppermute x7 -> x9, starting transfers between devices: 7.83 us -> 13.1 us  [exchange(): return lax.ppermute(value, 'tensor', swap)]
    dot_general x9, matrix products: 34.5 us -> 29.7 us  [nt(): lax.dot_general(left, right, (((1,), (1,)), ((), ())), preferred_element_...]
    pallas_call x0 -> x2, Pallas kernels: none -> 3.67 us  [the longest x1 2.04 us: on_device(): pl.pallas_call(finish_kernel, in_specs=[vmem] * 6, out_specs=[vmem] * 2,...]
    unnamed x73 -> x65, local copies, waits for them, and re-layouts: 8.67 us -> 8.97 us
  transfers between devices with their start and end apart: 25 -> 27, of which waited for: 13 -> 16; matrix products, arithmetic and copies ran while one was open for 17% -> 13% of each run, Pallas kernels for 11% -> 23%
where the time goes in v3:
time: 335 us; the launch traced here: 332 us
  Pallas kernels  132 us (39%)
  waiting for transfers between devices  82.9 us (25%)
  matrix products  37.4 us (11%)
  starting transfers between devices  31.6 us (9%)
  local copies, waits for them, and re-layouts  19.5 us (6%)
  between operations  14.9 us (4%)
  other arithmetic  13.5 us (4%)
    pallas_call x1, Pallas kernels, on_device(): pl.pallas_call(backward_kernel, grid=(groups,), in_specs=[SMEM_SPEC, pl.B...  46.5 us
    ppermute x16, waiting for transfers between devices, flip(): return lax.ppermute(value, 'dp', [(i, i ^ 1 << bit) for i in range(count)])  45.9 us
    dot_general x9, matrix products, nt(): lax.dot_general(left, right, (((1,), (1,)), ((), ())), preferred_element_...  29.7 us
    pallas_call x1, Pallas kernels, on_device(): pl.pallas_call(functools.partial(forward_kernel, shard=shard, state_shard...  28.5 us
    ppermute x9, waiting for transfers between devices, exchange(): return lax.ppermute(value, 'tensor', swap)  26.7 us
    ppermute x16, starting transfers between devices, flip(): return lax.ppermute(value, 'dp', [(i, i ^ 1 << bit) for i in range(count)])  18.5 us
    pallas_call x1, Pallas kernels, on_device(): pl.pallas_call(gate_kernel, grid=(groups,), in_specs=[SMEM_SPEC, SMEM_SPE...  16.5 us
    pallas_call x1, Pallas kernels, on_device(): pl.pallas_call(early_grad_kernel, grid=(tiles,), in_specs=[whole(width, t...  13.3 us
  transfers between devices with their start and end apart: 27, of which 16 were waited for; matrix products, arithmetic and copies ran while one was open for 13% of the time, Pallas kernels for 23%

profile of v3, /device:TPU:0, one launch (start us, length us, event | category | flops | bytes accessed | tf_op | source)
XLA Modules:
  0.0 331.5 jit_solution(3604360666282633024)
XLA Ops:
  7.2 2.3 fusion.61
  9.6 3.0 collective-permute-start
  13.0 2.7 collective-permute-start.4
  15.6 6.1 %collective-permute-done.4 = bf16[64,1024]{1,0:T(8,128)(2,1)S(1)} collective-permute-done((bf16[64,1024]{1,0:T(8,128)(2,1)S(1)}, bf16[64,1024]{1,0:T(8,128)(2,1)S(1)}, u32[]{:S(2)}, u32[]{:S(2)}) %collective-permute-start.4) | collective-permute-done | bytes 131104 | tf_op jit(solution)/shard_map/ppermute | solution.py:722
  21.8 2.7 collective-permute-done
  24.5 1.8 collective-permute-start.5
  27.0 4.9 %collective-permute-done.5 = bf16[2,64,1024]{2,1,0:T(8,128)(2,1)S(1)} collective-permute-done((bf16[2,64,1024]{2,1,0:T(8,128)(2,1)S(1)}, bf16[2,64,1024]{2,1,0:T(8,128)(2,1)S(1)}, u32[]{:S(2)}, u32[]{:S(2)}) %collective-permute-start.5) | collective-permute-done | bytes 262176 | tf_op jit(solution)/shard_map/ppermute | solution.py:722
  32.8 1.5 pack_small.1
  34.4 1.4 collective-permute-start.8
  35.8 2.9 collective-permute-done.8
  38.7 0.8 select_bitcast_fusion.15
  39.5 2.6 collective-permute-start.9
  42.1 4.9 %collective-permute-done.9 = bf16[2,64,384]{2,1,0:T(8,128)(2,1)S(1)} collective-permute-done((bf16[2,64,384]{2,1,0:T(8,128)(2,1)S(1)}, bf16[2,64,384]{2,1,0:T(8,128)(2,1)S(1)}, u32[]{:S(2)}, u32[]{:S(2)}) %collective-permute-start.9) | collective-permute-done | bytes 98336 | tf_op jit(solution)/shard_map/ppermute | solution.py:722
  47.1 1.9 collective-permute-start.10
  49.0 1.5 collective-permute-start.1
  50.5 1.5 collective-permute-start.6
  52.0 5.7 %collective-permute-done.10 = bf16[2,2,64,384]{3,2,1,0:T(8,128)(2,1)S(1)} collective-permute-done((bf16[2,2,64,384]{3,2,1,0:T(8,128)(2,1)S(1)}, bf16[2,2,64,384]{3,2,1,0:T(8,128)(2,1)S(1)}, u32[]{:S(2)}, u32[]{:S(2)}) %collective-permute-start.10) | collective-permute-done | bytes 196640 | tf_op jit(solution)/shard_map/ppermute | solution.py:722
  58.7 1.3 collective-permute-start.2
  60.1 1.1 pad_maximum_fusion.1
  61.4 11.9 %collective-permute-done.2 = bf16[256,1024]{1,0:T(8,128)(2,1)S(1)} collective-permute-done((bf16[256,1024]{1,0:T(8,128)(2,1)}, bf16[256,1024]{1,0:T(8,128)(2,1)S(1)}, u32[]{:S(2)}, u32[]{:S(2)}) %collective-permute-start.2) | collective-permute-done | bytes 524320 | tf_op jit(solution)/shard_map/ppermute | solution.py:794
  73.3 1.1 copy-done.12
  74.5 1.2 collective-permute-start.3
  76.5 1.1 select_bitcast_fusion.5
  77.6 1.0 copy.41
  79.0 1.5 copy.39
  80.5 28.5 %mixer_forward.1 = (bf16[1536,1024]{1,0:T(8,128)(2,1)}, bf16[1024,1536]{1,0:T(8,128)(2,1)}, f32[1536,1024]{1,0:T(8,128)}, f32[1536,256]{1,0:T(8,128)}, bf16[1536...) custom-call(s32[1,1]{1,0:T(1,128)} %bitcast.rank_ref, ...), custom_call_target="tpu_custom_call" | custom-call | flops 2200000000 | tf_op jit(solution)/shard_map/mixer_forward/pallas_call | solution.py:846
  109.0 1.9 collective-permute-done.3.other_ref
  110.9 16.5 %gate_forward.1 = (f32[1536,1024]{1,0:T(8,128)}, f32[1536,1024]{1,0:T(8,128)}, bf16[1024,1536]{1,0:T(8,128)(2,1)}, f32[8,1536]{1,0:T(8,128)}) custom-call(s32[1,1]{1,0:T(1,128)} %bitcast.rank_ref, s32[1,4]{1,0:T(1,128)} %len_ref.7, bf16[768,1024]{1,0:T(8,128)(2,1)} %own_ref.3, bf16[768,1024]{1,0:T(8,128)(2,1)} %collective-permute-done.3.other_ref, ...), custom_call_target="tpu_custom_call" | custom-call | flops 17600000000 | tf_op jit(solution)/shard_map/gate_forward/pallas_call | solution.py:886
  127.4 1.3 collective-permute-start.12
  128.7 3.1 collective-permute-done.12.other_sums_ref
  132.4 13.2 %gate_backward.1 = (bf16[1536,1024]{1,0:T(8,128)(2,1)}, bf16[1536,1024]{1,0:T(8,128)(2,1)}, bf16[1536,1024]{1,0:T(8,128)(2,1)}, f32[8,1024]{1,0:T(8,128)}) custom-call(f32[8,1536]{1,0:T(8,128)} %get-tuple-element.73.own_sums_ref, f32[8,1536]{1,0:T(8,128)} %copy-done.24, f32[1536,1024]{1,0:T(8,128)} %get-tuple-element.74.gate_ref, ...), custom_call_target="tpu_custom_call" | custom-call | flops 14300000256 | tf_op jit(solution)/shard_map/gate_backward/pallas_call | solution.py:912
  145.6 13.3 %early_weight_grads.1 = bf16[1024,2048]{1,0:T(8,128)(2,1)} custom-call(bf16[1024,1536]{1,0:T(8,128)(2,1)} %get-tuple-element.81.live_t_ref, bf16[1536,1024]{1,0:T(8,128)(2,1)} %get-tuple-element.76.low_ref, bf16[1024,1536]{1,0:T(8,128)(2,1)} %get-tuple-element.82.normed_t_ref, bf16[1536,1024]{1,0:T(8,128)(2,1)} %get-tuple-element.83.ggp_ref), custom_call_target="tpu_custom_call" | custom-call | flops 14300000256 | tf_op jit(solution)/shard_map/early_weight_grads/pallas_call | solution.py:933
  158.9 5.0 %fusion.15 = bf16[768,1024]{1,0:T(8,128)(2,1)} fusion(bf16[1024,2048]{1,0:T(8,128)(2,1)} %all-gather.2.cloned.1.call-done.w_ref.proj_ref, bf16[1536,1024]{1,0:T(8,128)(2,1)} %get-tuple-element.76.low_ref, s32[]{:T(128)S(6)} %select_n.184), kind=kOutput, calls=%fused_computation.24 | convolution fusion | flops 1611399168 | bytes 5242884 | tf_op jit(solution)/shard_map/dot_general | solution.py:33
  164.0 1.3 collective-permute-start.14
  168.1 46.5 %mixer_backward.1 = (bf16[1536,1024]{1,0:T(8,128)(2,1)}, bf16[1536,256]{1,0:T(8,128)(2,1)}, bf16[1536,128]{1,0:T(8,128)(2,1)}, f32[8,1024]{1,0:T(8,128)}, f32[8,128]{1,0:T(8,128)}) custom-call(s32[1,4]{1,0:T(1,128)} %len_ref.7, f32[1536,1024]{1,0:T(8,128)} %get-tuple-element.77.ipre_ref.halo_ref, f32[1536,1024]{1,0:T(8,128)} %get-tuple-element.77.ipre_ref.halo_ref, ...), custom_call_target="tpu_custom_call" | custom-call | flops 2200000000 | tf_op jit(solution)/shard_map/mixer_backward/pallas_call | solution.py:960
  214.6 2.1 constant_dynamic-slice_fusion.4
  217.5 3.3 fusion.45
  221.3 3.5 %fusion.9 = f32[768,1024]{1,0:T(8,128)} fusion(bf16[1024,2048]{1,0:T(8,128)(2,1)S(1)} %copy-done.18, bf16[1536,1024]{1,0:T(8,128)(2,1)S(1)} %copy-done.26, s32[]{:T(128)S(6)} %select_n.183), kind=kOutput, calls=%fused_computation.18 | convolution fusion | flops 1610612736 | bytes 6815748 | tf_op jit(solution)/shard_map/dot_general | solution.py:33
  226.0 10.3 %reduce-scatter.2.cloned.1.call-done = bf16[64,2048]{1,0:T(8,128)(2,1)} async-done(((bf16[1024,2048]{1,0:T(8,128)(2,1)}), bf16[64,2048]{1,0:T(8,128)(2,1)}) %reduce-scatter.2.cloned.1.call-update) | async-done | bytes 262160 | tf_op jit(solution)/shard_map/reduce_scatter | solution.py:956
  236.3 7.8 %convolution_convert_fusion = bf16[1024,1024]{1,0:T(8,128)(2,1)} fusion(bf16[1024,1536]{1,0:T(8,128)(2,1)} %get-tuple-element.82.normed_t_ref, bf16[1536,1024]{1,0:T(8,128)(2,1)} %get-tuple-element.91), kind=kOutput, calls=%fused_computation.15 | convolution fusion | flops 3222274048 | bytes 8388608 | tf_op jit(solution)/shard_map/dot_general | solution.py:29
  244.1 3.5 %fusion.18 = f32[768,1024]{1,0:T(8,128)} fusion(bf16[1024,1024]{1,0:T(8,128)(2,1)S(1)} %bitcast.127, bf16[1536,1024]{1,0:T(8,128)(2,1)S(1)} %copy-done.20, s32[]{:T(128)S(6)} %select_n.184), kind=kOutput, calls=%fused_computation.25 | convolution fusion | flops 1610612736 | bytes 6815748 | tf_op jit(solution)/shard_map/dot_general | solution.py:33
  247.6 8.4 %state_backward.1 = (bf16[1536,256]{1,0:T(8,128)(2,1)}, bf16[1024,384]{1,0:T(8,128)(2,1)}) custom-call(s32[1,1]{1,0:T(1,128)} %bitcast.rank_ref, s32[1,4]{1,0:T(1,128)} %len_ref.7, bf16[784,256]{1,0:T(8,128)(2,1)} %get-tuple-element.158.own_ref, bf16[784,256]{1,0:T(8,128)(2,1)} %copy-done.22, f32[1536,256]{1,0:T(8,128)} %get-tuple-element.94.spre_ref, ...), custom_call_target="tpu_custom_call" | custom-call | flops 8800000000 | tf_op jit(solution)/shard_map/state_backward/pallas_call | solution.py:1042
  255.9 1.4 constant_dynamic-slice_fusion.1
  258.3 1.4 copy-done.4
  259.7 1.0 copy-done.27
  260.6 5.5 %add_convert_fusion = bf16[768,1024]{1,0:T(8,128)(2,1)S(1)} fusion(f32[768,1024]{1,0:T(8,128)S(1)} %copy-done.4, f32[768,1024]{1,0:T(8,128)} %fusion.18, bf16[1024,2048]{1,0:T(8,128)(2,1)} %all-gather.2.cloned.1.call-done.w_ref.proj_ref, bf16[1536,1024]{1,0:T(8,128)(2,1)S(1)} %copy-done.27, s32[]{:T(128)S(6)} %select_n.184), kind=kOutput, calls=%fused_computation.11 | convolution fusion | flops 1612972032 | bytes 11534340 | tf_op jit(solution)/shard_map/dot_general | solution.py:33
  266.2 1.4 collective-permute-start.15
  267.8 1.0 collective-permute-start.21
  268.8 5.1 %fusion = bf16[768,1024]{1,0:T(8,128)(2,1)} fusion(bf16[768,1024]{1,0:T(8,128)(2,1)S(1)} %copy-done, bf16[768,1024]{1,0:T(8,128)(2,1)} %collective-permute-done.14, pred[768]{0:T(1024)(128)(4,1)S(1)} %add_compare_fusion, bf16[1024,2048]{1,0:T(8,128)(2,1)S(1)} %copy-done.19, bf16[1536,1024]{1,0:T(8,128)(2,1)S(1)} %copy-done.28, s32[]{:T(128)S(6)} %select_n.183), kind=kOutput, calls=%fused_computation.4 | convolution fusion | flops 1615331328 | bytes 8389636 | tf_op jit(solution)/shard_map/dot_general | solution.py:33
  274.6 1.5 collective-permute-start.22
  276.1 1.8 fusion.21
  277.9 3.4 %collective-permute-done.22 = bf16[2,64,384]{2,1,0:T(8,128)(2,1)S(1)} collective-permute-done((bf16[2,64,384]{2,1,0:T(8,128)(2,1)S(1)}, bf16[2,64,384]{2,1,0:T(8,128)(2,1)S(1)}, u32[]{:S(2)}, u32[]{:S(2)}) %collective-permute-start.22) | collective-permute-done | bytes 98336 | tf_op jit(solution)/shard_map/ppermute | solution.py:722
  281.9 1.1 collective-permute-start.17
  283.1 1.0 collective-permute-start.23
  284.8 10.2 %collective-permute-done.23 = bf16[64,384]{1,0:T(8,128)(2,1)S(1)} collective-permute-done((bf16[64,384]{1,0:T(8,128)(2,1)S(1)}, bf16[64,384]{1,0:T(8,128)(2,1)S(1)}, u32[]{:S(2)}, u32[]{:S(2)}) %collective-permute-start.23) | collective-permute-done | bytes 49184 | tf_op jit(solution)/shard_map/ppermute | solution.py:722
  295.9 6.8 %collective-permute-done.15 = bf16[768,1024]{1,0:T(8,128)(2,1)S(1)} collective-permute-done((bf16[768,1024]{1,0:T(8,128)(2,1)S(1)}, bf16[768,1024]{1,0:T(8,128)(2,1)S(1)}, u32[]{:S(2)}, u32[]{:S(2)}) %collective-permute-start.15) | collective-permute-done | bytes 1572896 | tf_op jit(solution)/shard_map/ppermute | solution.py:794
  302.7 1.4 fusion.1
  304.2 1.5 collective-permute-start.19
  305.7 7.0 %collective-permute-done.19 = bf16[64,1024]{1,0:T(8,128)(2,1)S(1)} collective-permute-done((bf16[64,1024]{1,0:T(8,128)(2,1)S(1)}, bf16[64,1024]{1,0:T(8,128)(2,1)S(1)}, u32[]{:S(2)}, u32[]{:S(2)}) %collective-permute-start.19) | collective-permute-done | bytes 131104 | tf_op jit(solution)/shard_map/ppermute | solution.py:722
  313.4 2.0 finish.1
  315.5 1.3 collective-permute-start.24
  316.8 3.9 %fusion.4 = f32[768,1024]{1,0:T(8,128)} fusion(bf16[768,1024]{1,0:T(8,128)(2,1)S(1)} %copy-done, bf16[768,1024]{1,0:T(8,128)(2,1)} %own_ref.3, f32[768,1024]{1,0:T(8,128)S(1)} %get-tuple-element.178, f32[768]{0:T(1024)S(1)} %broadcast_multiply_fusion, f32[768]{0:T(1024)S(1)} %get-tuple-element.177, f32[768]{0:T(1024)S(1)} %get-tuple-element.176), kind=kLoop, calls=%fused_computation.8 | loop fusion | flops 5505024 | bytes 9446400 | tf_op jit(solution)/shard_map/add | solution.py:1070
  321.3 1.6 unpack_small.1
  323.0 1.4 copy.48
  (130 shorter events, 16.2 us)
Async XLA Ops:
  7.2 5.4 %copy-start.5 = (bf16[64,2,1024]{2,1,0:T(2,128)(2,1)S(1)}, bf16[64,2,1024]{2,1,0:T(2,128)(2,1)}, u32[]{:S(2)}) copy-start(bf16[64,2,1024]{2,1,0:T(2,128)(2,1)} %param.18) | copy-start | bytes 786436
  7.2 19.1 %copy-start.13 = (bf16[1024,64]{0,1:T(8,128)(2,1)S(1)}, bf16[1024,64]{0,1:T(8,128)(2,1)}, u32[]{:S(2)}) copy-start(bf16[1024,64]{0,1:T(8,128)(2,1)} %param.29) | copy-start | bytes 393220
  7.2 103.7 %all-gather.2.cloned.1.call-start = ((), (), s32[]{:S(2)}) async-start(), calls=%async_computation.1 | async-start | bytes 4456448 | tf_op jit(solution)/shard_map/all_gather | solution.py:828
  9.6 22.6 %copy-start.14 = (bf16[64,16]{0,1:T(8,128)(2,1)S(1)}, bf16[64,16]{0,1:T(8,128)(2,1)}, u32[]{:S(2)}) copy-start(bf16[64,16]{0,1:T(8,128)(2,1)} %param.20) | copy-start | bytes 6148
  9.6 14.9 %collective-permute-start = (bf16[256,1024]{1,0:T(8,128)(2,1)S(1)}, bf16[256,1024]{1,0:T(8,128)(2,1)S(1)}, u32[]{:S(2)}, u32[]{:S(2)}) collective-permute-start(bf16[256,1024]{1,0:T(8,128)(2,1)S(1)} %get-tuple-element.153), channel_id=1, source_target_pairs={{0,1},{1,0},{2,3},{3,2},{4,5},{5,4},{6,7},{7,6},{8,9},{9,8},{10,11... | collective-permute-start | bytes 1572872 | tf_op jit(solution)/shard_map/ppermute | solution.py:794
  13.0 8.7 %collective-permute-start.4 = (bf16[64,1024]{1,0:T(8,128)(2,1)S(1)}, bf16[64,1024]{1,0:T(8,128)(2,1)S(1)}, u32[]{:S(2)}, u32[]{:S(2)}) collective-permute-start(bf16[64,1024]{1,0:T(8,128)(2,1)S(1)} %bitcast.134), channel_id=1, source_target_pairs={{0,16},{2,18},{4,20},{6,22},{8,24},{10,26},{12,28},{14,30},{16,0},... | collective-permute-start | bytes 393224 | tf_op jit(solution)/shard_map/ppermute | solution.py:722
  24.5 7.5 %collective-permute-start.5 = (bf16[2,64,1024]{2,1,0:T(8,128)(2,1)S(1)}, bf16[2,64,1024]{2,1,0:T(8,128)(2,1)S(1)}, u32[]{:S(2)}, u32[]{:S(2)}) collective-permute-start(bf16[2,64,1024]{2,1,0:T(8,128)(2,1)S(1)} %pad_maximum_fusion.5), channel_id=1, source_target_pairs={{0,8},{2,10},{4,12},{6,14},{8,0},{10,2},{12,4},{14,6},{16,24},{18,... | collective-permute-start | bytes 786440 | tf_op jit(solution)/shard_map/ppermute | solution.py:722
  32.1 204.2 %reduce-scatter.2.cloned.1.call-start = ((), (), s32[]{:S(2)}) async-start(), calls=%async_computation.2 | async-start | bytes 4456448 | tf_op jit(solution)/shard_map/reduce_scatter | solution.py:956
  34.4 4.3 %collective-permute-start.8 = (bf16[64,384]{1,0:T(8,128)(2,1)}, bf16[64,384]{1,0:T(8,128)(2,1)S(1)}, u32[]{:S(2)}, u32[]{:S(2)}) collective-permute-start(bf16[64,384]{1,0:T(8,128)(2,1)} %pack_small.1), channel_id=1, source_target_pairs={{0,4},{2,6},{4,0},{6,2},{8,12},{10,14},{12,8},{14,10},{16,20},{18,... | collective-permute-start | bytes 147464 | tf_op jit(solution)/shard_map/ppermute | solution.py:722
  39.5 7.5 %collective-permute-start.9 = (bf16[2,64,384]{2,1,0:T(8,128)(2,1)S(1)}, bf16[2,64,384]{2,1,0:T(8,128)(2,1)S(1)}, u32[]{:S(2)}, u32[]{:S(2)}) collective-permute-start(bf16[2,64,384]{2,1,0:T(8,128)(2,1)S(1)} %pad_maximum_fusion.8), channel_id=1, source_target_pairs={{0,16},{2,18},{4,20},{6,22},{8,24},{10,26},{12,28},{14,30},{16,0},... | collective-permute-start | bytes 294920 | tf_op jit(solution)/shard_map/ppermute | solution.py:722
  47.1 10.7 %collective-permute-start.10 = (bf16[2,2,64,384]{3,2,1,0:T(8,128)(2,1)S(1)}, bf16[2,2,64,384]{3,2,1,0:T(8,128)(2,1)S(1)}, u32[]{:S(2)}, u32[]{:S(2)}) collective-permute-start(bf16[2,2,64,384]{3,2,1,0:T(8,128)(2,1)S(1)} %pad_maximum_fusion.7), channel_id=1, source_target_pairs={{0,8},{2,10},{4,12},{6,14},{8,0},{10,2},{12,4},{14,6},{16,24},{18,... | collective-permute-start | bytes 589832 | tf_op jit(solution)/shard_map/ppermute | solution.py:722
  49.0 9.6 %collective-permute-start.1 = (bf16[256,1024]{1,0:T(8,128)(2,1)S(1)}, bf16[256,1024]{1,0:T(8,128)(2,1)S(1)}, u32[]{:S(2)}, u32[]{:S(2)}) collective-permute-start(bf16[256,1024]{1,0:T(8,128)(2,1)S(1)} %get-tuple-element.65), channel_id=1, source_target_pairs={{0,1},{1,0},{2,3},{3,2},{4,5},{5,4},{6,7},{7,6},{8,9},{9,8},{10,11... | collective-permute-start | bytes 1572872 | tf_op jit(solution)/shard_map/ppermute | solution.py:794
  50.5 9.5 %collective-permute-start.6 = (bf16[2,2,64,1024]{3,2,0,1:T(8,128)(2,1)S(1)}, bf16[2,2,64,1024]{3,2,0,1:T(8,128)(2,1)S(1)}, u32[]{:S(2)}, u32[]{:S(2)}) collective-permute-start(bf16[2,2,64,1024]{3,2,0,1:T(8,128)(2,1)S(1)} %pad_maximum_fusion.3), channel_id=1, source_target_pairs={{0,4},{2,6},{4,0},{6,2},{8,12},{10,14},{12,8},{14,10},{16,20},{18,... | collective-permute-start | bytes 1572872 | tf_op jit(solution)/shard_map/ppermute | solution.py:722
  58.6 17.9 %collective-permute-start.11 = (bf16[2,2,2,64,384]{4,3,2,0,1:T(8,128)(2,1)}, bf16[2,2,2,64,384]{4,3,2,0,1:T(8,128)(2,1)}, u32[]{:S(2)}, u32[]{:S(2)}) collective-permute-start(bf16[2,2,2,64,384]{4,3,2,0,1:T(8,128)(2,1)} %pad_maximum_fusion.4), channel_id=1, source_target_pairs={{0,2},{2,0},{4,6},{6,4},{8,10},{10,8},{12,14},{14,12},{16,18},{18,... | collective-permute-start | bytes 1179656 | tf_op jit(solution)/shard_map/ppermute | solution.py:722
  58.6 17.1 %copy-start.25 = (bf16[16]{0:T(256)(128)(2,1)S(1)}, bf16[16]{0:T(256)(128)(2,1)}, u32[]{:S(2)}) copy-start(bf16[16]{0:T(256)(128)(2,1)} %param.25) | copy-start | bytes 100
  58.6 17.1 %copy-start.16 = (bf16[16]{0:T(256)(128)(2,1)S(1)}, bf16[16]{0:T(256)(128)(2,1)}, u32[]{:S(2)}) copy-start(bf16[16]{0:T(256)(128)(2,1)} %param.26) | copy-start | bytes 100
  58.7 17.0 %copy-start.17 = (bf16[16]{0:T(256)(128)(2,1)S(1)}, bf16[16]{0:T(256)(128)(2,1)}, u32[]{:S(2)}) copy-start(bf16[16]{0:T(256)(128)(2,1)} %param.27) | copy-start | bytes 100
  58.7 14.6 %collective-permute-start.2 = (bf16[256,1024]{1,0:T(8,128)(2,1)}, bf16[256,1024]{1,0:T(8,128)(2,1)S(1)}, u32[]{:S(2)}, u32[]{:S(2)}) collective-permute-start(bf16[256,1024]{1,0:T(8,128)(2,1)} %get-tuple-element.66), channel_id=1, source_target_pairs={{0,1},{1,0},{2,3},{3,2},{4,5},{5,4},{6,7},{7,6},{8,9},{9,8},{10,11... | collective-permute-start | bytes 1572872 | tf_op jit(solution)/shard_map/ppermute | solution.py:794
  61.2 17.5 %collective-permute-start.7 = (bf16[2,2,2,64,1024]{4,3,0,1,2:T(8,128)(2,1)}, bf16[2,2,2,64,1024]{4,3,0,1,2:T(8,128)(2,1)S(1)}, u32[]{:S(2)}, u32[]{:S(2)}) collective-permute-start(bf16[2,2,2,64,1024]{4,3,0,1,2:T(8,128)(2,1)} %pad_maximum_fusion.1), channel_id=1, source_target_pairs={{0,2},{2,0},{4,6},{6,4},{8,10},{10,8},{12,14},{14,12},{16,18},{18,... | collective-permute-start | bytes 3145736 | tf_op jit(solution)/shard_map/ppermute | solution.py:722
  73.3 1.1 copy-start.12
  74.5 36.4 %collective-permute-start.3 = (bf16[768,1024]{1,0:T(8,128)(2,1)}, bf16[768,1024]{1,0:T(8,128)(2,1)}, u32[]{:S(2)}, u32[]{:S(2)}) collective-permute-start(bf16[768,1024]{1,0:T(8,128)(2,1)} %own_ref.3), channel_id=1, source_target_pairs={{0,1},{1,0},{2,3},{3,2},{4,5},{5,4},{6,7},{7,6},{8,9},{9,8},{10,11... | collective-permute-start | bytes 4718600 | tf_op jit(solution)/shard_map/ppermute | solution.py:794
  127.4 4.4 %collective-permute-start.12 = (f32[8,1536]{1,0:T(8,128)}, f32[8,1536]{1,0:T(8,128)S(1)}, u32[]{:S(2)}, u32[]{:S(2)}) collective-permute-start(f32[8,1536]{1,0:T(8,128)} %get-tuple-element.73.own_sums_ref), channel_id=1, source_target_pairs={{0,1},{1,0},{2,3},{3,2},{4,5},{5,4},{6,7},{7,6},{8,9},{9,8},{10,11... | collective-permute-start | bytes 147464 | tf_op jit(solution)/shard_map/ppermute | solution.py:794
  131.8 0.6 copy-start.24
  164.0 1.3 copy-start.15
  164.0 62.0 %collective-permute-start.14 = (bf16[768,1024]{1,0:T(8,128)(2,1)}, bf16[768,1024]{1,0:T(8,128)(2,1)}, u32[]{:S(2)}, u32[]{:S(2)}) collective-permute-start(bf16[768,1024]{1,0:T(8,128)(2,1)} %fusion.15), channel_id=1, source_target_pairs={{0,1},{1,0},{2,3},{3,2},{4,5},{5,4},{6,7},{7,6},{8,9},{9,8},{10,11... | collective-permute-start | bytes 4718600 | tf_op jit(solution)/shard_map/ppermute | solution.py:794
  168.1 49.4 %copy-start.1 = (bf16[2,2,2,2,64,384]{5,4,3,2,1,0:T(8,128)(2,1)S(1)}, bf16[2,2,2,2,64,384]{5,4,3,2,1,0:T(8,128)(2,1)}, u32[]{:S(2)}) copy-start(bf16[2,2,2,2,64,384]{5,4,3,2,1,0:T(8,128)(2,1)} %copy.41) | copy-start | bytes 2359300
  214.6 6.2 %copy-start.9 = (bf16[1536,128]{1,0:T(8,128)(2,1)S(1)}, bf16[1536,128]{1,0:T(8,128)(2,1)}, u32[]{:S(2)}) copy-start(bf16[1536,128]{1,0:T(8,128)(2,1)} %get-tuple-element.92.gstep_ref) | copy-start | bytes 1179652
  214.6 6.7 %copy-start.26 = (bf16[1536,1024]{1,0:T(8,128)(2,1)S(1)}, bf16[1536,1024]{1,0:T(8,128)(2,1)}, u32[]{:S(2)}) copy-start(bf16[1536,1024]{1,0:T(8,128)(2,1)} %get-tuple-element.83.ggp_ref) | copy-start | bytes 9437188
  216.7 8.5 %collective-permute-start.13 = (bf16[784,256]{1,0:T(8,128)(2,1)S(1)}, bf16[784,256]{1,0:T(8,128)(2,1)S(1)}, u32[]{:S(2)}, u32[]{:S(2)}) collective-permute-start(bf16[784,256]{1,0:T(8,128)(2,1)S(1)} %get-tuple-element.159), channel_id=1, source_target_pairs={{0,1},{1,0},{2,3},{3,2},{4,5},{5,4},{6,7},{7,6},{8,9},{9,8},{10,11... | collective-permute-start | bytes 1204232 | tf_op jit(solution)/shard_map/ppermute | solution.py:794
  217.5 3.9 %copy-start.18 = (bf16[1024,2048]{1,0:T(8,128)(2,1)S(1)}, bf16[1024,2048]{1,0:T(8,128)(2,1)}, u32[]{:S(2)}) copy-start(bf16[1024,2048]{1,0:T(8,128)(2,1)} %all-gather.2.cloned.1.call-done.w_ref.proj_ref) | copy-start | bytes 12582916
  225.2 0.8 copy-start.22
  236.3 7.8 %copy-start.7 = (bf16[2,2,2,2,64,1024]{5,4,3,2,1,0:T(8,128)(2,1)S(1)}, bf16[2,2,2,2,64,1024]{5,4,3,2,1,0:T(8,128)(2,1)}, u32[]{:S(2)}) copy-start(bf16[2,2,2,2,64,1024]{5,4,3,2,1,0:T(8,128)(2,1)} %copy.39) | copy-start | bytes 6291460
  236.3 7.8 %copy-start.20 = (bf16[1536,1024]{1,0:T(8,128)(2,1)S(1)}, bf16[1536,1024]{1,0:T(8,128)(2,1)}, u32[]{:S(2)}) copy-start(bf16[1536,1024]{1,0:T(8,128)(2,1)} %get-tuple-element.91) | copy-start | bytes 9437188
  255.9 1.8 copy-start.6
  257.4 10.2 %collective-permute-start.20 = (bf16[2,2,2,64,384]{4,3,2,0,1:T(8,128)(2,1)S(1)}, bf16[2,2,2,64,384]{4,3,2,0,1:T(8,128)(2,1)S(1)}, u32[]{:S(2)}, u32[]{:S(2)}) collective-permute-start(bf16[2,2,2,64,384]{4,3,2,0,1:T(8,128)(2,1)S(1)} %bitcast.132), channel_id=1, source_target_pairs={{0,2},{2,0},{4,6},{6,4},{8,10},{10,8},{12,14},{14,12},{16,18},{18,... | collective-permute-start | bytes 1179656 | tf_op jit(solution)/shard_map/ppermute | solution.py:722
  257.8 1.9 copy-start.4
  257.8 2.8 copy-start.27
  258.0 10.7 %copy-start = (bf16[768,1024]{1,0:T(8,128)(2,1)S(1)}, bf16[768,1024]{1,0:T(8,128)(2,1)}, u32[]{:S(2)}) copy-start(bf16[768,1024]{1,0:T(8,128)(2,1)} %own_ref.2) | copy-start | bytes 4718596
  258.0 10.7 %copy-start.19 = (bf16[1024,2048]{1,0:T(8,128)(2,1)S(1)}, bf16[1024,2048]{1,0:T(8,128)(2,1)}, u32[]{:S(2)}) copy-start(bf16[1024,2048]{1,0:T(8,128)(2,1)} %all-gather.2.cloned.1.call-done.w_ref.proj_ref) | copy-start | bytes 12582916
  258.1 10.7 %copy-start.28 = (bf16[1536,1024]{1,0:T(8,128)(2,1)S(1)}, bf16[1536,1024]{1,0:T(8,128)(2,1)}, u32[]{:S(2)}) copy-start(bf16[1536,1024]{1,0:T(8,128)(2,1)} %get-tuple-element.76.low_ref) | copy-start | bytes 9437188
  258.1 23.3 %collective-permute-start.16 = (bf16[2,2,2,64,1024]{4,3,0,1,2:T(8,128)(2,1)S(1)}, bf16[2,2,2,64,1024]{4,3,0,1,2:T(8,128)(2,1)S(1)}, u32[]{:S(2)}, u32[]{:S(2)}) collective-permute-start(bf16[2,2,2,64,1024]{4,3,0,1,2:T(8,128)(2,1)S(1)} %bitcast.129), channel_id=1, source_target_pairs={{0,2},{2,0},{4,6},{6,4},{8,10},{10,8},{12,14},{14,12},{16,18},{18,... | collective-permute-start | bytes 3145736 | tf_op jit(solution)/shard_map/ppermute | solution.py:722
  266.2 36.5 %collective-permute-start.15 = (bf16[768,1024]{1,0:T(8,128)(2,1)S(1)}, bf16[768,1024]{1,0:T(8,128)(2,1)S(1)}, u32[]{:S(2)}, u32[]{:S(2)}) collective-permute-start(bf16[768,1024]{1,0:T(8,128)(2,1)S(1)} %add_convert_fusion), channel_id=1, source_target_pairs={{0,1},{1,0},{2,3},{3,2},{4,5},{5,4},{6,7},{7,6},{8,9},{9,8},{10,11... | collective-permute-start | bytes 4718600 | tf_op jit(solution)/shard_map/ppermute | solution.py:794
  267.7 8.3 %copy-start.8 = (bf16[2,2,2,2,64,1024]{5,4,3,2,1,0:T(8,128)(2,1)S(1)}, bf16[2,2,2,2,64,1024]{5,4,3,2,1,0:T(8,128)(2,1)}, u32[]{:S(2)}) copy-start(bf16[2,2,2,2,64,1024]{5,4,3,2,1,0:T(8,128)(2,1)} %copy.39) | copy-start | bytes 6291460
  267.7 8.3 %copy-start.21 = (bf16[1536,1024]{1,0:T(8,128)(2,1)S(1)}, bf16[1536,1024]{1,0:T(8,128)(2,1)}, u32[]{:S(2)}) copy-start(bf16[1536,1024]{1,0:T(8,128)(2,1)} %get-tuple-element.91) | copy-start | bytes 9437188
  267.8 6.7 %collective-permute-start.21 = (bf16[2,2,64,384]{3,2,1,0:T(8,128)(2,1)S(1)}, bf16[2,2,64,384]{3,2,1,0:T(8,128)(2,1)S(1)}, u32[]{:S(2)}, u32[]{:S(2)}) collective-permute-start(bf16[2,2,64,384]{3,2,1,0:T(8,128)(2,1)S(1)} %dynamic-slice_bitcast_fusion.2), channel_id=1, source_target_pairs={{0,8},{2,10},{4,12},{6,14},{8,0},{10,2},{12,4},{14,6},{16,24},{18,... | collective-permute-start | bytes 589832 | tf_op jit(solution)/shard_map/ppermute | solution.py:722
  274.6 6.8 %collective-permute-start.22 = (bf16[2,64,384]{2,1,0:T(8,128)(2,1)S(1)}, bf16[2,64,384]{2,1,0:T(8,128)(2,1)S(1)}, u32[]{:S(2)}, u32[]{:S(2)}) collective-permute-start(bf16[2,64,384]{2,1,0:T(8,128)(2,1)S(1)} %dynamic-slice_bitcast_fusion.4), channel_id=1, source_target_pairs={{0,16},{2,18},{4,20},{6,22},{8,24},{10,26},{12,28},{14,30},{16,0},... | collective-permute-start | bytes 294920 | tf_op jit(solution)/shard_map/ppermute | solution.py:722
  277.9 6.1 %copy-start.10 = (bf16[64,2048]{1,0:T(8,128)(2,1)S(1)}, bf16[64,2048]{1,0:T(8,128)(2,1)}, u32[]{:S(2)}) copy-start(bf16[64,2048]{1,0:T(8,128)(2,1)} %reduce-scatter.2.cloned.1.call-done) | copy-start | bytes 786436
  281.4 21.3 %copy-start.2 = (bf16[2,2,2,2,64,384]{5,4,3,2,1,0:T(8,128)(2,1)S(1)}, bf16[2,2,2,2,64,384]{5,4,3,2,1,0:T(8,128)(2,1)}, u32[]{:S(2)}) copy-start(bf16[2,2,2,2,64,384]{5,4,3,2,1,0:T(8,128)(2,1)} %copy.41) | copy-start | bytes 2359300
  281.4 21.3 %copy-start.3 = (f32[768,1024]{1,0:T(8,128)S(1)}, f32[768,1024]{1,0:T(8,128)}, u32[]{:S(2)}) copy-start(f32[768,1024]{1,0:T(8,128)} %fusion.9) | copy-start | bytes 9437188
  281.4 21.3 %copy-start.11 = (bf16[1536,256]{1,0:T(8,128)(2,1)S(1)}, bf16[1536,256]{1,0:T(8,128)(2,1)}, u32[]{:S(2)}) copy-start(bf16[1536,256]{1,0:T(8,128)(2,1)} %get-tuple-element.99) | copy-start | bytes 2359300
  281.9 13.7 %collective-permute-start.17 = (bf16[2,2,64,1024]{3,2,0,1:T(8,128)(2,1)S(1)}, bf16[2,2,64,1024]{3,2,0,1:T(8,128)(2,1)S(1)}, u32[]{:S(2)}, u32[]{:S(2)}) collective-permute-start(bf16[2,2,64,1024]{3,2,0,1:T(8,128)(2,1)S(1)} %dynamic-slice_bitcast_fusion), channel_id=1, source_target_pairs={{0,4},{2,6},{4,0},{6,2},{8,12},{10,14},{12,8},{14,10},{16,20},{18,... | collective-permute-start | bytes 1572872 | tf_op jit(solution)/shard_map/ppermute | solution.py:722
  283.1 11.9 %collective-permute-start.23 = (bf16[64,384]{1,0:T(8,128)(2,1)S(1)}, bf16[64,384]{1,0:T(8,128)(2,1)S(1)}, u32[]{:S(2)}, u32[]{:S(2)}) collective-permute-start(bf16[64,384]{1,0:T(8,128)(2,1)S(1)} %dynamic-slice_bitcast_fusion.5), channel_id=1, source_target_pairs={{0,4},{2,6},{4,0},{6,2},{8,12},{10,14},{12,8},{14,10},{16,20},{18,... | collective-permute-start | bytes 147464 | tf_op jit(solution)/shard_map/ppermute | solution.py:722
  295.9 8.2 %collective-permute-start.18 = (bf16[2,64,1024]{2,1,0:T(8,128)(2,1)S(1)}, bf16[2,64,1024]{2,1,0:T(8,128)(2,1)S(1)}, u32[]{:S(2)}, u32[]{:S(2)}) collective-permute-start(bf16[2,64,1024]{2,1,0:T(8,128)(2,1)S(1)} %dynamic-slice_bitcast_fusion.1), channel_id=1, source_target_pairs={{0,8},{2,10},{4,12},{6,14},{8,0},{10,2},{12,4},{14,6},{16,24},{18,... | collective-permute-start | bytes 786440 | tf_op jit(solution)/shard_map/ppermute | solution.py:722
  304.2 8.5 %collective-permute-start.19 = (bf16[64,1024]{1,0:T(8,128)(2,1)S(1)}, bf16[64,1024]{1,0:T(8,128)(2,1)S(1)}, u32[]{:S(2)}, u32[]{:S(2)}) collective-permute-start(bf16[64,1024]{1,0:T(8,128)(2,1)S(1)} %dynamic-slice_bitcast_fusion.3), channel_id=1, source_target_pairs={{0,16},{2,18},{4,20},{6,22},{8,24},{10,26},{12,28},{14,30},{16,0},... | collective-permute-start | bytes 393224 | tf_op jit(solution)/shard_map/ppermute | solution.py:722
  315.5 5.2 %collective-permute-start.24 = (f32[64,384]{1,0:T(8,128)}, f32[64,384]{1,0:T(8,128)S(1)}, u32[]{:S(2)}, u32[]{:S(2)}) collective-permute-start(f32[64,384]{1,0:T(8,128)} %get-tuple-element.102.own_ref), channel_id=1, source_target_pairs={{0,1},{1,0},{2,3},{3,2},{4,5},{5,4},{6,7},{7,6},{8,9},{9,8},{10,11... | collective-permute-start | bytes 294920 | tf_op jit(solution)/shard_map/ppermute | solution.py:794
  320.7 0.6 copy-start.23
Sparse Core Ops, SparseCore 0:
  32.2 53.7 all-gather.1
  164.1 72.1 reduce-scatter.1

commit v4 on v3

--- a/solution.py
+++ b/solution.py
@@ -89,11 +89,11 @@
 
 
 def pack_kernel(
-    state_ref, step_ref, norm_ref, conv_ref, bias_ref, gate_ref, taps_ref, taps_bias_ref,
-    out_ref, turned, lanes,
+    inner_ref, state_ref, step_ref, norm_ref, conv_ref, bias_ref, gate_ref, taps_ref,
+    taps_bias_ref, out_ref, turned, lanes,
 ):
     shard, heads = step_ref.shape
-    states = state_ref.shape[1]
+    inner, states = inner_ref.shape[1], state_ref.shape[1]
     state_shard = taps_ref.shape[1]
     base = 3 * heads
     turned[...] = jnp.zeros_like(turned)
@@ -107,8 +107,9 @@
     step = step_ref[...].astype(F32)
     for copy in range(3):
         lanes[:, copy * heads : (copy + 1) * heads] = step
-    out_ref[:, :states] = state_ref[...]
-    out_ref[:, states:] = (turned[...].T[0:shard, :] + lanes[...]).astype(BF16)
+    out_ref[:, :inner] = inner_ref[...]
+    out_ref[:, inner : inner + states] = state_ref[...]
+    out_ref[:, inner + states :] = (turned[...].T[0:shard, :] + lanes[...]).astype(BF16)
 
 
 def lower_matrix(upper=False):
@@ -191,10 +192,10 @@
 
 
 def forward_kernel(
-    rank_ref, len_ref, own_ref, other_ref, w_ref, rest_ref, head_ref,
+    rank_ref, len_ref, own_ref, other_ref, w_ref, head_ref,
     normed_ref, normed_t_ref, ipre_ref, spre_ref, sact_ref, stepin_ref, mixed_ref, sprev_ref,
     rows_ref, taps_ref,
-    ext, state, spread, lower, fac, read, mask, scores, weighted, *, shard, state_shard,
+    ext, state, spread, lower, fac, read, mask, scores, weighted, factors, *, shard, state_shard,
 ):
     inner = rows_ref.shape[1]
     channels = ext.shape[1]
@@ -210,7 +211,8 @@
         state[...] = jnp.zeros_like(state)
         spread[...] = spread_matrix(heads, LANES // PAIR_HEADS)
         lower[...] = lower_matrix()
-        packed = rest_ref[:, 2 * size :].astype(F32).T
+        factors[...] = jnp.zeros_like(factors)
+        packed = w_ref[:, channels:].astype(F32).T
         base = 3 * heads
         rows_ref[0:7, :] = packed[base : base + 7, :]
         once = lax.broadcasted_iota(jnp.int32, (16, LANES), 1) < heads
@@ -218,7 +220,7 @@
         rows_ref[7:8, :] = nn(skip_row, spread[...])[0:1, :]
         taps_ref[...] = nn(
             packed[base + 8 : base + 16, :].astype(BF16),
-            spaced_matrix(2 * size, rest_ref.shape[0], state_shard, shard, True),
+            spaced_matrix(2 * size, w_ref.shape[0], state_shard, shard, True),
         )
 
     mine = rank_ref[0, 0] == group // (pl.num_programs(0) // 2)
@@ -230,10 +232,10 @@
         normed_ref[sl, :] = (hidden * inv * gain).astype(BF16)
 
     normed_t_ref[...] = normed_ref[...].T
-    pre = nn(normed_ref[...], w_ref[...])
+    pre = nn(normed_ref[...], w_ref[:, :inner])
     ext[8 : 8 + GROUP, 0:inner] = pre
     ipre_ref[...] = pre
-    rest = nn(normed_ref[...], rest_ref[...])
+    rest = nn(normed_ref[...], w_ref[:, inner:])
     ext[8 : 8 + GROUP, inner:channels] = rest[:, : 2 * size]
     spre_ref[...] = rest[:, : 2 * size]
     lane = lax.broadcasted_iota(jnp.int32, (1, LANES), 1)
@@ -274,37 +276,30 @@
     sprev_ref[...] = held
     read[...] = nn(queries, held)
 
-    masks = head_masks()
+    first_head = lax.broadcasted_iota(jnp.int32, (1, LANES), 1) < LANES // PAIR_HEADS
+    lo, hi = slice(0, HALF), slice(HALF, GROUP)
     for pair in range(inner // LANES):
         sl = slice(pair * LANES, (pair + 1) * LANES)
         total = conv(sl, rows_ref[ROW_TAP : ROW_TAP + 4, sl], rows_ref[ROW_BIAS : ROW_BIAS + 1, sl])
         values = (total * sigmoid(total)).astype(BF16).astype(F32)
-        stepped = values * fac[0:GROUP, sl]
+        stepped = (values * fac[0:GROUP, sl]).astype(BF16)
         weighted[:, sl] = (values * fac[GROUP : 2 * GROUP, sl]).astype(BF16)
-        top, bottom, low_values, high_values = [], [], [], []
+        slot = pair % 2
         for which in range(PAIR_HEADS):
             head = pair * PAIR_HEADS + which
             column = cum[:, head : head + 1]
             row = cum_rows[head : head + 1, :]
-
-            def factor(rs, cs):
+            for rs, cs in ((lo, lo), (hi, lo), (hi, hi)):
                 gap = column[rs] - row[:, cs] + mask[rs, cs]
-                return (jnp.exp2(gap) * scores[rs, cs]).astype(BF16)
-
-            lo, hi = slice(0, HALF), slice(HALF, GROUP)
-            top.append(factor(lo, lo))
-            bottom.append(factor(hi, lo))
-            bottom.append(factor(hi, hi))
-            masked = (stepped * masks[which]).astype(BF16)
-            low_values.append(masked[:HALF])
-            high_values.append(masked)
-        upper_part = nn(jnp.concatenate(top, axis=1), jnp.concatenate(low_values, axis=0))
-        lower_part = nn(jnp.concatenate(bottom, axis=1), jnp.concatenate(high_values, axis=0))
-        rest = fac[2 * GROUP : 3 * GROUP, sl] * read[:, sl] + (
-            rows_ref[ROW_SKIP : ROW_SKIP + 1, sl] * values
+                place = slice(which * GROUP + rs.start, which * GROUP + rs.stop)
+                factors[slot, place, cs] = (jnp.exp2(gap) * scores[rs, cs]).astype(BF16)
+        both = nn(factors[slot], stepped)
+        within = jnp.where(first_head, both[:GROUP], both[GROUP:])
+        mixed_ref[:, sl] = (
+            within
+            + fac[2 * GROUP : 3 * GROUP, sl] * read[:, sl]
+            + rows_ref[ROW_SKIP : ROW_SKIP + 1, sl] * values
         )
-        mixed_ref[0:HALF, sl] = upper_part + rest[:HALF]
-        mixed_ref[HALF:GROUP, sl] = lower_part + rest[HALF:]
 
     state[...] = fac[3 * GROUP : 3 * GROUP + 1, :] * state[...] + tn(keys, weighted[...])
     ext[0:8, :] = ext[GROUP : GROUP + 8, :]
@@ -374,16 +369,15 @@
     gain_ref[0:1, :] += total
 
 
-def early_grad_kernel(live_t_ref, low_ref, normed_t_ref, ggp_ref, out_ref):
-    half = pl.num_programs(0) // 2
-
-    @pl.when(pl.program_id(0) < half)
-    def _():
-        out_ref[...] = nn(live_t_ref[...], low_ref[...]).astype(BF16)
-
-    @pl.when(pl.program_id(0) >= half)
-    def _():
-        out_ref[...] = nn(normed_t_ref[...], ggp_ref[...]).astype(BF16)
+def product_kernel(left_ref, right_ref, out_ref):
+    out_ref[...] = nn(left_ref[...], right_ref[...]).astype(out_ref.dtype)
+
+
+def normed_grad_kernel(
+    begin_ref, gate_ref, inner_ref, step_ref, w_gate_ref, w_inner_ref, w_step_ref, out_ref
+):
+    total = nt(gate_ref[...], w_gate_ref[...]) + nt(inner_ref[...], w_inner_ref[...])
+    out_ref[...] = (total + nt(step_ref[...], w_step_ref[...])).astype(out_ref.dtype)
 
 
 def backward_kernel(
@@ -391,7 +385,7 @@
     rows_ref, head_ref,
     gip_ref, gkq_ref, gstep_ref, conv_ref, heads_ref,
     ext, cext, gstate, spread, collect, lower, upper, fac, reads, mask, scores, gscores,
-    weighted, entered, sums,
+    weighted, entered, sums, factors,
 ):
     inner = rows_ref.shape[1]
     heads = inner // (LANES // PAIR_HEADS)
@@ -409,6 +403,7 @@
         collect[...] = collect_matrix(heads, LANES // PAIR_HEADS)
         lower[...] = lower_matrix()
         upper[...] = lower_matrix(upper=True)
+        factors[...] = jnp.zeros_like(factors)
         conv_ref[...] = jnp.zeros_like(conv_ref)
         heads_ref[...] = jnp.zeros_like(heads_ref)
 
@@ -438,6 +433,7 @@
     reads[...] = nn(keys, held)
 
     masks = head_masks()
+    first_head = lax.broadcasted_iota(jnp.int32, (1, LANES), 1) < LANES // PAIR_HEADS
     lo, hi = slice(0, HALF), slice(HALF, GROUP)
     for pair in range(inner // LANES):
         sl = slice(pair * LANES, (pair + 1) * LANES)
@@ -458,42 +454,25 @@
         upstream_wide = upstream.astype(F32)
         entered[:, sl] = (upstream_wide * fac[2 * GROUP : 3 * GROUP, sl]).astype(BF16)
 
-        top, bottom, top_grads, low_grads = [], [], [], []
-        g00 = g01 = g11 = None
-        split_up = [(upstream_wide * one).astype(BF16) for one in masks]
-        grads_low = nt(stepped[HALF:], jnp.concatenate([one[HALF:] for one in split_up], axis=0))
+        slot = pair % 2
+        split = [(values * step_wide * one).astype(BF16) for one in masks]
+        grads = nn(jnp.concatenate(split, axis=0), upstream.T)
+        blocks = [None, None, None]
         for which in range(PAIR_HEADS):
             head = pair * PAIR_HEADS + which
             column = cum[:, head : head + 1]
             row = cum_rows[head : head + 1, :]
-            masked = split_up[which]
-            grads_top = nt(stepped[:HALF], masked)
-
-            def factors(rs, cs, grads):
-                gap = row[:, cs] - column[rs] + mask[rs, cs]
-                factor = jnp.exp2(gap)
-                return (factor * scores[rs, cs]).astype(BF16), factor * grads
-
-            a00, d00 = factors(lo, lo, grads_top[:, lo])
-            a01, d01 = factors(lo, hi, grads_top[:, hi])
-            a11, d11 = factors(hi, hi, grads_low[:, which * HALF : (which + 1) * HALF])
-            g00 = d00 if g00 is None else g00 + d00
-            g01 = d01 if g01 is None else g01 + d01
-            g11 = d11 if g11 is None else g11 + d11
-            top.extend([a00, a01])
-            bottom.append(a11)
-            top_grads.append(masked)
-            low_grads.append(masked[HALF:])
-        gscores[lo, lo] += g00
-        gscores[lo, hi] += g01
-        gscores[hi, hi] += g11
-        raw = jnp.concatenate(
-            [
-                nn(jnp.concatenate(top, axis=1), jnp.concatenate(top_grads, axis=0)),
-                nn(jnp.concatenate(bottom, axis=1), jnp.concatenate(low_grads, axis=0)),
-            ],
-            axis=0,
-        )
+            for index, (rs, cs) in enumerate(((lo, lo), (lo, hi), (hi, hi))):
+                factor = jnp.exp2(row[:, cs] - column[rs] + mask[rs, cs])
+                place = slice(which * GROUP + rs.start, which * GROUP + rs.stop)
+                factors[slot, place, cs] = (factor * scores[rs, cs]).astype(BF16)
+                part = factor * grads[place, cs]
+                blocks[index] = part if blocks[index] is None else blocks[index] + part
+        gscores[lo, lo] += blocks[0]
+        gscores[lo, hi] += blocks[1]
+        gscores[hi, hi] += blocks[2]
+        both = nn(factors[slot], upstream)
+        raw = jnp.where(first_head, both[:GROUP], both[GROUP:])
         skip = rows_ref[ROW_SKIP : ROW_SKIP + 1, sl]
         across = reads[:, sl]
 
@@ -722,12 +701,16 @@
     return lax.ppermute(value, "dp", [(i, i ^ (1 << bit)) for i in range(count)])
 
 
-def gather_by_bits(value, rank, count, spread_first, before_second=None):
+def after(value, *others):
+    return lax.optimization_barrier((value, *others))[0]
+
+
+def gather_by_bits(value, rank, count, spread_first, waits):
     held, begun = [], []
     rows, lanes = value.shape
     for bit in reversed(bit_order(count, spread_first)):
-        if len(begun) == 1 and before_second is not None:
-            value = lax.optimization_barrier((value, before_second))[0]
+        if 0 < len(begun) <= len(waits):
+            value = after(value, waits[len(begun) - 1])
         begun.append(value)
         other = flip(value, bit, count)
         held = sorted(held + [bit], reverse=True)
@@ -738,20 +721,30 @@
     return value.reshape(count * rows, lanes), begun
 
 
-def scatter_by_bits(value, rank, count, spread_first):
-    left = list(reversed(range(count.bit_length() - 1)))
-    rows, lanes = value.shape[0] // count, value.shape[1]
-    value = value.reshape([2] * len(left) + [rows, lanes])
-    for bit in bit_order(count, spread_first):
-        axis = left.index(bit)
-        mine = (rank >> bit) & 1
-        away = lax.dynamic_index_in_dim(value, 1 - mine, axis, keepdims=False)
-        here = lax.dynamic_index_in_dim(value, mine, axis, keepdims=False)
-        left.remove(bit)
-        value = here.astype(F32) + flip(away, bit, count).astype(F32)
-        if left:
-            value = value.astype(BF16)
-    return value
+class HalvingSum:
+    def __init__(self, value, rank, count, spread_first):
+        self.rank, self.count = rank, count
+        self.left = list(reversed(range(count.bit_length() - 1)))
+        self.order = bit_order(count, spread_first)
+        rows = value.shape[0] // count
+        self.value = value.reshape([2] * len(self.left) + [rows, value.shape[1]])
+
+    def start(self):
+        bit = self.order.pop(0)
+        axis = self.left.index(bit)
+        mine = (self.rank >> bit) & 1
+        self.away = lax.dynamic_index_in_dim(self.value, 1 - mine, axis, keepdims=False)
+        self.here = lax.dynamic_index_in_dim(self.value, mine, axis, keepdims=False)
+        self.came = flip(self.away, bit, self.count)
+        self.bit = bit
+
+    def step(self, *others):
+        came = after(self.came, *others) if others else self.came
+        self.left.remove(self.bit)
+        self.value = self.here.astype(F32) + came.astype(F32)
+        if self.left:
+            self.value = self.value.astype(BF16)
+            self.start()
 
 
 def on_device(
@@ -794,41 +787,34 @@
         return lax.ppermute(value, "tensor", swap)
 
     pieces = []
-    for part in range(half_groups):
-        piece = hidden_in[part * GROUP : (part + 1) * GROUP]
-        if pieces:
-            piece = lax.optimization_barrier((piece, pieces[-1]))[0]
-        pieces.append(exchange(piece))
+    cuts = [0, GROUP // 4] + [GROUP * count for count in range(1, half_groups + 1)]
+    for begin, end in zip(cuts, cuts[1:]):
+        piece = hidden_in[begin:end]
+        pieces.append(exchange(after(piece, pieces[-1]) if pieces else piece))
     hidden_other = jnp.concatenate(pieces, axis=0)
-    cotangent_other = exchange(lax.optimization_barrier((cotangent, hidden_other))[0])
+    cotangent_other = exchange(after(cotangent, pieces[-1]))
 
     state_shard = conv_state.shape[1]
-    rest_shard = pl.pallas_call(
+    first_shard = pl.pallas_call(
         pack_kernel,
-        in_specs=[pl.BlockSpec(memory_space=pltpu.VMEM)] * 8,
+        in_specs=[pl.BlockSpec(memory_space=pltpu.VMEM)] * 9,
         out_specs=pl.BlockSpec(memory_space=pltpu.VMEM),
-        out_shape=shape_of((shard, 2 * size + LANES), BF16),
+        out_shape=shape_of((shard, channels + LANES), BF16),
         scratch_shapes=[
             pltpu.VMEM((LANES, max(LANES, shard)), F32),
             pltpu.VMEM((shard, LANES), F32),
         ],
         compiler_params=params(),
-        cost_estimate=cost(2),
+        cost_estimate=cost(0),
         name="pack_small",
     )(
-        proj_state, proj_step, norm_gain[None, :], conv_inner.reshape(taps, shard),
+        projection_gate_inner[:, 1], proj_state, proj_step, norm_gain[None, :], conv_inner.reshape(taps, shard),
         conv_inner_bias, gate_gain, conv_state, conv_state_bias[None, :],
     )
-    w_inner, begun = gather_by_bits(
-        projection_gate_inner[:, 1], shard_rank, shard_count, False, pieces[0]
-    )
-    w_rest, _ = gather_by_bits(rest_shard, shard_rank, shard_count, True)
+    w_first, begun = gather_by_bits(first_shard, shard_rank, shard_count, False, pieces)
     second_shard = jnp.concatenate([projection_gate_inner[:, 0], proj_out.T], axis=1)
-    second_shard = lax.optimization_barrier((second_shard, begun[min(2, len(begun) - 1)]))[0]
+    second_shard = after(second_shard, begun[min(2, len(begun) - 1)])
     w_second = lax.all_gather(second_shard, "dp", axis=0, tiled=True)
-    w_state = w_rest[:, : 2 * size]
-    w_step = w_rest[:, 2 * size :]
-    w_gate = w_second[:, :inner]
     w_out = w_second[:, inner:]
 
     rate = -jnp.exp(decay_log.astype(F32))
@@ -848,7 +834,7 @@
         grid=(groups,),
         in_specs=[
             SMEM_SPEC, SMEM_SPEC, half_block, half_block,
-            whole(width, inner), whole(width, 2 * size + LANES), whole(8, LANES),
+            whole(width, channels + LANES), whole(8, LANES),
         ],
         out_specs=[
             by_group(width), pl.BlockSpec((width, GROUP), lambda i: (0, i)), by_group(inner), by_group(2 * size), by_group(2 * size),
@@ -877,11 +863,12 @@
             pltpu.VMEM((GROUP, GROUP), F32),
             pltpu.VMEM((GROUP, GROUP), F32),
             pltpu.VMEM((GROUP, inner), BF16),
+            pltpu.VMEM((2, PAIR_HEADS * GROUP, GROUP), BF16),
         ],
         compiler_params=params(),
         cost_estimate=cost(2),
         name="mixer_forward",
-    )(rank, lengths, hidden_in, hidden_other, w_inner, w_rest, head_rows)
+    )(rank, lengths, hidden_in, hidden_other, w_first, head_rows)
 
     gate_pre, grad_out_low, live_t, sums = pl.pallas_call(
         gate_kernel,
@@ -928,32 +915,16 @@
         name="gate_backward",
     )(sums, sums_other, gate_pre, grad_out_low, mixed, rows)
 
-    tiles = 2 * inner // GROUP
-    half_tiles = tiles // 2
-    first_grads = pl.pallas_call(
-        early_grad_kernel,
-        grid=(tiles,),
-        in_specs=[
-            whole(width, tokens),
-            pl.BlockSpec((tokens, GROUP), lambda i: (0, jnp.minimum(i, half_tiles - 1))),
-            whole(width, tokens),
-            pl.BlockSpec((tokens, GROUP), lambda i: (0, jnp.maximum(i - half_tiles, 0))),
-        ],
-        out_specs=pl.BlockSpec((width, GROUP), lambda i: (0, i)),
-        out_shape=shape_of((width, 2 * inner), BF16),
-        compiler_params=params(),
-        cost_estimate=cost(13),
-        name="early_weight_grads",
-    )(live_t, out_low, normed_t, grad_gate_low)
-
+    first_grads = jnp.concatenate(
+        [nn(live_t, out_low).astype(BF16), nn(normed_t, grad_gate_low).astype(BF16)], axis=1
+    )
     def rows_of(value, which):
         return lax.dynamic_slice_in_dim(value, which * half_rows, half_rows)
 
+    first_sum = lax.psum_scatter(first_grads, "dp", scatter_dimension=0, tiled=True)
+    out_low = after(out_low, first_grads)
     mix_away = nt(rows_of(out_low, 1 - tensor_rank), w_out).astype(BF16)
-    grad_first, first_grads, mix_away = lax.optimization_barrier(
-        (grad_first, first_grads, mix_away)
-    )
-    first_sum = lax.psum_scatter(first_grads, "dp", scatter_dimension=0, tiled=True)
+    grad_first = after(grad_first, mix_away)
     mix_other = exchange(mix_away)
     mix_here = nt(rows_of(out_low, tensor_rank), w_out)
     last = groups - 1
@@ -1002,6 +973,7 @@
             pltpu.VMEM((GROUP, inner), BF16),
             pltpu.VMEM((GROUP, inner), BF16),
             pltpu.VMEM((4 * GROUP, inner), BF16),
+            pltpu.VMEM((2, PAIR_HEADS * GROUP, GROUP), BF16),
         ],
         compiler_params=params(),
         cost_estimate=cost(2),
@@ -1015,30 +987,62 @@
     kq_own = lax.dynamic_slice_in_dim(grad_kq, tensor_rank * (half_rows - HALO), window)
     kq_away = lax.dynamic_slice_in_dim(grad_kq, (1 - tensor_rank) * (half_rows - HALO), window)
     kq_other = exchange(kq_away)
-    grad_inner_low, kq_other, mix_other, first_sum = lax.optimization_barrier(
-        (grad_inner_low, kq_other, mix_other, first_sum)
-    )
+
+    grad_inner_low = after(grad_inner_low, mix_other)
+    inner_grads = pl.pallas_call(
+        product_kernel,
+        grid=(inner // GROUP,),
+        in_specs=[whole(width, tokens), pl.BlockSpec((tokens, GROUP), lambda i: (0, i))],
+        out_specs=pl.BlockSpec((width, GROUP), lambda i: (0, i)),
+        out_shape=shape_of((width, inner), BF16),
+        compiler_params=params(),
+        cost_estimate=cost(0),
+        name="inner_weight_grads",
+    )(normed_t, grad_inner_low)
+    inner_sum = HalvingSum(inner_grads, shard_rank, shard_count, False)
+    inner_sum.start()
+
+    def normed_part(which, gip, dtype):
+        def block(i, begin):
+            return (begin[0] + i, 0)
+
+        return pl.pallas_call(
+            normed_grad_kernel,
+            grid_spec=pltpu.PrefetchScalarGridSpec(
+                num_scalar_prefetch=1,
+                grid=(half_groups,),
+                in_specs=[
+                    pl.BlockSpec((GROUP, inner), block),
+                    pl.BlockSpec((GROUP, inner), block),
+                    pl.BlockSpec((GROUP, LANES), block),
+                    pl.BlockSpec((width, inner), lambda i, begin: (0, 0)),
+                    pl.BlockSpec((width, inner), lambda i, begin: (0, 0)),
+                    pl.BlockSpec((width, LANES), lambda i, begin: (0, channels // LANES)),
+                ],
+                out_specs=pl.BlockSpec((GROUP, width), lambda i, begin: (i, 0)),
+            ),
+            out_shape=shape_of((half_rows, width), dtype),
+            compiler_params=params(),
+            cost_estimate=cost(0),
+            name="normed_grads",
+        )(
+            (which * half_groups).astype(jnp.int32).reshape(1),
+            grad_gate_low, gip, grad_step_low, w_second, w_first, w_first,
+        )
+
+    grad_inner_low, first_sum, _ = lax.optimization_barrier(
+        (grad_inner_low, first_sum, inner_sum.away)
+    )
+    normed_away = normed_part(1 - tensor_rank, grad_inner_low, BF16)
+    normed_other = exchange(normed_away)
     mix = mix_here + mix_other.astype(F32)
     slot = tensor_rank * half_rows + jnp.arange(half_rows, dtype=jnp.int32)
     valid_half = slot < jnp.sum(lengths[0])
     hidden_wide = hidden_in.astype(F32)
     block_out = (hidden_wide + jnp.where(valid_half[:, None], mix, 0.0)).astype(BF16)
 
-
-    def partial_normed(which):
-        return (
-            nt(rows_of(grad_gate_low, which), w_gate)
-            + nt(rows_of(grad_inner_low, which), w_inner)
-            + nt(rows_of(grad_step_low, which), w_step)
-        )
-
-    normed_away = exchange(partial_normed(1 - tensor_rank).astype(BF16))
-    normed_here = partial_normed(tensor_rank)
-    inner_sum = scatter_by_bits(
-        nn(normed_t, grad_inner_low).astype(BF16), shard_rank, shard_count, False
-    )
-
     vmem = pl.BlockSpec(memory_space=pltpu.VMEM)
+    kq_other = after(kq_other, normed_away)
     grad_state_low, rest_grads = pl.pallas_call(
         functools.partial(
             state_grad_kernel, shard=shard, state_shard=state_shard, heads=heads
@@ -1053,16 +1057,30 @@
             pltpu.VMEM((LANES, width), F32),
         ],
         compiler_params=params(),
-        cost_estimate=cost(8),
+        cost_estimate=cost(0),
         name="state_backward",
     )(
         rank, lengths, kq_own, kq_other, state_pre, state_rows, normed_t, grad_step_low,
         conv_rows, gain_rows, head_sums,
     )
-    rest_sum = scatter_by_bits(rest_grads, shard_rank, shard_count, True)
-
-    grad_normed = normed_here + normed_away.astype(F32)
-    grad_normed = grad_normed + nt(rows_of(grad_state_low, tensor_rank), w_state)
+    rest_sum = HalvingSum(rest_grads, shard_rank, shard_count, True)
+    rest_sum.start()
+    inner_sum.step()
+    normed_here = normed_part(
+        tensor_rank, after(grad_inner_low, rest_sum.away, inner_sum.away), F32
+    )
+    rest_sum.step(inner_sum.away, normed_here)
+    while inner_sum.left or rest_sum.left:
+        if inner_sum.left:
+            inner_sum.step()
+        if rest_sum.left:
+            rest_sum.step(inner_sum.away, normed_other)
+    inner_sum, rest_sum = inner_sum.value, rest_sum.value
+
+    grad_normed = normed_here + normed_other.astype(F32)
+    grad_normed = grad_normed + nt(
+        rows_of(grad_state_low, tensor_rank), w_first[:, inner:channels]
+    )
     gain = rows[ROW_NORM][None, :]
     inv_rms = lax.rsqrt(jnp.mean(hidden_wide * hidden_wide, axis=1, keepdims=True) + NORM_EPS)
     scaled_in = grad_normed * gain

time: 335 us -> 325 us (0.970)
  matrix products: 37.4 us -> 21.5 us
  Pallas kernels: 132 us -> 144 us
  waiting for transfers between devices: 82.9 us -> 78.5 us
  starting transfers between devices: 31.6 us -> 28 us
    dot_general x9 -> x3, matrix products: 29.7 us -> 12.2 us  [nt(): lax.dot_general(left, right, (((1,), (1,)), ((), ())), preferred_element_...]
    ppermute x16 -> x12, waiting for transfers between devices: 45.9 us -> 59.6 us  [flip(): return lax.ppermute(value, 'dp', [(i, i ^ 1 << bit) for i in range(count)])]
    pallas_call x1 -> x3, Pallas kernels: 13.3 us -> 24.3 us  [the longest x2 16.4 us: normed_part(): pl.pallas_call(normed_grad_kernel, grid_spec=pltpu.PrefetchScalarGridSpec...]
    reduce_scatter x1, waiting for transfers between devices: 10.3 us -> 0.02 us  [on_device(): lax.psum_scatter(first_grads, 'dp', scatter_dimension=0, tiled=True)]
    ppermute x9 -> x10, waiting for transfers between devices: 26.7 us -> 18.9 us  [exchange(): return lax.ppermute(value, 'tensor', swap)]
    concatenate x0 -> x2, other arithmetic: none -> 4.82 us  [the longest x1 2.44 us: on_device(): hidden_other = jnp.concatenate(pieces, axis=0)]
    ppermute x16 -> x12, starting transfers between devices: 18.5 us -> 14.3 us  [flip(): return lax.ppermute(value, 'dp', [(i, i ^ 1 << bit) for i in range(count)])]
    unnamed x65 -> x45, local copies, waits for them, and re-layouts: 8.97 us -> 7.08 us
  transfers between devices with their start and end apart: 27 -> 24, of which waited for: 16 -> 13; matrix products, arithmetic and copies ran while one was open for 13% -> 11% of each run, Pallas kernels for 23% -> 34%
where the time goes in v4:
time: 325 us; the launch traced here: 321 us
  Pallas kernels  144 us (44%)
  waiting for transfers between devices  78.5 us (24%)
  starting transfers between devices  28 us (9%)
  matrix products  21.5 us (7%)
  local copies, waits for them, and re-layouts  17.7 us (5%)
  other arithmetic  16.8 us (5%)
  between operations  15 us (5%)
    ppermute x12, waiting for transfers between devices, flip(): return lax.ppermute(value, 'dp', [(i, i ^ 1 << bit) for i in range(count)])  59.6 us
    pallas_call x1, Pallas kernels, on_device(): pl.pallas_call(backward_kernel, grid=(groups,), in_specs=[SMEM_SPEC, pl.B...  46.6 us
    pallas_call x1, Pallas kernels, on_device(): pl.pallas_call(functools.partial(forward_kernel, shard=shard, state_shard...  28.8 us
    ppermute x10, waiting for transfers between devices, exchange(): return lax.ppermute(value, 'tensor', swap)  18.9 us
    pallas_call x1, Pallas kernels, on_device(): pl.pallas_call(gate_kernel, grid=(groups,), in_specs=[SMEM_SPEC, SMEM_SPE...  16.5 us
    pallas_call x2, Pallas kernels, normed_part(): pl.pallas_call(normed_grad_kernel, grid_spec=pltpu.PrefetchScalarGridSpec...  16.4 us
    ppermute x12, starting transfers between devices, flip(): return lax.ppermute(value, 'dp', [(i, i ^ 1 << bit) for i in range(count)])  14.3 us
    ppermute x10, starting transfers between devices, exchange(): return lax.ppermute(value, 'tensor', swap)  13.6 us
  transfers between devices with their start and end apart: 24, of which 13 were waited for; matrix products, arithmetic and copies ran while one was open for 11% of the time, Pallas kernels for 34%

profile of v4, /device:TPU:0, one launch (start us, length us, event | category | flops | bytes accessed | tf_op | source)
XLA Modules:
  0.0 321.1 jit_solution(3815863885901184554)
XLA Ops:
  7.2 1.6 fusion.34
  8.8 0.7 copy.73
  9.5 1.4 copy.41.step_ref
  10.9 1.8 pack_small.1
  12.7 4.0 %collective-permute-start.5 = (bf16[64,1408]{1,0:T(8,128)(2,1)}, bf16[64,1408]{1,0:T(8,128)(2,1)S(1)}, u32[]{:S(2)}, u32[]{:S(2)}) collective-permute-start(bf16[64,1408]{1,0:T(8,128)(2,1)} %pack_small.1), channel_id=1, source_target_pairs={{0,16},{2,18},{4,20},{6,22},{8,24},{10,26},{12,28},{14,30},{16,0},... | collective-permute-start | bytes 540680 | tf_op jit(solution)/shard_map/ppermute | solution.py:701
  16.7 0.9 slice.36
  17.6 1.6 collective-permute-start
  19.2 6.1 %collective-permute-done.5 = bf16[64,1408]{1,0:T(8,128)(2,1)S(1)} collective-permute-done((bf16[64,1408]{1,0:T(8,128)(2,1)}, bf16[64,1408]{1,0:T(8,128)(2,1)S(1)}, u32[]{:S(2)}, u32[]{:S(2)}) %collective-permute-start.5) | collective-permute-done | bytes 180256 | tf_op jit(solution)/shard_map/ppermute | solution.py:701
  25.3 1.0 select_bitcast_fusion.7
  27.0 0.8 collective-permute-start.6
  27.9 0.7 pad_maximum_fusion.6
  28.7 1.5 collective-permute-start.1
  30.2 6.4 %collective-permute-done.6 = bf16[2,64,1408]{2,1,0:T(8,128)(2,1)S(1)} collective-permute-done((bf16[2,64,1408]{2,1,0:T(8,128)(2,1)S(1)}, bf16[2,64,1408]{2,1,0:T(8,128)(2,1)S(1)}, u32[]{:S(2)}, u32[]{:S(2)}) %collective-permute-start.6) | collective-permute-done | bytes 360480 | tf_op jit(solution)/shard_map/ppermute | solution.py:701
  36.8 2.8 collective-permute-done.1
  39.6 1.6 collective-permute-start.7
  41.3 1.6 collective-permute-start.2
  42.9 16.5 %collective-permute-done.7 = bf16[2,2,64,1408]{3,2,0,1:T(8,128)(2,1)S(1)} collective-permute-done((bf16[2,2,64,1408]{3,2,0,1:T(8,128)(2,1)S(1)}, bf16[2,2,64,1408]{3,2,0,1:T(8,128)(2,1)S(1)}, u32[]{:S(2)}, u32[]{:S(2)}) %collective-permute-start.7) | collective-permute-done | bytes 720928 | tf_op jit(solution)/shard_map/ppermute | solution.py:701
  59.8 1.6 collective-permute-start.3
  61.3 12.8 %collective-permute-done.3 = bf16[256,1024]{1,0:T(8,128)(2,1)} collective-permute-done((bf16[256,1024]{1,0:T(8,128)(2,1)S(1)}, bf16[256,1024]{1,0:T(8,128)(2,1)}, u32[]{:S(2)}, u32[]{:S(2)}) %collective-permute-start.3) | collective-permute-done | bytes 524320 | tf_op jit(solution)/shard_map/ppermute | solution.py:787
  74.2 1.5 collective-permute-start.4
  76.4 2.4 pad_maximum_fusion.2.other_ref
  79.4 1.8 copy.42
  81.2 28.8 %mixer_forward.1 = (bf16[1536,1024]{1,0:T(8,128)(2,1)}, bf16[1024,1536]{1,0:T(8,128)(2,1)}, f32[1536,1024]{1,0:T(8,128)}, f32[1536,256]{1,0:T(8,128)}, bf16[1536...) custom-call(s32[1,1]{1,0:T(1,128)} %bitcast.rank_ref, ...), custom_call_target="tpu_custom_call" | custom-call | flops 2200000000 | tf_op jit(solution)/shard_map/mixer_forward/pallas_call | solution.py:832
  110.5 16.5 %gate_forward.1 = (f32[1536,1024]{1,0:T(8,128)}, f32[1536,1024]{1,0:T(8,128)}, bf16[1024,1536]{1,0:T(8,128)(2,1)}, f32[8,1536]{1,0:T(8,128)}) custom-call(s32[1,1]{1,0:T(1,128)} %bitcast.rank_ref, s32[1,4]{1,0:T(1,128)} %len_ref.7, bf16[768,1024]{1,0:T(8,128)(2,1)} %own_ref.3, bf16[768,1024]{1,0:T(8,128)(2,1)} %collective-permute-done.4.other_ref, ...), custom_call_target="tpu_custom_call" | custom-call | flops 17600000000 | tf_op jit(solution)/shard_map/gate_forward/pallas_call | solution.py:873
  127.0 1.6 collective-permute-start.9
  128.6 2.8 collective-permute-done.9.other_sums_ref
  132.0 13.4 %gate_backward.1 = (bf16[1536,1024]{1,0:T(8,128)(2,1)}, bf16[1536,1024]{1,0:T(8,128)(2,1)}, bf16[1536,1024]{1,0:T(8,128)(2,1)}, f32[8,1024]{1,0:T(8,128)}) custom-call(f32[8,1536]{1,0:T(8,128)} %get-tuple-element.83.own_sums_ref, f32[8,1536]{1,0:T(8,128)} %copy-done.17, f32[1536,1024]{1,0:T(8,128)} %get-tuple-element.84.gate_ref, ...), custom_call_target="tpu_custom_call" | custom-call | flops 14300000256 | tf_op jit(solution)/shard_map/gate_backward/pallas_call | solution.py:899
  145.4 5.7 %convolution_convert_fusion.1 = bf16[1024,1024]{1,0:T(8,128)(2,1)S(1)} fusion(bf16[1024,1536]{1,0:T(8,128)(2,1)S(1)} %copy-done.19, bf16[1536,1024]{1,0:T(8,128)(2,1)} %get-tuple-element.90), kind=kOutput, calls=%fused_computation.16 | convolution fusion | flops 3222274048 | bytes 8388608 | tf_op jit(solution)/shard_map/dot_general | solution.py:29
  151.1 3.6 %convolution_convert_fusion = bf16[1024,1024]{1,0:T(8,128)(2,1)S(1)} fusion(bf16[1024,1536]{1,0:T(8,128)(2,1)S(1)} %copy-done.3, bf16[1536,1024]{1,0:T(8,128)(2,1)S(1)} %copy-done.4), kind=kOutput, calls=%fused_computation.15 | convolution fusion | flops 3222274048 | bytes 8388608 | tf_op jit(solution)/shard_map/dot_general | solution.py:29
  154.7 2.4 pad_maximum_fusion
  157.1 3.9 %fusion.11 = bf16[768,1024]{1,0:T(8,128)(2,1)S(1)} fusion(bf16[1024,2048]{1,0:T(8,128)(2,1)} %all-gather.2.cloned.1.call-done.w_ref.proj_ref.w_gate_ref, bf16[1536,1024]{1,0:T(8,128)(2,1)} %get-tuple-element.90, s32[]{:T(128)S(6)} %select_n.118), kind=kOutput, calls=%fused_computation.21 | convolution fusion | flops 1611399168 | bytes 5242884 | tf_op jit(solution)/shard_map/dot_general | solution.py:33
  161.0 1.6 collective-permute-start.10
  162.6 46.6 %mixer_backward.1 = (bf16[1536,1024]{1,0:T(8,128)(2,1)}, bf16[1536,256]{1,0:T(8,128)(2,1)}, bf16[1536,128]{1,0:T(8,128)(2,1)}, f32[8,1024]{1,0:T(8,128)}, f32[8,128]{1,0:T(8,128)}) custom-call(s32[1,4]{1,0:T(1,128)} %len_ref.7, f32[1536,1024]{1,0:T(8,128)} %get-tuple-element.91.ipre_ref.halo_ref, f32[1536,1024]{1,0:T(8,128)} %get-tuple-element.91.ipre_ref.halo_ref, ...), custom_call_target="tpu_custom_call" | custom-call | flops 2200000000 | tf_op jit(solution)/shard_map/mixer_backward/pallas_call | solution.py:931
  209.3 8.0 %inner_weight_grads.1 = bf16[1024,1024]{1,0:T(8,128)(2,1)} custom-call(bf16[1024,1536]{1,0:T(8,128)(2,1)} %get-tuple-element.88.left_ref.normed_t_ref, bf16[1536,1024]{1,0:T(8,128)(2,1)} %get-tuple-element.109.right_ref.inner_ref), custom_call_target="tpu_custom_call" | custom-call | tf_op jit(solution)/shard_map/inner_weight_grads/pallas_call | solution.py:992
  217.2 1.8 constant_dynamic-slice_fusion.1
  219.1 2.6 collective-permute-done.12
  222.3 1.6 collective-permute-start.14
  223.9 12.4 %collective-permute-done.14 = bf16[2,2,64,1024]{3,2,0,1:T(8,128)(2,1)S(1)} collective-permute-done((bf16[2,2,64,1024]{3,2,0,1:T(8,128)(2,1)S(1)}, bf16[2,2,64,1024]{3,2,0,1:T(8,128)(2,1)S(1)}, u32[]{:S(2)}, u32[]{:S(2)}) %collective-permute-start.14) | collective-permute-done | bytes 524320 | tf_op jit(solution)/shard_map/ppermute | solution.py:701
  237.3 0.8 constant_dynamic-slice_fusion.3
  239.3 0.8 copy.59
  240.1 0.8 slice.41
  240.9 3.3 %collective-permute-done.15 = bf16[2,64,1024]{2,1,0:T(8,128)(2,1)S(1)} collective-permute-done((bf16[2,64,1024]{2,1,0:T(8,128)(2,1)S(1)}, bf16[2,64,1024]{2,1,0:T(8,128)(2,1)S(1)}, u32[]{:S(2)}, u32[]{:S(2)}) %collective-permute-start.15) | collective-permute-done | bytes 262176 | tf_op jit(solution)/shard_map/ppermute | solution.py:701
  244.3 8.2 %normed_grads.2 = bf16[768,1024]{1,0:T(8,128)(2,1)} custom-call(s32[1]{0:T(128)} %bitcast.22.begin_ref, bf16[1536,1024]{1,0:T(8,128)(2,1)} %get-tuple-element.89.gate_ref, bf16[1536,1024]{1,0:T(8,128)(2,1)} %get-tuple-element.109.right_ref.inner_ref, bf16[1536,128]{1,0:T(8,128)(2,1)} %get-tuple-element.101.step_ref.gstep_ref, ...), custom_call_target="tpu_custom_call" | custom-call | tf_op jit(solution)/shard_map/normed_grads/pallas_call | solution.py:1009
  253.1 3.4 %collective-permute-start.16 = (bf16[64,1024]{1,0:T(8,128)(2,1)S(1)}, bf16[64,1024]{1,0:T(8,128)(2,1)S(1)}, u32[]{:S(2)}, u32[]{:S(2)}) collective-permute-start(bf16[64,1024]{1,0:T(8,128)(2,1)S(1)} %dynamic-slice_bitcast_fusion.3), channel_id=1, source_target_pairs={{0,16},{2,18},{4,20},{6,22},{8,24},{10,26},{12,28},{14,30},{16,0},... | collective-permute-start | bytes 393224 | tf_op jit(solution)/shard_map/ppermute | solution.py:701
  256.4 0.8 copy-done.7
  257.2 8.5 %state_backward.1 = (bf16[1536,256]{1,0:T(8,128)(2,1)}, bf16[1024,384]{1,0:T(8,128)(2,1)}) custom-call(s32[1,1]{1,0:T(1,128)} %bitcast.rank_ref, s32[1,4]{1,0:T(1,128)} %len_ref.7, bf16[784,256]{1,0:T(8,128)(2,1)} %get-tuple-element.172.own_ref, bf16[784,256]{1,0:T(8,128)(2,1)} %copy-done.7, f32[1536,256]{1,0:T(8,128)} %get-tuple-element.103.spre_ref, ...), custom_call_target="tpu_custom_call" | custom-call | tf_op jit(solution)/shard_map/state_backward/pallas_call | solution.py:1046
  265.7 1.2 constant_dynamic-slice_fusion
  266.9 0.8 copy.71
  267.7 5.0 %fusion = bf16[768,1024]{1,0:T(8,128)(2,1)} fusion(bf16[768,1024]{1,0:T(8,128)(2,1)S(1)} %copy-done.2, bf16[768,1024]{1,0:T(8,128)(2,1)} %copy-done.15, pred[768]{0:T(1024)(128)(4,1)S(1)} %add_compare_fusion, bf16[1024,2048]{1,0:T(8,128)(2,1)S(1)} %copy-done, bf16[1536,1024]{1,0:T(8,128)(2,1)} %get-tuple-element.90, s32[]{:T(128)S(6)} %select_n.117), kind=kOutput, calls=%fused_computation.5 | convolution fusion | flops 1615331328 | bytes 8389636 | tf_op jit(solution)/shard_map/dot_general | solution.py:33
  272.7 0.8 convert_add_fusion.6.inner_ref
  273.5 8.2 %normed_grads.3 = f32[768,1024]{1,0:T(8,128)} custom-call(s32[1]{0:T(128)} %bitcast.19.begin_ref, bf16[1536,1024]{1,0:T(8,128)(2,1)} %get-tuple-element.89.gate_ref, bf16[1536,1024]{1,0:T(8,128)(2,1)} %get-tuple-element.109.right_ref.inner_ref, bf16[1536,128]{1,0:T(8,128)(2,1)} %get-tuple-element.101.step_ref.gstep_ref, ...), custom_call_target="tpu_custom_call" | custom-call | tf_op jit(solution)/shard_map/normed_grads/pallas_call | solution.py:1009
  281.7 1.2 fusion.21
  282.9 0.7 collective-permute-start.18
  283.6 0.8 convert_bitcast_fusion
  284.3 5.9 %collective-permute-done.18 = bf16[2,2,64,384]{3,2,1,0:T(8,128)(2,1)S(1)} collective-permute-done((bf16[2,2,64,384]{3,2,1,0:T(8,128)(2,1)S(1)}, bf16[2,2,64,384]{3,2,1,0:T(8,128)(2,1)S(1)}, u32[]{:S(2)}, u32[]{:S(2)}) %collective-permute-start.18) | collective-permute-done | bytes 196640 | tf_op jit(solution)/shard_map/ppermute | solution.py:701
  290.9 3.3 %fusion.1 = (f32[768]{0:T(1024)S(1)}, f32[768]{0:T(1024)S(1)}, f32[768,1024]{1,0:T(8,128)S(1)}) fusion(bf16[768,1024]{1,0:T(8,128)(2,1)S(1)} %copy-done.2, f32[1024]{0:T(1024)S(1)} %bitcast.117, bf16[1024,1408]{1,0:T(8,128)(2,1)} %bitcast.108, bf16[1536,256]{1,0:T(8,128)(2,1)S(1)} %copy-done.9, s32[]{:T(128)S(6)} %select_n.117, ...), kind=kOutput, calls=%fused_computation.6 | convolution fusion | flops 409729536 | bytes 10364932 | tf_op jit(solution)/shard_map/dot_general | solution.py:33
  294.2 3.7 %collective-permute-done.19 = bf16[2,64,384]{2,1,0:T(8,128)(2,1)S(1)} collective-permute-done((bf16[2,64,384]{2,1,0:T(8,128)(2,1)S(1)}, bf16[2,64,384]{2,1,0:T(8,128)(2,1)S(1)}, u32[]{:S(2)}, u32[]{:S(2)}) %collective-permute-start.19) | collective-permute-done | bytes 98336 | tf_op jit(solution)/shard_map/ppermute | solution.py:701
  297.9 1.6 collective-permute-start.20
  299.5 2.6 collective-permute-done.20
  302.7 2.0 finish.1
  304.8 1.5 collective-permute-start.21
  306.3 3.9 %fusion.4 = f32[768,1024]{1,0:T(8,128)} fusion(bf16[768,1024]{1,0:T(8,128)(2,1)S(1)} %copy-done.2, bf16[768,1024]{1,0:T(8,128)(2,1)} %own_ref.3, f32[768,1024]{1,0:T(8,128)S(1)} %get-tuple-element.183, f32[768]{0:T(1024)S(1)} %broadcast_multiply_fusion, f32[768]{0:T(1024)S(1)} %get-tuple-element.182, f32[768]{0:T(1024)S(1)} %get-tuple-element.181), kind=kLoop, calls=%fused_computation.9 | loop fusion | flops 5505024 | bytes 9446400 | tf_op jit(solution)/shard_map/add | solution.py:1088
  310.8 1.6 unpack_small.1
  312.4 1.4 copy.51
  (95 shorter events, 9.3 us)
Async XLA Ops:
  7.2 20.7 %copy-start.1 = (bf16[768,1024]{1,0:T(8,128)(2,1)S(1)}, bf16[768,1024]{1,0:T(8,128)(2,1)}, u32[]{:S(2)}) copy-start(bf16[768,1024]{1,0:T(8,128)(2,1)} %own_ref.2) | copy-start | bytes 4718596
  7.2 20.7 %copy-start.11 = (bf16[1024,64]{0,1:T(8,128)(2,1)S(1)}, bf16[1024,64]{0,1:T(8,128)(2,1)}, u32[]{:S(2)}) copy-start(bf16[1024,64]{0,1:T(8,128)(2,1)} %param.29) | copy-start | bytes 393220
  7.2 103.3 %all-gather.2.cloned.1.call-start = ((), (), s32[]{:S(2)}) async-start(), calls=%async_computation.1 | async-start | bytes 4456448 | tf_op jit(solution)/shard_map/all_gather | solution.py:817
  12.7 12.7 %collective-permute-start.5 = (bf16[64,1408]{1,0:T(8,128)(2,1)}, bf16[64,1408]{1,0:T(8,128)(2,1)S(1)}, u32[]{:S(2)}, u32[]{:S(2)}) collective-permute-start(bf16[64,1408]{1,0:T(8,128)(2,1)} %pack_small.1), channel_id=1, source_target_pairs={{0,16},{2,18},{4,20},{6,22},{8,24},{10,26},{12,28},{14,30},{16,0},... | collective-permute-start | bytes 540680 | tf_op jit(solution)/shard_map/ppermute | solution.py:701
  17.6 8.7 %collective-permute-start = (bf16[64,1024]{1,0:T(8,128)(2,1)S(1)}, bf16[64,1024]{1,0:T(8,128)(2,1)S(1)}, u32[]{:S(2)}, u32[]{:S(2)}) collective-permute-start(bf16[64,1024]{1,0:T(8,128)(2,1)S(1)} %slice.36), channel_id=1, source_target_pairs={{0,1},{1,0},{2,3},{3,2},{4,5},{5,4},{6,7},{7,6},{8,9},{9,8},{10,11... | collective-permute-start | bytes 393224 | tf_op jit(solution)/shard_map/ppermute | solution.py:787
  26.4 0.7 copy-start.10
  27.0 9.6 %collective-permute-start.6 = (bf16[2,64,1408]{2,1,0:T(8,128)(2,1)S(1)}, bf16[2,64,1408]{2,1,0:T(8,128)(2,1)S(1)}, u32[]{:S(2)}, u32[]{:S(2)}) collective-permute-start(bf16[2,64,1408]{2,1,0:T(8,128)(2,1)S(1)} %pad_maximum_fusion.5), channel_id=1, source_target_pairs={{0,8},{2,10},{4,12},{6,14},{8,0},{10,2},{12,4},{14,6},{16,24},{18,... | collective-permute-start | bytes 1081352 | tf_op jit(solution)/shard_map/ppermute | solution.py:701
  28.7 10.9 %collective-permute-start.1 = (bf16[192,1024]{1,0:T(8,128)(2,1)S(1)}, bf16[192,1024]{1,0:T(8,128)(2,1)}, u32[]{:S(2)}, u32[]{:S(2)}) collective-permute-start(bf16[192,1024]{1,0:T(8,128)(2,1)S(1)} %slice.35), channel_id=1, source_target_pairs={{0,1},{1,0},{2,3},{3,2},{4,5},{5,4},{6,7},{7,6},{8,9},{9,8},{10,11... | collective-permute-start | bytes 1179656 | tf_op jit(solution)/shard_map/ppermute | solution.py:787
  39.6 204.7 %reduce-scatter.2.cloned.1.call-start = ((), (), s32[]{:S(2)}) async-start(), calls=%async_computation.2 | async-start | bytes 4456448 | tf_op jit(solution)/shard_map/reduce_scatter | solution.py:924
  39.6 19.8 %collective-permute-start.7 = (bf16[2,2,64,1408]{3,2,0,1:T(8,128)(2,1)S(1)}, bf16[2,2,64,1408]{3,2,0,1:T(8,128)(2,1)S(1)}, u32[]{:S(2)}, u32[]{:S(2)}) collective-permute-start(bf16[2,2,64,1408]{3,2,0,1:T(8,128)(2,1)S(1)} %pad_maximum_fusion.4), channel_id=1, source_target_pairs={{0,4},{2,6},{4,0},{6,2},{8,12},{10,14},{12,8},{14,10},{16,20},{18,... | collective-permute-start | bytes 2162696 | tf_op jit(solution)/shard_map/ppermute | solution.py:701
  41.2 20.1 %copy-start.13 = (bf16[16]{0:T(256)(128)(2,1)S(1)}, bf16[16]{0:T(256)(128)(2,1)}, u32[]{:S(2)}) copy-start(bf16[16]{0:T(256)(128)(2,1)} %param.26) | copy-start | bytes 100
  41.2 20.1 %copy-start.14 = (bf16[16]{0:T(256)(128)(2,1)S(1)}, bf16[16]{0:T(256)(128)(2,1)}, u32[]{:S(2)}) copy-start(bf16[16]{0:T(256)(128)(2,1)} %param.27) | copy-start | bytes 100
  41.3 34.5 %copy-start.18 = (bf16[16]{0:T(256)(128)(2,1)S(1)}, bf16[16]{0:T(256)(128)(2,1)}, u32[]{:S(2)}) copy-start(bf16[16]{0:T(256)(128)(2,1)} %param.25) | copy-start | bytes 100
  41.3 18.4 %collective-permute-start.2 = (bf16[256,1024]{1,0:T(8,128)(2,1)S(1)}, bf16[256,1024]{1,0:T(8,128)(2,1)S(1)}, u32[]{:S(2)}, u32[]{:S(2)}) collective-permute-start(bf16[256,1024]{1,0:T(8,128)(2,1)S(1)} %get-tuple-element.73), channel_id=1, source_target_pairs={{0,1},{1,0},{2,3},{3,2},{4,5},{5,4},{6,7},{7,6},{8,9},{9,8},{10,11... | collective-permute-start | bytes 1572872 | tf_op jit(solution)/shard_map/ppermute | solution.py:787
  59.7 19.2 %collective-permute-start.8 = (bf16[2,2,2,64,1408]{4,3,0,1,2:T(8,128)(2,1)S(1)}, bf16[2,2,2,64,1408]{4,3,0,1,2:T(8,128)(2,1)S(1)}, u32[]{:S(2)}, u32[]{:S(2)}) collective-permute-start(bf16[2,2,2,64,1408]{4,3,0,1,2:T(8,128)(2,1)S(1)} %pad_maximum_fusion.3), channel_id=1, source_target_pairs={{0,2},{2,0},{4,6},{6,4},{8,10},{10,8},{12,14},{14,12},{16,18},{18,... | collective-permute-start | bytes 4325384 | tf_op jit(solution)/shard_map/ppermute | solution.py:701
  59.8 14.4 %collective-permute-start.3 = (bf16[256,1024]{1,0:T(8,128)(2,1)S(1)}, bf16[256,1024]{1,0:T(8,128)(2,1)}, u32[]{:S(2)}, u32[]{:S(2)}) collective-permute-start(bf16[256,1024]{1,0:T(8,128)(2,1)S(1)} %get-tuple-element.74), channel_id=1, source_target_pairs={{0,1},{1,0},{2,3},{3,2},{4,5},{5,4},{6,7},{7,6},{8,9},{9,8},{10,11... | collective-permute-start | bytes 1572872 | tf_op jit(solution)/shard_map/ppermute | solution.py:787
  74.2 36.3 %collective-permute-start.4 = (bf16[768,1024]{1,0:T(8,128)(2,1)}, bf16[768,1024]{1,0:T(8,128)(2,1)}, u32[]{:S(2)}, u32[]{:S(2)}) collective-permute-start(bf16[768,1024]{1,0:T(8,128)(2,1)} %own_ref.3), channel_id=1, source_target_pairs={{0,1},{1,0},{2,3},{3,2},{4,5},{5,4},{6,7},{7,6},{8,9},{9,8},{10,11... | collective-permute-start | bytes 4718600 | tf_op jit(solution)/shard_map/ppermute | solution.py:787
  127.0 4.4 %collective-permute-start.9 = (f32[8,1536]{1,0:T(8,128)}, f32[8,1536]{1,0:T(8,128)S(1)}, u32[]{:S(2)}, u32[]{:S(2)}) collective-permute-start(f32[8,1536]{1,0:T(8,128)} %get-tuple-element.83.own_sums_ref), channel_id=1, source_target_pairs={{0,1},{1,0},{2,3},{3,2},{4,5},{5,4},{6,7},{7,6},{8,9},{9,8},{10,11... | collective-permute-start | bytes 147464 | tf_op jit(solution)/shard_map/ppermute | solution.py:787
  131.4 0.6 copy-start.17
  132.0 13.4 %copy-start.19 = (bf16[1024,1536]{1,0:T(8,128)(2,1)S(1)}, bf16[1024,1536]{1,0:T(8,128)(2,1)}, u32[]{:S(2)}) copy-start(bf16[1024,1536]{1,0:T(8,128)(2,1)} %get-tuple-element.87) | copy-start | bytes 9437188
  145.4 5.7 %copy-start.3 = (bf16[1024,1536]{1,0:T(8,128)(2,1)S(1)}, bf16[1024,1536]{1,0:T(8,128)(2,1)}, u32[]{:S(2)}) copy-start(bf16[1024,1536]{1,0:T(8,128)(2,1)} %get-tuple-element.88.left_ref.normed_t_ref) | copy-start | bytes 9437188
  145.4 5.7 %copy-start.4 = (bf16[1536,1024]{1,0:T(8,128)(2,1)S(1)}, bf16[1536,1024]{1,0:T(8,128)(2,1)}, u32[]{:S(2)}) copy-start(bf16[1536,1024]{1,0:T(8,128)(2,1)} %get-tuple-element.89.gate_ref) | copy-start | bytes 9437188
  161.0 48.2 %collective-permute-start.10 = (bf16[768,1024]{1,0:T(8,128)(2,1)S(1)}, bf16[768,1024]{1,0:T(8,128)(2,1)S(1)}, u32[]{:S(2)}, u32[]{:S(2)}) collective-permute-start(bf16[768,1024]{1,0:T(8,128)(2,1)S(1)} %fusion.11), channel_id=1, source_target_pairs={{0,1},{1,0},{2,3},{3,2},{4,5},{5,4},{6,7},{7,6},{8,9},{9,8},{10,11... | collective-permute-start | bytes 4718600 | tf_op jit(solution)/shard_map/ppermute | solution.py:787
  209.2 8.0 %copy-start.15 = (bf16[768,1024]{1,0:T(8,128)(2,1)}, bf16[768,1024]{1,0:T(8,128)(2,1)S(1)}, u32[]{:S(2)}) copy-start(bf16[768,1024]{1,0:T(8,128)(2,1)S(1)} %collective-permute-done.10) | copy-start | bytes 4718596
  219.1 2.7 collective-permute-start.12
  221.8 14.9 %copy-start.12 = (s32[1,4]{1,0:T(1,128)S(1)}, s32[1,4]{1,0:T(1,128)}, u32[]{:S(2)}) copy-start(s32[1,4]{1,0:T(1,128)} %len_ref.7) | copy-start | bytes 52
  222.2 15.1 %copy-start.6 = (bf16[1536,256]{1,0:T(8,128)(2,1)S(1)}, bf16[1536,256]{1,0:T(8,128)(2,1)}, u32[]{:S(2)}) copy-start(bf16[1536,256]{1,0:T(8,128)(2,1)} %get-tuple-element.100) | copy-start | bytes 2359300
  222.2 17.1 %copy-start.5 = (bf16[64,2,1024]{2,1,0:T(2,128)(2,1)S(1)}, bf16[64,2,1024]{2,1,0:T(2,128)(2,1)}, u32[]{:S(2)}) copy-start(bf16[64,2,1024]{2,1,0:T(2,128)(2,1)} %param.18) | copy-start | bytes 786436
  222.3 14.0 %collective-permute-start.14 = (bf16[2,2,64,1024]{3,2,0,1:T(8,128)(2,1)S(1)}, bf16[2,2,64,1024]{3,2,0,1:T(8,128)(2,1)S(1)}, u32[]{:S(2)}, u32[]{:S(2)}) collective-permute-start(bf16[2,2,64,1024]{3,2,0,1:T(8,128)(2,1)S(1)} %dynamic-slice_bitcast_fusion), channel_id=1, source_target_pairs={{0,4},{2,6},{4,0},{6,2},{8,12},{10,14},{12,8},{14,10},{16,20},{18,... | collective-permute-start | bytes 1572872 | tf_op jit(solution)/shard_map/ppermute | solution.py:701
  236.6 7.6 %collective-permute-start.15 = (bf16[2,64,1024]{2,1,0:T(8,128)(2,1)S(1)}, bf16[2,64,1024]{2,1,0:T(8,128)(2,1)S(1)}, u32[]{:S(2)}, u32[]{:S(2)}) collective-permute-start(bf16[2,64,1024]{2,1,0:T(8,128)(2,1)S(1)} %dynamic-slice_bitcast_fusion.1), channel_id=1, source_target_pairs={{0,8},{2,10},{4,12},{6,14},{8,0},{10,2},{12,4},{14,6},{16,24},{18,... | collective-permute-start | bytes 786440 | tf_op jit(solution)/shard_map/ppermute | solution.py:701
  238.1 18.3 %collective-permute-start.11 = (bf16[784,256]{1,0:T(8,128)(2,1)S(1)}, bf16[784,256]{1,0:T(8,128)(2,1)S(1)}, u32[]{:S(2)}, u32[]{:S(2)}) collective-permute-start(bf16[784,256]{1,0:T(8,128)(2,1)S(1)} %get-tuple-element.171), channel_id=1, source_target_pairs={{0,1},{1,0},{2,3},{3,2},{4,5},{5,4},{6,7},{7,6},{8,9},{9,8},{10,11... | collective-permute-start | bytes 1204232 | tf_op jit(solution)/shard_map/ppermute | solution.py:787
  252.4 37.8 %collective-permute-start.13 = (bf16[768,1024]{1,0:T(8,128)(2,1)}, bf16[768,1024]{1,0:T(8,128)(2,1)S(1)}, u32[]{:S(2)}, u32[]{:S(2)}) collective-permute-start(bf16[768,1024]{1,0:T(8,128)(2,1)} %normed_grads.2), channel_id=1, source_target_pairs={{0,1},{1,0},{2,3},{3,2},{4,5},{5,4},{6,7},{7,6},{8,9},{9,8},{10,11... | collective-permute-start | bytes 4718600 | tf_op jit(solution)/shard_map/ppermute | solution.py:787
  253.1 19.7 %collective-permute-start.16 = (bf16[64,1024]{1,0:T(8,128)(2,1)S(1)}, bf16[64,1024]{1,0:T(8,128)(2,1)S(1)}, u32[]{:S(2)}, u32[]{:S(2)}) collective-permute-start(bf16[64,1024]{1,0:T(8,128)(2,1)S(1)} %dynamic-slice_bitcast_fusion.3), channel_id=1, source_target_pairs={{0,16},{2,18},{4,20},{6,22},{8,24},{10,26},{12,28},{14,30},{16,0},... | collective-permute-start | bytes 393224 | tf_op jit(solution)/shard_map/ppermute | solution.py:701
  256.4 0.8 copy-start.7
  257.2 10.5 %copy-start = (bf16[1024,2048]{1,0:T(8,128)(2,1)S(1)}, bf16[1024,2048]{1,0:T(8,128)(2,1)}, u32[]{:S(2)}) copy-start(bf16[1024,2048]{1,0:T(8,128)(2,1)} %all-gather.2.cloned.1.call-done.w_ref.proj_ref.w_gate_ref) | copy-start | bytes 12582916
  257.2 10.5 %copy-start.2 = (bf16[768,1024]{1,0:T(8,128)(2,1)S(1)}, bf16[768,1024]{1,0:T(8,128)(2,1)}, u32[]{:S(2)}) copy-start(bf16[768,1024]{1,0:T(8,128)(2,1)} %own_ref.2) | copy-start | bytes 4718596
  267.7 14.0 %collective-permute-start.17 = (bf16[2,2,2,64,384]{4,3,2,0,1:T(8,128)(2,1)}, bf16[2,2,2,64,384]{4,3,2,0,1:T(8,128)(2,1)}, u32[]{:S(2)}, u32[]{:S(2)}) collective-permute-start(bf16[2,2,2,64,384]{4,3,2,0,1:T(8,128)(2,1)} %bitcast.100), channel_id=1, source_target_pairs={{0,2},{2,0},{4,6},{6,4},{8,10},{10,8},{12,14},{14,12},{16,18},{18,... | collective-permute-start | bytes 1179656 | tf_op jit(solution)/shard_map/ppermute | solution.py:701
  273.5 10.1 %copy-start.8 = (bf16[64,2048]{1,0:T(8,128)(2,1)S(1)}, bf16[64,2048]{1,0:T(8,128)(2,1)}, u32[]{:S(2)}) copy-start(bf16[64,2048]{1,0:T(8,128)(2,1)} %reduce-scatter.2.cloned.1.call-done) | copy-start | bytes 786436
  281.7 9.2 %copy-start.9 = (bf16[1536,256]{1,0:T(8,128)(2,1)S(1)}, bf16[1536,256]{1,0:T(8,128)(2,1)}, u32[]{:S(2)}) copy-start(bf16[1536,256]{1,0:T(8,128)(2,1)} %get-tuple-element.110) | copy-start | bytes 2359300
  282.9 7.4 %collective-permute-start.18 = (bf16[2,2,64,384]{3,2,1,0:T(8,128)(2,1)S(1)}, bf16[2,2,64,384]{3,2,1,0:T(8,128)(2,1)S(1)}, u32[]{:S(2)}, u32[]{:S(2)}) collective-permute-start(bf16[2,2,64,384]{3,2,1,0:T(8,128)(2,1)S(1)} %dynamic-slice_bitcast_fusion.2), channel_id=1, source_target_pairs={{0,8},{2,10},{4,12},{6,14},{8,0},{10,2},{12,4},{14,6},{16,24},{18,... | collective-permute-start | bytes 589832 | tf_op jit(solution)/shard_map/ppermute | solution.py:701
  290.4 7.5 %collective-permute-start.19 = (bf16[2,64,384]{2,1,0:T(8,128)(2,1)S(1)}, bf16[2,64,384]{2,1,0:T(8,128)(2,1)S(1)}, u32[]{:S(2)}, u32[]{:S(2)}) collective-permute-start(bf16[2,64,384]{2,1,0:T(8,128)(2,1)S(1)} %dynamic-slice_bitcast_fusion.4), channel_id=1, source_target_pairs={{0,16},{2,18},{4,20},{6,22},{8,24},{10,26},{12,28},{14,30},{16,0},... | collective-permute-start | bytes 294920 | tf_op jit(solution)/shard_map/ppermute | solution.py:701
  297.9 4.2 %collective-permute-start.20 = (bf16[64,384]{1,0:T(8,128)(2,1)S(1)}, bf16[64,384]{1,0:T(8,128)(2,1)S(1)}, u32[]{:S(2)}, u32[]{:S(2)}) collective-permute-start(bf16[64,384]{1,0:T(8,128)(2,1)S(1)} %dynamic-slice_bitcast_fusion.5), channel_id=1, source_target_pairs={{0,4},{2,6},{4,0},{6,2},{8,12},{10,14},{12,8},{14,10},{16,20},{18,... | collective-permute-start | bytes 147464 | tf_op jit(solution)/shard_map/ppermute | solution.py:701
  304.8 5.4 %collective-permute-start.21 = (f32[64,384]{1,0:T(8,128)}, f32[64,384]{1,0:T(8,128)S(1)}, u32[]{:S(2)}, u32[]{:S(2)}) collective-permute-start(f32[64,384]{1,0:T(8,128)} %get-tuple-element.116.own_ref), channel_id=1, source_target_pairs={{0,1},{1,0},{2,3},{3,2},{4,5},{5,4},{6,7},{7,6},{8,9},{9,8},{10,11... | collective-permute-start | bytes 294920 | tf_op jit(solution)/shard_map/ppermute | solution.py:787
  310.1 0.6 copy-start.16
Sparse Core Ops, SparseCore 0:
  39.7 54.0 all-gather.1
  157.3 73.3 reduce-scatter.1

commit v5 on v4

--- a/solution.py
+++ b/solution.py
@@ -18,6 +18,9 @@
 
 LANE_CONV, LANE_GATE, LANE_STATE, LANE_HEADS, LANE_GAIN = 16, 21, 24, 32, 127
 HALO = 16
+
+STRIP = 32
+STRIPS = [slice(at, at + STRIP) for at in range(0, GROUP, STRIP)]
 
 F32 = jnp.float32
 BF16 = jnp.bfloat16
@@ -185,6 +188,17 @@
     return step, cum, key_factor, entry, decay
 
 
+def strip_at(strip, base):
+    return slice(base + strip.start, base + strip.stop)
+
+
+def fold_rows(value):
+    total = value[0:8]
+    for at in range(8, STRIP, 8):
+        total = total + value[at : at + 8]
+    return total
+
+
 def head_masks():
     lane = lax.broadcasted_iota(jnp.int32, (1, LANES), 1)
     first = (lane < LANES // 2).astype(F32)
@@ -195,7 +209,8 @@
     rank_ref, len_ref, own_ref, other_ref, w_ref, head_ref,
     normed_ref, normed_t_ref, ipre_ref, spre_ref, sact_ref, stepin_ref, mixed_ref, sprev_ref,
     rows_ref, taps_ref,
-    ext, state, spread, lower, fac, read, mask, scores, weighted, factors, *, shard, state_shard,
+    ext, state, spread, lower, fac, read, mask, scores, weighted, factors,
+    values, stepped, both, *, shard, state_shard,
 ):
     inner = rows_ref.shape[1]
     channels = ext.shape[1]
@@ -246,19 +261,22 @@
     position = position_of(ends, token)
     keep = [(position >= offset).astype(F32) for offset in (1, 2, 3)]
 
-    def conv(sl, taps, bias):
-        total = bias + taps[3:4, :] * ext[8 : 8 + GROUP, sl]
+    def conv(strip, sl, taps, bias):
+        at = strip.start
+        total = bias + taps[3:4, :] * ext[8 + at : 8 + at + STRIP, sl]
         for offset in (1, 2, 3):
-            total = total + keep[offset - 1] * (
-                taps[3 - offset : 4 - offset, :] * ext[8 - offset : 8 - offset + GROUP, sl]
+            total = total + keep[offset - 1][strip] * (
+                taps[3 - offset : 4 - offset, :]
+                * ext[8 - offset + at : 8 - offset + at + STRIP, sl]
             )
         return total
 
     for part in range(2):
         sl = slice(inner + part * size, inner + (part + 1) * size)
         own = slice(part * size, (part + 1) * size)
-        total = conv(sl, taps_ref[0:4, own], taps_ref[4:5, own])
-        sact_ref[:, own] = (total * sigmoid(total)).astype(BF16)
+        for strip in STRIPS:
+            total = conv(strip, sl, taps_ref[0:4, own], taps_ref[4:5, own])
+            sact_ref[strip, own] = (total * sigmoid(total)).astype(BF16)
     keys = sact_ref[:, :size]
     queries = sact_ref[:, size:]
     scores[...] = nt(queries, keys)
@@ -280,26 +298,33 @@
     lo, hi = slice(0, HALF), slice(HALF, GROUP)
     for pair in range(inner // LANES):
         sl = slice(pair * LANES, (pair + 1) * LANES)
-        total = conv(sl, rows_ref[ROW_TAP : ROW_TAP + 4, sl], rows_ref[ROW_BIAS : ROW_BIAS + 1, sl])
-        values = (total * sigmoid(total)).astype(BF16).astype(F32)
-        stepped = (values * fac[0:GROUP, sl]).astype(BF16)
-        weighted[:, sl] = (values * fac[GROUP : 2 * GROUP, sl]).astype(BF16)
         slot = pair % 2
+        taps, bias = rows_ref[ROW_TAP : ROW_TAP + 4, sl], rows_ref[ROW_BIAS : ROW_BIAS + 1, sl]
+        for strip in STRIPS:
+            total = conv(strip, sl, taps, bias)
+            value = (total * sigmoid(total)).astype(BF16).astype(F32)
+            values[slot, strip] = value
+            stepped[slot, strip] = (value * fac[strip, sl]).astype(BF16)
+            weighted[strip, sl] = (value * fac[strip_at(strip, GROUP), sl]).astype(BF16)
         for which in range(PAIR_HEADS):
             head = pair * PAIR_HEADS + which
-            column = cum[:, head : head + 1]
-            row = cum_rows[head : head + 1, :]
-            for rs, cs in ((lo, lo), (hi, lo), (hi, hi)):
-                gap = column[rs] - row[:, cs] + mask[rs, cs]
-                place = slice(which * GROUP + rs.start, which * GROUP + rs.stop)
-                factors[slot, place, cs] = (jnp.exp2(gap) * scores[rs, cs]).astype(BF16)
-        both = nn(factors[slot], stepped)
-        within = jnp.where(first_head, both[:GROUP], both[GROUP:])
-        mixed_ref[:, sl] = (
-            within
-            + fac[2 * GROUP : 3 * GROUP, sl] * read[:, sl]
-            + rows_ref[ROW_SKIP : ROW_SKIP + 1, sl] * values
-        )
+            for strip in STRIPS:
+                column = jnp.broadcast_to(cum[strip, head : head + 1], (STRIP, LANES))
+                place = strip_at(strip, which * GROUP)
+                for cs in (lo, hi) if strip.start >= HALF else (lo,):
+                    gap = column - cum_rows[head : head + 1, cs] + mask[strip, cs]
+                    factors[slot, place, cs] = (jnp.exp2(gap) * scores[strip, cs]).astype(BF16)
+        both[slot] = nn(factors[slot], stepped[slot])
+        skip = rows_ref[ROW_SKIP : ROW_SKIP + 1, sl]
+        for strip in STRIPS:
+            within = jnp.where(
+                first_head, both[slot, strip], both[slot, strip_at(strip, GROUP)]
+            )
+            mixed_ref[strip, sl] = (
+                within
+                + fac[strip_at(strip, 2 * GROUP), sl] * read[strip, sl]
+                + skip * values[slot, strip]
+            )
 
     state[...] = fac[3 * GROUP : 3 * GROUP + 1, :] * state[...] + tn(keys, weighted[...])
     ext[0:8, :] = ext[GROUP : GROUP + 8, :]
@@ -352,21 +377,27 @@
     inv_all = lax.rsqrt(columns[:, 0:1] / inner_all + NORM_EPS)
     slope_all = inv_all * inv_all * inv_all * columns[:, 4:5] / inner_all
     gain = rows_ref[ROW_GATE : ROW_GATE + 1, :]
-    total = jnp.zeros((1, gate_ref.shape[1]), F32)
-    for part in range(8):
-        sl = slice(part * 32, part * 32 + 32)
-        inv, slope = inv_all[sl], slope_all[sl]
-        gate, gol, mixed = gate_ref[sl, :], gol_ref[sl, :], mixed_ref[sl, :]
-        logistic = sigmoid(gate)
-        silu = gate * logistic
-        gated = mixed * silu
-        scaled = gated * inv
-        low_ref[sl, :] = (scaled * gain).astype(BF16)
-        total = total + jnp.sum(gol * scaled, axis=0, keepdims=True)
-        grad = inv * (gol * gain) - gated * slope
-        first_ref[sl, :] = (grad * silu).astype(BF16)
-        ggp_ref[sl, :] = (grad * mixed * (logistic * (1.0 + gate * (1.0 - logistic)))).astype(BF16)
-    gain_ref[0:1, :] += total
+    for part in range(gate_ref.shape[1] // GROUP):
+        sl = slice(part * GROUP, (part + 1) * GROUP)
+        gain_row = gain[:, sl]
+        total = jnp.zeros((8, GROUP), F32)
+        for at in range(0, GROUP, 16):
+            strip = slice(at, at + 16)
+            inv, slope = inv_all[strip], slope_all[strip]
+            gate, gol, mixed = gate_ref[strip, sl], gol_ref[strip, sl], mixed_ref[strip, sl]
+            logistic = sigmoid(gate)
+            silu = gate * logistic
+            gated = mixed * silu
+            scaled = gated * inv
+            low_ref[strip, sl] = (scaled * gain_row).astype(BF16)
+            product = gol * scaled
+            total = total + product[0:8] + product[8:16]
+            grad = inv * (gol * gain_row) - gated * slope
+            first_ref[strip, sl] = (grad * silu).astype(BF16)
+            ggp_ref[strip, sl] = (
+                grad * mixed * (logistic * (1.0 + gate * (1.0 - logistic)))
+            ).astype(BF16)
+        gain_ref[0:1, sl] += jnp.sum(total, axis=0, keepdims=True)
 
 
 def product_kernel(left_ref, right_ref, out_ref):
@@ -385,7 +416,7 @@
     rows_ref, head_ref,
     gip_ref, gkq_ref, gstep_ref, conv_ref, heads_ref,
     ext, cext, gstate, spread, collect, lower, upper, fac, reads, mask, scores, gscores,
-    weighted, entered, sums, factors,
+    weighted, entered, sums, factors, values, slopes, split, grads, both,
 ):
     inner = rows_ref.shape[1]
     heads = inner // (LANES // PAIR_HEADS)
@@ -438,65 +469,84 @@
     for pair in range(inner // LANES):
         sl = slice(pair * LANES, (pair + 1) * LANES)
         taps = rows_ref[ROW_TAP : ROW_TAP + 4, sl]
-        shifted = [ext[8 - offset : 8 - offset + GROUP, sl] for offset in range(4)]
-        total = rows_ref[ROW_BIAS : ROW_BIAS + 1, sl] + taps[3:4, :] * shifted[0]
-        for offset in (1, 2, 3):
-            total = total + keep[offset - 1] * (taps[3 - offset : 4 - offset, :] * shifted[offset])
-        logistic = sigmoid(total)
-        values = (total * logistic).astype(BF16).astype(F32)
-        slope = logistic * (1.0 + total * (1.0 - logistic))
-        step_wide = fac[0:GROUP, sl]
-        key_wide = fac[GROUP : 2 * GROUP, sl]
-        stepped = (values * step_wide).astype(BF16)
-        stepped_wide = stepped.astype(F32)
-        weighted[:, sl] = (values * key_wide).astype(BF16)
-        upstream = first_ref[:, sl]
-        upstream_wide = upstream.astype(F32)
-        entered[:, sl] = (upstream_wide * fac[2 * GROUP : 3 * GROUP, sl]).astype(BF16)
-
+        bias = rows_ref[ROW_BIAS : ROW_BIAS + 1, sl]
+        skip = rows_ref[ROW_SKIP : ROW_SKIP + 1, sl]
         slot = pair % 2
-        split = [(values * step_wide * one).astype(BF16) for one in masks]
-        grads = nn(jnp.concatenate(split, axis=0), upstream.T)
-        blocks = [None, None, None]
-        for which in range(PAIR_HEADS):
-            head = pair * PAIR_HEADS + which
-            column = cum[:, head : head + 1]
-            row = cum_rows[head : head + 1, :]
-            for index, (rs, cs) in enumerate(((lo, lo), (lo, hi), (hi, hi))):
-                factor = jnp.exp2(row[:, cs] - column[rs] + mask[rs, cs])
-                place = slice(which * GROUP + rs.start, which * GROUP + rs.stop)
-                factors[slot, place, cs] = (factor * scores[rs, cs]).astype(BF16)
-                part = factor * grads[place, cs]
-                blocks[index] = part if blocks[index] is None else blocks[index] + part
-        gscores[lo, lo] += blocks[0]
-        gscores[lo, hi] += blocks[1]
-        gscores[hi, hi] += blocks[2]
-        both = nn(factors[slot], upstream)
-        raw = jnp.where(first_head, both[:GROUP], both[GROUP:])
-        skip = rows_ref[ROW_SKIP : ROW_SKIP + 1, sl]
-        across = reads[:, sl]
-
-        balance = upstream_wide * (mixed_ref[:, sl] - skip * values) - stepped_wide * raw
-        high = balance.astype(BF16)
-        sums[0:GROUP, sl] = high
-        sums[GROUP : 2 * GROUP, sl] = (balance - high.astype(F32)).astype(BF16)
-        sums[2 * GROUP : 3 * GROUP, sl] = (values * raw).astype(BF16)
-        sums[3 * GROUP : 4 * GROUP, sl] = (values * across).astype(BF16)
-        conv_ref[5:6, sl] += jnp.sum(upstream_wide * values, axis=0, keepdims=True)
-        inner_grad = step_wide * raw + key_wide * across + skip * upstream_wide
-        grad = inner_grad * slope
-        cext[0:GROUP, sl] = grad
-        conv_ref[3:4, sl] += jnp.sum(grad * shifted[0], axis=0, keepdims=True)
-        conv_ref[4:5, sl] += jnp.sum(grad, axis=0, keepdims=True)
-        result = taps[3:4, :] * grad
-        for offset in (1, 2, 3):
-            conv_ref[3 - offset : 4 - offset, sl] += jnp.sum(
-                keep[offset - 1] * grad * shifted[offset], axis=0, keepdims=True
-            )
-            result = result + ahead[offset - 1] * (
-                taps[3 - offset : 4 - offset, :] * cext[offset : offset + GROUP, sl]
-            )
-        gip_ref[:, sl] = result.astype(BF16)
+
+        def shifted(strip, offset):
+            return ext[8 - offset + strip.start : 8 - offset + strip.stop, sl]
+
+        for strip in STRIPS:
+            total = bias + taps[3:4, :] * shifted(strip, 0)
+            for offset in (1, 2, 3):
+                total = total + keep[offset - 1][strip] * (
+                    taps[3 - offset : 4 - offset, :] * shifted(strip, offset)
+                )
+            logistic = sigmoid(total)
+            value = (total * logistic).astype(BF16).astype(F32)
+            values[slot, strip] = value
+            slopes[slot, strip] = logistic * (1.0 + total * (1.0 - logistic))
+            step_value = value * fac[strip, sl]
+            for which in range(PAIR_HEADS):
+                split[slot, strip_at(strip, which * GROUP)] = (step_value * masks[which]).astype(
+                    BF16
+                )
+            weighted[strip, sl] = (value * fac[strip_at(strip, GROUP), sl]).astype(BF16)
+            entered[strip, sl] = (
+                first_ref[strip, sl].astype(F32) * fac[strip_at(strip, 2 * GROUP), sl]
+            ).astype(BF16)
+
+        grads[slot] = nn(split[slot], first_ref[:, sl].T)
+        for strip in STRIPS:
+            columns = [
+                jnp.broadcast_to(cum[strip, head : head + 1], (STRIP, LANES))
+                for head in range(pair * PAIR_HEADS, (pair + 1) * PAIR_HEADS)
+            ]
+            for cs in (lo, hi) if strip.start < HALF else (hi,):
+                total = gscores[strip, cs]
+                for which in range(PAIR_HEADS):
+                    head = pair * PAIR_HEADS + which
+                    place = strip_at(strip, which * GROUP)
+                    gap = cum_rows[head : head + 1, cs] - columns[which] + mask[strip, cs]
+                    factor = jnp.exp2(gap)
+                    factors[slot, place, cs] = (factor * scores[strip, cs]).astype(BF16)
+                    total = total + factor * grads[slot, place, cs]
+                gscores[strip, cs] = total
+
+        both[slot] = nn(factors[slot], first_ref[:, sl])
+        folds = [jnp.zeros((8, LANES), F32) for _ in range(6)]
+        for strip in STRIPS:
+            raw = jnp.where(first_head, both[slot, strip], both[slot, strip_at(strip, GROUP)])
+            value = values[slot, strip]
+            upstream = first_ref[strip, sl].astype(F32)
+            across = reads[strip, sl]
+            stepped = (value * fac[strip, sl]).astype(BF16).astype(F32)
+            balance = upstream * (mixed_ref[strip, sl] - skip * value) - stepped * raw
+            high = balance.astype(BF16)
+            sums[strip, sl] = high
+            sums[strip_at(strip, GROUP), sl] = (balance - high.astype(F32)).astype(BF16)
+            sums[strip_at(strip, 2 * GROUP), sl] = (value * raw).astype(BF16)
+            sums[strip_at(strip, 3 * GROUP), sl] = (value * across).astype(BF16)
+            grad = (
+                fac[strip, sl] * raw + fac[strip_at(strip, GROUP), sl] * across + skip * upstream
+            ) * slopes[slot, strip]
+            cext[strip, sl] = grad
+            folds[5] = folds[5] + fold_rows(upstream * value)
+            folds[4] = folds[4] + fold_rows(grad)
+            folds[3] = folds[3] + fold_rows(grad * shifted(strip, 0))
+            for offset in (1, 2, 3):
+                folds[3 - offset] = folds[3 - offset] + fold_rows(
+                    keep[offset - 1][strip] * grad * shifted(strip, offset)
+                )
+        for row in range(6):
+            conv_ref[row : row + 1, sl] += jnp.sum(folds[row], axis=0, keepdims=True)
+        for strip in STRIPS:
+            result = taps[3:4, :] * cext[strip, sl]
+            for offset in (1, 2, 3):
+                result = result + ahead[offset - 1][strip] * (
+                    taps[3 - offset : 4 - offset, :] * cext[strip_at(strip, offset), sl]
+                )
+            gip_ref[strip, sl] = result.astype(BF16)
 
     cext[GROUP : GROUP + 8, :] = cext[0:8, :]
     state = sprev_ref[...]
@@ -739,6 +789,8 @@
         self.bit = bit
 
     def step(self, *others):
+        if not self.left:
+            return
         came = after(self.came, *others) if others else self.came
         self.left.remove(self.bit)
         self.value = self.here.astype(F32) + came.astype(F32)
@@ -787,7 +839,7 @@
         return lax.ppermute(value, "tensor", swap)
 
     pieces = []
-    cuts = [0, GROUP // 4] + [GROUP * count for count in range(1, half_groups + 1)]
+    cuts = [0, half_rows // 6, half_rows * 7 // 12, half_rows]
     for begin, end in zip(cuts, cuts[1:]):
         piece = hidden_in[begin:end]
         pieces.append(exchange(after(piece, pieces[-1]) if pieces else piece))
@@ -864,6 +916,9 @@
             pltpu.VMEM((GROUP, GROUP), F32),
             pltpu.VMEM((GROUP, inner), BF16),
             pltpu.VMEM((2, PAIR_HEADS * GROUP, GROUP), BF16),
+            pltpu.VMEM((2, GROUP, LANES), F32),
+            pltpu.VMEM((2, GROUP, LANES), BF16),
+            pltpu.VMEM((2, PAIR_HEADS * GROUP, LANES), F32),
         ],
         compiler_params=params(),
         cost_estimate=cost(2),
@@ -974,6 +1029,11 @@
             pltpu.VMEM((GROUP, inner), BF16),
             pltpu.VMEM((4 * GROUP, inner), BF16),
             pltpu.VMEM((2, PAIR_HEADS * GROUP, GROUP), BF16),
+            pltpu.VMEM((2, GROUP, LANES), F32),
+            pltpu.VMEM((2, GROUP, LANES), F32),
+            pltpu.VMEM((2, PAIR_HEADS * GROUP, LANES), BF16),
+            pltpu.VMEM((2, PAIR_HEADS * GROUP, GROUP), F32),
+            pltpu.VMEM((2, PAIR_HEADS * GROUP, LANES), F32),
         ],
         compiler_params=params(),
         cost_estimate=cost(2),
@@ -1035,14 +1095,9 @@
     )
     normed_away = normed_part(1 - tensor_rank, grad_inner_low, BF16)
     normed_other = exchange(normed_away)
-    mix = mix_here + mix_other.astype(F32)
-    slot = tensor_rank * half_rows + jnp.arange(half_rows, dtype=jnp.int32)
-    valid_half = slot < jnp.sum(lengths[0])
-    hidden_wide = hidden_in.astype(F32)
-    block_out = (hidden_wide + jnp.where(valid_half[:, None], mix, 0.0)).astype(BF16)
-
+    inner_sum.step()
     vmem = pl.BlockSpec(memory_space=pltpu.VMEM)
-    kq_other = after(kq_other, normed_away)
+    kq_other = after(kq_other, normed_away, inner_sum.away)
     grad_state_low, rest_grads = pl.pallas_call(
         functools.partial(
             state_grad_kernel, shard=shard, state_shard=state_shard, heads=heads
@@ -1065,7 +1120,7 @@
     )
     rest_sum = HalvingSum(rest_grads, shard_rank, shard_count, True)
     rest_sum.start()
-    inner_sum.step()
+    inner_sum.step(rest_sum.away)
     normed_here = normed_part(
         tensor_rank, after(grad_inner_low, rest_sum.away, inner_sum.away), F32
     )
@@ -1076,6 +1131,13 @@
         if rest_sum.left:
             rest_sum.step(inner_sum.away, normed_other)
     inner_sum, rest_sum = inner_sum.value, rest_sum.value
+
+    mix = mix_here + after(mix_other, normed_here).astype(F32)
+    slot = tensor_rank * half_rows + jnp.arange(half_rows, dtype=jnp.int32)
+    valid_half = slot < jnp.sum(lengths[0])
+    hidden_wide = hidden_in.astype(F32)
+    block_out = (hidden_wide + jnp.where(valid_half[:, None], mix, 0.0)).astype(BF16)
+
 
     grad_normed = normed_here + normed_other.astype(F32)
     grad_normed = grad_normed + nt(

time: 325 us -> 307 us (0.945)
  waiting for transfers between devices: 78.5 us -> 54.5 us
    ppermute x12, waiting for transfers between devices: 59.6 us -> 40.4 us  [flip(): return lax.ppermute(value, 'dp', [(i, i ^ 1 << bit) for i in range(count)])]
    ppermute x10 -> x9, waiting for transfers between devices: 18.9 us -> 13.4 us  [exchange(): return lax.ppermute(value, 'tensor', swap)]
    ppermute x10 -> x9, starting transfers between devices: 13.6 us -> 11.2 us  [exchange(): return lax.ppermute(value, 'tensor', swap)]
    unnamed x45 -> x47, local copies, waits for them, and re-layouts: 7.08 us -> 6.44 us
  transfers between devices with their start and end apart: 24 -> 23, of which waited for: 13 -> 10; matrix products, arithmetic and copies ran while one was open for 11% -> 13% of each run, Pallas kernels for 34% -> 37%
where the time goes in v5:
time: 307 us; the launch traced here: 303 us
  Pallas kernels  147 us (48%)
  waiting for transfers between devices  54.5 us (18%)
  starting transfers between devices  26 us (8%)
  local copies, waits for them, and re-layouts  20.2 us (7%)
  matrix products  20.2 us (7%)
  other arithmetic  19.9 us (6%)
  between operations  15 us (5%)
    pallas_call x1, Pallas kernels, on_device(): pl.pallas_call(backward_kernel, grid=(groups,), in_specs=[SMEM_SPEC, pl.B...  48.6 us
    ppermute x12, waiting for transfers between devices, flip(): return lax.ppermute(value, 'dp', [(i, i ^ 1 << bit) for i in range(count)])  40.4 us
    pallas_call x1, Pallas kernels, on_device(): pl.pallas_call(functools.partial(forward_kernel, shard=shard, state_shard...  30.3 us
    pallas_call x1, Pallas kernels, on_device(): pl.pallas_call(gate_kernel, grid=(groups,), in_specs=[SMEM_SPEC, SMEM_SPE...  16.5 us
    pallas_call x2, Pallas kernels, normed_part(): pl.pallas_call(normed_grad_kernel, grid_spec=pltpu.PrefetchScalarGridSpec...  16.3 us
    ppermute x12, starting transfers between devices, flip(): return lax.ppermute(value, 'dp', [(i, i ^ 1 << bit) for i in range(count)])  14.7 us
    ppermute x9, waiting for transfers between devices, exchange(): return lax.ppermute(value, 'tensor', swap)  13.4 us
    pallas_call x1, Pallas kernels, on_device(): pl.pallas_call(functools.partial(gate_grad_kernel, inner_all=inner_all),...  13.4 us
  transfers between devices with their start and end apart: 23, of which 10 were waited for; matrix products, arithmetic and copies ran while one was open for 13% of the time, Pallas kernels for 37%

profile of v5, /device:TPU:0, one launch (start us, length us, event | category | flops | bytes accessed | tf_op | source)
XLA Modules:
  0.0 302.7 jit_solution(2865461140963737874)
XLA Ops:
  7.2 1.6 fusion.30
  9.6 1.4 copy.41.step_ref
  10.9 1.8 pack_small.1
  12.7 4.0 %collective-permute-start.4 = (bf16[64,1408]{1,0:T(8,128)(2,1)}, bf16[64,1408]{1,0:T(8,128)(2,1)S(1)}, u32[]{:S(2)}, u32[]{:S(2)}) collective-permute-start(bf16[64,1408]{1,0:T(8,128)(2,1)} %pack_small.1), channel_id=1, source_target_pairs={{0,16},{2,18},{4,20},{6,22},{8,24},{10,26},{12,28},{14,30},{16,0},... | collective-permute-start | bytes 540680 | tf_op jit(solution)/shard_map/ppermute | solution.py:751
  16.7 1.0 slice.32
  17.7 1.6 collective-permute-start
  19.3 6.0 %collective-permute-done.4 = bf16[64,1408]{1,0:T(8,128)(2,1)S(1)} collective-permute-done((bf16[64,1408]{1,0:T(8,128)(2,1)}, bf16[64,1408]{1,0:T(8,128)(2,1)S(1)}, u32[]{:S(2)}, u32[]{:S(2)}) %collective-permute-start.4) | collective-permute-done | bytes 180256 | tf_op jit(solution)/shard_map/ppermute | solution.py:751
  25.3 1.0 select_bitcast_fusion.7
  26.4 0.9 collective-permute-start.5
  27.3 0.7 pad_maximum_fusion.6
  28.0 0.9 fusion.29
  28.9 1.5 collective-permute-start.1
  30.4 5.6 %collective-permute-done.5 = bf16[2,64,1408]{2,1,0:T(8,128)(2,1)S(1)} collective-permute-done((bf16[2,64,1408]{2,1,0:T(8,128)(2,1)S(1)}, bf16[2,64,1408]{2,1,0:T(8,128)(2,1)S(1)}, u32[]{:S(2)}, u32[]{:S(2)}) %collective-permute-start.5) | collective-permute-done | bytes 360480 | tf_op jit(solution)/shard_map/ppermute | solution.py:751
  36.2 9.2 %collective-permute-done.1 = bf16[320,1024]{1,0:T(8,128)(2,1)} collective-permute-done((bf16[320,1024]{1,0:T(8,128)(2,1)S(1)}, bf16[320,1024]{1,0:T(8,128)(2,1)}, u32[]{:S(2)}, u32[]{:S(2)}) %collective-permute-start.1) | collective-permute-done | bytes 655392 | tf_op jit(solution)/shard_map/ppermute | solution.py:839
  45.5 1.6 collective-permute-start.6
  47.0 1.5 collective-permute-start.2
  48.5 16.7 %collective-permute-done.6 = bf16[2,2,64,1408]{3,2,0,1:T(8,128)(2,1)S(1)} collective-permute-done((bf16[2,2,64,1408]{3,2,0,1:T(8,128)(2,1)S(1)}, bf16[2,2,64,1408]{3,2,0,1:T(8,128)(2,1)S(1)}, u32[]{:S(2)}, u32[]{:S(2)}) %collective-permute-start.6) | collective-permute-done | bytes 720928 | tf_op jit(solution)/shard_map/ppermute | solution.py:751
  65.7 1.6 collective-permute-start.3
  68.0 2.5 pad_maximum_fusion.2.other_ref
  70.5 1.6 select_bitcast_fusion.1
  72.5 1.8 copy.42
  74.2 30.3 %mixer_forward.1 = (bf16[1536,1024]{1,0:T(8,128)(2,1)}, bf16[1024,1536]{1,0:T(8,128)(2,1)}, f32[1536,1024]{1,0:T(8,128)}, f32[1536,256]{1,0:T(8,128)}, bf16[1536...) custom-call(s32[1,1]{1,0:T(1,128)} %bitcast.rank_ref, ...), custom_call_target="tpu_custom_call" | custom-call | flops 2200000000 | tf_op jit(solution)/shard_map/mixer_forward/pallas_call | solution.py:884
  104.6 16.5 %gate_forward.1 = (f32[1536,1024]{1,0:T(8,128)}, f32[1536,1024]{1,0:T(8,128)}, bf16[1024,1536]{1,0:T(8,128)(2,1)}, f32[8,1536]{1,0:T(8,128)}) custom-call(s32[1,1]{1,0:T(1,128)} %bitcast.rank_ref, s32[1,4]{1,0:T(1,128)} %len_ref.7, bf16[768,1024]{1,0:T(8,128)(2,1)} %own_ref.3, bf16[768,1024]{1,0:T(8,128)(2,1)} %collective-permute-done.3.other_ref, ...), custom_call_target="tpu_custom_call" | custom-call | flops 17600000000 | tf_op jit(solution)/shard_map/gate_forward/pallas_call | solution.py:928
  121.3 4.2 %collective-permute-done.8.other_sums_ref = f32[8,1536]{1,0:T(8,128)S(1)} collective-permute-done((f32[8,1536]{1,0:T(8,128)}, f32[8,1536]{1,0:T(8,128)S(1)}, u32[]{:S(2)}, u32[]{:S(2)}) %collective-permute-start.8) | collective-permute-done | bytes 49184 | tf_op jit(solution)/shard_map/ppermute | solution.py:839
  126.1 13.4 %gate_backward.1 = (bf16[1536,1024]{1,0:T(8,128)(2,1)}, bf16[1536,1024]{1,0:T(8,128)(2,1)}, bf16[1536,1024]{1,0:T(8,128)(2,1)}, f32[8,1024]{1,0:T(8,128)}) custom-call(f32[8,1536]{1,0:T(8,128)} %get-tuple-element.83.own_sums_ref, f32[8,1536]{1,0:T(8,128)} %copy-done.18, f32[1536,1024]{1,0:T(8,128)} %get-tuple-element.84.gate_ref, ...), custom_call_target="tpu_custom_call" | custom-call | flops 14300000256 | tf_op jit(solution)/shard_map/gate_backward/pallas_call | solution.py:954
  139.5 5.7 %convolution_convert_fusion.1 = bf16[1024,1024]{1,0:T(8,128)(2,1)S(1)} fusion(bf16[1024,1536]{1,0:T(8,128)(2,1)S(1)} %copy-done.20, bf16[1536,1024]{1,0:T(8,128)(2,1)} %get-tuple-element.90), kind=kOutput, calls=%fused_computation.16 | convolution fusion | flops 3222274048 | bytes 8388608 | tf_op jit(solution)/shard_map/dot_general | solution.py:32
  145.2 3.6 %convolution_convert_fusion = bf16[1024,1024]{1,0:T(8,128)(2,1)S(1)} fusion(bf16[1024,1536]{1,0:T(8,128)(2,1)S(1)} %copy-done.3, bf16[1536,1024]{1,0:T(8,128)(2,1)S(1)} %copy-done.4), kind=kOutput, calls=%fused_computation.15 | convolution fusion | flops 3222274048 | bytes 8388608 | tf_op jit(solution)/shard_map/dot_general | solution.py:32
  148.8 2.4 pad_maximum_fusion
  151.2 3.9 %fusion.11 = bf16[768,1024]{1,0:T(8,128)(2,1)S(1)} fusion(bf16[1024,2048]{1,0:T(8,128)(2,1)} %all-gather.2.cloned.1.call-done.w_ref.proj_ref.w_gate_ref, bf16[1536,1024]{1,0:T(8,128)(2,1)} %get-tuple-element.90, s32[]{:T(128)S(6)} %select_n.118), kind=kOutput, calls=%fused_computation.21 | convolution fusion | flops 1611399168 | bytes 5242884 | tf_op jit(solution)/shard_map/dot_general | solution.py:36
  155.3 48.6 %mixer_backward.1 = (bf16[1536,1024]{1,0:T(8,128)(2,1)}, bf16[1536,256]{1,0:T(8,128)(2,1)}, bf16[1536,128]{1,0:T(8,128)(2,1)}, f32[8,1024]{1,0:T(8,128)}, f32[8,128]{1,0:T(8,128)}) custom-call(s32[1,4]{1,0:T(1,128)} %len_ref.7, f32[1536,1024]{1,0:T(8,128)} %get-tuple-element.91.ipre_ref.halo_ref, f32[1536,1024]{1,0:T(8,128)} %get-tuple-element.91.ipre_ref.halo_ref, ...), custom_call_target="tpu_custom_call" | custom-call | flops 2200000000 | tf_op jit(solution)/shard_map/mixer_backward/pallas_call | solution.py:986
  203.9 8.0 %inner_weight_grads.1 = bf16[1024,1024]{1,0:T(8,128)(2,1)} custom-call(bf16[1024,1536]{1,0:T(8,128)(2,1)} %get-tuple-element.88.left_ref.normed_t_ref, bf16[1536,1024]{1,0:T(8,128)(2,1)} %get-tuple-element.110.right_ref.inner_ref), custom_call_target="tpu_custom_call" | custom-call | tf_op jit(solution)/shard_map/inner_weight_grads/pallas_call | solution.py:1052
  212.0 1.8 constant_dynamic-slice_fusion.2
  213.9 2.1 constant_dynamic-slice_fusion.3
  216.0 1.9 collective-permute-start.10
  218.3 0.8 dynamic-slice_bitcast_fusion
  219.2 1.4 collective-permute-start.12
  221.2 0.7 copy.59
  222.6 0.8 slice.37
  224.1 8.1 %normed_grads.2 = bf16[768,1024]{1,0:T(8,128)(2,1)} custom-call(s32[1]{0:T(128)} %bitcast.22.begin_ref, bf16[1536,1024]{1,0:T(8,128)(2,1)} %get-tuple-element.89.gate_ref, bf16[1536,1024]{1,0:T(8,128)(2,1)} %get-tuple-element.110.right_ref.inner_ref, bf16[1536,128]{1,0:T(8,128)(2,1)} %get-tuple-element.101.step_ref.gstep_ref, ...), custom_call_target="tpu_custom_call" | custom-call | tf_op jit(solution)/shard_map/normed_grads/pallas_call | solution.py:1069
  232.2 1.4 collective-permute-start.13
  233.6 8.4 %state_backward.1 = (bf16[1536,256]{1,0:T(8,128)(2,1)}, bf16[1024,384]{1,0:T(8,128)(2,1)}) custom-call(s32[1,1]{1,0:T(1,128)} %bitcast.rank_ref, s32[1,4]{1,0:T(1,128)} %len_ref.7, bf16[784,256]{1,0:T(8,128)(2,1)} %get-tuple-element.176.own_ref, bf16[784,256]{1,0:T(8,128)(2,1)} %collective-permute-done.10.other_ref, ...), custom_call_target="tpu_custom_call" | custom-call | tf_op jit(solution)/shard_map/state_backward/pallas_call | solution.py:1101
  242.0 1.4 constant_dynamic-slice_fusion
  243.4 0.8 copy.71
  244.2 0.8 copy-done.10
  245.0 1.2 fusion.16
  246.3 0.9 collective-permute-start.14
  247.2 3.2 %fusion.9 = f32[768,1024]{1,0:T(8,128)S(1)} fusion(bf16[1024,2048]{1,0:T(8,128)(2,1)S(1)} %copy-done, bf16[1536,1024]{1,0:T(8,128)(2,1)} %get-tuple-element.90, s32[]{:T(128)S(6)} %select_n.117), kind=kOutput, calls=%fused_computation.19 | convolution fusion | flops 1610612736 | bytes 6815748 | tf_op jit(solution)/shard_map/dot_general | solution.py:36
  250.5 0.8 convert_bitcast_fusion
  251.3 8.1 %normed_grads.3 = f32[768,1024]{1,0:T(8,128)} custom-call(s32[1]{0:T(128)} %bitcast.19.begin_ref, bf16[1536,1024]{1,0:T(8,128)(2,1)} %get-tuple-element.89.gate_ref, bf16[1536,1024]{1,0:T(8,128)(2,1)} %get-tuple-element.110.right_ref.inner_ref, bf16[1536,128]{1,0:T(8,128)(2,1)} %get-tuple-element.101.step_ref.gstep_ref, ...), custom_call_target="tpu_custom_call" | custom-call | tf_op jit(solution)/shard_map/normed_grads/pallas_call | solution.py:1069
  259.4 1.2 fusion.22
  260.7 1.8 collective-permute-start.15
  262.6 1.3 collective-permute-start.17
  263.9 6.5 %collective-permute-done.15 = bf16[64,1024]{1,0:T(8,128)(2,1)S(1)} collective-permute-done((bf16[64,1024]{1,0:T(8,128)(2,1)S(1)}, bf16[64,1024]{1,0:T(8,128)(2,1)S(1)}, u32[]{:S(2)}, u32[]{:S(2)}) %collective-permute-start.15) | collective-permute-done | bytes 131104 | tf_op jit(solution)/shard_map/ppermute | solution.py:751
  270.4 0.7 convert_add_fusion.6.inner_ref
  271.9 1.3 collective-permute-start.18
  273.1 3.7 %fusion.1 = (f32[768]{0:T(1024)S(1)}, f32[768]{0:T(1024)S(1)}, f32[768,1024]{1,0:T(8,128)S(1)}) fusion(bf16[768,1024]{1,0:T(8,128)(2,1)S(1)} %copy-done.2, f32[1024]{0:T(1024)S(1)} %bitcast.117, bf16[1024,1408]{1,0:T(8,128)(2,1)} %bitcast.108, bf16[1536,256]{1,0:T(8,128)(2,1)S(1)} %copy-done.12, s32[]{:T(128)S(6)} %select_n.117, ...), kind=kOutput, calls=%fused_computation.6 | convolution fusion | flops 409729536 | bytes 10364932 | tf_op jit(solution)/shard_map/dot_general | solution.py:36
  276.9 2.1 collective-permute-done.18
  279.1 1.3 collective-permute-start.19
  280.4 2.8 collective-permute-done.19
  283.9 2.1 finish.1
  286.0 1.4 collective-permute-start.20
  287.3 4.4 %fusion.4 = (f32[768,1024]{1,0:T(8,128)}, bf16[768,1024]{1,0:T(8,128)(2,1)}) fusion(bf16[768,1024]{1,0:T(8,128)(2,1)S(1)} %copy-done.2, bf16[768,1024]{1,0:T(8,128)(2,1)} %own_ref.3, f32[768,1024]{1,0:T(8,128)S(1)} %get-tuple-element.187, f32[768]{0:T(1024)S(1)} %broadcast_multiply_fusion, f32[768]{0:T(1024)S(1)} %get-tuple-element.186, ...), kind=kLoop, calls=%fused_computation.9 | loop fusion | flops 9437184 | bytes 15738624 | tf_op jit(solution)/shard_map/add | solution.py:1150
  292.4 1.6 unpack_small.1
  294.0 1.4 copy.51
  (94 shorter events, 8.3 us)
Async XLA Ops:
  7.2 20.8 %copy-start.1 = (bf16[768,1024]{1,0:T(8,128)(2,1)S(1)}, bf16[768,1024]{1,0:T(8,128)(2,1)}, u32[]{:S(2)}) copy-start(bf16[768,1024]{1,0:T(8,128)(2,1)} %own_ref.2) | copy-start | bytes 4718596
  7.2 20.1 %copy-start.13 = (bf16[1024,64]{0,1:T(8,128)(2,1)S(1)}, bf16[1024,64]{0,1:T(8,128)(2,1)}, u32[]{:S(2)}) copy-start(bf16[1024,64]{0,1:T(8,128)(2,1)} %param.29) | copy-start | bytes 393220
  7.2 97.4 %all-gather.2.cloned.1.call-start = ((), (), s32[]{:S(2)}) async-start(), calls=%async_computation.1 | async-start | bytes 4456448 | tf_op jit(solution)/shard_map/all_gather | solution.py:869
  12.7 12.7 %collective-permute-start.4 = (bf16[64,1408]{1,0:T(8,128)(2,1)}, bf16[64,1408]{1,0:T(8,128)(2,1)S(1)}, u32[]{:S(2)}, u32[]{:S(2)}) collective-permute-start(bf16[64,1408]{1,0:T(8,128)(2,1)} %pack_small.1), channel_id=1, source_target_pairs={{0,16},{2,18},{4,20},{6,22},{8,24},{10,26},{12,28},{14,30},{16,0},... | collective-permute-start | bytes 540680 | tf_op jit(solution)/shard_map/ppermute | solution.py:751
  17.7 8.7 %collective-permute-start = (bf16[128,1024]{1,0:T(8,128)(2,1)S(1)}, bf16[128,1024]{1,0:T(8,128)(2,1)S(1)}, u32[]{:S(2)}, u32[]{:S(2)}) collective-permute-start(bf16[128,1024]{1,0:T(8,128)(2,1)S(1)} %slice.32), channel_id=1, source_target_pairs={{0,1},{1,0},{2,3},{3,2},{4,5},{5,4},{6,7},{7,6},{8,9},{9,8},{10,11... | collective-permute-start | bytes 786440 | tf_op jit(solution)/shard_map/ppermute | solution.py:839
  26.4 9.7 %collective-permute-start.5 = (bf16[2,64,1408]{2,1,0:T(8,128)(2,1)S(1)}, bf16[2,64,1408]{2,1,0:T(8,128)(2,1)S(1)}, u32[]{:S(2)}, u32[]{:S(2)}) collective-permute-start(bf16[2,64,1408]{2,1,0:T(8,128)(2,1)S(1)} %pad_maximum_fusion.5), channel_id=1, source_target_pairs={{0,8},{2,10},{4,12},{6,14},{8,0},{10,2},{12,4},{14,6},{16,24},{18,... | collective-permute-start | bytes 1081352 | tf_op jit(solution)/shard_map/ppermute | solution.py:751
  28.9 16.5 %collective-permute-start.1 = (bf16[320,1024]{1,0:T(8,128)(2,1)S(1)}, bf16[320,1024]{1,0:T(8,128)(2,1)}, u32[]{:S(2)}, u32[]{:S(2)}) collective-permute-start(bf16[320,1024]{1,0:T(8,128)(2,1)S(1)} %get-tuple-element.73), channel_id=1, source_target_pairs={{0,1},{1,0},{2,3},{3,2},{4,5},{5,4},{6,7},{7,6},{8,9},{9,8},{10,11... | collective-permute-start | bytes 1966088 | tf_op jit(solution)/shard_map/ppermute | solution.py:839
  36.2 29.4 %copy-start.15 = (bf16[16]{0:T(256)(128)(2,1)S(1)}, bf16[16]{0:T(256)(128)(2,1)}, u32[]{:S(2)}) copy-start(bf16[16]{0:T(256)(128)(2,1)} %param.26) | copy-start | bytes 100
  36.2 29.4 %copy-start.16 = (bf16[16]{0:T(256)(128)(2,1)S(1)}, bf16[16]{0:T(256)(128)(2,1)}, u32[]{:S(2)}) copy-start(bf16[16]{0:T(256)(128)(2,1)} %param.27) | copy-start | bytes 100
  36.2 29.4 %copy-start.6 = (bf16[768,1024]{1,0:T(8,128)(2,1)S(1)}, bf16[768,1024]{1,0:T(8,128)(2,1)}, u32[]{:S(2)}) copy-start(bf16[768,1024]{1,0:T(8,128)(2,1)} %own_ref.3) | copy-start | bytes 4718596
  36.2 31.0 %copy-start.19 = (bf16[16]{0:T(256)(128)(2,1)S(1)}, bf16[16]{0:T(256)(128)(2,1)}, u32[]{:S(2)}) copy-start(bf16[16]{0:T(256)(128)(2,1)} %param.25) | copy-start | bytes 100
  45.4 178.6 %reduce-scatter.2.cloned.1.call-start = ((), (), s32[]{:S(2)}) async-start(), calls=%async_computation.2 | async-start | bytes 4456448 | tf_op jit(solution)/shard_map/reduce_scatter | solution.py:979
  45.5 19.8 %collective-permute-start.6 = (bf16[2,2,64,1408]{3,2,0,1:T(8,128)(2,1)S(1)}, bf16[2,2,64,1408]{3,2,0,1:T(8,128)(2,1)S(1)}, u32[]{:S(2)}, u32[]{:S(2)}) collective-permute-start(bf16[2,2,64,1408]{3,2,0,1:T(8,128)(2,1)S(1)} %pad_maximum_fusion.4), channel_id=1, source_target_pairs={{0,4},{2,6},{4,0},{6,2},{8,12},{10,14},{12,8},{14,10},{16,20},{18,... | collective-permute-start | bytes 2162696 | tf_op jit(solution)/shard_map/ppermute | solution.py:751
  47.0 18.5 %collective-permute-start.2 = (bf16[320,1024]{1,0:T(8,128)(2,1)}, bf16[320,1024]{1,0:T(8,128)(2,1)S(1)}, u32[]{:S(2)}, u32[]{:S(2)}) collective-permute-start(bf16[320,1024]{1,0:T(8,128)(2,1)} %get-tuple-element.74), channel_id=1, source_target_pairs={{0,1},{1,0},{2,3},{3,2},{4,5},{5,4},{6,7},{7,6},{8,9},{9,8},{10,11... | collective-permute-start | bytes 1966088 | tf_op jit(solution)/shard_map/ppermute | solution.py:839
  65.5 1.7 copy-start.9
  65.5 5.0 %collective-permute-start.7 = (bf16[2,2,2,64,1408]{4,3,0,1,2:T(8,128)(2,1)S(1)}, bf16[2,2,2,64,1408]{4,3,0,1,2:T(8,128)(2,1)}, u32[]{:S(2)}, u32[]{:S(2)}) collective-permute-start(bf16[2,2,2,64,1408]{4,3,0,1,2:T(8,128)(2,1)S(1)} %pad_maximum_fusion.3), channel_id=1, source_target_pairs={{0,2},{2,0},{4,6},{6,4},{8,10},{10,8},{12,14},{14,12},{16,18},{18,... | collective-permute-start | bytes 4325384 | tf_op jit(solution)/shard_map/ppermute | solution.py:751
  65.7 38.9 %collective-permute-start.3 = (bf16[768,1024]{1,0:T(8,128)(2,1)S(1)}, bf16[768,1024]{1,0:T(8,128)(2,1)}, u32[]{:S(2)}, u32[]{:S(2)}) collective-permute-start(bf16[768,1024]{1,0:T(8,128)(2,1)S(1)} %copy-done.6), channel_id=1, source_target_pairs={{0,1},{1,0},{2,3},{3,2},{4,5},{5,4},{6,7},{7,6},{8,9},{9,8},{10,11... | collective-permute-start | bytes 4718600 | tf_op jit(solution)/shard_map/ppermute | solution.py:839
  121.2 4.4 %collective-permute-start.8 = (f32[8,1536]{1,0:T(8,128)}, f32[8,1536]{1,0:T(8,128)S(1)}, u32[]{:S(2)}, u32[]{:S(2)}) collective-permute-start(f32[8,1536]{1,0:T(8,128)} %get-tuple-element.83.own_sums_ref), channel_id=1, source_target_pairs={{0,1},{1,0},{2,3},{3,2},{4,5},{5,4},{6,7},{7,6},{8,9},{9,8},{10,11... | collective-permute-start | bytes 147464 | tf_op jit(solution)/shard_map/ppermute | solution.py:839
  125.5 0.6 copy-start.18
  126.1 13.4 %copy-start.20 = (bf16[1024,1536]{1,0:T(8,128)(2,1)S(1)}, bf16[1024,1536]{1,0:T(8,128)(2,1)}, u32[]{:S(2)}) copy-start(bf16[1024,1536]{1,0:T(8,128)(2,1)} %get-tuple-element.87) | copy-start | bytes 9437188
  139.5 5.7 %copy-start.3 = (bf16[1024,1536]{1,0:T(8,128)(2,1)S(1)}, bf16[1024,1536]{1,0:T(8,128)(2,1)}, u32[]{:S(2)}) copy-start(bf16[1024,1536]{1,0:T(8,128)(2,1)} %get-tuple-element.88.left_ref.normed_t_ref) | copy-start | bytes 9437188
  139.5 5.7 %copy-start.4 = (bf16[1536,1024]{1,0:T(8,128)(2,1)S(1)}, bf16[1536,1024]{1,0:T(8,128)(2,1)}, u32[]{:S(2)}) copy-start(bf16[1536,1024]{1,0:T(8,128)(2,1)} %get-tuple-element.89.gate_ref) | copy-start | bytes 9437188
  155.1 48.8 %collective-permute-start.9 = (bf16[768,1024]{1,0:T(8,128)(2,1)S(1)}, bf16[768,1024]{1,0:T(8,128)(2,1)S(1)}, u32[]{:S(2)}, u32[]{:S(2)}) collective-permute-start(bf16[768,1024]{1,0:T(8,128)(2,1)S(1)} %fusion.11), channel_id=1, source_target_pairs={{0,1},{1,0},{2,3},{3,2},{4,5},{5,4},{6,7},{7,6},{8,9},{9,8},{10,11... | collective-permute-start | bytes 4718600 | tf_op jit(solution)/shard_map/ppermute | solution.py:839
  203.9 8.0 %copy-start.7 = (bf16[768,1024]{1,0:T(8,128)(2,1)}, bf16[768,1024]{1,0:T(8,128)(2,1)S(1)}, u32[]{:S(2)}) copy-start(bf16[768,1024]{1,0:T(8,128)(2,1)S(1)} %collective-permute-done.9) | copy-start | bytes 4718596
  213.8 6.8 %copy-start.14 = (s32[1,4]{1,0:T(1,128)S(1)}, s32[1,4]{1,0:T(1,128)}, u32[]{:S(2)}) copy-start(s32[1,4]{1,0:T(1,128)} %len_ref.7) | copy-start | bytes 52
  213.8 7.4 %copy-start.5 = (bf16[64,2,1024]{2,1,0:T(2,128)(2,1)S(1)}, bf16[64,2,1024]{2,1,0:T(2,128)(2,1)}, u32[]{:S(2)}) copy-start(bf16[64,2,1024]{2,1,0:T(2,128)(2,1)} %param.18) | copy-start | bytes 786436
  213.8 4.1 %collective-permute-start.11 = (bf16[2,2,2,64,1024]{4,3,0,1,2:T(8,128)(2,1)S(1)}, bf16[2,2,2,64,1024]{4,3,0,1,2:T(8,128)(2,1)S(1)}, u32[]{:S(2)}, u32[]{:S(2)}) collective-permute-start(bf16[2,2,2,64,1024]{4,3,0,1,2:T(8,128)(2,1)S(1)} %bitcast.111), channel_id=1, source_target_pairs={{0,2},{2,0},{4,6},{6,4},{8,10},{10,8},{12,14},{14,12},{16,18},{18,... | collective-permute-start | bytes 3145736 | tf_op jit(solution)/shard_map/ppermute | solution.py:751
  216.0 17.6 %collective-permute-start.10 = (bf16[784,256]{1,0:T(8,128)(2,1)}, bf16[784,256]{1,0:T(8,128)(2,1)}, u32[]{:S(2)}, u32[]{:S(2)}) collective-permute-start(bf16[784,256]{1,0:T(8,128)(2,1)} %get-tuple-element.175), channel_id=1, source_target_pairs={{0,1},{1,0},{2,3},{3,2},{4,5},{5,4},{6,7},{7,6},{8,9},{9,8},{10,11... | collective-permute-start | bytes 1204232 | tf_op jit(solution)/shard_map/ppermute | solution.py:839
  219.2 25.0 %collective-permute-start.12 = (bf16[2,2,64,1024]{3,2,0,1:T(8,128)(2,1)}, bf16[2,2,64,1024]{3,2,0,1:T(8,128)(2,1)S(1)}, u32[]{:S(2)}, u32[]{:S(2)}) collective-permute-start(bf16[2,2,64,1024]{3,2,0,1:T(8,128)(2,1)} %dynamic-slice_bitcast_fusion), channel_id=1, source_target_pairs={{0,4},{2,6},{4,0},{6,2},{8,12},{10,14},{12,8},{14,10},{16,20},{18,... | collective-permute-start | bytes 1572872 | tf_op jit(solution)/shard_map/ppermute | solution.py:751
  232.2 39.6 %collective-permute-start.13 = (bf16[768,1024]{1,0:T(8,128)(2,1)}, bf16[768,1024]{1,0:T(8,128)(2,1)S(1)}, u32[]{:S(2)}, u32[]{:S(2)}) collective-permute-start(bf16[768,1024]{1,0:T(8,128)(2,1)} %normed_grads.2), channel_id=1, source_target_pairs={{0,1},{1,0},{2,3},{3,2},{4,5},{5,4},{6,7},{7,6},{8,9},{9,8},{10,11... | collective-permute-start | bytes 4718600 | tf_op jit(solution)/shard_map/ppermute | solution.py:839
  242.0 5.2 %copy-start = (bf16[1024,2048]{1,0:T(8,128)(2,1)S(1)}, bf16[1024,2048]{1,0:T(8,128)(2,1)}, u32[]{:S(2)}) copy-start(bf16[1024,2048]{1,0:T(8,128)(2,1)} %all-gather.2.cloned.1.call-done.w_ref.proj_ref.w_gate_ref) | copy-start | bytes 12582916
  244.2 0.8 copy-start.10
  246.3 4.2 %copy-start.11 = (bf16[64,2048]{1,0:T(8,128)(2,1)S(1)}, bf16[64,2048]{1,0:T(8,128)(2,1)}, u32[]{:S(2)}) copy-start(bf16[64,2048]{1,0:T(8,128)(2,1)} %reduce-scatter.2.cloned.1.call-done) | copy-start | bytes 786436
  246.3 13.2 %collective-permute-start.14 = (bf16[2,64,1024]{2,1,0:T(8,128)(2,1)S(1)}, bf16[2,64,1024]{2,1,0:T(8,128)(2,1)}, u32[]{:S(2)}, u32[]{:S(2)}) collective-permute-start(bf16[2,64,1024]{2,1,0:T(8,128)(2,1)S(1)} %dynamic-slice_bitcast_fusion.1), channel_id=1, source_target_pairs={{0,8},{2,10},{4,12},{6,14},{8,0},{10,2},{12,4},{14,6},{16,24},{18,... | collective-permute-start | bytes 786440 | tf_op jit(solution)/shard_map/ppermute | solution.py:751
  250.4 12.0 %collective-permute-start.16 = (bf16[2,2,2,64,384]{4,3,2,0,1:T(8,128)(2,1)}, bf16[2,2,2,64,384]{4,3,2,0,1:T(8,128)(2,1)S(1)}, u32[]{:S(2)}, u32[]{:S(2)}) collective-permute-start(bf16[2,2,2,64,384]{4,3,2,0,1:T(8,128)(2,1)} %bitcast.100), channel_id=1, source_target_pairs={{0,2},{2,0},{4,6},{6,4},{8,10},{10,8},{12,14},{14,12},{16,18},{18,... | collective-permute-start | bytes 1179656 | tf_op jit(solution)/shard_map/ppermute | solution.py:751
  259.4 13.7 %copy-start.2 = (bf16[768,1024]{1,0:T(8,128)(2,1)S(1)}, bf16[768,1024]{1,0:T(8,128)(2,1)}, u32[]{:S(2)}) copy-start(bf16[768,1024]{1,0:T(8,128)(2,1)} %own_ref.2) | copy-start | bytes 4718596
  259.4 13.7 %copy-start.12 = (bf16[1536,256]{1,0:T(8,128)(2,1)S(1)}, bf16[1536,256]{1,0:T(8,128)(2,1)}, u32[]{:S(2)}) copy-start(bf16[1536,256]{1,0:T(8,128)(2,1)} %get-tuple-element.112) | copy-start | bytes 2359300
  260.7 9.8 %collective-permute-start.15 = (bf16[64,1024]{1,0:T(8,128)(2,1)S(1)}, bf16[64,1024]{1,0:T(8,128)(2,1)S(1)}, u32[]{:S(2)}, u32[]{:S(2)}) collective-permute-start(bf16[64,1024]{1,0:T(8,128)(2,1)S(1)} %dynamic-slice_bitcast_fusion.3), channel_id=1, source_target_pairs={{0,16},{2,18},{4,20},{6,22},{8,24},{10,26},{12,28},{14,30},{16,0},... | collective-permute-start | bytes 393224 | tf_op jit(solution)/shard_map/ppermute | solution.py:751
  262.6 9.2 %collective-permute-start.17 = (bf16[2,2,64,384]{3,2,1,0:T(8,128)(2,1)S(1)}, bf16[2,2,64,384]{3,2,1,0:T(8,128)(2,1)S(1)}, u32[]{:S(2)}, u32[]{:S(2)}) collective-permute-start(bf16[2,2,64,384]{3,2,1,0:T(8,128)(2,1)S(1)} %dynamic-slice_bitcast_fusion.2), channel_id=1, source_target_pairs={{0,8},{2,10},{4,12},{6,14},{8,0},{10,2},{12,4},{14,6},{16,24},{18,... | collective-permute-start | bytes 589832 | tf_op jit(solution)/shard_map/ppermute | solution.py:751
  271.8 1.4 copy-start.8
  271.9 7.2 %collective-permute-start.18 = (bf16[2,64,384]{2,1,0:T(8,128)(2,1)S(1)}, bf16[2,64,384]{2,1,0:T(8,128)(2,1)S(1)}, u32[]{:S(2)}, u32[]{:S(2)}) collective-permute-start(bf16[2,64,384]{2,1,0:T(8,128)(2,1)S(1)} %dynamic-slice_bitcast_fusion.4), channel_id=1, source_target_pairs={{0,16},{2,18},{4,20},{6,22},{8,24},{10,26},{12,28},{14,30},{16,0},... | collective-permute-start | bytes 294920 | tf_op jit(solution)/shard_map/ppermute | solution.py:751
  279.1 4.2 %collective-permute-start.19 = (bf16[64,384]{1,0:T(8,128)(2,1)S(1)}, bf16[64,384]{1,0:T(8,128)(2,1)S(1)}, u32[]{:S(2)}, u32[]{:S(2)}) collective-permute-start(bf16[64,384]{1,0:T(8,128)(2,1)S(1)} %dynamic-slice_bitcast_fusion.5), channel_id=1, source_target_pairs={{0,4},{2,6},{4,0},{6,2},{8,12},{10,14},{12,8},{14,10},{16,20},{18,... | collective-permute-start | bytes 147464 | tf_op jit(solution)/shard_map/ppermute | solution.py:751
  286.0 5.8 %collective-permute-start.20 = (f32[64,384]{1,0:T(8,128)}, f32[64,384]{1,0:T(8,128)S(1)}, u32[]{:S(2)}, u32[]{:S(2)}) collective-permute-start(f32[64,384]{1,0:T(8,128)} %get-tuple-element.118.own_ref), channel_id=1, source_target_pairs={{0,1},{1,0},{2,3},{3,2},{4,5},{5,4},{6,7},{7,6},{8,9},{9,8},{10,11... | collective-permute-start | bytes 294920 | tf_op jit(solution)/shard_map/ppermute | solution.py:839
  291.7 0.7 copy-start.17
Sparse Core Ops, SparseCore 0:
  45.5 54.0 all-gather.1
  151.4 72.6 reduce-scatter.1

commit v6 on v4

--- a/solution.py
+++ b/solution.py
@@ -195,7 +195,7 @@
     rank_ref, len_ref, own_ref, other_ref, w_ref, head_ref,
     normed_ref, normed_t_ref, ipre_ref, spre_ref, sact_ref, stepin_ref, mixed_ref, sprev_ref,
     rows_ref, taps_ref,
-    ext, state, spread, lower, fac, read, mask, scores, weighted, factors, *, shard, state_shard,
+    ext, state, spread, lower, fac, read, mask, scores, weighted, *, shard, state_shard,
 ):
     inner = rows_ref.shape[1]
     channels = ext.shape[1]
@@ -211,7 +211,6 @@
         state[...] = jnp.zeros_like(state)
         spread[...] = spread_matrix(heads, LANES // PAIR_HEADS)
         lower[...] = lower_matrix()
-        factors[...] = jnp.zeros_like(factors)
         packed = w_ref[:, channels:].astype(F32).T
         base = 3 * heads
         rows_ref[0:7, :] = packed[base : base + 7, :]
@@ -276,30 +275,37 @@
     sprev_ref[...] = held
     read[...] = nn(queries, held)
 
-    first_head = lax.broadcasted_iota(jnp.int32, (1, LANES), 1) < LANES // PAIR_HEADS
-    lo, hi = slice(0, HALF), slice(HALF, GROUP)
+    masks = head_masks()
     for pair in range(inner // LANES):
         sl = slice(pair * LANES, (pair + 1) * LANES)
         total = conv(sl, rows_ref[ROW_TAP : ROW_TAP + 4, sl], rows_ref[ROW_BIAS : ROW_BIAS + 1, sl])
         values = (total * sigmoid(total)).astype(BF16).astype(F32)
-        stepped = (values * fac[0:GROUP, sl]).astype(BF16)
+        stepped = values * fac[0:GROUP, sl]
         weighted[:, sl] = (values * fac[GROUP : 2 * GROUP, sl]).astype(BF16)
-        slot = pair % 2
+        top, bottom, low_values, high_values = [], [], [], []
         for which in range(PAIR_HEADS):
             head = pair * PAIR_HEADS + which
             column = cum[:, head : head + 1]
             row = cum_rows[head : head + 1, :]
-            for rs, cs in ((lo, lo), (hi, lo), (hi, hi)):
+
+            def factor(rs, cs):
                 gap = column[rs] - row[:, cs] + mask[rs, cs]
-                place = slice(which * GROUP + rs.start, which * GROUP + rs.stop)
-                factors[slot, place, cs] = (jnp.exp2(gap) * scores[rs, cs]).astype(BF16)
-        both = nn(factors[slot], stepped)
-        within = jnp.where(first_head, both[:GROUP], both[GROUP:])
-        mixed_ref[:, sl] = (
-            within
-            + fac[2 * GROUP : 3 * GROUP, sl] * read[:, sl]
-            + rows_ref[ROW_SKIP : ROW_SKIP + 1, sl] * values
+                return (jnp.exp2(gap) * scores[rs, cs]).astype(BF16)
+
+            lo, hi = slice(0, HALF), slice(HALF, GROUP)
+            top.append(factor(lo, lo))
+            bottom.append(factor(hi, lo))
+            bottom.append(factor(hi, hi))
+            masked = (stepped * masks[which]).astype(BF16)
+            low_values.append(masked[:HALF])
+            high_values.append(masked)
+        upper_part = nn(jnp.concatenate(top, axis=1), jnp.concatenate(low_values, axis=0))
+        lower_part = nn(jnp.concatenate(bottom, axis=1), jnp.concatenate(high_values, axis=0))
+        rest = fac[2 * GROUP : 3 * GROUP, sl] * read[:, sl] + (
+            rows_ref[ROW_SKIP : ROW_SKIP + 1, sl] * values
         )
+        mixed_ref[0:HALF, sl] = upper_part + rest[:HALF]
+        mixed_ref[HALF:GROUP, sl] = lower_part + rest[HALF:]
 
     state[...] = fac[3 * GROUP : 3 * GROUP + 1, :] * state[...] + tn(keys, weighted[...])
     ext[0:8, :] = ext[GROUP : GROUP + 8, :]
@@ -352,21 +358,27 @@
     inv_all = lax.rsqrt(columns[:, 0:1] / inner_all + NORM_EPS)
     slope_all = inv_all * inv_all * inv_all * columns[:, 4:5] / inner_all
     gain = rows_ref[ROW_GATE : ROW_GATE + 1, :]
-    total = jnp.zeros((1, gate_ref.shape[1]), F32)
-    for part in range(8):
-        sl = slice(part * 32, part * 32 + 32)
-        inv, slope = inv_all[sl], slope_all[sl]
-        gate, gol, mixed = gate_ref[sl, :], gol_ref[sl, :], mixed_ref[sl, :]
-        logistic = sigmoid(gate)
-        silu = gate * logistic
-        gated = mixed * silu
-        scaled = gated * inv
-        low_ref[sl, :] = (scaled * gain).astype(BF16)
-        total = total + jnp.sum(gol * scaled, axis=0, keepdims=True)
-        grad = inv * (gol * gain) - gated * slope
-        first_ref[sl, :] = (grad * silu).astype(BF16)
-        ggp_ref[sl, :] = (grad * mixed * (logistic * (1.0 + gate * (1.0 - logistic)))).astype(BF16)
-    gain_ref[0:1, :] += total
+    for part in range(gate_ref.shape[1] // GROUP):
+        sl = slice(part * GROUP, (part + 1) * GROUP)
+        gain_row = gain[:, sl]
+        total = jnp.zeros((8, GROUP), F32)
+        for at in range(0, GROUP, 16):
+            strip = slice(at, at + 16)
+            inv, slope = inv_all[strip], slope_all[strip]
+            gate, gol, mixed = gate_ref[strip, sl], gol_ref[strip, sl], mixed_ref[strip, sl]
+            logistic = sigmoid(gate)
+            silu = gate * logistic
+            gated = mixed * silu
+            scaled = gated * inv
+            low_ref[strip, sl] = (scaled * gain_row).astype(BF16)
+            product = gol * scaled
+            total = total + product[0:8] + product[8:16]
+            grad = inv * (gol * gain_row) - gated * slope
+            first_ref[strip, sl] = (grad * silu).astype(BF16)
+            ggp_ref[strip, sl] = (
+                grad * mixed * (logistic * (1.0 + gate * (1.0 - logistic)))
+            ).astype(BF16)
+        gain_ref[0:1, sl] += jnp.sum(total, axis=0, keepdims=True)
 
 
 def product_kernel(left_ref, right_ref, out_ref):
@@ -385,7 +397,7 @@
     rows_ref, head_ref,
     gip_ref, gkq_ref, gstep_ref, conv_ref, heads_ref,
     ext, cext, gstate, spread, collect, lower, upper, fac, reads, mask, scores, gscores,
-    weighted, entered, sums, factors,
+    weighted, entered, sums,
 ):
     inner = rows_ref.shape[1]
     heads = inner // (LANES // PAIR_HEADS)
@@ -403,7 +415,6 @@
         collect[...] = collect_matrix(heads, LANES // PAIR_HEADS)
         lower[...] = lower_matrix()
         upper[...] = lower_matrix(upper=True)
-        factors[...] = jnp.zeros_like(factors)
         conv_ref[...] = jnp.zeros_like(conv_ref)
         heads_ref[...] = jnp.zeros_like(heads_ref)
 
@@ -433,7 +444,6 @@
     reads[...] = nn(keys, held)
 
     masks = head_masks()
-    first_head = lax.broadcasted_iota(jnp.int32, (1, LANES), 1) < LANES // PAIR_HEADS
     lo, hi = slice(0, HALF), slice(HALF, GROUP)
     for pair in range(inner // LANES):
         sl = slice(pair * LANES, (pair + 1) * LANES)
@@ -454,25 +464,42 @@
         upstream_wide = upstream.astype(F32)
         entered[:, sl] = (upstream_wide * fac[2 * GROUP : 3 * GROUP, sl]).astype(BF16)
 
-        slot = pair % 2
-        split = [(values * step_wide * one).astype(BF16) for one in masks]
-        grads = nn(jnp.concatenate(split, axis=0), upstream.T)
-        blocks = [None, None, None]
+        top, bottom, top_grads, low_grads = [], [], [], []
+        g00 = g01 = g11 = None
+        split_up = [(upstream_wide * one).astype(BF16) for one in masks]
+        grads_low = nt(stepped[HALF:], jnp.concatenate([one[HALF:] for one in split_up], axis=0))
         for which in range(PAIR_HEADS):
             head = pair * PAIR_HEADS + which
             column = cum[:, head : head + 1]
             row = cum_rows[head : head + 1, :]
-            for index, (rs, cs) in enumerate(((lo, lo), (lo, hi), (hi, hi))):
-                factor = jnp.exp2(row[:, cs] - column[rs] + mask[rs, cs])
-                place = slice(which * GROUP + rs.start, which * GROUP + rs.stop)
-                factors[slot, place, cs] = (factor * scores[rs, cs]).astype(BF16)
-                part = factor * grads[place, cs]
-                blocks[index] = part if blocks[index] is None else blocks[index] + part
-        gscores[lo, lo] += blocks[0]
-        gscores[lo, hi] += blocks[1]
-        gscores[hi, hi] += blocks[2]
-        both = nn(factors[slot], upstream)
-        raw = jnp.where(first_head, both[:GROUP], both[GROUP:])
+            masked = split_up[which]
+            grads_top = nt(stepped[:HALF], masked)
+
+            def factors(rs, cs, grads):
+                gap = row[:, cs] - column[rs] + mask[rs, cs]
+                factor = jnp.exp2(gap)
+                return (factor * scores[rs, cs]).astype(BF16), factor * grads
+
+            a00, d00 = factors(lo, lo, grads_top[:, lo])
+            a01, d01 = factors(lo, hi, grads_top[:, hi])
+            a11, d11 = factors(hi, hi, grads_low[:, which * HALF : (which + 1) * HALF])
+            g00 = d00 if g00 is None else g00 + d00
+            g01 = d01 if g01 is None else g01 + d01
+            g11 = d11 if g11 is None else g11 + d11
+            top.extend([a00, a01])
+            bottom.append(a11)
+            top_grads.append(masked)
+            low_grads.append(masked[HALF:])
+        gscores[lo, lo] += g00
+        gscores[lo, hi] += g01
+        gscores[hi, hi] += g11
+        raw = jnp.concatenate(
+            [
+                nn(jnp.concatenate(top, axis=1), jnp.concatenate(top_grads, axis=0)),
+                nn(jnp.concatenate(bottom, axis=1), jnp.concatenate(low_grads, axis=0)),
+            ],
+            axis=0,
+        )
         skip = rows_ref[ROW_SKIP : ROW_SKIP + 1, sl]
         across = reads[:, sl]
 
@@ -739,6 +766,8 @@
         self.bit = bit
 
     def step(self, *others):
+        if not self.left:
+            return
         came = after(self.came, *others) if others else self.came
         self.left.remove(self.bit)
         self.value = self.here.astype(F32) + came.astype(F32)
@@ -787,7 +816,7 @@
         return lax.ppermute(value, "tensor", swap)
 
     pieces = []
-    cuts = [0, GROUP // 4] + [GROUP * count for count in range(1, half_groups + 1)]
+    cuts = [0, half_rows // 6, half_rows * 5 // 12, half_rows]
     for begin, end in zip(cuts, cuts[1:]):
         piece = hidden_in[begin:end]
         pieces.append(exchange(after(piece, pieces[-1]) if pieces else piece))
@@ -863,7 +892,6 @@
             pltpu.VMEM((GROUP, GROUP), F32),
             pltpu.VMEM((GROUP, GROUP), F32),
             pltpu.VMEM((GROUP, inner), BF16),
-            pltpu.VMEM((2, PAIR_HEADS * GROUP, GROUP), BF16),
         ],
         compiler_params=params(),
         cost_estimate=cost(2),
@@ -926,7 +954,6 @@
     mix_away = nt(rows_of(out_low, 1 - tensor_rank), w_out).astype(BF16)
     grad_first = after(grad_first, mix_away)
     mix_other = exchange(mix_away)
-    mix_here = nt(rows_of(out_low, tensor_rank), w_out)
     last = groups - 1
     grad_inner_low, grad_kq, grad_step_low, conv_rows, head_sums = pl.pallas_call(
         backward_kernel,
@@ -973,7 +1000,6 @@
             pltpu.VMEM((GROUP, inner), BF16),
             pltpu.VMEM((GROUP, inner), BF16),
             pltpu.VMEM((4 * GROUP, inner), BF16),
-            pltpu.VMEM((2, PAIR_HEADS * GROUP, GROUP), BF16),
         ],
         compiler_params=params(),
         cost_estimate=cost(2),
@@ -1035,14 +1061,9 @@
     )
     normed_away = normed_part(1 - tensor_rank, grad_inner_low, BF16)
     normed_other = exchange(normed_away)
-    mix = mix_here + mix_other.astype(F32)
-    slot = tensor_rank * half_rows + jnp.arange(half_rows, dtype=jnp.int32)
-    valid_half = slot < jnp.sum(lengths[0])
-    hidden_wide = hidden_in.astype(F32)
-    block_out = (hidden_wide + jnp.where(valid_half[:, None], mix, 0.0)).astype(BF16)
-
+    inner_sum.step()
     vmem = pl.BlockSpec(memory_space=pltpu.VMEM)
-    kq_other = after(kq_other, normed_away)
+    kq_other = after(kq_other, normed_away, inner_sum.away)
     grad_state_low, rest_grads = pl.pallas_call(
         functools.partial(
             state_grad_kernel, shard=shard, state_shard=state_shard, heads=heads
@@ -1065,17 +1086,25 @@
     )
     rest_sum = HalvingSum(rest_grads, shard_rank, shard_count, True)
     rest_sum.start()
-    inner_sum.step()
+    inner_sum.step(rest_sum.away)
     normed_here = normed_part(
         tensor_rank, after(grad_inner_low, rest_sum.away, inner_sum.away), F32
     )
     rest_sum.step(inner_sum.away, normed_here)
+    gap = rest_sum.away
+    inner_sum.step(gap, normed_other)
     while inner_sum.left or rest_sum.left:
-        if inner_sum.left:
-            inner_sum.step()
-        if rest_sum.left:
-            rest_sum.step(inner_sum.away, normed_other)
+        rest_sum.step(inner_sum.away)
+        inner_sum.step()
     inner_sum, rest_sum = inner_sum.value, rest_sum.value
+
+    mix_here = nt(rows_of(after(out_low, gap), tensor_rank), w_out)
+    mix = mix_here + after(mix_other, gap).astype(F32)
+    slot = tensor_rank * half_rows + jnp.arange(half_rows, dtype=jnp.int32)
+    valid_half = slot < jnp.sum(lengths[0])
+    hidden_wide = hidden_in.astype(F32)
+    block_out = (hidden_wide + jnp.where(valid_half[:, None], mix, 0.0)).astype(BF16)
+
 
     grad_normed = normed_here + normed_other.astype(F32)
     grad_normed = grad_normed + nt(

time: 325 us -> 297 us (0.914)
  waiting for transfers between devices: 78.5 us -> 53 us
    ppermute x12, waiting for transfers between devices: 59.6 us -> 35.6 us  [flip(): return lax.ppermute(value, 'dp', [(i, i ^ 1 << bit) for i in range(count)])]
    ppermute x10 -> x9, waiting for transfers between devices: 18.9 us -> 11.6 us  [exchange(): return lax.ppermute(value, 'tensor', swap)]
    reduce_scatter x1, waiting for transfers between devices: 0.02 us -> 5.8 us  [on_device(): lax.psum_scatter(first_grads, 'dp', scatter_dimension=0, tiled=True)]
    ppermute x10 -> x9, starting transfers between devices: 13.6 us -> 13 us  [exchange(): return lax.ppermute(value, 'tensor', swap)]
  transfers between devices with their start and end apart: 24 -> 23, of which waited for: 13 -> 11; matrix products, arithmetic and copies ran while one was open for 11% -> 13% of each run, Pallas kernels for 34% -> 36%
where the time goes in v6:
time: 297 us; the launch traced here: 296 us
  Pallas kernels  142 us (48%)
  waiting for transfers between devices  53 us (18%)
  starting transfers between devices  27.8 us (9%)
  matrix products  20.6 us (7%)
  other arithmetic  19.4 us (7%)
  local copies, waits for them, and re-layouts  18.4 us (6%)
  between operations  14.5 us (5%)
    pallas_call x1, Pallas kernels, on_device(): pl.pallas_call(backward_kernel, grid=(groups,), in_specs=[SMEM_SPEC, pl.B...  46.3 us
    ppermute x12, waiting for transfers between devices, flip(): return lax.ppermute(value, 'dp', [(i, i ^ 1 << bit) for i in range(count)])  35.6 us
    pallas_call x1, Pallas kernels, on_device(): pl.pallas_call(functools.partial(forward_kernel, shard=shard, state_shard...  28.1 us
    pallas_call x1, Pallas kernels, on_device(): pl.pallas_call(gate_kernel, grid=(groups,), in_specs=[SMEM_SPEC, SMEM_SPE...  16.6 us
    pallas_call x2, Pallas kernels, normed_part(): pl.pallas_call(normed_grad_kernel, grid_spec=pltpu.PrefetchScalarGridSpec...  16.2 us
    ppermute x12, starting transfers between devices, flip(): return lax.ppermute(value, 'dp', [(i, i ^ 1 << bit) for i in range(count)])  14.7 us
    pallas_call x1, Pallas kernels, on_device(): pl.pallas_call(functools.partial(gate_grad_kernel, inner_all=inner_all),...  13.3 us
    ppermute x9, starting transfers between devices, exchange(): return lax.ppermute(value, 'tensor', swap)  13 us
  transfers between devices with their start and end apart: 23, of which 11 were waited for; matrix products, arithmetic and copies ran while one was open for 13% of the time, Pallas kernels for 36%

profile of v6, /device:TPU:0, one launch (start us, length us, event | category | flops | bytes accessed | tf_op | source)
XLA Modules:
  0.0 296.0 jit_solution(550709431172873669)
XLA Ops:
  7.2 1.6 fusion.29
  9.5 1.4 copy.41.step_ref
  10.9 1.8 pack_small.1
  12.7 4.0 %collective-permute-start.4 = (bf16[64,1408]{1,0:T(8,128)(2,1)}, bf16[64,1408]{1,0:T(8,128)(2,1)S(1)}, u32[]{:S(2)}, u32[]{:S(2)}) collective-permute-start(bf16[64,1408]{1,0:T(8,128)(2,1)} %pack_small.1), channel_id=1, source_target_pairs={{0,16},{2,18},{4,20},{6,22},{8,24},{10,26},{12,28},{14,30},{16,0},... | collective-permute-start | bytes 540680 | tf_op jit(solution)/shard_map/ppermute | solution.py:728
  16.7 1.0 slice.32
  17.7 1.6 collective-permute-start
  19.3 6.1 %collective-permute-done.4 = bf16[64,1408]{1,0:T(8,128)(2,1)S(1)} collective-permute-done((bf16[64,1408]{1,0:T(8,128)(2,1)}, bf16[64,1408]{1,0:T(8,128)(2,1)S(1)}, u32[]{:S(2)}, u32[]{:S(2)}) %collective-permute-start.4) | collective-permute-done | bytes 180256 | tf_op jit(solution)/shard_map/ppermute | solution.py:728
  25.3 1.0 select_bitcast_fusion.7
  26.4 0.9 collective-permute-start.5
  28.1 1.5 collective-permute-start.1
  29.6 6.4 %collective-permute-done.5 = bf16[2,64,1408]{2,1,0:T(8,128)(2,1)S(1)} collective-permute-done((bf16[2,64,1408]{2,1,0:T(8,128)(2,1)S(1)}, bf16[2,64,1408]{2,1,0:T(8,128)(2,1)S(1)}, u32[]{:S(2)}, u32[]{:S(2)}) %collective-permute-start.5) | collective-permute-done | bytes 360480 | tf_op jit(solution)/shard_map/ppermute | solution.py:728
  36.2 2.8 collective-permute-done.1
  39.0 1.6 collective-permute-start.6
  40.7 1.6 collective-permute-start.2
  42.3 16.6 %collective-permute-done.6 = bf16[2,2,64,1408]{3,2,0,1:T(8,128)(2,1)} collective-permute-done((bf16[2,2,64,1408]{3,2,0,1:T(8,128)(2,1)S(1)}, bf16[2,2,64,1408]{3,2,0,1:T(8,128)(2,1)}, u32[]{:S(2)}, u32[]{:S(2)}) %collective-permute-start.6) | collective-permute-done | bytes 720928 | tf_op jit(solution)/shard_map/ppermute | solution.py:728
  58.9 1.2 select_bitcast_fusion.3
  60.3 1.4 collective-permute-done.2
  61.7 1.6 collective-permute-start.3
  64.0 2.5 pad_maximum_fusion.2.other_ref
  67.1 1.8 copy.42
  68.9 28.1 %mixer_forward.1 = (bf16[1536,1024]{1,0:T(8,128)(2,1)}, bf16[1024,1536]{1,0:T(8,128)(2,1)}, f32[1536,1024]{1,0:T(8,128)}, f32[1536,256]{1,0:T(8,128)}, bf16[1536...) custom-call(s32[1,1]{1,0:T(1,128)} %bitcast.rank_ref, ...), custom_call_target="tpu_custom_call" | custom-call | flops 2200000000 | tf_op jit(solution)/shard_map/mixer_forward/pallas_call | solution.py:861
  97.0 1.9 collective-permute-done.3.other_ref
  98.9 16.6 %gate_forward.1 = (f32[1536,1024]{1,0:T(8,128)}, f32[1536,1024]{1,0:T(8,128)}, bf16[1024,1536]{1,0:T(8,128)(2,1)}, f32[8,1536]{1,0:T(8,128)}) custom-call(s32[1,1]{1,0:T(1,128)} %bitcast.rank_ref, s32[1,4]{1,0:T(1,128)} %len_ref.7, bf16[768,1024]{1,0:T(8,128)(2,1)} %own_ref.3, bf16[768,1024]{1,0:T(8,128)(2,1)} %collective-permute-done.3.other_ref, ...), custom_call_target="tpu_custom_call" | custom-call | flops 17600000000 | tf_op jit(solution)/shard_map/gate_forward/pallas_call | solution.py:901
  115.4 1.6 collective-permute-start.8
  117.0 2.8 collective-permute-done.8.other_sums_ref
  120.4 13.3 %gate_backward.1 = (bf16[1536,1024]{1,0:T(8,128)(2,1)}, bf16[1536,1024]{1,0:T(8,128)(2,1)}, bf16[1536,1024]{1,0:T(8,128)(2,1)}, f32[8,1024]{1,0:T(8,128)}) custom-call(f32[8,1536]{1,0:T(8,128)} %get-tuple-element.85.own_sums_ref, f32[8,1536]{1,0:T(8,128)} %copy-done.17, f32[1536,1024]{1,0:T(8,128)} %get-tuple-element.86.gate_ref, ...), custom_call_target="tpu_custom_call" | custom-call | flops 14300000256 | tf_op jit(solution)/shard_map/gate_backward/pallas_call | solution.py:927
  133.8 5.7 %convolution_convert_fusion.1 = bf16[1024,1024]{1,0:T(8,128)(2,1)S(1)} fusion(bf16[1024,1536]{1,0:T(8,128)(2,1)S(1)} %copy-done.19, bf16[1536,1024]{1,0:T(8,128)(2,1)} %get-tuple-element.114), kind=kOutput, calls=%fused_computation.16 | convolution fusion | flops 3222274048 | bytes 8388608 | tf_op jit(solution)/shard_map/dot_general | solution.py:29
  139.5 3.6 %convolution_convert_fusion = bf16[1024,1024]{1,0:T(8,128)(2,1)S(1)} fusion(bf16[1024,1536]{1,0:T(8,128)(2,1)S(1)} %copy-done.3, bf16[1536,1024]{1,0:T(8,128)(2,1)S(1)} %copy-done.5), kind=kOutput, calls=%fused_computation.15 | convolution fusion | flops 3222274048 | bytes 8388608 | tf_op jit(solution)/shard_map/dot_general | solution.py:29
  143.1 2.4 pad_maximum_fusion
  145.5 3.9 %fusion.11 = bf16[768,1024]{1,0:T(8,128)(2,1)S(1)} fusion(bf16[1024,2048]{1,0:T(8,128)(2,1)} %all-gather.2.cloned.1.call-done.w_ref.proj_ref.w_gate_ref, bf16[1536,1024]{1,0:T(8,128)(2,1)} %get-tuple-element.114, s32[]{:T(128)S(6)} %select_n.117), kind=kOutput, calls=%fused_computation.21 | convolution fusion | flops 1611399168 | bytes 5242884 | tf_op jit(solution)/shard_map/dot_general | solution.py:33
  149.4 1.6 collective-permute-start.10
  151.0 46.3 %mixer_backward.1 = (bf16[1536,1024]{1,0:T(8,128)(2,1)}, bf16[1536,256]{1,0:T(8,128)(2,1)}, bf16[1536,128]{1,0:T(8,128)(2,1)}, f32[8,1024]{1,0:T(8,128)}, f32[8,128]{1,0:T(8,128)}) custom-call(s32[1,4]{1,0:T(1,128)} %len_ref.7, f32[1536,1024]{1,0:T(8,128)} %get-tuple-element.93.ipre_ref.halo_ref, f32[1536,1024]{1,0:T(8,128)} %get-tuple-element.93.ipre_ref.halo_ref, ...), custom_call_target="tpu_custom_call" | custom-call | flops 2200000000 | tf_op jit(solution)/shard_map/mixer_backward/pallas_call | solution.py:958
  197.3 8.0 %inner_weight_grads.1 = bf16[1024,1024]{1,0:T(8,128)(2,1)} custom-call(bf16[1024,1536]{1,0:T(8,128)(2,1)} %get-tuple-element.90.left_ref.normed_t_ref, bf16[1536,1024]{1,0:T(8,128)(2,1)} %get-tuple-element.112.right_ref.inner_ref), custom_call_target="tpu_custom_call" | custom-call | tf_op jit(solution)/shard_map/inner_weight_grads/pallas_call | solution.py:1018
  205.3 1.8 constant_dynamic-slice_fusion.2
  207.2 2.1 constant_dynamic-slice_fusion.4
  210.3 0.8 dynamic-slice_bitcast_fusion
  212.4 5.8 %reduce-scatter.2.cloned.1.call-done = bf16[64,2048]{1,0:T(8,128)(2,1)} async-done(((bf16[1024,2048]{1,0:T(8,128)(2,1)}), bf16[64,2048]{1,0:T(8,128)(2,1)}) %reduce-scatter.2.cloned.1.call-update) | async-done | bytes 262160 | tf_op jit(solution)/shard_map/reduce_scatter | solution.py:952
  218.2 7.9 %normed_grads.2 = bf16[768,1024]{1,0:T(8,128)(2,1)} custom-call(s32[1]{0:T(128)} %bitcast.19.begin_ref, bf16[1536,1024]{1,0:T(8,128)(2,1)} %get-tuple-element.91.gate_ref, bf16[1536,1024]{1,0:T(8,128)(2,1)} %get-tuple-element.112.right_ref.inner_ref, bf16[1536,128]{1,0:T(8,128)(2,1)} %get-tuple-element.103.step_ref.gstep_ref, ...), custom_call_target="tpu_custom_call" | custom-call | tf_op jit(solution)/shard_map/normed_grads/pallas_call | solution.py:1035
  226.1 1.6 collective-permute-start.14
  228.3 0.8 copy.59
  229.1 0.8 slice.37
  229.8 0.8 copy-done.9
  230.6 8.4 %state_backward.1 = (bf16[1536,256]{1,0:T(8,128)(2,1)}, bf16[1024,384]{1,0:T(8,128)(2,1)}) custom-call(s32[1,1]{1,0:T(1,128)} %bitcast.rank_ref, s32[1,4]{1,0:T(1,128)} %len_ref.7, bf16[784,256]{1,0:T(8,128)(2,1)} %get-tuple-element.178.own_ref, bf16[784,256]{1,0:T(8,128)(2,1)} %copy-done.9, f32[1536,256]{1,0:T(8,128)} %get-tuple-element.105.spre_ref, ...), custom_call_target="tpu_custom_call" | custom-call | tf_op jit(solution)/shard_map/state_backward/pallas_call | solution.py:1067
  238.9 1.2 constant_dynamic-slice_fusion.1
  240.3 1.2 fusion.16
  241.6 0.9 collective-permute-start.15
  242.5 8.3 %normed_grads.3 = f32[768,1024]{1,0:T(8,128)} custom-call(s32[1]{0:T(128)} %bitcast.29.begin_ref, bf16[1536,1024]{1,0:T(8,128)(2,1)} %get-tuple-element.91.gate_ref, bf16[1536,1024]{1,0:T(8,128)(2,1)} %get-tuple-element.112.right_ref.inner_ref, bf16[1536,128]{1,0:T(8,128)(2,1)} %get-tuple-element.103.step_ref.gstep_ref, ...), custom_call_target="tpu_custom_call" | custom-call | tf_op jit(solution)/shard_map/normed_grads/pallas_call | solution.py:1035
  250.8 0.8 convert_bitcast_fusion
  251.7 1.3 collective-permute-start.17
  253.0 5.0 %fusion.7 = f32[768,1024]{1,0:T(8,128)} fusion(bf16[1024,2048]{1,0:T(8,128)(2,1)S(1)} %copy-done, bf16[1536,1024]{1,0:T(8,128)(2,1)} %get-tuple-element.114, s32[]{:T(128)S(6)} %select_n.125), kind=kOutput, calls=%fused_computation.17 | convolution fusion | flops 1610612736 | bytes 6815748 | tf_op jit(solution)/shard_map/dot_general | solution.py:33
  258.0 2.8 collective-permute-done.14
  260.8 1.0 fusion.22
  261.8 1.9 collective-permute-start.16
  263.8 1.2 collective-permute-start.18
  265.0 2.4 fusion.1
  267.4 5.1 %collective-permute-done.18 = bf16[2,64,384]{2,1,0:T(8,128)(2,1)S(1)} collective-permute-done((bf16[2,64,384]{2,1,0:T(8,128)(2,1)S(1)}, bf16[2,64,384]{2,1,0:T(8,128)(2,1)S(1)}, u32[]{:S(2)}, u32[]{:S(2)}) %collective-permute-start.18) | collective-permute-done | bytes 98336 | tf_op jit(solution)/shard_map/ppermute | solution.py:728
  272.6 2.3 collective-permute-start.19
  274.9 0.7 convert_add_fusion.6.inner_ref
  275.6 1.3 collective-permute-done.19
  277.6 2.0 finish.1
  279.6 1.5 collective-permute-start.20
  281.1 4.4 %fusion.4 = (f32[768,1024]{1,0:T(8,128)}, bf16[768,1024]{1,0:T(8,128)(2,1)}) fusion(bf16[768,1024]{1,0:T(8,128)(2,1)S(1)} %copy-done.2, bf16[768,1024]{1,0:T(8,128)(2,1)} %own_ref.3, f32[768,1024]{1,0:T(8,128)S(1)} %get-tuple-element.189, f32[768]{0:T(1024)S(1)} %broadcast_multiply_fusion, f32[768]{0:T(1024)S(1)} %get-tuple-element.188, ...), kind=kLoop, calls=%fused_computation.9 | loop fusion | flops 9437184 | bytes 15738624 | tf_op jit(solution)/shard_map/add | solution.py:1117
  286.1 1.6 unpack_small.1
  287.8 1.4 copy.51
  (93 shorter events, 8.7 us)
Async XLA Ops:
  7.2 20.1 %copy-start.1 = (bf16[768,1024]{1,0:T(8,128)(2,1)S(1)}, bf16[768,1024]{1,0:T(8,128)(2,1)}, u32[]{:S(2)}) copy-start(bf16[768,1024]{1,0:T(8,128)(2,1)} %own_ref.2) | copy-start | bytes 4718596
  7.2 20.2 %copy-start.12 = (bf16[1024,64]{0,1:T(8,128)(2,1)S(1)}, bf16[1024,64]{0,1:T(8,128)(2,1)}, u32[]{:S(2)}) copy-start(bf16[1024,64]{0,1:T(8,128)(2,1)} %param.29) | copy-start | bytes 393220
  7.2 91.7 %all-gather.2.cloned.1.call-start = ((), (), s32[]{:S(2)}) async-start(), calls=%async_computation.1 | async-start | bytes 4456448 | tf_op jit(solution)/shard_map/all_gather | solution.py:846
  12.7 12.7 %collective-permute-start.4 = (bf16[64,1408]{1,0:T(8,128)(2,1)}, bf16[64,1408]{1,0:T(8,128)(2,1)S(1)}, u32[]{:S(2)}, u32[]{:S(2)}) collective-permute-start(bf16[64,1408]{1,0:T(8,128)(2,1)} %pack_small.1), channel_id=1, source_target_pairs={{0,16},{2,18},{4,20},{6,22},{8,24},{10,26},{12,28},{14,30},{16,0},... | collective-permute-start | bytes 540680 | tf_op jit(solution)/shard_map/ppermute | solution.py:728
  17.7 8.7 %collective-permute-start = (bf16[128,1024]{1,0:T(8,128)(2,1)S(1)}, bf16[128,1024]{1,0:T(8,128)(2,1)S(1)}, u32[]{:S(2)}, u32[]{:S(2)}) collective-permute-start(bf16[128,1024]{1,0:T(8,128)(2,1)S(1)} %slice.32), channel_id=1, source_target_pairs={{0,1},{1,0},{2,3},{3,2},{4,5},{5,4},{6,7},{7,6},{8,9},{9,8},{10,11... | collective-permute-start | bytes 786440 | tf_op jit(solution)/shard_map/ppermute | solution.py:816
  26.4 9.7 %collective-permute-start.5 = (bf16[2,64,1408]{2,1,0:T(8,128)(2,1)S(1)}, bf16[2,64,1408]{2,1,0:T(8,128)(2,1)S(1)}, u32[]{:S(2)}, u32[]{:S(2)}) collective-permute-start(bf16[2,64,1408]{2,1,0:T(8,128)(2,1)S(1)} %pad_maximum_fusion.5), channel_id=1, source_target_pairs={{0,8},{2,10},{4,12},{6,14},{8,0},{10,2},{12,4},{14,6},{16,24},{18,... | collective-permute-start | bytes 1081352 | tf_op jit(solution)/shard_map/ppermute | solution.py:728
  28.1 10.9 %collective-permute-start.1 = (bf16[192,1024]{1,0:T(8,128)(2,1)S(1)}, bf16[192,1024]{1,0:T(8,128)(2,1)}, u32[]{:S(2)}, u32[]{:S(2)}) collective-permute-start(bf16[192,1024]{1,0:T(8,128)(2,1)S(1)} %slice.31), channel_id=1, source_target_pairs={{0,1},{1,0},{2,3},{3,2},{4,5},{5,4},{6,7},{7,6},{8,9},{9,8},{10,11... | collective-permute-start | bytes 1179656 | tf_op jit(solution)/shard_map/ppermute | solution.py:816
  39.0 179.2 %reduce-scatter.2.cloned.1.call-start = ((), (), s32[]{:S(2)}) async-start(), calls=%async_computation.2 | async-start | bytes 4456448 | tf_op jit(solution)/shard_map/reduce_scatter | solution.py:952
  39.0 19.9 %collective-permute-start.6 = (bf16[2,2,64,1408]{3,2,0,1:T(8,128)(2,1)S(1)}, bf16[2,2,64,1408]{3,2,0,1:T(8,128)(2,1)}, u32[]{:S(2)}, u32[]{:S(2)}) collective-permute-start(bf16[2,2,64,1408]{3,2,0,1:T(8,128)(2,1)S(1)} %pad_maximum_fusion.4), channel_id=1, source_target_pairs={{0,4},{2,6},{4,0},{6,2},{8,12},{10,14},{12,8},{14,10},{16,20},{18,... | collective-permute-start | bytes 2162696 | tf_op jit(solution)/shard_map/ppermute | solution.py:728
  40.6 21.0 %copy-start.14 = (bf16[16]{0:T(256)(128)(2,1)S(1)}, bf16[16]{0:T(256)(128)(2,1)}, u32[]{:S(2)}) copy-start(bf16[16]{0:T(256)(128)(2,1)} %param.26) | copy-start | bytes 100
  40.6 21.0 %copy-start.15 = (bf16[16]{0:T(256)(128)(2,1)S(1)}, bf16[16]{0:T(256)(128)(2,1)}, u32[]{:S(2)}) copy-start(bf16[16]{0:T(256)(128)(2,1)} %param.27) | copy-start | bytes 100
  40.7 22.6 %copy-start.18 = (bf16[16]{0:T(256)(128)(2,1)S(1)}, bf16[16]{0:T(256)(128)(2,1)}, u32[]{:S(2)}) copy-start(bf16[16]{0:T(256)(128)(2,1)} %param.25) | copy-start | bytes 100
  40.7 21.0 %collective-permute-start.2 = (bf16[448,1024]{1,0:T(8,128)(2,1)S(1)}, bf16[448,1024]{1,0:T(8,128)(2,1)}, u32[]{:S(2)}, u32[]{:S(2)}) collective-permute-start(bf16[448,1024]{1,0:T(8,128)(2,1)S(1)} %slice.30), channel_id=1, source_target_pairs={{0,1},{1,0},{2,3},{3,2},{4,5},{5,4},{6,7},{7,6},{8,9},{9,8},{10,11... | collective-permute-start | bytes 2752520 | tf_op jit(solution)/shard_map/ppermute | solution.py:816
  61.7 4.9 %collective-permute-start.7 = (bf16[2,2,2,64,1408]{4,3,0,1,2:T(8,128)(2,1)S(1)}, bf16[2,2,2,64,1408]{4,3,0,1,2:T(8,128)(2,1)S(1)}, u32[]{:S(2)}, u32[]{:S(2)}) collective-permute-start(bf16[2,2,2,64,1408]{4,3,0,1,2:T(8,128)(2,1)S(1)} %pad_maximum_fusion.3), channel_id=1, source_target_pairs={{0,2},{2,0},{4,6},{6,4},{8,10},{10,8},{12,14},{14,12},{16,18},{18,... | collective-permute-start | bytes 4325384 | tf_op jit(solution)/shard_map/ppermute | solution.py:728
  61.7 37.2 %collective-permute-start.3 = (bf16[768,1024]{1,0:T(8,128)(2,1)}, bf16[768,1024]{1,0:T(8,128)(2,1)}, u32[]{:S(2)}, u32[]{:S(2)}) collective-permute-start(bf16[768,1024]{1,0:T(8,128)(2,1)} %own_ref.3), channel_id=1, source_target_pairs={{0,1},{1,0},{2,3},{3,2},{4,5},{5,4},{6,7},{7,6},{8,9},{9,8},{10,11... | collective-permute-start | bytes 4718600 | tf_op jit(solution)/shard_map/ppermute | solution.py:816
  115.4 4.4 %collective-permute-start.8 = (f32[8,1536]{1,0:T(8,128)}, f32[8,1536]{1,0:T(8,128)S(1)}, u32[]{:S(2)}, u32[]{:S(2)}) collective-permute-start(f32[8,1536]{1,0:T(8,128)} %get-tuple-element.85.own_sums_ref), channel_id=1, source_target_pairs={{0,1},{1,0},{2,3},{3,2},{4,5},{5,4},{6,7},{7,6},{8,9},{9,8},{10,11... | collective-permute-start | bytes 147464 | tf_op jit(solution)/shard_map/ppermute | solution.py:816
  119.8 0.6 copy-start.17
  120.4 13.3 %copy-start.19 = (bf16[1024,1536]{1,0:T(8,128)(2,1)S(1)}, bf16[1024,1536]{1,0:T(8,128)(2,1)}, u32[]{:S(2)}) copy-start(bf16[1024,1536]{1,0:T(8,128)(2,1)} %get-tuple-element.89) | copy-start | bytes 9437188
  133.8 5.7 %copy-start.3 = (bf16[1024,1536]{1,0:T(8,128)(2,1)S(1)}, bf16[1024,1536]{1,0:T(8,128)(2,1)}, u32[]{:S(2)}) copy-start(bf16[1024,1536]{1,0:T(8,128)(2,1)} %get-tuple-element.90.left_ref.normed_t_ref) | copy-start | bytes 9437188
  133.8 5.7 %copy-start.5 = (bf16[1536,1024]{1,0:T(8,128)(2,1)S(1)}, bf16[1536,1024]{1,0:T(8,128)(2,1)}, u32[]{:S(2)}) copy-start(bf16[1536,1024]{1,0:T(8,128)(2,1)} %get-tuple-element.91.gate_ref) | copy-start | bytes 9437188
  149.4 47.9 %collective-permute-start.10 = (bf16[768,1024]{1,0:T(8,128)(2,1)S(1)}, bf16[768,1024]{1,0:T(8,128)(2,1)S(1)}, u32[]{:S(2)}, u32[]{:S(2)}) collective-permute-start(bf16[768,1024]{1,0:T(8,128)(2,1)S(1)} %fusion.11), channel_id=1, source_target_pairs={{0,1},{1,0},{2,3},{3,2},{4,5},{5,4},{6,7},{7,6},{8,9},{9,8},{10,11... | collective-permute-start | bytes 4718600 | tf_op jit(solution)/shard_map/ppermute | solution.py:816
  197.3 8.0 %copy-start.8 = (bf16[768,1024]{1,0:T(8,128)(2,1)}, bf16[768,1024]{1,0:T(8,128)(2,1)S(1)}, u32[]{:S(2)}) copy-start(bf16[768,1024]{1,0:T(8,128)(2,1)S(1)} %collective-permute-done.10) | copy-start | bytes 4718596
  207.1 4.6 %copy-start.13 = (s32[1,4]{1,0:T(1,128)S(1)}, s32[1,4]{1,0:T(1,128)}, u32[]{:S(2)}) copy-start(s32[1,4]{1,0:T(1,128)} %len_ref.7) | copy-start | bytes 52
  207.1 2.7 collective-permute-start.11
  209.3 20.5 %collective-permute-start.9 = (bf16[784,256]{1,0:T(8,128)(2,1)}, bf16[784,256]{1,0:T(8,128)(2,1)S(1)}, u32[]{:S(2)}, u32[]{:S(2)}) collective-permute-start(bf16[784,256]{1,0:T(8,128)(2,1)} %get-tuple-element.177), channel_id=1, source_target_pairs={{0,1},{1,0},{2,3},{3,2},{4,5},{5,4},{6,7},{7,6},{8,9},{9,8},{10,11... | collective-permute-start | bytes 1204232 | tf_op jit(solution)/shard_map/ppermute | solution.py:816
  211.1 29.2 %collective-permute-start.13 = (bf16[2,2,64,1024]{3,2,0,1:T(8,128)(2,1)}, bf16[2,2,64,1024]{3,2,0,1:T(8,128)(2,1)}, u32[]{:S(2)}, u32[]{:S(2)}) collective-permute-start(bf16[2,2,64,1024]{3,2,0,1:T(8,128)(2,1)} %dynamic-slice_bitcast_fusion), channel_id=1, source_target_pairs={{0,4},{2,6},{4,0},{6,2},{8,12},{10,14},{12,8},{14,10},{16,20},{18,... | collective-permute-start | bytes 1572872 | tf_op jit(solution)/shard_map/ppermute | solution.py:728
  218.2 10.1 %copy-start.7 = (bf16[64,2,1024]{2,1,0:T(2,128)(2,1)S(1)}, bf16[64,2,1024]{2,1,0:T(2,128)(2,1)}, u32[]{:S(2)}) copy-start(bf16[64,2,1024]{2,1,0:T(2,128)(2,1)} %param.18) | copy-start | bytes 786436
  226.1 34.7 %collective-permute-start.14 = (bf16[768,1024]{1,0:T(8,128)(2,1)}, bf16[768,1024]{1,0:T(8,128)(2,1)S(1)}, u32[]{:S(2)}, u32[]{:S(2)}) collective-permute-start(bf16[768,1024]{1,0:T(8,128)(2,1)} %normed_grads.2), channel_id=1, source_target_pairs={{0,1},{1,0},{2,3},{3,2},{4,5},{5,4},{6,7},{7,6},{8,9},{9,8},{10,11... | collective-permute-start | bytes 4718600 | tf_op jit(solution)/shard_map/ppermute | solution.py:816
  229.8 0.8 copy-start.9
  240.2 11.4 %collective-permute-start.12 = (bf16[2,2,2,64,384]{4,3,2,0,1:T(8,128)(2,1)S(1)}, bf16[2,2,2,64,384]{4,3,2,0,1:T(8,128)(2,1)S(1)}, u32[]{:S(2)}, u32[]{:S(2)}) collective-permute-start(bf16[2,2,2,64,384]{4,3,2,0,1:T(8,128)(2,1)S(1)} %bitcast.115), channel_id=1, source_target_pairs={{0,2},{2,0},{4,6},{6,4},{8,10},{10,8},{12,14},{14,12},{16,18},{18,... | collective-permute-start | bytes 1179656 | tf_op jit(solution)/shard_map/ppermute | solution.py:728
  241.6 16.4 %collective-permute-start.15 = (bf16[2,64,1024]{2,1,0:T(8,128)(2,1)S(1)}, bf16[2,64,1024]{2,1,0:T(8,128)(2,1)}, u32[]{:S(2)}, u32[]{:S(2)}) collective-permute-start(bf16[2,64,1024]{2,1,0:T(8,128)(2,1)S(1)} %dynamic-slice_bitcast_fusion.1), channel_id=1, source_target_pairs={{0,8},{2,10},{4,12},{6,14},{8,0},{10,2},{12,4},{14,6},{16,24},{18,... | collective-permute-start | bytes 786440 | tf_op jit(solution)/shard_map/ppermute | solution.py:728
  242.5 8.3 %copy-start.10 = (bf16[64,2048]{1,0:T(8,128)(2,1)S(1)}, bf16[64,2048]{1,0:T(8,128)(2,1)}, u32[]{:S(2)}) copy-start(bf16[64,2048]{1,0:T(8,128)(2,1)} %reduce-scatter.2.cloned.1.call-done) | copy-start | bytes 786436
  242.5 10.5 %copy-start = (bf16[1024,2048]{1,0:T(8,128)(2,1)S(1)}, bf16[1024,2048]{1,0:T(8,128)(2,1)}, u32[]{:S(2)}) copy-start(bf16[1024,2048]{1,0:T(8,128)(2,1)} %all-gather.2.cloned.1.call-done.w_ref.proj_ref.w_gate_ref) | copy-start | bytes 12582916
  251.7 13.3 %copy-start.2 = (bf16[768,1024]{1,0:T(8,128)(2,1)S(1)}, bf16[768,1024]{1,0:T(8,128)(2,1)}, u32[]{:S(2)}) copy-start(bf16[768,1024]{1,0:T(8,128)(2,1)} %own_ref.2) | copy-start | bytes 4718596
  251.7 13.3 %copy-start.11 = (bf16[1536,256]{1,0:T(8,128)(2,1)S(1)}, bf16[1536,256]{1,0:T(8,128)(2,1)}, u32[]{:S(2)}) copy-start(bf16[1536,256]{1,0:T(8,128)(2,1)} %get-tuple-element.116) | copy-start | bytes 2359300
  251.7 12.0 %collective-permute-start.17 = (bf16[2,2,64,384]{3,2,1,0:T(8,128)(2,1)S(1)}, bf16[2,2,64,384]{3,2,1,0:T(8,128)(2,1)S(1)}, u32[]{:S(2)}, u32[]{:S(2)}) collective-permute-start(bf16[2,2,64,384]{3,2,1,0:T(8,128)(2,1)S(1)} %dynamic-slice_bitcast_fusion.2), channel_id=1, source_target_pairs={{0,8},{2,10},{4,12},{6,14},{8,0},{10,2},{12,4},{14,6},{16,24},{18,... | collective-permute-start | bytes 589832 | tf_op jit(solution)/shard_map/ppermute | solution.py:728
  253.0 12.0 %copy-start.4 = (f32[768,1024]{1,0:T(8,128)S(1)}, f32[768,1024]{1,0:T(8,128)}, u32[]{:S(2)}) copy-start(f32[768,1024]{1,0:T(8,128)} %normed_grads.3) | copy-start | bytes 9437188
  261.8 13.0 %collective-permute-start.16 = (bf16[64,1024]{1,0:T(8,128)(2,1)S(1)}, bf16[64,1024]{1,0:T(8,128)(2,1)S(1)}, u32[]{:S(2)}, u32[]{:S(2)}) collective-permute-start(bf16[64,1024]{1,0:T(8,128)(2,1)S(1)} %dynamic-slice_bitcast_fusion.3), channel_id=1, source_target_pairs={{0,16},{2,18},{4,20},{6,22},{8,24},{10,26},{12,28},{14,30},{16,0},... | collective-permute-start | bytes 393224 | tf_op jit(solution)/shard_map/ppermute | solution.py:728
  263.8 8.7 %collective-permute-start.18 = (bf16[2,64,384]{2,1,0:T(8,128)(2,1)S(1)}, bf16[2,64,384]{2,1,0:T(8,128)(2,1)S(1)}, u32[]{:S(2)}, u32[]{:S(2)}) collective-permute-start(bf16[2,64,384]{2,1,0:T(8,128)(2,1)S(1)} %dynamic-slice_bitcast_fusion.4), channel_id=1, source_target_pairs={{0,16},{2,18},{4,20},{6,22},{8,24},{10,26},{12,28},{14,30},{16,0},... | collective-permute-start | bytes 294920 | tf_op jit(solution)/shard_map/ppermute | solution.py:728
  267.4 13.8 %copy-start.6 = (f32[768,1024]{1,0:T(8,128)S(1)}, f32[768,1024]{1,0:T(8,128)}, u32[]{:S(2)}) copy-start(f32[768,1024]{1,0:T(8,128)} %fusion.7) | copy-start | bytes 9437188
  272.6 4.4 %collective-permute-start.19 = (bf16[64,384]{1,0:T(8,128)(2,1)S(1)}, bf16[64,384]{1,0:T(8,128)(2,1)S(1)}, u32[]{:S(2)}, u32[]{:S(2)}) collective-permute-start(bf16[64,384]{1,0:T(8,128)(2,1)S(1)} %dynamic-slice_bitcast_fusion.5), channel_id=1, source_target_pairs={{0,4},{2,6},{4,0},{6,2},{8,12},{10,14},{12,8},{14,10},{16,20},{18,... | collective-permute-start | bytes 147464 | tf_op jit(solution)/shard_map/ppermute | solution.py:728
  279.6 5.9 %collective-permute-start.20 = (f32[64,384]{1,0:T(8,128)}, f32[64,384]{1,0:T(8,128)S(1)}, u32[]{:S(2)}, u32[]{:S(2)}) collective-permute-start(f32[64,384]{1,0:T(8,128)} %get-tuple-element.122.own_ref), channel_id=1, source_target_pairs={{0,1},{1,0},{2,3},{3,2},{4,5},{5,4},{6,7},{7,6},{8,9},{9,8},{10,11... | collective-permute-start | bytes 294920 | tf_op jit(solution)/shard_map/ppermute | solution.py:816
  285.5 0.6 copy-start.16
Sparse Core Ops, SparseCore 0:
  39.1 54.0 all-gather.1
  145.6 72.4 reduce-scatter.1
